TPU v7x, 128 devices: a whole 4x4x4 slice. The times are simulated.
128 devices in a mesh: dp: 16 (over z_lo, y, core), expert: 8 (over x, z_hi).
Axes of the slice: x: 4, y: 4, z: 4 (z_hi: 2, z_lo: 2; z = z_hi * 2 + z_lo), core: 2. Of those that a mesh axis runs over, the one named last changes fastest.
Arguments:
- tokens: bfloat16 [2, 8, 1280, 1536], P(None, 'expert', 'dp'), may hold values from -6 to 6
- lengths: int32 [2, 8, 3], P(None, 'expert'), may hold values from 1 to 1200, as said below
- routes: int32 [2, 8, 1280, 6], P(None, 'expert', 'dp'), may hold values from 0 to 15, all different within a row; in each aligned block of 80 rows (0 to 79, 80 to 159, ..., all dimensions but the last counted through in order) at most 45 rows name the same one
- cotangent: bfloat16 [2, 8, 1280, 1536], P(None, 'expert', 'dp'), may hold values from -6 to 6
- input_weight: bfloat16 [1536, 6448], P('dp'), may hold values from -0.15625 to 0.15625
- filter_weight: float32 [4, 3328], replicated, may hold values from -3 to 3
- filter_bias: float32 [3328], replicated, may hold values from -3 to 3
- step_bias: float32 [48], replicated, may hold values from -6.9 to -2.25
- decay_log: float32 [48], replicated, may hold values from 0 to 3
- skip_gain: float32 [48], replicated, may hold values from 0.5 to 1.5
- norm_gain: float32 [1536], replicated, may hold values from 0.5 to 1.5
- gated_gain: float32 [3072], replicated, may hold values from 0.5 to 1.5
- output_weight: bfloat16 [3072, 1536], P('dp'), may hold values from -0.109375 to 0.109375
- moe_gain: float32 [1536], replicated, may hold values from 0.5 to 1.5
- router_weight: bfloat16 [1536, 16], P('dp'), may hold values from -0.078125 to 0.078125
- shared_gate_up: bfloat16 [1536, 2048], P('dp'), may hold values from -0.15625 to 0.15625
- shared_down: bfloat16 [1024, 1536], P('dp'), may hold values from -0.375 to 0.375
- expert_gate_up: bfloat16 [16, 1536, 1024], P('expert'), may hold values from -0.15625 to 0.15625
- expert_down: bfloat16 [16, 512, 1536], P('expert'), may hold values from -1 to 1
Outputs:
- block_output: bfloat16 [2, 8, 1280, 1536], P(None, 'expert', 'dp')
- tokens_grad: float32 [2, 8, 1280, 1536], P(None, 'expert', 'dp')
- input_weight_grad: float32 [1536, 6448], P('dp')
- filter_weight_grad: float32 [4, 3328], replicated
- filter_bias_grad: float32 [3328], replicated
- step_bias_grad: float32 [48], replicated
- decay_log_grad: float32 [48], replicated
- skip_gain_grad: float32 [48], replicated
- norm_gain_grad: float32 [1536], replicated
- gated_gain_grad: float32 [3072], replicated
- output_weight_grad: float32 [3072, 1536], P('dp')
- moe_gain_grad: float32 [1536], replicated
- router_weight_grad: float32 [1536, 16], P('dp')
- shared_gate_up_grad: float32 [1536, 2048], P('dp')
- shared_down_grad: float32 [1024, 1536], P('dp')
- expert_gate_up_grad: float32 [16, 1536, 1024], P('expert', 'dp')
- expert_down_grad: float32 [16, 512, 1536], P('expert', 'dp')
Inputs may be any that keep to these rules, and one draw needn't show every extreme that they name: Each row gives the lengths of the three documents packed in order into one group's 1280 positions; the first and the last have 80 tokens together, each at least 1, so the middle one has 1200. `routes`: each row names 6 different experts. Within the rows of one device (aligned blocks of 80 rows) no expert is named by more than 45 rows, and in some blocks one expert is named by exactly 45.
All inputs are finite; a program needn't handle non-finite values.
Results may differ from a plain program's by a relative error of at most 0.024.
Values may be sent and summed in bfloat16 or wider, within the bound.
A program may use at most 384 MiB of HBM per device.

v0:
```python
import jax
import jax.numpy as jnp
from jax import lax
from jax.sharding import PartitionSpec as P

D = 1536
H = 48
P_SIZE = 64
S = 128
K = 4
FE = 512
FS = 1024
TOP = 6
MB = 2
DI = 3072
CONV = 3328
IN_W = 6448


HIGHEST = lax.Precision.HIGHEST
EPSILON = 1e-05


def shifted(value, axis, steps):
    count = lax.axis_size(axis)
    first, last = (max(0, -steps), min(count, count - steps))
    return lax.ppermute(value, axis, [(source, source + steps) for source in range(first, last)])


def prefix(shard, axis, combine, identity):
    count, position = (lax.axis_size(axis), lax.axis_index(axis))
    everything = jax.tree.map(lambda part: lax.all_gather(part, axis), shard)
    start = jax.tree.map(
        lambda part, zero: jnp.broadcast_to(jnp.asarray(zero, part.dtype), part.shape),
        shard,
        identity,
    )

    def hop(k, before):
        reached = k < position
        new = combine(before, jax.tree.map(lambda part: part[k], everything))
        return jax.tree.map(lambda a, b: jnp.where(reached, a, b), new, before)

    return lax.fori_loop(0, count, hop, start)


def carried_in(shard, axis, join, neutral):
    count = lax.axis_size(axis)
    place = lax.axis_index(axis)
    ahead = count - 1 - place
    gathered = jax.tree.map(
        lambda a, kind: lax.all_gather(a.astype(kind), axis),
        shard,
        jax.tree.map(lambda a: jnp.bfloat16 if a.dtype == jnp.float32 else a.dtype, shard),
    )
    state = jax.tree.map(lambda a, e: jnp.zeros_like(a) + jnp.asarray(e, a.dtype), shard, neutral)

    def one(hop, state):
        source = count - 1 - hop
        return join(
            state,
            jax.tree.map(
                lambda a, own: lax.dynamic_index_in_dim(a, source, 0, False).astype(own.dtype),
                gathered,
                shard,
            ),
        )

    return lax.fori_loop(0, ahead, one, state)


def rms_scale(values, gain):
    return values * lax.rsqrt(jnp.mean(values * values, axis=-1, keepdims=True) + EPSILON) * gain


def doc_number(positions, lengths_row):
    first = (positions >= lengths_row[0]).astype(jnp.int32)
    return first + (positions >= lengths_row[0] + lengths_row[1]).astype(jnp.int32)


def filter_apply(extended, filter_weight, filter_bias, docs_ext, docs):
    count = docs.shape[0]
    total = jnp.zeros((count, CONV), jnp.float32) + filter_bias[None, :]
    for offset in range(K):
        same_doc = (docs_ext[offset : offset + count] == docs).astype(jnp.float32)
        total = (
            total
            + same_doc[:, None] * filter_weight[offset][None, :] * extended[offset : offset + count]
        )
    return jax.nn.silu(total)


def prepare(filtered, step_raw, step_bias):
    count = filtered.shape[0]
    head_inputs = filtered[:, :DI].reshape(count, H, P_SIZE)
    write_proj = filtered[:, DI : DI + S]
    read_proj = filtered[:, DI + S :]
    step_size = jax.nn.softplus(step_raw + step_bias[None, :])
    return (head_inputs, write_proj, read_proj, step_size)


def block_cumulative(step_size, decay_log):
    return jnp.cumsum(step_size * (-jnp.exp(decay_log))[None, :], axis=0)


def carry_terms(head_inputs, write_proj, step_size, cumulative, docs, keep_last):
    last = cumulative[-1]
    same_last = (docs == docs[-1]).astype(jnp.float32)
    weight = jnp.exp(last[None, :] - cumulative) * same_last[:, None] * step_size
    scaled = head_inputs * weight[:, :, None]
    state = jnp.einsum("shp,sn->hpn", scaled, write_proj, precision=HIGHEST)
    return (jnp.exp(last) * keep_last, state)


def scan_readout(
    head_inputs, write_proj, read_proj, step_size, cumulative, docs, keep, state_in, skip_gain
):
    count = docs.shape[0]
    scores = jnp.dot(read_proj, write_proj.T, precision=HIGHEST)
    rows = lax.broadcasted_iota(jnp.int32, (count, count), 0)
    cols = lax.broadcasted_iota(jnp.int32, (count, count), 1)
    allowed = (cols <= rows) & (docs[:, None] == docs[None, :])
    spans = cumulative.T[:, :, None] - cumulative.T[:, None, :]
    weights = jnp.exp(jnp.where(allowed[None], spans, -1e30)) * scores[None]
    scaled = head_inputs * step_size[:, :, None]
    inner = jnp.einsum("hts,shp->thp", weights, scaled, precision=HIGHEST)
    carry_gate = jnp.exp(cumulative) * keep[:, None]
    carried = (
        jnp.einsum("tn,hpn->thp", read_proj, state_in, precision=HIGHEST) * carry_gate[:, :, None]
    )
    return inner + carried + skip_gain[None, :, None] * head_inputs


def chain_states(earlier, later):
    return (earlier[0] * later[0], later[0][:, None, None] * earlier[1] + later[1])


def body(
    tokens,
    lengths,
    routes,
    cotangent,
    input_weight,
    filter_weight,
    filter_bias,
    step_bias,
    decay_log,
    skip_gain,
    norm_gain,
    gated_gain,
    output_weight,
    moe_gain,
    router_weight,
    shared_gate_up,
    shared_down,
    expert_gate_up,
    expert_down,
):
    local = tokens.shape[2]
    expert_local = expert_gate_up.shape[0]
    expert_groups = lax.axis_size("expert")
    expert_count = expert_local * expert_groups
    capacity = min(local, 3 * local * TOP // (2 * expert_count))
    device_start = lax.axis_index("dp") * local
    positions = device_start + jnp.arange(local, dtype=jnp.int32)
    rim_positions = device_start - (K - 1) + jnp.arange(local + K - 1, dtype=jnp.int32)
    expert_ids = jnp.arange(expert_count, dtype=jnp.int32)
    identity = (jnp.ones((H,), jnp.float32), jnp.zeros((H, P_SIZE, S), jnp.float32))
    input_acc = jnp.zeros((D, IN_W), jnp.float32)
    output_acc = jnp.zeros((DI, D), jnp.float32)
    router_acc = jnp.zeros((D, expert_count), jnp.float32)
    shared_up_acc = jnp.zeros((D, 2 * FS), jnp.float32)
    shared_down_acc = jnp.zeros((FS, D), jnp.float32)
    expert_up_acc = jnp.zeros((expert_local, D, 2 * FE), jnp.float32)
    expert_down_acc = jnp.zeros((expert_local, FE, D), jnp.float32)
    filter_weight_acc = jnp.zeros_like(filter_weight)
    filter_bias_acc = jnp.zeros_like(filter_bias)
    step_bias_acc = jnp.zeros_like(step_bias)
    decay_acc = jnp.zeros_like(decay_log)
    skip_acc = jnp.zeros_like(skip_gain)
    norm_acc = jnp.zeros_like(norm_gain)
    gated_acc = jnp.zeros_like(gated_gain)
    moe_gain_acc = jnp.zeros_like(moe_gain)
    block_rows = []
    stream_grads = []
    for micro in range(MB):
        in_full, out_full, router_full, shared_up_full, shared_down_full = (
            lax.all_gather(input_weight, "dp", axis=0, tiled=True),
            lax.all_gather(output_weight, "dp", axis=0, tiled=True),
            lax.all_gather(router_weight, "dp", axis=0, tiled=True),
            lax.all_gather(shared_gate_up, "dp", axis=0, tiled=True),
            lax.all_gather(shared_down, "dp", axis=0, tiled=True),
        )
        stream = tokens[micro, 0].astype(jnp.float32)
        lengths_row = lengths[micro, 0]
        route_rows = routes[micro, 0]
        docs = doc_number(positions, lengths_row)
        docs_ext = doc_number(rim_positions, lengths_row)
        keep = (docs == doc_number(device_start - 1, lengths_row)).astype(jnp.float32)
        normed_wide, norm_pull = jax.vjp(rms_scale, stream, norm_gain)
        normed = normed_wide.astype(jnp.bfloat16)
        projected = jnp.dot(normed, in_full, preferred_element_type=jnp.float32)
        gate_part = projected[:, :DI]
        filter_in = projected[:, DI : DI + CONV].astype(jnp.bfloat16)
        step_raw = projected[:, DI + CONV :]
        rim_rows = shifted(filter_in[local - (K - 1) :], "dp", 1)
        extended = jnp.concatenate([rim_rows, filter_in], axis=0).astype(jnp.float32)

        def mixer_front(ext_values, raw_steps, taps, tap_bias, bias_steps, decay_values):
            filtered = filter_apply(ext_values, taps, tap_bias, docs_ext, docs)
            head_inputs, write_proj, read_proj, step_size = prepare(filtered, raw_steps, bias_steps)
            return (
                head_inputs,
                write_proj,
                read_proj,
                step_size,
                block_cumulative(step_size, decay_values),
            )

        front_out, front_pull = jax.vjp(
            mixer_front, extended, step_raw, filter_weight, filter_bias, step_bias, decay_log
        )
        head_inputs, write_proj, read_proj, step_size, cumulative = front_out

        def carry_part(inputs_now, write_now, steps_now, cumulative_now):
            return carry_terms(inputs_now, write_now, steps_now, cumulative_now, docs, keep[-1])

        carry_out, carry_pull = jax.vjp(carry_part, head_inputs, write_proj, step_size, cumulative)
        decay_total = carry_out[0]
        _, state_in = prefix(carry_out, "dp", chain_states, identity)

        def readout(
            inputs_now,
            write_now,
            read_now,
            steps_now,
            cumulative_now,
            state_now,
            skip_now,
            gate_now,
            gain_now,
        ):
            scan_out = scan_readout(
                inputs_now,
                write_now,
                read_now,
                steps_now,
                cumulative_now,
                docs,
                keep,
                state_now,
                skip_now,
            )
            return rms_scale(scan_out.reshape(local, DI) * jax.nn.silu(gate_now), gain_now)

        gated_wide, readout_pull = jax.vjp(
            readout,
            head_inputs,
            write_proj,
            read_proj,
            step_size,
            cumulative,
            state_in,
            skip_gain,
            gate_part,
            gated_gain,
        )
        gated = gated_wide.astype(jnp.bfloat16)
        mixer = jnp.dot(gated, out_full, preferred_element_type=jnp.float32)
        after_mixer = stream + mixer
        moe_wide, moe_norm_pull = jax.vjp(rms_scale, after_mixer, moe_gain)
        moe_in = moe_wide.astype(jnp.bfloat16)
        logits = jnp.dot(moe_in, router_full, preferred_element_type=jnp.float32)

        def gating(values):
            return jax.nn.softmax(jnp.take_along_axis(values, route_rows, axis=1), axis=1)

        gates, gating_pull = jax.vjp(gating, logits)
        shared_pre = jnp.dot(moe_in, shared_up_full, preferred_element_type=jnp.float32)

        def shared_act(values):
            return jax.nn.silu(values[:, :FS]) * values[:, FS:]

        shared_wide, shared_pull = jax.vjp(shared_act, shared_pre)
        shared_hidden = shared_wide.astype(jnp.bfloat16)
        shared_out = jnp.dot(shared_hidden, shared_down_full, preferred_element_type=jnp.float32)
        chosen = (route_rows[:, :, None] == expert_ids[None, None, :]).astype(jnp.int32)
        per_expert = jnp.sum(chosen, axis=1)
        earlier_count = jnp.cumsum(per_expert, axis=0) - per_expert
        rank = jnp.sum(chosen * earlier_count[:, None, :], axis=2)
        flat_slot = (route_rows * capacity + rank).reshape(-1)
        outgoing = (
            jnp.zeros((expert_count * capacity, D), jnp.bfloat16)
            .at[flat_slot]
            .set(jnp.repeat(moe_in, TOP, axis=0))
            .reshape(expert_groups, expert_local, capacity, D)
        )
        arrived = lax.all_to_all(outgoing, "expert", split_axis=0, concat_axis=0, tiled=True)
        gate_up = jnp.einsum(
            "necd,edf->necf", arrived, expert_gate_up, preferred_element_type=jnp.float32
        )
        hidden = (jax.nn.silu(gate_up[..., :FE]) * gate_up[..., FE:]).astype(jnp.bfloat16)
        result = jnp.einsum(
            "necf,efd->necd", hidden, expert_down, preferred_element_type=jnp.float32
        ).astype(jnp.bfloat16)
        returned_piece = lax.all_to_all(result, "expert", split_axis=0, concat_axis=0, tiled=True)
        returned_rows = (
            returned_piece.reshape(expert_count * capacity, D)[flat_slot]
            .reshape(local, TOP, D)
            .astype(jnp.float32)
        )
        moe_sum = jnp.einsum("tk,tkd->td", gates, returned_rows, precision=HIGHEST)
        block_rows.append((after_mixer + moe_sum + shared_out).astype(jnp.bfloat16))
        incoming = cotangent[micro, 0].astype(jnp.float32)
        row_grads = (gates[:, :, None] * incoming[:, None, :]).astype(jnp.bfloat16)
        gate_grads = jnp.einsum("td,tkd->tk", incoming, returned_rows, precision=HIGHEST)
        held = lax.optimization_barrier(
            (input_weight, output_weight, router_weight, shared_gate_up, shared_down, gate_grads)
        )
        in_full, out_full, router_full, shared_up_full, shared_down_full = (
            lax.all_gather(held[0], "dp", axis=0, tiled=True),
            lax.all_gather(held[1], "dp", axis=0, tiled=True),
            lax.all_gather(held[2], "dp", axis=0, tiled=True),
            lax.all_gather(held[3], "dp", axis=0, tiled=True),
            lax.all_gather(held[4], "dp", axis=0, tiled=True),
        )
        back_slots = (
            jnp.zeros((expert_count * capacity, D), jnp.bfloat16)
            .at[flat_slot]
            .set(row_grads.reshape(local * TOP, D))
            .reshape(expert_groups, expert_local, capacity, D)
        )
        arrived_grads = lax.all_to_all(
            back_slots, "expert", split_axis=0, concat_axis=0, tiled=True
        )

        def expert_act(values):
            return jax.nn.silu(values[..., :FE]) * values[..., FE:]

        hidden_again, act_pull = jax.vjp(expert_act, gate_up)
        hidden_low = hidden_again.astype(jnp.bfloat16)
        expert_down_acc = expert_down_acc + jnp.einsum(
            "necf,necd->efd", hidden_low, arrived_grads, preferred_element_type=jnp.float32
        )
        hidden_grad = jnp.einsum(
            "necd,efd->necf", arrived_grads, expert_down, preferred_element_type=jnp.float32
        )
        pre_low = act_pull(hidden_grad)[0].astype(jnp.bfloat16)
        expert_up_acc = expert_up_acc + jnp.einsum(
            "necd,necf->edf", arrived, pre_low, preferred_element_type=jnp.float32
        )
        input_grads = jnp.einsum(
            "necf,edf->necd", pre_low, expert_gate_up, preferred_element_type=jnp.float32
        )
        back_inputs = lax.all_to_all(input_grads, "expert", split_axis=0, concat_axis=0, tiled=True)
        expert_in_grad = jnp.sum(
            back_inputs.reshape(expert_count * capacity, D)[flat_slot].reshape(local, TOP, D),
            axis=1,
        )
        logit_grads = gating_pull(gate_grads)[0]
        moe_values = moe_in.astype(jnp.float32)
        router_acc = router_acc + jnp.dot(moe_values.T, logit_grads, precision=HIGHEST)
        router_back = jnp.dot(logit_grads, router_full.astype(jnp.float32).T, precision=HIGHEST)
        incoming_low = incoming.astype(jnp.bfloat16)
        shared_down_acc = shared_down_acc + jnp.dot(
            shared_hidden.T, incoming_low, preferred_element_type=jnp.float32
        )
        shared_hidden_grad = jnp.dot(
            incoming_low, shared_down_full.T, preferred_element_type=jnp.float32
        )
        shared_pre_low = shared_pull(shared_hidden_grad)[0].astype(jnp.bfloat16)
        shared_up_acc = shared_up_acc + jnp.dot(
            moe_in.T, shared_pre_low, preferred_element_type=jnp.float32
        )
        shared_back = jnp.dot(shared_pre_low, shared_up_full.T, preferred_element_type=jnp.float32)
        moe_in_grad = expert_in_grad + shared_back + router_back
        after_from_norm, moe_gain_grad = moe_norm_pull(moe_in_grad)
        moe_gain_acc = moe_gain_acc + moe_gain_grad
        after_grad = incoming + after_from_norm
        after_low = after_grad.astype(jnp.bfloat16)
        output_acc = output_acc + jnp.dot(gated.T, after_low, preferred_element_type=jnp.float32)
        gated_grad = jnp.dot(after_low, out_full.T, preferred_element_type=jnp.float32)
        readout_grads = readout_pull(gated_grad)
        _, state_out_grad = carried_in(
            (decay_total, readout_grads[5]), "dp", chain_states, identity
        )
        decay_grad = jnp.sum(state_out_grad * state_in, axis=(1, 2))
        carry_grads = carry_pull((decay_grad, state_out_grad))
        front_grads = front_pull(
            (
                readout_grads[0] + carry_grads[0],
                readout_grads[1] + carry_grads[1],
                readout_grads[2],
                readout_grads[3] + carry_grads[2],
                readout_grads[4] + carry_grads[3],
            )
        )
        skip_acc = skip_acc + readout_grads[6]
        gated_acc = gated_acc + readout_grads[8]
        filter_weight_acc = filter_weight_acc + front_grads[2]
        filter_bias_acc = filter_bias_acc + front_grads[3]
        step_bias_acc = step_bias_acc + front_grads[4]
        decay_acc = decay_acc + front_grads[5]
        extended_grad = front_grads[0]
        rim_grad = shifted(extended_grad[: K - 1].astype(jnp.bfloat16), "dp", -1).astype(
            jnp.float32
        )
        filter_in_grad = extended_grad[K - 1 :] + jnp.concatenate(
            [jnp.zeros((local - (K - 1), CONV), jnp.float32), rim_grad], axis=0
        )
        projected_grad = jnp.concatenate(
            [readout_grads[7], filter_in_grad, front_grads[1]], axis=1
        ).astype(jnp.bfloat16)
        input_acc = input_acc + jnp.dot(
            normed.T, projected_grad, preferred_element_type=jnp.float32
        )
        normed_grad = jnp.dot(projected_grad, in_full.T, preferred_element_type=jnp.float32)
        stream_from_norm, norm_gain_grad = norm_pull(normed_grad)
        norm_acc = norm_acc + norm_gain_grad
        stream_grads.append(after_grad + stream_from_norm)
    scattered = (
        lax.psum_scatter(
            input_acc.astype(jnp.bfloat16), "dp", scatter_dimension=0, tiled=True
        ).astype(jnp.float32),
        lax.psum_scatter(
            output_acc.astype(jnp.bfloat16), "dp", scatter_dimension=0, tiled=True
        ).astype(jnp.float32),
        lax.psum_scatter(
            router_acc.astype(jnp.bfloat16), "dp", scatter_dimension=0, tiled=True
        ).astype(jnp.float32),
        lax.psum_scatter(
            shared_up_acc.astype(jnp.bfloat16), "dp", scatter_dimension=0, tiled=True
        ).astype(jnp.float32),
        lax.psum_scatter(
            shared_down_acc.astype(jnp.bfloat16), "dp", scatter_dimension=0, tiled=True
        ).astype(jnp.float32),
        lax.psum_scatter(
            expert_up_acc.astype(jnp.bfloat16), "dp", scatter_dimension=1, tiled=True
        ).astype(jnp.float32),
        lax.psum_scatter(
            expert_down_acc.astype(jnp.bfloat16), "dp", scatter_dimension=1, tiled=True
        ).astype(jnp.float32),
    )
    dense = (
        lax.psum(scattered[0].astype(jnp.bfloat16), "expert").astype(jnp.float32),
        lax.psum(scattered[1].astype(jnp.bfloat16), "expert").astype(jnp.float32),
        lax.psum(scattered[2].astype(jnp.bfloat16), "expert").astype(jnp.float32),
        lax.psum(scattered[3].astype(jnp.bfloat16), "expert").astype(jnp.float32),
        lax.psum(scattered[4].astype(jnp.bfloat16), "expert").astype(jnp.float32),
    )
    small = lax.psum(
        (
            filter_weight_acc,
            filter_bias_acc,
            step_bias_acc,
            decay_acc,
            skip_acc,
            norm_acc,
            gated_acc,
            moe_gain_acc,
        ),
        ("dp", "expert"),
    )
    block_output = jnp.stack(block_rows, axis=0)[:, None]
    tokens_grad = jnp.stack(stream_grads, axis=0)[:, None]
    return (
        block_output,
        tokens_grad,
        dense[0],
        small[0],
        small[1],
        small[2],
        small[3],
        small[4],
        small[5],
        small[6],
        dense[1],
        small[7],
        dense[2],
        dense[3],
        dense[4],
        scattered[5],
        scattered[6],
    )


def solution(mesh):
    in_specs = (
        P(None, "expert", "dp", None),
        P(None, "expert", None),
        P(None, "expert", "dp", None),
        P(None, "expert", "dp", None),
        P("dp", None),
        P(),
        P(),
        P(),
        P(),
        P(),
        P(),
        P(),
        P("dp", None),
        P(),
        P("dp", None),
        P("dp", None),
        P("dp", None),
        P("expert", None, None),
        P("expert", None, None),
    )
    out_specs = (
        P(None, "expert", "dp", None),
        P(None, "expert", "dp", None),
        P("dp", None),
        P(),
        P(),
        P(),
        P(),
        P(),
        P(),
        P(),
        P("dp", None),
        P(),
        P("dp", None),
        P("dp", None),
        P("dp", None),
        P("expert", "dp", None),
        P("expert", "dp", None),
    )
    return jax.shard_map(body, mesh=mesh, in_specs=in_specs, out_specs=out_specs, check_vma=False)
```

profile of v0, /device:TPU:1, one launch (start us, length us, event | category | flops | bytes accessed | tf_op | source)
XLA Modules:
  0.0 2404.2 jit_solution(16511714721787809338)
XLA Ops:
  17.6 102.9 %all-gather.28.cloned.1.call-done = bf16[1536,6448]{1,0:T(8,128)(2,1)} async-done(((bf16[96,6448]{1,0:T(8,128)(2,1)}), bf16[1536,6448]{1,0:T(8,128)(2,1)}) %all-gather.28.cloned.1.call-update) | async-done | bytes 19808272 | tf_op jit(solution)/shard_map/all_gather | solution.py:188
  204.8 87.7 %all-gather.52.cloned.1.call-done = f32[768,64,128]{2,1,0:T(8,128)} async-done(((f32[48,64,128]{2,1,0:T(8,128)}), f32[768,64,128]{2,1,0:T(8,128)}) %all-gather.52.cloned.1.call-update) | async-done | bytes 25165840 | tf_op jit(solution)/shard_map/all_gather | solution.py:32
  292.5 52.6 %while.58 = (s32[]{:T(128)}, f32[48,64,128]{2,1,0:T(8,128)}, s32[]{:T(128)}, f32[16,48]{1,0:T(8,128)S(1)}, f32[16,48,64,128]{3,2,1,0:T(8,128)}, /*index=5*/s32[]{:T(128)}, s32[]{:T(128)}) while((s32[]{:T(128)}, f32[48,64,128]{2,1,0:T(8,128)}, s32[]{:T(128)}, f32[16,48]{1,0:T(8,128)S(1)}, f32[16,48,64,128]{3,2,1,0:T(8,128)}, ...), condition=%wide.region_3.5_spmd.clone, body=%wide.region_2.4_spmd.clone.sunk | while | flops 1572868 | bytes 4719273 | solution.py:44
  459.0 25.8 %all-to-all-done.4 = bf16[8,2,45,1536]{3,1,2,0:T(2,128)(2,1)} async-done(((bf16[8,2,45,1536]{3,1,2,0:T(2,128)(2,1)}), bf16[8,2,45,1536]{3,1,2,0:T(2,128)(2,1)}, u32[]{:S(2)}, u32[]{:S(2)}) %all-to-all-start.4) | async-done | bytes 2211872 | tf_op jit(solution)/shard_map/all_to_all | solution.py:333
  501.7 33.4 %all-to-all-done.1 = bf16[8,2,45,1536]{3,1,2,0:T(2,128)(2,1)} async-done(((bf16[8,2,45,1536]{3,1,2,0:T(2,128)(2,1)}), bf16[8,2,45,1536]{3,1,2,0:T(2,128)(2,1)}, u32[]{:S(2)}, u32[]{:S(2)}) %all-to-all-start.1) | async-done | bytes 2211872 | tf_op jit(solution)/shard_map/all_to_all | solution.py:306
  599.3 63.3 %while.59 = (s32[]{:T(128)}, f32[48,64,128]{2,1,0:T(8,128)}, s32[]{:T(128)}, f32[16,48]{1,0:T(8,128)}, f32[16,48,64,128]{3,2,1,0:T(8,128)}, /*index=5*/s32[]{:T(128)}, s32[]{:T(128)}) while((s32[]{:T(128)}, f32[48,64,128]{2,1,0:T(8,128)}, s32[]{:T(128)}, f32[16,48]{1,0:T(8,128)}, f32[16,48,64,128]{3,2,1,0:T(8,128)}, ...), condition=%wide.region_15.18_spmd.clone, body=%wide.region_14.17_spmd.clone.sunk | while | flops 1572868 | bytes 4719273 | solution.py:44
  707.5 25.1 %scatter_fusion = f32[80,16]{0,1:T(8,128)S(1)} fusion(f32[80,16]{0,1:T(8,128)S(1)} %broadcast_in_dim.67.clone, s32[480]{0:T(512)S(1)} %reshape.811, f32[480]{0:T(512)S(1)} %reshape.813), kind=kCustom, calls=%fused_computation.10 | custom fusion | flops 480 | bytes 9600 | tf_op jit(solution)/shard_map/transpose(jvp(jit(take_along_axis)))/scatter-add | solution.py:276
  840.0 24.0 all-to-all-done.6
  879.8 30.9 %all-to-all-done.3 = bf16[8,2,45,1536]{3,1,2,0:T(2,128)(2,1)S(1)} async-done(((bf16[8,2,45,1536]{3,1,2,0:T(2,128)(2,1)}), bf16[8,2,45,1536]{3,1,2,0:T(2,128)(2,1)S(1)}, u32[]{:S(2)}, u32[]{:S(2)}) %all-to-all-start.3) | async-done | bytes 2211872 | tf_op jit(solution)/shard_map/all_to_all | solution.py:306
  966.2 25.1 %scatter_fusion.1 = f32[80,16]{0,1:T(8,128)S(1)} fusion(f32[80,16]{0,1:T(8,128)S(1)} %broadcast_in_dim.67, s32[480]{0:T(512)S(1)} %reshape.817, f32[480]{0:T(512)S(1)} %reshape.819), kind=kCustom, calls=%fused_computation.11 | custom fusion | flops 480 | bytes 9600 | tf_op jit(solution)/shard_map/transpose(jvp(jit(take_along_axis)))/scatter-add | solution.py:276
  1043.9 52.3 %all-gather.40.cloned.1.call-done = bf16[3072,1536]{1,0:T(8,128)(2,1)} async-done(((bf16[192,1536]{1,0:T(8,128)(2,1)}), bf16[3072,1536]{1,0:T(8,128)(2,1)}) %all-gather.40.cloned.1.call-update) | async-done | bytes 9437200 | tf_op jit(solution)/shard_map/all_gather | solution.py:322
  1104.6 51.3 %all-gather.48.cloned.1.call-done = bf16[3072,1536]{1,0:T(8,128)(2,1)} async-done(((bf16[192,1536]{1,0:T(8,128)(2,1)}), bf16[3072,1536]{1,0:T(8,128)(2,1)}) %all-gather.48.cloned.1.call-update) | async-done | bytes 9437200 | tf_op jit(solution)/shard_map/all_gather | solution.py:322
  1327.5 31.3 %while.56 = (s32[]{:T(128)}, f32[48,64,128]{2,1,0:T(8,128)S(1)}, s32[]{:T(128)}, bf16[16,48]{1,0:T(8,128)(2,1)}, bf16[16,48,64,128]{3,2,1,0:T(8,128)(2,1)}, /*index=5*/s32[]{:T(128)}, s32[]{:T(128)}, s32[]{:T(128)}, s32[]{:T(128)}) while((s32[]{:T(128)}, f32[48,64,128]{2,1,0:T(8,128)S(1)}, s32[]{:T(128)}, bf16[16,48]{1,0:T(8,128)(2,1)}, ...), condition=%wide.region_32.35_spmd, body=%wide.region_31.34_spmd.sunk | while | flops 1179702 | bytes 3932787 | solution.py:69
  1366.8 21.8 while.57
  1446.8 22.7 add_convert_fusion
  1506.3 50.5 %reduce-scatter.18.cloned.1.call-done = bf16[2,96,1024]{2,1,0:T(8,128)(2,1)} async-done(((bf16[2,1536,1024]{2,1,0:T(8,128)(2,1)}), bf16[2,96,1024]{2,1,0:T(8,128)(2,1)}) %reduce-scatter.18.cloned.1.call-update) | async-done | bytes 393232 | tf_op jit(solution)/shard_map/reduce_scatter | solution.py:437
  1563.5 59.6 %reduce-scatter.16.cloned.1.call-done = bf16[64,1536]{1,0:T(8,128)(2,1)} async-done(((bf16[1024,1536]{1,0:T(8,128)(2,1)}), bf16[64,1536]{1,0:T(8,128)(2,1)}) %reduce-scatter.16.cloned.1.call-update) | async-done | bytes 196624 | tf_op jit(solution)/shard_map/reduce_scatter | solution.py:434
  1623.1 71.8 %reduce-scatter.14.cloned.1.call-done = bf16[96,2048]{1,0:T(8,128)(2,1)} async-done(((bf16[1536,2048]{1,0:T(8,128)(2,1)}), bf16[96,2048]{1,0:T(8,128)(2,1)}) %reduce-scatter.14.cloned.1.call-update) | async-done | bytes 393232 | tf_op jit(solution)/shard_map/reduce_scatter | solution.py:431
  1694.8 78.6 %reduce-scatter.12.cloned.1.call-done = bf16[192,1536]{1,0:T(8,128)(2,1)} async-done(((bf16[3072,1536]{1,0:T(8,128)(2,1)}), bf16[192,1536]{1,0:T(8,128)(2,1)}) %reduce-scatter.12.cloned.1.call-update) | async-done | bytes 589840 | tf_op jit(solution)/shard_map/reduce_scatter | solution.py:425
  1773.4 117.9 %reduce-scatter.10.cloned.1.call-done = bf16[96,6448]{1,0:T(8,128)(2,1)} async-done(((bf16[1536,6448]{1,0:T(8,128)(2,1)}), bf16[96,6448]{1,0:T(8,128)(2,1)}) %reduce-scatter.10.cloned.1.call-update) | async-done | bytes 1238032 | tf_op jit(solution)/shard_map/reduce_scatter | solution.py:422
  1891.4 109.4 %all-gather.50.cloned.1.call-done = bf16[1536,6448]{1,0:T(8,128)(2,1)} async-done(((bf16[96,6448]{1,0:T(8,128)(2,1)}), bf16[1536,6448]{1,0:T(8,128)(2,1)}) %all-gather.50.cloned.1.call-update) | async-done | bytes 19808272 | tf_op jit(solution)/shard_map/all_gather | solution.py:321
  2010.6 99.9 %all-gather.42.cloned.1.call-done = bf16[1536,6448]{1,0:T(8,128)(2,1)} async-done(((bf16[96,6448]{1,0:T(8,128)(2,1)}), bf16[1536,6448]{1,0:T(8,128)(2,1)}) %all-gather.42.cloned.1.call-update) | async-done | bytes 19808272 | tf_op jit(solution)/shard_map/all_gather | solution.py:321
  2125.1 111.2 %all-reduce.41.cloned.1.call-done = (bf16[96,6448]{1,0:T(8,128)(2,1)}, bf16[192,1536]{1,0:T(8,128)(2,1)}, bf16[96,2048]{1,0:T(8,128)(2,1)}, bf16[64,1536]{1,0:T(8,128)(2,1)}) async-done(((bf16[96,6448]{1,0:T(8,128)(2,1)}, bf16[192,1536]{1,0:T(8,128)(2,1)}, bf16[96,2048]{1,0:T(8,128)(2,1)}, bf16[64,1536]{1,0:T(8,128)(2,1)}), (bf16[96,6448]{1,0:T(8,128)(2,1)}, bf16[192,1536]{1,0:T(8,128)(2,1)}, ...) | async-done | bytes 2417680 | tf_op jit(solution)/shard_map/psum | solution.py:445
  2242.1 145.2 %all-reduce.39.cloned.1.call-done = (f32[4,3328]{1,0:T(4,128)}, f32[3328]{0:T(1024)}, f32[48]{0:T(128)}, f32[48]{0:T(128)}, f32[48]{0:T(128)}, /*index=5*/f32[1536]{0:T(1024)}, f32[3072]{0:T(1024)}, f32[1536]{0:T(1024)}) async-done(((f32[4,3328]{1,0:T(4,128)}, f32[3328]{0:T(1024)}, f32[48]{0:T(128)}, f32[48]{0:T(128)}, f32[48]{0:T(128)}, /*index=5*/f32[1536]{0:T(1024)}, f32[3072]{0:T(1024)}, ...) | async-done | bytes 91728 | tf_op jit(solution)/shard_map/psum | solution.py:451
  (1029 shorter events, 1056.0 us)
Async XLA Ops:
  8.0 284.5 %all-gather.52.cloned.1.call-start = ((), (), s32[]{:S(2)}) async-start(), calls=%async_computation.33 | async-start | bytes 26738688 | tf_op jit(solution)/shard_map/all_gather | solution.py:32
  160.3 198.7 %all-gather.30.cloned.1.call-start = ((), (), s32[]{:S(2)}) async-start(), calls=%async_computation.16 | async-start | bytes 10027008 | tf_op jit(solution)/shard_map/all_gather | solution.py:189
  161.1 438.2 %all-gather.54.cloned.1.call-start = ((), (), s32[]{:S(2)}) async-start(), calls=%async_computation.34 | async-start | bytes 26738688 | tf_op jit(solution)/shard_map/all_gather | solution.py:32
  183.9 498.8 %all-gather.32.cloned.1.call-start = ((), (), s32[]{:S(2)}) async-start(), calls=%async_computation.17 | async-start | bytes 6684672 | tf_op jit(solution)/shard_map/all_gather | solution.py:191
  501.6 255.8 %all-gather.36.cloned.1.call-start = ((), (), s32[]{:S(2)}) async-start(), calls=%async_computation.19 | async-start | bytes 3342336 | tf_op jit(solution)/shard_map/all_gather | solution.py:325
  554.8 206.6 %all-gather.38.cloned.1.call-start = ((), (), s32[]{:S(2)}) async-start(), calls=%async_computation.20 | async-start | bytes 6684672 | tf_op jit(solution)/shard_map/all_gather | solution.py:324
  594.7 138.0 %all-to-all-start.5 = ((f32[8,2,45,1536]{3,1,2,0:T(2,128)}), f32[8,2,45,1536]{3,1,2,0:T(2,128)}, u32[]{:S(2)}, u32[]{:S(2)}) async-start(f32[8,2,45,1536]{3,1,2,0:T(2,128)} %copy.409), calls=%async_computation.5 | async-start | bytes 8847360 | tf_op jit(solution)/shard_map/all_to_all | solution.py:355
  879.8 141.8 %all-gather.44.cloned.1.call-start = ((), (), s32[]{:S(2)}) async-start(), calls=%async_computation.23 | async-start | bytes 3342336 | tf_op jit(solution)/shard_map/all_gather | solution.py:325
  922.0 174.3 %all-gather.40.cloned.1.call-start = ((), (), s32[]{:S(2)}) async-start(), calls=%async_computation.21 | async-start | bytes 10027008 | tf_op jit(solution)/shard_map/all_gather | solution.py:322
  922.5 233.3 %all-gather.48.cloned.1.call-start = ((), (), s32[]{:S(2)}) async-start(), calls=%async_computation.25 | async-start | bytes 10027008 | tf_op jit(solution)/shard_map/all_gather | solution.py:322
  938.8 388.5 %all-gather.56.cloned.1.call-start = ((), (), s32[]{:S(2)}) async-start(), calls=%async_computation.35 | async-start | bytes 13369344 | tf_op jit(solution)/shard_map/all_gather | solution.py:52
  1173.8 192.8 %all-gather.58.cloned.1.call-start = ((), (), s32[]{:S(2)}) async-start(), calls=%async_computation.36 | async-start | bytes 13369344 | tf_op jit(solution)/shard_map/all_gather | solution.py:52
  1185.1 288.6 %all-gather.34.cloned.1.call-start = ((), (), s32[]{:S(2)}) async-start(), calls=%async_computation.18 | async-start | bytes 3342336 | tf_op jit(solution)/shard_map/all_gather | solution.py:192
  1185.6 293.3 %reduce-scatter.22.cloned.1.call-start = ((), (), s32[]{:S(2)}) async-start(), calls=%async_computation.37 | async-start | bytes 417792
  1193.2 307.7 %reduce-scatter.20.cloned.1.call-start = ((), (), s32[]{:S(2)}) async-start(), calls=%async_computation.32 | async-start | bytes 3342336 | tf_op jit(solution)/shard_map/reduce_scatter | solution.py:440
  1200.5 356.3 %reduce-scatter.18.cloned.1.call-start = ((), (), s32[]{:S(2)}) async-start(), calls=%async_computation.31 | async-start | bytes 6684672 | tf_op jit(solution)/shard_map/reduce_scatter | solution.py:437
  1221.9 401.2 %reduce-scatter.16.cloned.1.call-start = ((), (), s32[]{:S(2)}) async-start(), calls=%async_computation.30 | async-start | bytes 3342336 | tf_op jit(solution)/shard_map/reduce_scatter | solution.py:434
  1226.8 468.1 %reduce-scatter.14.cloned.1.call-start = ((), (), s32[]{:S(2)}) async-start(), calls=%async_computation.29 | async-start | bytes 6684672 | tf_op jit(solution)/shard_map/reduce_scatter | solution.py:431
  1234.2 539.3 %reduce-scatter.12.cloned.1.call-start = ((), (), s32[]{:S(2)}) async-start(), calls=%async_computation.28 | async-start | bytes 10027008 | tf_op jit(solution)/shard_map/reduce_scatter | solution.py:425
  1254.2 637.1 %reduce-scatter.10.cloned.1.call-start = ((), (), s32[]{:S(2)}) async-start(), calls=%async_computation.27 | async-start | bytes 21307392 | tf_op jit(solution)/shard_map/reduce_scatter | solution.py:422
  1469.6 531.3 %all-gather.50.cloned.1.call-start = ((), (), s32[]{:S(2)}) async-start(), calls=%async_computation.26 | async-start | bytes 21307392 | tf_op jit(solution)/shard_map/all_gather | solution.py:321
  1470.3 640.2 %all-gather.42.cloned.1.call-start = ((), (), s32[]{:S(2)}) async-start(), calls=%async_computation.22 | async-start | bytes 21307392 | tf_op jit(solution)/shard_map/all_gather | solution.py:321
  1471.1 765.2 %all-reduce.41.cloned.1.call-start = ((), (), s32[]{:S(2)}) async-start(), calls=%async_computation.39 | async-start | bytes 4866048 | tf_op jit(solution)/shard_map/psum | solution.py:445
  1891.4 496.0 %all-reduce.39.cloned.1.call-start = ((), (), s32[]{:S(2)}) async-start(), calls=%async_computation.38 | async-start | bytes 199680 | tf_op jit(solution)/shard_map/psum | solution.py:451
  (258 other events, 8559.9 us)
Sparse Core Ops, SparseCore 0:
  9.8 110.7 all-gather.27
  160.4 132.0 all-gather.51
  294.2 57.7 all-gather.29
  353.6 203.4 all-gather.53
  558.6 42.7 all-gather.31
  603.0 63.5 all-gather.35
  668.3 43.7 all-gather.37
  921.3 70.7 all-gather.43
  993.9 42.8 all-gather.45
  1038.3 57.8 all-gather.39
  1097.9 57.9 all-gather.47
  1173.9 72.7 all-gather.55
  1249.0 72.7 all-gather.57
  1362.7 56.4 reduce-scatter.21
  1421.5 63.8 reduce-scatter.19
  1487.8 69.0 reduce-scatter.17
  1559.2 63.7 reduce-scatter.15
  1625.6 69.1 reduce-scatter.13
  1697.2 76.1 reduce-scatter.11
  1776.0 115.2 reduce-scatter.9
  1893.1 107.6 all-gather.49
  2002.7 107.7 all-gather.41
  2113.4 122.8 all-reduce.40
  2243.5 143.8 all-reduce.38
  (1 shorter events, 36.4 us)
where the time goes:
time: 2420 us; the launch traced here: 2400 us
  waiting for transfers between devices  1280 us (53%)
  matrix products  342 us (14%)
  other arithmetic  292 us (12%)
  local copies, waits for them, and re-layouts  253 us (10%)
  blocking collectives  154 us (6%)
  starting transfers between devices  57.6 us (2%)
    all_gather x2, waiting for transfers between devices, body(): lax.all_gather(held[0], 'dp', axis=0, tiled=True)  209 us
    psum x1, waiting for transfers between devices, body(): lax.psum((filter_weight_acc, filter_bias_acc, step_bias_acc, decay_acc, s...  145 us
    reduce_scatter x1, waiting for transfers between devices, body(): lax.psum_scatter(input_acc.astype(jnp.bfloat16), 'dp', scatter_dimension=...  118 us
    psum x1, waiting for transfers between devices, body(): lax.psum(scattered[0].astype(jnp.bfloat16), 'expert').astype(jnp.float32)  111 us
    select_n x32, other arithmetic, hop(): return jax.tree.map(lambda a, b: jnp.where(reached, a, b), new, before)  105 us
    all_gather x2, waiting for transfers between devices, body(): lax.all_gather(held[1], 'dp', axis=0, tiled=True)  104 us
    all_gather x1, waiting for transfers between devices, body(): lax.all_gather(input_weight, 'dp', axis=0, tiled=True)  103 us
    all_gather x2, waiting for transfers between devices, prefix(): everything = jax.tree.map(lambda part: lax.all_gather(part, axis), shard)  87.8 us
  transfers between devices with their start and end apart: 37, of which 20 were waited for; matrix products, arithmetic and copies ran while one was open for 32% of the time, Pallas kernels for 0%

commit v1 on v0

v1 whole, which is shorter than its diff:
```python
import jax
import jax.numpy as jnp
from jax import lax
from jax.sharding import PartitionSpec as P

D = 1536
H = 48
PS = 64
S = 128
K = 4
FE = 512
FS = 1024
TOP = 6
MB = 2
DI = 3072
CONV = 3328
IN_W = 6448
EPSILON = 1e-05
BF = jnp.bfloat16
F32 = jnp.float32


def mm(a, b):
    return jnp.dot(a, b, preferred_element_type=F32)


def mm_nt(a, b):
    return lax.dot_general(a, b, (((1,), (1,)), ((), ())), preferred_element_type=F32)


def mm_tn(a, b):
    return lax.dot_general(a, b, (((0,), (0,)), ((), ())), preferred_element_type=F32)


def rms_scale(values, gain):
    return values * lax.rsqrt(jnp.mean(values * values, axis=-1, keepdims=True) + EPSILON) * gain


def doc_number(positions, lengths_rows):
    first = (positions >= lengths_rows[:, :1]).astype(jnp.int32)
    return first + (positions >= lengths_rows[:, :1] + lengths_rows[:, 1:2]).astype(jnp.int32)


def hi_lo(v):
    hi = v.astype(BF)
    return hi, (v - hi.astype(F32)).astype(BF)


def mixer_local(proj, taps, tap_bias, bias_steps, decay_log, skip, docs, docs_ext, heads):
    nb, mb, loc, _ = proj.shape
    di = heads * PS
    width = di + 2 * S
    gate = proj[..., :di]
    seq = jnp.moveaxis(proj[..., di : di + width], 0, 1).reshape(mb, nb * loc, width)
    seq = seq.astype(BF).astype(F32)
    raw = proj[..., di + width : di + width + heads]
    ext = jnp.pad(seq, ((0, 0), (K - 1, 0), (0, 0)))
    count = nb * loc
    total = jnp.zeros((mb, count, width), F32) + tap_bias
    for k in range(K):
        same = (docs_ext[:, k : k + count] == docs).astype(F32)
        total = total + same[:, :, None] * taps[k] * ext[:, k : k + count]
    filtered = jnp.moveaxis(jax.nn.silu(total).reshape(mb, nb, loc, width), 1, 0)
    x = filtered[..., :di].reshape(nb, mb, loc, heads, PS)
    write = filtered[..., di : di + S]
    read = filtered[..., di + S :]
    steps = jax.nn.softplus(raw + bias_steps)
    cum = jnp.cumsum(steps * (-jnp.exp(decay_log)), axis=2)
    bdocs = jnp.moveaxis(docs.reshape(mb, nb, loc), 1, 0)
    last_doc = bdocs[:, :, -1]
    prev_doc = jnp.concatenate([jnp.zeros_like(last_doc[:1]), last_doc[:-1]], axis=0)
    keep = (bdocs == prev_doc[:, :, None]).astype(F32)
    last = cum[:, :, -1]
    same_last = (bdocs == last_doc[:, :, None]).astype(F32)
    weight = jnp.exp(last[:, :, None] - cum) * same_last[..., None] * steps
    scaled = x * weight[..., None]
    states = jnp.einsum("bmshp,bmsn->mhbpn", scaled, write)
    running = jnp.cumsum(last, axis=0)
    before = running - last
    spans = before[:, None] - running[None]
    rows = lax.broadcasted_iota(jnp.int32, (nb, nb), 0)
    cols = lax.broadcasted_iota(jnp.int32, (nb, nb), 1)
    passes = (cols < rows)[:, :, None] & (prev_doc[:, None] == last_doc[None])
    chain = jnp.exp(jnp.where(passes[..., None], spans, -1e30))
    state_in = jnp.einsum("bcmh,mhcpn->mhbpn", chain, states)
    scores = jnp.einsum("bmtn,bmsn->bmts", read, write)
    r2 = lax.broadcasted_iota(jnp.int32, (loc, loc), 0)
    c2 = lax.broadcasted_iota(jnp.int32, (loc, loc), 1)
    allowed = (c2 <= r2) & (bdocs[:, :, :, None] == bdocs[:, :, None, :])
    cum_t = jnp.moveaxis(cum, 3, 2)
    inner_spans = cum_t[..., :, None] - cum_t[..., None, :]
    weights = jnp.exp(jnp.where(allowed[:, :, None], inner_spans, -1e30)) * scores[:, :, None]
    inner = jnp.einsum("bmhts,bmshp->bmthp", weights, x * steps[..., None])
    carried = jnp.einsum("bmtn,mhbpn->bmthp", read, state_in)
    carried = carried * (jnp.exp(cum) * keep[..., None])[..., None]
    out = inner + carried + skip[:, None] * x
    return out.reshape(nb, mb, loc, di) * jax.nn.silu(gate)


def body(
    tokens,
    lengths,
    routes,
    cotangent,
    input_weight,
    filter_weight,
    filter_bias,
    step_bias,
    decay_log,
    skip_gain,
    norm_gain,
    gated_gain,
    output_weight,
    moe_gain,
    router_weight,
    shared_gate_up,
    shared_down,
    expert_gate_up,
    expert_down,
):
    nd, ne = lax.axis_size("dp"), lax.axis_size("expert")
    me_d, me_e = lax.axis_index("dp"), lax.axis_index("expert")
    loc = tokens.shape[2]
    heads = H // nd
    di = heads * PS
    rows_t = MB * loc
    experts = expert_gate_up.shape[0] * ne
    el = expert_gate_up.shape[0]
    dr = D // nd
    fs = FS // ne
    fsr = FS // nd
    fsl = fsr // ne

    pad = 128 - heads
    blocks = jnp.concatenate(
        [
            jnp.moveaxis(input_weight[:, :DI].reshape(dr, nd, di), 1, 0),
            jnp.moveaxis(input_weight[:, DI : 2 * DI].reshape(dr, nd, di), 1, 0),
            jnp.broadcast_to(input_weight[None, :, 2 * DI : 2 * DI + 2 * S], (nd, dr, 2 * S)),
            jnp.moveaxis(input_weight[:, DI + CONV :].reshape(dr, nd, heads), 1, 0),
            jnp.zeros((nd, dr, pad), BF),
        ],
        axis=2,
    )
    w_in = lax.all_to_all(blocks, "dp", 0, 0, tiled=True).reshape(D, -1)
    wcols = w_in.shape[1]

    sg = shared_gate_up.reshape(dr, 2, nd, ne, fsl)
    sg = lax.dynamic_index_in_dim(sg, me_e, 3, False).reshape(dr, 2 * fs)
    sd = lax.dynamic_slice_in_dim(shared_down, me_e * fsl, fsl, 0)
    sg_full = lax.all_gather(sg, "dp", axis=0, tiled=True)
    sd_full = lax.all_gather(sd, "dp", axis=0, tiled=True)
    router_full = lax.all_gather(router_weight, "dp", axis=0, tiled=True)

    stream = tokens.reshape(rows_t, D).astype(F32)
    incoming = cotangent.reshape(rows_t, D)
    route_rows = routes.reshape(rows_t, TOP)
    inc_all = lax.all_gather(incoming, "expert", axis=0, tiled=True)

    normed_wide, norm_pull = jax.vjp(rms_scale, stream, norm_gain)
    normed = normed_wide.astype(BF)
    normed_all = lax.all_gather(normed, "dp", axis=0, tiled=True)
    proj = mm(normed_all, w_in).reshape(nd, MB, loc, wcols)

    count = nd * loc
    docs = doc_number(jnp.arange(count, dtype=jnp.int32)[None], lengths[:, 0])
    docs_ext = doc_number(jnp.arange(count + K - 1, dtype=jnp.int32)[None] - (K - 1), lengths[:, 0])
    taps = jnp.concatenate(
        [lax.dynamic_slice_in_dim(filter_weight, me_d * di, di, 1), filter_weight[:, DI:]], axis=1
    )
    tap_bias = jnp.concatenate(
        [lax.dynamic_slice_in_dim(filter_bias, me_d * di, di, 0), filter_bias[DI:]], axis=0
    )
    my_heads = lambda v: lax.dynamic_slice_in_dim(v, me_d * heads, heads, 0)
    my_gain = lax.dynamic_slice_in_dim(gated_gain, me_d * di, di, 0)

    def mixer(p, a, b, c, d, e):
        return mixer_local(p, a, b, c, d, e, docs, docs_ext, heads)

    y, mixer_pull = jax.vjp(
        mixer, proj, taps, tap_bias, my_heads(step_bias), my_heads(decay_log), my_heads(skip_gain)
    )
    y = y.reshape(nd * rows_t, di)
    square = jnp.sum(y * y, axis=1, keepdims=True)
    partial = mm((y * my_gain).astype(BF), output_weight)
    sq_hi, sq_lo = hi_lo(square)
    payload = jnp.concatenate(
        [partial.astype(BF), sq_hi, sq_lo, jnp.zeros((nd * rows_t, 126), BF)], axis=1
    )
    summed = lax.psum_scatter(payload, "dp", scatter_dimension=0, tiled=True).astype(F32)
    r = lax.rsqrt((summed[:, D : D + 1] + summed[:, D + 1 : D + 2]) / DI + EPSILON)
    mixed = summed[:, :D] * r
    after_mixer = stream + mixed
    moe_wide, moe_pull = jax.vjp(rms_scale, after_mixer, moe_gain)
    moe_in = moe_wide.astype(BF)
    logits = mm(moe_in, router_full)
    chosen = (route_rows[:, :, None] == jnp.arange(experts, dtype=jnp.int32)).astype(F32)
    picked = jnp.sum(chosen * logits[:, None, :], axis=2)
    gates = jax.nn.softmax(picked, axis=1)
    table = jnp.sum(chosen * gates[:, :, None], axis=1)
    t_hi, t_lo = hi_lo(table)
    moe_payload = jnp.concatenate(
        [moe_in, t_hi, t_lo, jnp.zeros((rows_t, 128 - 2 * experts), BF)], axis=1
    )
    moe_all = lax.all_gather(moe_payload, "expert", axis=0, tiled=True)
    x_all = moe_all[:, :D]
    table_all = moe_all[:, D : D + experts].astype(F32) + moe_all[
        :, D + experts : D + 2 * experts
    ].astype(F32)
    my_gates = lax.dynamic_slice_in_dim(table_all, me_e * el, el, 1)
    n_tok = x_all.shape[0]

    w_up = jnp.concatenate(
        [expert_gate_up[i][:, :FE] for i in range(el)]
        + [sg_full[:, :fs]]
        + [expert_gate_up[i][:, FE:] for i in range(el)]
        + [sg_full[:, fs:]],
        axis=1,
    )
    w_down = jnp.concatenate([expert_down[i] for i in range(el)] + [sd_full], axis=0)
    width = w_down.shape[0]
    scale = jnp.concatenate(
        [jnp.broadcast_to(my_gates[:, i : i + 1], (n_tok, FE)) for i in range(el)]
        + [jnp.ones((n_tok, fs), F32)],
        axis=1,
    )
    pre = mm(x_all, w_up)
    a, b = pre[:, :width], pre[:, width:]
    sig = jax.nn.sigmoid(a)
    act = a * sig
    hidden = act * b
    u = mm_nt(inc_all, w_down)
    prod = u * hidden
    gate_grad = jnp.concatenate(
        [jnp.sum(prod[:, i * FE : (i + 1) * FE], axis=1, keepdims=True) for i in range(el)], axis=1
    )
    gh = (scale * hidden).astype(BF)
    gu = scale * u
    pre_grad = jnp.concatenate(
        [gu * b * (sig + act * (1.0 - sig)), gu * act], axis=1
    ).astype(BF)
    out_part = mm(gh, w_down)
    dx_part = mm_nt(pre_grad, w_up)
    d_up = mm_tn(x_all, pre_grad)
    d_down = mm_tn(gh, inc_all)
    spread = lax.dynamic_update_slice(
        jnp.zeros((n_tok, experts), F32), gate_grad, (0, me_e * el)
    )
    s_hi, s_lo = hi_lo(spread)
    back = jnp.concatenate(
        [
            out_part.astype(BF),
            dx_part.astype(BF),
            s_hi,
            s_lo,
            jnp.zeros((n_tok, 128 - 2 * experts), BF),
        ],
        axis=1,
    )
    back_sum = lax.psum_scatter(back, "expert", scatter_dimension=0, tiled=True).astype(F32)
    block_output = (after_mixer + back_sum[:, :D]).astype(BF)
    inc = incoming.astype(F32)
    spread_sum = (
        back_sum[:, 2 * D : 2 * D + experts] + back_sum[:, 2 * D + experts : 2 * D + 2 * experts]
    )
    logit_grad = table * (spread_sum - jnp.sum(table * spread_sum, axis=1, keepdims=True))
    logit_low = logit_grad.astype(BF)
    router_part = mm_tn(moe_in, logit_low)
    moe_in_grad = back_sum[:, D : 2 * D] + mm_nt(logit_low, router_full)
    after_from_norm, moe_gain_grad = moe_pull(moe_in_grad)
    after_grad = inc + after_from_norm
    after_low = after_grad.astype(BF)
    s = jnp.sum(after_low.astype(F32) * mixed, axis=1, keepdims=True)
    r_hi, r_lo = hi_lo(r)
    d_hi, d_lo = hi_lo(s)
    grad_payload = jnp.concatenate(
        [after_low, r_hi, r_lo, d_hi, d_lo, jnp.zeros((rows_t, 124), BF)], axis=1
    )
    grad_all = lax.all_gather(grad_payload, "dp", axis=0, tiled=True)
    after_all = grad_all[:, :D]
    extra = grad_all[:, D : D + 4].astype(F32)
    r_all = extra[:, 0:1] + extra[:, 1:2]
    s_all = extra[:, 2:3] + extra[:, 3:4]
    gated_grad = mm_nt(after_all, output_weight)
    yr = y * r_all
    output_part = mm_tn((yr * my_gain).astype(BF), after_all)
    gated_gain_part = jnp.sum(gated_grad * yr, axis=0)
    dy = r_all * (gated_grad * my_gain) - yr * (r_all * s_all / DI)
    pulls = mixer_pull(dy.reshape(nd, MB, loc, di))
    d_proj = pulls[0].astype(BF).reshape(nd * rows_t, wcols)
    normed_part = mm_nt(d_proj, w_in)
    normed_grad = lax.psum_scatter(
        normed_part.astype(BF), "dp", scatter_dimension=0, tiled=True
    ).astype(F32)
    d_win = mm_tn(normed_all, d_proj).astype(BF)
    stream_from_norm, norm_gain_grad = norm_pull(normed_grad)
    tokens_grad = after_grad + stream_from_norm

    back_in = lax.all_to_all(d_win.reshape(nd, dr, wcols), "dp", 0, 0, tiled=True)
    in_rows = jnp.concatenate(
        [
            jnp.moveaxis(back_in[:, :, :di], 0, 1).reshape(dr, DI),
            jnp.moveaxis(back_in[:, :, di : 2 * di], 0, 1).reshape(dr, DI),
            jnp.sum(back_in[:, :, 2 * di : 2 * di + 2 * S].astype(F32), axis=0).astype(BF),
            jnp.moveaxis(back_in[:, :, 2 * di + 2 * S : 2 * di + 2 * S + heads], 0, 1).reshape(
                dr, H
            ),
        ],
        axis=1,
    )
    input_grad, output_grad = lax.psum((in_rows, output_part.astype(BF)), "expert")
    d_up = d_up.astype(BF)
    d_down = d_down.astype(BF)
    up_blocks = d_up.reshape(nd, dr, 2 * width)
    down_blocks = jnp.stack(
        [d_down[i * FE : (i + 1) * FE].reshape(nd, FE // nd, D) for i in range(el)], axis=1
    ).reshape(nd, el * FE // nd, D)
    down_blocks = jnp.concatenate([down_blocks, d_down[el * FE :].reshape(nd, fsl, D)], axis=1)
    up_sum = lax.psum_scatter(up_blocks, "dp", scatter_dimension=0, tiled=True)[0]
    down_sum = lax.psum_scatter(down_blocks, "dp", scatter_dimension=0, tiled=True)[0]
    expert_up_grad = jnp.stack(
        [
            jnp.concatenate(
                [
                    up_sum[:, i * FE : (i + 1) * FE],
                    up_sum[:, width + i * FE : width + (i + 1) * FE],
                ],
                axis=1,
            )
            for i in range(el)
        ],
        axis=0,
    ).astype(F32)
    expert_down_grad = down_sum[: el * FE // nd].reshape(el, FE // nd, D).astype(F32)
    sg_part = jnp.concatenate([up_sum[:, el * FE : width], up_sum[:, width + el * FE :]], axis=1)
    sg_all = lax.all_gather(sg_part, "expert")
    sd_all = lax.all_gather(down_sum[el * FE // nd :], "expert")
    shared_up_grad = (
        jnp.moveaxis(sg_all.reshape(ne, dr, 2, nd, fsl), 0, 3).reshape(dr, 2 * FS).astype(F32)
    )
    shared_down_grad = sd_all.reshape(fsr, D).astype(F32)

    def spread_heads(v, size, chunk):
        return lax.dynamic_update_slice(
            jnp.zeros(v.shape[:-1] + (size,), F32), v, (0,) * (v.ndim - 1) + (me_d * chunk,)
        )

    fw = jnp.concatenate([spread_heads(pulls[1][:, :di], DI, di), pulls[1][:, di:]], axis=1)
    fb = jnp.concatenate([spread_heads(pulls[2][:di], DI, di), pulls[2][di:]], axis=0)
    small = lax.psum(
        (
            fw,
            fb,
            spread_heads(pulls[3], H, heads),
            spread_heads(pulls[4], H, heads),
            spread_heads(pulls[5], H, heads),
            norm_gain_grad,
            spread_heads(gated_gain_part, DI, di),
            moe_gain_grad,
            router_part,
        ),
        ("dp", "expert"),
    )
    router_grad = lax.dynamic_slice_in_dim(small[8], me_d * dr, dr, 0)
    shape = (MB, 1, loc, D)
    return (
        block_output.reshape(shape),
        tokens_grad.reshape(shape),
        input_grad.astype(F32),
        small[0],
        small[1],
        small[2],
        small[3],
        small[4],
        small[5],
        small[6],
        output_grad.astype(F32),
        small[7],
        router_grad,
        shared_up_grad,
        shared_down_grad,
        expert_up_grad,
        expert_down_grad,
    )


def solution(mesh):
    in_specs = (
        P(None, "expert", "dp", None),
        P(None, "expert", None),
        P(None, "expert", "dp", None),
        P(None, "expert", "dp", None),
        P("dp", None),
        P(),
        P(),
        P(),
        P(),
        P(),
        P(),
        P(),
        P("dp", None),
        P(),
        P("dp", None),
        P("dp", None),
        P("dp", None),
        P("expert", None, None),
        P("expert", None, None),
    )
    out_specs = (
        P(None, "expert", "dp", None),
        P(None, "expert", "dp", None),
        P("dp", None),
        P(),
        P(),
        P(),
        P(),
        P(),
        P(),
        P(),
        P("dp", None),
        P(),
        P("dp", None),
        P("dp", None),
        P("dp", None),
        P("expert", "dp", None),
        P("expert", "dp", None),
    )
    return jax.shard_map(body, mesh=mesh, in_specs=in_specs, out_specs=out_specs, check_vma=False)
```

time: 2420 us -> 1340 us (0.55)
  waiting for transfers between devices: 1280 us -> 678 us
  other arithmetic: 292 us -> 110 us
  matrix products: 342 us -> 167 us
  starting transfers between devices: 57.6 us -> 13.3 us
  blocking collectives: 154 us -> 119 us
    all_gather x16 -> x4, waiting for transfers between devices: 515 us -> 102 us  [the longest x1 49.8 us: body(): inc_all = lax.all_gather(incoming, 'expert', axis=0, tiled=True)]
    reduce_scatter x6 -> x2, waiting for transfers between devices: 378 us -> 0.02 us  [the longest x1 0.02 us: body(): lax.psum_scatter(down_blocks, 'dp', scatter_dimension=0, tiled=True)[0]]
    unnamed x26 -> x15, waiting for transfers between devices: 5.79 us -> 236 us
    dot_general x70 -> x28, matrix products: 342 us -> 162 us  [the longest x5 49.1 us: mm_nt(): lax.dot_general(a, b, (((1,), (1,)), ((), ())), preferred_element_type=F32)]
    select_n x35 -> x1, other arithmetic: 106 us -> 0.72 us  [mixer_local(): steps = jax.nn.softplus(raw + bias_steps)]
    reshape x38 -> x15, local copies, waits for them, and re-layouts: 92.4 us -> 26.2 us  [the longest x1 6.92 us: mixer_local(): jax.nn.silu(total).reshape(mb, nb, loc, width)]
    all_to_all x8 -> x2, waiting for transfers between devices: 127 us -> 63 us  [the longest x1 39.2 us: body(): w_in = lax.all_to_all(blocks, 'dp', 0, 0, tiled=True).reshape(D, -1)]
    concatenate x0 -> x10, local copies, waits for them, and re-layouts: none -> 59.8 us  [the longest x1 38.1 us: body(): jnp.concatenate([partial.astype(BF), sq_hi, sq_lo, jnp.zeros((nd * rows_t...]
  transfers between devices with their start and end apart: 37 -> 14, of which waited for: 20 -> 12; matrix products, arithmetic and copies ran while one was open for 32% -> 19% of each run, Pallas kernels for 0% -> 0%
where the time goes in v1:
time: 1340 us
  waiting for transfers between devices  678 us (51%)
  local copies, waits for them, and re-layouts  233 us (17%)
  matrix products  167 us (12%)
  blocking collectives  119 us (9%)
  other arithmetic  110 us (8%)
  between operations  16.8 us (1%)
    unnamed x15, waiting for transfers between devices  236 us
    psum x2, waiting for transfers between devices, body(): lax.psum((fw, fb, spread_heads(pulls[3], H, heads), spread_heads(pulls[4]...  177 us
    psum x1, waiting for transfers between devices, body(): lax.psum((in_rows, output_part.astype(BF)), 'expert')  100 us
    unnamed x336, local copies, waits for them, and re-layouts  56.5 us
    all_gather x1, waiting for transfers between devices, body(): inc_all = lax.all_gather(incoming, 'expert', axis=0, tiled=True)  49.8 us
    dot_general x5, matrix products, mm_nt(): lax.dot_general(a, b, (((1,), (1,)), ((), ())), preferred_element_type=F32)  49.1 us
    dot_general x5, matrix products, mm(): return jnp.dot(a, b, preferred_element_type=F32)  41.5 us
    dot_general x5, matrix products, mm_tn(): lax.dot_general(a, b, (((0,), (0,)), ((), ())), preferred_element_type=F32)  41.4 us
  transfers between devices with their start and end apart: 14, of which 12 were waited for; matrix products, arithmetic and copies ran while one was open for 19% of the time, Pallas kernels for 0%

profile of v1, /device:TPU:1, one launch (start us, length us, event | category | flops | bytes accessed | tf_op | source)
XLA Modules:
  0.0 1335.4 jit_solution(15184551137359602415)
XLA Ops:
  44.3 39.2 %all-to-all-done = bf16[16,96,768]{2,1,0:T(8,128)(2,1)} async-done(((bf16[16,96,768]{2,1,0:T(8,128)(2,1)}), bf16[16,96,768]{2,1,0:T(8,128)(2,1)}, u32[]{:S(2)}, u32[]{:S(2)}) %all-to-all-start) | async-done | bytes 2359328 | tf_op jit(solution)/shard_map/all_to_all | solution.py:145
  193.1 38.1 %concatenate.65 = bf16[2560,1664]{0,1:T(8,128)(2,1)} concatenate(bf16[2560,1536]{0,1:T(8,128)(2,1)} %convolution_convert_fusion.2, bf16[2560,1]{0,1:T(2,128)(2,1)S(1)} %get-tuple-element.268, bf16[2560,1]{0,1:T(2,128)(2,1)S(1)} %get-tuple-element.267, bf16[2560,126]{0,1:T(8,128)(2,1)S(1)} %broadcast_in_dim.78), dimensions={1} | concatenate | bytes 17039360 | tf_op jit(solution)/shard_map/concatenate | solution.py:187
  231.2 12.2 copy.894
  244.2 19.1 %all-gather.1 = bf16[16,96,16]{1,2,0:T(8,128)(2,1)S(1)} all-gather(bf16[1,96,16]{1,2,0:T(8,128)(2,1)S(1)} %bitcast.300), channel_id=1, replica_groups=mesh['dp'=16,'expert'=8] {'dp'}, dimensions={0}, use_global_device_ids=true | all-gather | bytes 52224 | tf_op jit(solution)/shard_map/all_gather | solution.py:153
  263.6 52.3 %reduce-scatter.16.cloned.1.call-done = bf16[160,1664]{1,0:T(8,128)(2,1)} async-done(((bf16[2560,1664]{1,0:T(8,128)(2,1)}), bf16[160,1664]{1,0:T(8,128)(2,1)}) %reduce-scatter.16.cloned.1.call-update) | async-done | bytes 532496
  329.3 22.3 %all_gather.35 = bf16[128,1536]{1,0:T(8,128)(2,1)} all-gather(bf16[8,1536]{1,0:T(8,128)(2,1)S(1)} %constant_dynamic-slice_fusion.1), channel_id=1, replica_groups=mesh['dp'=16,'expert'=8] {'dp'}, dimensions={0}, use_global_device_ids=true | all-gather | bytes 417792 | tf_op jit(solution)/shard_map/all_gather | solution.py:152
  351.6 20.7 %all_gather.34 = bf16[1536,256]{1,0:T(8,128)(2,1)S(1)} all-gather(bf16[96,256]{1,0:T(8,128)(2,1)S(1)} %copy.804), channel_id=1, replica_groups=mesh['dp'=16,'expert'=8] {'dp'}, dimensions={0}, use_global_device_ids=true | all-gather | bytes 835584 | tf_op jit(solution)/shard_map/all_gather | solution.py:151
  379.4 18.8 %all-gather.9.cloned.1.call-done = bf16[1280,1664]{1,0:T(8,128)(2,1)} async-done(((bf16[160,1664]{1,0:T(8,128)(2,1)}), bf16[1280,1664]{1,0:T(8,128)(2,1)}) %all-gather.9.cloned.1.call-update) | async-done | bytes 4259856 | tf_op jit(solution)/shard_map/all_gather | solution.py:205
  400.3 15.6 %fusion.21 = f32[1280,2304]{1,0:T(8,128)} fusion(bf16[1536,2304]{1,0:T(8,128)(2,1)} %copy-done.68, bf16[1280,1664]{1,0:T(8,128)(2,1)} %all-gather.9.cloned.1.call-done), kind=kOutput, calls=%fused_computation.64 | convolution fusion | flops 9059696640 | bytes 22806528 | tf_op jit(solution)/shard_map/dot_general | solution.py:24
  415.9 49.8 %all-gather.11.cloned.1.call-done = bf16[1280,1536]{1,0:T(8,128)(2,1)} async-done(((bf16[160,1536]{1,0:T(8,128)(2,1)}), bf16[1280,1536]{1,0:T(8,128)(2,1)}) %all-gather.11.cloned.1.call-update) | async-done | bytes 3932176 | tf_op jit(solution)/shard_map/all_gather | solution.py:158
  467.7 14.9 %multiply_convert_fusion.1 = (bf16[1280,1152]{1,0:T(8,128)(2,1)}, bf16[1280,1152]{1,0:T(8,128)(2,1)}, f32[1280,1152]{1,0:T(8,128)}, bf16[1280,1152]{1,0:T(8,128)(2,1)}) fusion(f32[1280,2304]{1,0:T(8,128)} %fusion.21, f32[1280,512]{1,0:T(8,128)} %broadcast_in_dim.85, f32[1280,512]{1,0:T(8,128)S(1)} %broadcast_in_dim.81, f32[1152]{0:T(1024)S(1)} %pad.105.clone, ...), kind=kOutput, calls=%fused_computation.27 | convolution fusion | flops 4568481792 | bytes 39260672 | tf_op jit(solution)/shard_map/dot_general | solution.py:28
  495.3 13.5 %convolution_convert_fusion.5 = bf16[1280,1536]{1,0:T(8,128)(2,1)} fusion(bf16[1536,2304]{1,0:T(8,128)(2,1)} %copy-done.68, bf16[1280,1152]{1,0:T(8,128)(2,1)S(1)} %copy-done.151, bf16[1280,1152]{1,0:T(8,128)(2,1)S(1)} %copy-done.150), kind=kOutput, calls=%fused_computation.8 | convolution fusion | flops 9073459200 | bytes 16908288 | tf_op jit(solution)/shard_map/dot_general | solution.py:28
  508.8 13.4 %concatenate.72 = bf16[1280,3200]{1,0:T(8,128)(2,1)} concatenate(bf16[1280,1536]{1,0:T(8,128)(2,1)} %convolution_convert_fusion.3, bf16[1280,1536]{1,0:T(8,128)(2,1)} %convolution_convert_fusion.5, bf16[1280,16]{1,0:T(8,128)(2,1)S(1)} %copy.806, bf16[1280,16]{1,0:T(8,128)(2,1)S(1)} %copy.807, bf16[1280,96]{1,0:T(8,128)(2,1)S(1)} %broadcast_in_dim.90), dimensions={1} | concatenate | bytes 16384000 | tf_op jit(solution)/shard_map/concatenate | solution.py:250
  523.6 111.8 %reduce-scatter.18.cloned.1.call-done = bf16[160,3200]{1,0:T(8,128)(2,1)} async-done(((bf16[1280,3200]{1,0:T(8,128)(2,1)}), bf16[160,3200]{1,0:T(8,128)(2,1)}) %reduce-scatter.18.cloned.1.call-update) | async-done | bytes 1024016
  654.1 15.0 %convolution_convert_fusion = bf16[1536,2304]{1,0:T(8,128)(2,1)} fusion(bf16[1280,1152]{1,0:T(8,128)(2,1)} %get-tuple-element.224, bf16[1280,1152]{1,0:T(8,128)(2,1)} %get-tuple-element.223, bf16[1280,1664]{1,0:T(8,128)(2,1)} %all-gather.9.cloned.1.call-done), kind=kOutput, calls=%fused_computation.1 | convolution fusion | flops 9075032064 | bytes 16908288 | tf_op jit(solution)/shard_map/dot_general | solution.py:32
  669.2 26.0 %all-gather.13.cloned.1.call-done = bf16[2560,1664]{1,0:T(8,128)(2,1)} async-done(((bf16[160,1664]{1,0:T(8,128)(2,1)}), bf16[2560,1664]{1,0:T(8,128)(2,1)}) %all-gather.13.cloned.1.call-update) | async-done | bytes 8519696 | tf_op jit(solution)/shard_map/all_gather | solution.py:279
  781.4 19.8 %fusion.173 = f32[16,2,80,3]{3,0,1,2:T(8,128)S(1)} fusion(f32[16,2,80,3]{3,0,1,2:T(8,128)S(1)} %copy.838), kind=kOutput, calls=%fused_computation.327 | output fusion | flops 606720 | bytes 61440 | tf_op jit(solution)/shard_map/transpose(jvp(jit(cumsum)))/reduce_window_sum | solution.py:68
  841.9 23.8 %all-to-all-done.1 = bf16[16,96,768]{2,1,0:T(8,128)(2,1)} async-done(((bf16[16,96,768]{2,1,0:T(8,128)(2,1)}), bf16[16,96,768]{2,1,0:T(8,128)(2,1)}, u32[]{:S(2)}, u32[]{:S(2)}) %all-to-all-start.1) | async-done | bytes 2359328 | tf_op jit(solution)/shard_map/all_to_all | solution.py:299
  887.9 28.0 %all_gather.40 = bf16[8,8,1536]{2,1,0:T(8,128)(2,1)S(1)} all-gather(bf16[1,8,1536]{2,1,0:T(8,128)(2,1)S(1)} %slice.397), channel_id=1, replica_groups=mesh['dp'=16,'expert'=8] {'expert'}, dimensions={0}, use_global_device_ids=true | all-gather | bytes 221184 | tf_op jit(solution)/shard_map/all_gather | solution.py:337
  917.5 28.5 %all-gather = bf16[768,256]{1,0:T(8,128)(2,1)S(1)} all-gather(bf16[96,256]{1,0:T(8,128)(2,1)S(1)} %pad_maximum_fusion.10), channel_id=2, replica_groups=mesh['dp'=16,'expert'=8] {'expert'}, dimensions={0}, use_global_device_ids=true | all-gather | bytes 442368 | tf_op jit(solution)/shard_map/all_gather | solution.py:336
  949.2 37.6 %all-reduce.23.cloned.1.call-done = f32[1536,16]{0,1:T(8,128)} async-done(((f32[1536,16]{0,1:T(8,128)}), f32[1536,16]{0,1:T(8,128)}) %all-reduce.23.cloned.1.call-update) | async-done | bytes 98320 | tf_op jit(solution)/shard_map/psum | solution.py:350
  991.4 100.4 %all-reduce.27.cloned.1.call-done = (bf16[96,6448]{1,0:T(8,128)(2,1)}, bf16[192,1536]{1,0:T(8,128)(2,1)}) async-done(((bf16[96,6448]{1,0:T(8,128)(2,1)}, bf16[192,1536]{1,0:T(8,128)(2,1)}), (bf16[96,6448]{1,0:T(8,128)(2,1)}, bf16[192,1536]{1,0:T(8,128)(2,1)})) %all-reduce.27.cloned.1.call-update) | async-done | bytes 1827856 | tf_op jit(solution)/shard_map/psum | solution.py:311
  1096.0 70.8 %reduce-scatter.20.cloned.1.call-done = bf16[160,1536]{1,0:T(8,128)(2,1)} async-done(((bf16[2560,1536]{1,0:T(8,128)(2,1)}), bf16[160,1536]{1,0:T(8,128)(2,1)}) %reduce-scatter.20.cloned.1.call-update) | async-done | bytes 491536
  1178.7 139.4 %all-reduce.25.cloned.1.call-done = (f32[4,3328]{1,0:T(4,128)}, f32[3328]{0:T(1024)}, f32[48]{0:T(128)}, f32[48]{0:T(128)}, f32[48]{0:T(128)}, /*index=5*/f32[1536]{0:T(1024)}, f32[3072]{0:T(1024)}, f32[1536]{0:T(1024)}) async-done(((f32[4,3328]{1,0:T(4,128)}, f32[3328]{0:T(1024)}, f32[48]{0:T(128)}, f32[48]{0:T(128)}, f32[48]{0:T(128)}, /*index=5*/f32[1536]{0:T(1024)}, f32[3072]{0:T(1024)}, ...) | async-done | bytes 91728 | tf_op jit(solution)/shard_map/psum | solution.py:350
  (612 shorter events, 387.6 us)
Async XLA Ops:
  7.2 178.8 %copy-start = (bf16[192,1536]{1,0:T(8,128)(2,1)S(1)}, bf16[192,1536]{1,0:T(8,128)(2,1)}, u32[]{:S(2)}) copy-start(bf16[192,1536]{1,0:T(8,128)(2,1)} %param.31) | copy-start | bytes 1769476
  7.2 83.3 %all-gather.7.cloned.1.call-start = ((), (), s32[]{:S(2)}) async-start(), calls=%async_computation.7 | async-start | bytes 8355840 | tf_op jit(solution)/shard_map/all_gather | solution.py:162
  10.1 307.3 %copy-start.8 = (f32[160,1536]{0,1:T(8,128)}, f32[160,1536]{0,1:T(8,128)S(1)}, u32[]{:S(2)}) copy-start(f32[160,1536]{0,1:T(8,128)S(1)} %copy.799) | copy-start | bytes 2949124
  29.0 54.5 %all-to-all-start = ((bf16[16,96,768]{2,1,0:T(8,128)(2,1)}), bf16[16,96,768]{2,1,0:T(8,128)(2,1)}, u32[]{:S(2)}, u32[]{:S(2)}) async-start(bf16[16,96,768]{2,1,0:T(8,128)(2,1)} %concatenate.63), calls=%async_computation | async-start | bytes 4718592 | tf_op jit(solution)/shard_map/all_to_all | solution.py:145
  36.4 279.5 %reduce-scatter.16.cloned.1.call-start = ((), (), s32[]{:S(2)}) async-start(), calls=%async_computation.14 | async-start | bytes 9052160
  42.2 99.7 %copy-start.65 = (f32[16,2,80]{2,0,1:T(8,128)}, f32[16,2,80]{2,0,1:T(8,128)S(1)}, u32[]{:S(2)}) copy-start(f32[16,2,80]{2,0,1:T(8,128)S(1)} %get-tuple-element.270) | copy-start | bytes 30724
  243.5 154.6 %all-gather.9.cloned.1.call-start = ((), (), s32[]{:S(2)}) async-start(), calls=%async_computation.8 | async-start | bytes 4792320 | tf_op jit(solution)/shard_map/all_gather | solution.py:205
  317.8 323.0 %copy-start.101 = (f32[160]{0:T(256)}, f32[160]{0:T(256)S(1)}, u32[]{:S(2)}) copy-start(f32[160]{0:T(256)S(1)} %fusion.143) | copy-start | bytes 1924
  321.3 144.4 %all-gather.11.cloned.1.call-start = ((), (), s32[]{:S(2)}) async-start(), calls=%async_computation.9 | async-start | bytes 4423680 | tf_op jit(solution)/shard_map/all_gather | solution.py:158
  321.9 313.5 %reduce-scatter.18.cloned.1.call-start = ((), (), s32[]{:S(2)}) async-start(), calls=%async_computation.15 | async-start | bytes 9216000
  522.3 172.8 %all-gather.13.cloned.1.call-start = ((), (), s32[]{:S(2)}) async-start(), calls=%async_computation.10 | async-start | bytes 9052160 | tf_op jit(solution)/shard_map/all_gather | solution.py:279
  523.6 117.2 %copy-start.36 = (bf16[160,1536]{0,1:T(8,128)(2,1)}, bf16[160,1536]{0,1:T(8,128)(2,1)S(1)}, u32[]{:S(2)}) copy-start(bf16[160,1536]{0,1:T(8,128)(2,1)S(1)} %copy.810) | copy-start | bytes 1474564
  643.6 241.8 %reduce-scatter.14.cloned.1.call-start = ((), (), s32[]{:S(2)}) async-start(), calls=%async_computation.13 | async-start | bytes 3760128 | tf_op jit(solution)/shard_map/reduce_scatter | solution.py:320
  654.0 262.7 %reduce-scatter.12.cloned.1.call-start = ((), (), s32[]{:S(2)}) async-start(), calls=%async_computation.12 | async-start | bytes 7520256 | tf_op jit(solution)/shard_map/reduce_scatter | solution.py:319
  828.8 36.9 %all-to-all-start.1 = ((bf16[16,96,768]{2,1,0:T(8,128)(2,1)}), bf16[16,96,768]{2,1,0:T(8,128)(2,1)}, u32[]{:S(2)}, u32[]{:S(2)}) async-start(bf16[16,96,768]{2,1,0:T(8,128)(2,1)} %bitcast.270), calls=%async_computation.1 | async-start | bytes 4718592 | tf_op jit(solution)/shard_map/all_to_all | solution.py:299
  834.3 152.6 %all-reduce.23.cloned.1.call-start = ((), (), s32[]{:S(2)}) async-start(), calls=%async_computation.11 | async-start | bytes 196608 | tf_op jit(solution)/shard_map/psum | solution.py:350
  836.1 255.7 %all-reduce.27.cloned.1.call-start = ((), (), s32[]{:S(2)}) async-start(), calls=%async_computation.18 | async-start | bytes 3686400 | tf_op jit(solution)/shard_map/psum | solution.py:311
  874.0 292.8 %reduce-scatter.20.cloned.1.call-start = ((), (), s32[]{:S(2)}) async-start(), calls=%async_computation.16 | async-start | bytes 8355840
  885.4 432.8 %all-reduce.25.cloned.1.call-start = ((), (), s32[]{:S(2)}) async-start(), calls=%async_computation.17 | async-start | bytes 199680 | tf_op jit(solution)/shard_map/psum | solution.py:350
  989.3 178.8 %copy-start.144 = (f32[48]{0:T(128)}, f32[48]{0:T(128)S(1)}, u32[]{:S(2)}) copy-start(f32[48]{0:T(128)S(1)} %dynamic_update_slice.24) | copy-start | bytes 580
  989.7 178.4 %copy-start.145 = (f32[48]{0:T(128)}, f32[48]{0:T(128)S(1)}, u32[]{:S(2)}) copy-start(f32[48]{0:T(128)S(1)} %dynamic_update_slice.26) | copy-start | bytes 580
  990.0 178.1 %copy-start.91 = (f32[3072]{0:T(1024)}, f32[3072]{0:T(1024)S(1)}, u32[]{:S(2)}) copy-start(f32[3072]{0:T(1024)S(1)} %dynamic_update_slice.27) | copy-start | bytes 36868
  990.8 177.4 %copy-start.143 = (f32[48]{0:T(128)}, f32[48]{0:T(128)S(1)}, u32[]{:S(2)}) copy-start(f32[48]{0:T(128)S(1)} %multiply_dynamic-update-slice_fusion) | copy-start | bytes 580
  1091.8 76.4 %copy-start.112 = (f32[160]{0:T(256)S(1)}, f32[160]{0:T(256)}, u32[]{:S(2)}) copy-start(f32[160]{0:T(256)} %copy-done.111) | copy-start | bytes 1924
  (149 other events, 1547.5 us)
Sparse Core Ops, SparseCore 0:
  11.7 78.7 all-gather.6
  243.7 72.2 reduce-scatter.15
  321.4 76.6 all-gather.8
  400.3 65.2 all-gather.10
  522.4 112.9 reduce-scatter.17
  643.8 51.3 all-gather.12
  697.7 62.1 reduce-scatter.13
  762.5 70.8 reduce-scatter.11
  840.4 146.3 all-reduce.22
  990.6 101.1 all-reduce.26
  1094.2 72.5 reduce-scatter.19
  1173.9 144.2 all-reduce.24

commit v2 on v1

--- a/solution.py
+++ b/solution.py
@@ -1,6 +1,10 @@
+import functools
+
 import jax
 import jax.numpy as jnp
 from jax import lax
+from jax.experimental import pallas as pl
+from jax.experimental.pallas import tpu as pltpu
 from jax.sharding import PartitionSpec as P
 
 D = 1536
@@ -18,6 +22,8 @@
 EPSILON = 1e-05
 BF = jnp.bfloat16
 F32 = jnp.float32
+MESH = pl.DeviceIdType.MESH
+VMEM_LIMIT = 60 * 1024 * 1024
 
 
 def mm(a, b):
@@ -97,6 +103,317 @@
     return out.reshape(nb, mb, loc, di) * jax.nn.silu(gate)
 
 
+def places(axis):
+    me = lax.axis_index(axis)
+    if axis == "dp":
+        core, ring, pair = lax.rem(me, 2), lax.rem(me // 2, 4), me // 8
+
+        def at(hop, other, sibling=0):
+            z = lax.rem(pair + other, 2)
+            return (z * 4 + lax.rem(ring + hop + 4, 4)) * 2 + lax.rem(core + sibling, 2)
+    else:
+        pair, ring = lax.rem(me, 2), me // 2
+
+        def at(hop, other, sibling=0):
+            return lax.rem(ring + hop + 4, 4) * 2 + lax.rem(pair + other, 2)
+
+    return me, at
+
+
+def greet(axis, peers):
+    barrier = pltpu.get_barrier_semaphore()
+    for peer in peers:
+        pl.semaphore_signal(barrier, inc=1, device_id={axis: peer}, device_id_type=MESH)
+    pl.semaphore_wait(barrier, len(peers))
+
+
+def gather_kernel(axis, x, out, send, recv, own_sem):
+    me, at = places(axis)
+    cores = axis == "dp"
+    half = x.shape[0] // 2
+    up, down, pair, sib = at(1, 0), at(-1, 0), at(0, 1), at(0, 0, 1)
+    greet(axis, [up, down, pair] + ([sib] if cores else []))
+    whole = pl.ds(0, 2 * half)
+    first, second = pl.ds(0, half), pl.ds(half, half)
+    started = []
+
+    def push(number, slot, rows, peer, src=None):
+        copy = pltpu.make_async_remote_copy(
+            src_ref=(out.at[slot] if src is None else src).at[rows],
+            dst_ref=out.at[slot].at[rows],
+            send_sem=send.at[number],
+            recv_sem=recv.at[number],
+            device_id={axis: peer},
+            device_id_type=MESH,
+        )
+        copy.start()
+        started.append(copy)
+
+    def arrived(number, slot, rows):
+        pltpu.make_async_copy(out.at[slot].at[rows], out.at[slot].at[rows], recv.at[number]).wait()
+
+    push(0, me, whole, up, x)
+    push(1, me, whole, down, x)
+    push(2, me, whole, pair, x)
+    if cores:
+        push(3, me, whole, sib, x)
+    own = pltpu.make_async_copy(x, out.at[me], own_sem)
+    own.start()
+    arrived(2, pair, whole)
+    push(4, pair, whole, up)
+    push(5, pair, whole, down)
+    if cores:
+        push(6, pair, whole, sib)
+    arrived(0, down, whole)
+    push(7, down, first, up)
+    arrived(1, up, whole)
+    push(8, up, second, down)
+    if cores:
+        push(9, down, whole, sib)
+        push(10, up, whole, sib)
+    arrived(4, at(-1, 1), whole)
+    push(11, at(-1, 1), first, up)
+    arrived(5, at(1, 1), whole)
+    push(12, at(1, 1), second, down)
+    if cores:
+        push(13, at(-1, 1), whole, sib)
+        push(14, at(1, 1), whole, sib)
+    arrived(7, at(2, 0), first)
+    arrived(8, at(2, 0), second)
+    if cores:
+        push(15, at(2, 0), whole, sib)
+    arrived(11, at(2, 1), first)
+    arrived(12, at(2, 1), second)
+    if cores:
+        push(16, at(2, 1), whole, sib)
+        for number, hop, other in (
+            (3, 0, 0),
+            (6, 0, 1),
+            (9, -1, 0),
+            (10, 1, 0),
+            (13, -1, 1),
+            (14, 1, 1),
+            (15, 2, 0),
+            (16, 2, 1),
+        ):
+            arrived(number, at(hop, other, 1), whole)
+    own.wait()
+    for copy in started:
+        copy.wait_send()
+
+
+def gather(x, axis, number):
+    n = lax.axis_size(axis)
+    return pl.pallas_call(
+        functools.partial(gather_kernel, axis),
+        out_shape=jax.ShapeDtypeStruct((n,) + x.shape, x.dtype),
+        in_specs=[pl.BlockSpec(memory_space=pl.ANY)],
+        out_specs=pl.BlockSpec(memory_space=pl.ANY),
+        scratch_shapes=[
+            pltpu.SemaphoreType.DMA((17,)),
+            pltpu.SemaphoreType.DMA((17,)),
+            pltpu.SemaphoreType.DMA,
+        ],
+        compiler_params=pltpu.CompilerParams(
+            collective_id=number, has_side_effects=True, vmem_limit_bytes=VMEM_LIMIT
+        ),
+        name="gather_" + axis,
+    )(x)
+
+
+ORDER = ((2, 1), (2, 0), (1, 1), (-1, 1), (1, 0), (-1, 0), (0, 1), (0, 0))
+
+
+def reduce_kernel(axis, x, out, acc, sib_buf, a_buf, b_buf, c_buf, d_buf, e_buf, send, recv, load):
+    me, at = places(axis)
+    cores = axis == "dp"
+    rows = x.shape[1]
+    half = rows // 2
+    step = 32 if half % 32 == 0 else 16
+    up, down, pair, sib = at(1, 0), at(-1, 0), at(0, 1), at(0, 0, 1)
+    greet(axis, [up, down, pair] + ([sib] if cores else []))
+    whole, first, second = pl.ds(0, rows), pl.ds(0, half), pl.ds(half, half)
+    started = []
+
+    def push(number, src, dst, peer):
+        copy = pltpu.make_async_remote_copy(
+            src_ref=src,
+            dst_ref=dst,
+            send_sem=send.at[number],
+            recv_sem=recv.at[number],
+            device_id={axis: peer},
+            device_id_type=MESH,
+        )
+        copy.start()
+        started.append(copy)
+
+    def arrived(number, dst):
+        pltpu.make_async_copy(dst, dst, recv.at[number]).wait()
+
+    def add(dst, offset, count, *srcs):
+        @pl.loop(0, count // step)
+        def _(i):
+            at_rows = pl.ds(pl.multiple_of(offset + i * step, step), step)
+            total = dst[at_rows, :].astype(F32)
+            for src, src_offset in srcs:
+                total += src[pl.ds(pl.multiple_of(src_offset + i * step, step), step), :].astype(F32)
+            dst[at_rows, :] = total.astype(dst.dtype)
+
+    loads = []
+    for k, (hop, other) in enumerate(ORDER):
+        if cores:
+            push(k, x.at[at(hop, other, 1)], sib_buf.at[k], sib)
+        copy = pltpu.make_async_copy(x.at[at(hop, other)], acc.at[k], load.at[k])
+        copy.start()
+        loads.append(copy)
+
+    def ready(k):
+        loads[k].wait()
+        if cores:
+            arrived(k, sib_buf.at[k])
+            add(acc.at[k], 0, rows, (sib_buf.at[k], 0))
+
+    ready(0)
+    push(8, acc.at[0].at[first], a_buf.at[0], up)
+    push(9, acc.at[0].at[second], b_buf.at[0], down)
+    ready(1)
+    push(10, acc.at[1].at[first], a_buf.at[1], up)
+    push(11, acc.at[1].at[second], b_buf.at[1], down)
+    ready(2)
+    ready(3)
+    arrived(8, a_buf.at[0])
+    add(acc.at[2], 0, half, (a_buf.at[0], 0))
+    push(12, acc.at[2], c_buf.at[0], up)
+    arrived(9, b_buf.at[0])
+    add(acc.at[3], half, half, (b_buf.at[0], 0))
+    push(13, acc.at[3], d_buf.at[0], down)
+    ready(4)
+    ready(5)
+    arrived(10, a_buf.at[1])
+    add(acc.at[4], 0, half, (a_buf.at[1], 0))
+    push(14, acc.at[4], c_buf.at[1], up)
+    arrived(11, b_buf.at[1])
+    add(acc.at[5], half, half, (b_buf.at[1], 0))
+    push(15, acc.at[5], d_buf.at[1], down)
+    ready(6)
+    ready(7)
+    arrived(12, c_buf.at[0])
+    arrived(13, d_buf.at[0])
+    add(acc.at[6], 0, rows, (c_buf.at[0], 0), (d_buf.at[0], 0))
+    push(16, acc.at[6], e_buf, pair)
+    arrived(14, c_buf.at[1])
+    arrived(15, d_buf.at[1])
+    arrived(16, e_buf)
+
+    @pl.loop(0, rows // step)
+    def _(i):
+        at_rows = pl.ds(pl.multiple_of(i * step, step), step)
+        out[at_rows, :] = (
+            acc[7, at_rows, :].astype(F32)
+            + c_buf[1, at_rows, :].astype(F32)
+            + d_buf[1, at_rows, :].astype(F32)
+            + e_buf[at_rows, :].astype(F32)
+        )
+
+    for copy in started:
+        copy.wait_send()
+
+
+def reduce_scatter(x, axis, number):
+    n, rows, columns = x.shape
+    half = rows // 2
+    buf = lambda *shape: pltpu.VMEM(shape + (columns,), BF)
+    return pl.pallas_call(
+        functools.partial(reduce_kernel, axis),
+        out_shape=jax.ShapeDtypeStruct((rows, columns), F32),
+        in_specs=[pl.BlockSpec(memory_space=pl.ANY)],
+        out_specs=pl.BlockSpec(memory_space=pltpu.VMEM),
+        scratch_shapes=[
+            buf(8, rows),
+            buf(8 if axis == "dp" else 1, rows if axis == "dp" else 16),
+            buf(2, half),
+            buf(2, half),
+            buf(2, rows),
+            buf(2, rows),
+            buf(rows),
+            pltpu.SemaphoreType.DMA((17,)),
+            pltpu.SemaphoreType.DMA((17,)),
+            pltpu.SemaphoreType.DMA((8,)),
+        ],
+        compiler_params=pltpu.CompilerParams(
+            collective_id=number, has_side_effects=True, vmem_limit_bytes=VMEM_LIMIT
+        ),
+        name="reduce_" + axis,
+    )(x)
+
+
+def exchange_kernel(plan, *refs):
+    count = len(plan)
+    ins, outs = refs[:count], refs[count : 2 * count]
+    send, recv, own_sem = refs[2 * count :]
+    axes = sorted({axis for _, axis in plan})
+    barrier = pltpu.get_barrier_semaphore()
+    total = 0
+    for axis in axes:
+        n, me = lax.axis_size(axis), lax.axis_index(axis)
+        for k in range(1, n):
+            pl.semaphore_signal(
+                barrier, inc=1, device_id={axis: lax.rem(me + k, n)}, device_id_type=MESH
+            )
+        total += n - 1
+    pl.semaphore_wait(barrier, total)
+    copies = []
+    number = 0
+    for index, (kind, axis) in enumerate(plan):
+        n, me = lax.axis_size(axis), lax.axis_index(axis)
+        x, out = ins[index], outs[index]
+        for k in range(1, n):
+            peer = lax.rem(me + k, n)
+            copy = pltpu.make_async_remote_copy(
+                src_ref=x if kind == "gather" else x.at[peer],
+                dst_ref=out.at[me],
+                send_sem=send.at[number],
+                recv_sem=recv.at[number],
+                device_id={axis: peer},
+                device_id_type=MESH,
+            )
+            copy.start()
+            copies.append(copy)
+            number += 1
+        own = pltpu.make_async_copy(
+            x if kind == "gather" else x.at[me], out.at[me], own_sem.at[index]
+        )
+        own.start()
+        copies.append(own)
+    for copy in copies:
+        copy.wait()
+
+
+def exchange(plan, arrays, number):
+    shapes, transfers = [], 0
+    for (kind, axis), x in zip(plan, arrays):
+        n = lax.axis_size(axis)
+        transfers += n - 1
+        shapes.append(
+            jax.ShapeDtypeStruct((n,) + x.shape if kind == "gather" else x.shape, x.dtype)
+        )
+    return pl.pallas_call(
+        functools.partial(exchange_kernel, plan),
+        out_shape=shapes,
+        in_specs=[pl.BlockSpec(memory_space=pl.ANY)] * len(arrays),
+        out_specs=[pl.BlockSpec(memory_space=pl.ANY)] * len(arrays),
+        scratch_shapes=[
+            pltpu.SemaphoreType.DMA((transfers,)),
+            pltpu.SemaphoreType.DMA((transfers,)),
+            pltpu.SemaphoreType.DMA((len(arrays),)),
+        ],
+        compiler_params=pltpu.CompilerParams(
+            collective_id=number, has_side_effects=True, vmem_limit_bytes=VMEM_LIMIT
+        ),
+        name="exchange",
+    )(*arrays)
+
+
 def body(
     tokens,
     lengths,
@@ -148,9 +465,9 @@
     sg = shared_gate_up.reshape(dr, 2, nd, ne, fsl)
     sg = lax.dynamic_index_in_dim(sg, me_e, 3, False).reshape(dr, 2 * fs)
     sd = lax.dynamic_slice_in_dim(shared_down, me_e * fsl, fsl, 0)
-    sg_full = lax.all_gather(sg, "dp", axis=0, tiled=True)
-    sd_full = lax.all_gather(sd, "dp", axis=0, tiled=True)
-    router_full = lax.all_gather(router_weight, "dp", axis=0, tiled=True)
+    packed = jnp.concatenate([sg.reshape(-1), sd.reshape(-1), router_weight.reshape(-1)])
+    packed_cols = packed.size // rows_t
+    packed = jnp.pad(packed.reshape(rows_t, -1), ((0, 0), (0, 256 - packed_cols)))
 
     stream = tokens.reshape(rows_t, D).astype(F32)
     incoming = cotangent.reshape(rows_t, D)
@@ -159,8 +476,15 @@
 
     normed_wide, norm_pull = jax.vjp(rms_scale, stream, norm_gain)
     normed = normed_wide.astype(BF)
-    normed_all = lax.all_gather(normed, "dp", axis=0, tiled=True)
-    proj = mm(normed_all, w_in).reshape(nd, MB, loc, wcols)
+    normed_all = gather(jnp.concatenate([normed, packed], axis=1), "dp", 1)
+    packed_all = normed_all[:, :, D:].reshape(nd, rows_t, 256)[:, :, : packed_cols]
+    packed_all = packed_all.reshape(nd, -1)
+    sg_full = packed_all[:, : sg.size].reshape(D, 2 * fs)
+    sd_full = packed_all[:, sg.size : sg.size + sd.size].reshape(fs, D)
+    router_full = packed_all[:, sg.size + sd.size :].reshape(D, experts)
+    normed_all = normed_all.reshape(nd * rows_t, D + 256)
+    w_wide = jnp.pad(w_in, ((0, 256), (0, 0)))
+    proj = mm(normed_all, w_wide).reshape(nd, MB, loc, wcols)
 
     count = nd * loc
     docs = doc_number(jnp.arange(count, dtype=jnp.int32)[None], lengths[:, 0])
@@ -182,12 +506,13 @@
     )
     y = y.reshape(nd * rows_t, di)
     square = jnp.sum(y * y, axis=1, keepdims=True)
-    partial = mm((y * my_gain).astype(BF), output_weight)
+    out_wide = jnp.pad(output_weight, ((0, 0), (0, 128)))
+    column = lax.broadcasted_iota(jnp.int32, (1, D + 128), 1)
+    partial = mm((y * my_gain).astype(BF), out_wide)
     sq_hi, sq_lo = hi_lo(square)
-    payload = jnp.concatenate(
-        [partial.astype(BF), sq_hi, sq_lo, jnp.zeros((nd * rows_t, 126), BF)], axis=1
-    )
-    summed = lax.psum_scatter(payload, "dp", scatter_dimension=0, tiled=True).astype(F32)
+    payload = jnp.where(column == D, sq_hi.astype(F32), partial)
+    payload = jnp.where(column == D + 1, sq_lo.astype(F32), payload).astype(BF)
+    summed = reduce_scatter(payload.reshape(nd, rows_t, D + 128), "dp", 2)
     r = lax.rsqrt((summed[:, D : D + 1] + summed[:, D + 1 : D + 2]) / DI + EPSILON)
     mixed = summed[:, :D] * r
     after_mixer = stream + mixed
@@ -202,13 +527,12 @@
     moe_payload = jnp.concatenate(
         [moe_in, t_hi, t_lo, jnp.zeros((rows_t, 128 - 2 * experts), BF)], axis=1
     )
-    moe_all = lax.all_gather(moe_payload, "expert", axis=0, tiled=True)
-    x_all = moe_all[:, :D]
+    moe_all = gather(moe_payload, "expert", 3).reshape(ne * rows_t, D + 128)
     table_all = moe_all[:, D : D + experts].astype(F32) + moe_all[
         :, D + experts : D + 2 * experts
     ].astype(F32)
     my_gates = lax.dynamic_slice_in_dim(table_all, me_e * el, el, 1)
-    n_tok = x_all.shape[0]
+    n_tok = ne * rows_t
 
     w_up = jnp.concatenate(
         [expert_gate_up[i][:, :FE] for i in range(el)]
@@ -217,6 +541,7 @@
         + [sg_full[:, fs:]],
         axis=1,
     )
+    w_up = jnp.pad(w_up, ((0, 128), (0, 0)))
     w_down = jnp.concatenate([expert_down[i] for i in range(el)] + [sd_full], axis=0)
     width = w_down.shape[0]
     scale = jnp.concatenate(
@@ -224,7 +549,7 @@
         + [jnp.ones((n_tok, fs), F32)],
         axis=1,
     )
-    pre = mm(x_all, w_up)
+    pre = mm(moe_all, w_up)
     a, b = pre[:, :width], pre[:, width:]
     sig = jax.nn.sigmoid(a)
     act = a * sig
@@ -241,32 +566,21 @@
     ).astype(BF)
     out_part = mm(gh, w_down)
     dx_part = mm_nt(pre_grad, w_up)
-    d_up = mm_tn(x_all, pre_grad)
+    d_up = mm_tn(moe_all, pre_grad)[:D]
     d_down = mm_tn(gh, inc_all)
-    spread = lax.dynamic_update_slice(
-        jnp.zeros((n_tok, experts), F32), gate_grad, (0, me_e * el)
-    )
-    s_hi, s_lo = hi_lo(spread)
-    back = jnp.concatenate(
-        [
-            out_part.astype(BF),
-            dx_part.astype(BF),
-            s_hi,
-            s_lo,
-            jnp.zeros((n_tok, 128 - 2 * experts), BF),
-        ],
-        axis=1,
-    )
-    back_sum = lax.psum_scatter(back, "expert", scatter_dimension=0, tiled=True).astype(F32)
-    block_output = (after_mixer + back_sum[:, :D]).astype(BF)
+    for i in range(el):
+        g_hi, g_lo = hi_lo(gate_grad[:, i : i + 1])
+        place = D + me_e * el + i
+        dx_part = jnp.where(column == place, g_hi.astype(F32), dx_part)
+        dx_part = jnp.where(column == place + experts, g_lo.astype(F32), dx_part)
+    out_sum = lax.psum_scatter(out_part.astype(BF), "expert", scatter_dimension=0, tiled=True)
+    back_sum = reduce_scatter(dx_part.astype(BF).reshape(ne, rows_t, D + 128), "expert", 4)
     inc = incoming.astype(F32)
-    spread_sum = (
-        back_sum[:, 2 * D : 2 * D + experts] + back_sum[:, 2 * D + experts : 2 * D + 2 * experts]
-    )
+    spread_sum = back_sum[:, D : D + experts] + back_sum[:, D + experts : D + 2 * experts]
     logit_grad = table * (spread_sum - jnp.sum(table * spread_sum, axis=1, keepdims=True))
     logit_low = logit_grad.astype(BF)
     router_part = mm_tn(moe_in, logit_low)
-    moe_in_grad = back_sum[:, D : 2 * D] + mm_nt(logit_low, router_full)
+    moe_in_grad = back_sum[:, :D] + mm_nt(logit_low, router_full)
     after_from_norm, moe_gain_grad = moe_pull(moe_in_grad)
     after_grad = inc + after_from_norm
     after_low = after_grad.astype(BF)
@@ -276,39 +590,23 @@
     grad_payload = jnp.concatenate(
         [after_low, r_hi, r_lo, d_hi, d_lo, jnp.zeros((rows_t, 124), BF)], axis=1
     )
-    grad_all = lax.all_gather(grad_payload, "dp", axis=0, tiled=True)
-    after_all = grad_all[:, :D]
+    grad_all = gather(grad_payload, "dp", 5).reshape(nd * rows_t, D + 128)
     extra = grad_all[:, D : D + 4].astype(F32)
     r_all = extra[:, 0:1] + extra[:, 1:2]
     s_all = extra[:, 2:3] + extra[:, 3:4]
-    gated_grad = mm_nt(after_all, output_weight)
+    gated_grad = mm_nt(grad_all, out_wide)
     yr = y * r_all
-    output_part = mm_tn((yr * my_gain).astype(BF), after_all)
+    output_part = mm_tn((yr * my_gain).astype(BF), grad_all)[:, :D]
     gated_gain_part = jnp.sum(gated_grad * yr, axis=0)
     dy = r_all * (gated_grad * my_gain) - yr * (r_all * s_all / DI)
     pulls = mixer_pull(dy.reshape(nd, MB, loc, di))
     d_proj = pulls[0].astype(BF).reshape(nd * rows_t, wcols)
     normed_part = mm_nt(d_proj, w_in)
-    normed_grad = lax.psum_scatter(
-        normed_part.astype(BF), "dp", scatter_dimension=0, tiled=True
-    ).astype(F32)
-    d_win = mm_tn(normed_all, d_proj).astype(BF)
+    normed_grad = reduce_scatter(normed_part.astype(BF).reshape(nd, rows_t, D), "dp", 6)
+    d_win = mm_tn(normed_all, d_proj)[:D].astype(BF)
     stream_from_norm, norm_gain_grad = norm_pull(normed_grad)
     tokens_grad = after_grad + stream_from_norm
 
-    back_in = lax.all_to_all(d_win.reshape(nd, dr, wcols), "dp", 0, 0, tiled=True)
-    in_rows = jnp.concatenate(
-        [
-            jnp.moveaxis(back_in[:, :, :di], 0, 1).reshape(dr, DI),
-            jnp.moveaxis(back_in[:, :, di : 2 * di], 0, 1).reshape(dr, DI),
-            jnp.sum(back_in[:, :, 2 * di : 2 * di + 2 * S].astype(F32), axis=0).astype(BF),
-            jnp.moveaxis(back_in[:, :, 2 * di + 2 * S : 2 * di + 2 * S + heads], 0, 1).reshape(
-                dr, H
-            ),
-        ],
-        axis=1,
-    )
-    input_grad, output_grad = lax.psum((in_rows, output_part.astype(BF)), "expert")
     d_up = d_up.astype(BF)
     d_down = d_down.astype(BF)
     up_blocks = d_up.reshape(nd, dr, 2 * width)
@@ -332,41 +630,103 @@
         axis=0,
     ).astype(F32)
     expert_down_grad = down_sum[: el * FE // nd].reshape(el, FE // nd, D).astype(F32)
-    sg_part = jnp.concatenate([up_sum[:, el * FE : width], up_sum[:, width + el * FE :]], axis=1)
-    sg_all = lax.all_gather(sg_part, "expert")
-    sd_all = lax.all_gather(down_sum[el * FE // nd :], "expert")
-    shared_up_grad = (
-        jnp.moveaxis(sg_all.reshape(ne, dr, 2, nd, fsl), 0, 3).reshape(dr, 2 * FS).astype(F32)
-    )
-    shared_down_grad = sd_all.reshape(fsr, D).astype(F32)
+    shared_part = jnp.concatenate(
+        [
+            up_sum[:, el * FE : width],
+            up_sum[:, width + el * FE :],
+            down_sum[el * FE // nd :].reshape(dr, -1),
+        ],
+        axis=1,
+    )
 
     def spread_heads(v, size, chunk):
         return lax.dynamic_update_slice(
             jnp.zeros(v.shape[:-1] + (size,), F32), v, (0,) * (v.ndim - 1) + (me_d * chunk,)
         )
 
-    fw = jnp.concatenate([spread_heads(pulls[1][:, :di], DI, di), pulls[1][:, di:]], axis=1)
-    fb = jnp.concatenate([spread_heads(pulls[2][:di], DI, di), pulls[2][di:]], axis=0)
-    small = lax.psum(
+    small_parts = (
+        jnp.concatenate([spread_heads(pulls[1][:, :di], DI, di), pulls[1][:, di:]], axis=1),
+        jnp.concatenate([spread_heads(pulls[2][:di], DI, di), pulls[2][di:]], axis=0),
+        spread_heads(pulls[3], H, heads),
+        spread_heads(pulls[4], H, heads),
+        spread_heads(pulls[5], H, heads),
+        norm_gain_grad,
+        spread_heads(gated_gain_part, DI, di),
+        moe_gain_grad,
+        router_part,
+    )
+    sizes = [part.size for part in small_parts]
+    lanes = -(-sum(sizes) // (nd * 1024)) * 8
+    small_flat = jnp.concatenate([part.reshape(-1) for part in small_parts])
+    small_flat = jnp.pad(small_flat, (0, nd * lanes * 128 - sum(sizes))).reshape(nd, lanes, 128)
+
+    main = 2 * di
+    back_in, small_in = exchange(
+        (("all", "dp"), ("all", "dp")), (d_win.reshape(nd, dr, wcols), small_flat), 7
+    )
+    misc = jnp.concatenate(
+        [
+            jnp.sum(back_in[:, :, main : main + 2 * S].astype(F32), axis=0),
+            jnp.moveaxis(back_in[:, :, main + 2 * S : main + 2 * S + heads], 0, 1)
+            .reshape(dr, H)
+            .astype(F32),
+        ],
+        axis=1,
+    )
+    misc_size = misc.size
+    misc_rows = -(-misc_size // (ne * 1024)) * 8
+    misc = jnp.pad(misc.reshape(-1), (0, ne * misc_rows * 128 - misc_size))
+    got = exchange(
+        (("all", "expert"), ("all", "expert"), ("all", "expert"), ("gather", "expert")),
         (
-            fw,
-            fb,
-            spread_heads(pulls[3], H, heads),
-            spread_heads(pulls[4], H, heads),
-            spread_heads(pulls[5], H, heads),
-            norm_gain_grad,
-            spread_heads(gated_gain_part, DI, di),
-            moe_gain_grad,
-            router_part,
+            back_in[:, :, :main].reshape(ne, nd // ne * dr, main),
+            misc.reshape(ne, misc_rows, 128),
+            output_part.astype(BF).reshape(ne, 48, -1),
+            jnp.sum(small_in, axis=0),
         ),
-        ("dp", "expert"),
-    )
+        8,
+    )
+    main_sum, misc_sum, out_grad_sum, small_sum = [jnp.sum(v.astype(F32), axis=0) for v in got]
+    main_all, misc_all, out_grad_all, shared_all, small_all = exchange(
+        (
+            ("gather", "expert"),
+            ("gather", "expert"),
+            ("gather", "expert"),
+            ("gather", "expert"),
+            ("gather", "dp"),
+        ),
+        (main_sum.astype(BF), misc_sum, out_grad_sum.astype(BF), shared_part, small_sum),
+        9,
+    )
+    main_all = main_all.reshape(nd, dr, main).astype(F32)
+    misc_all = misc_all.reshape(-1)[:misc_size].reshape(dr, 2 * S + H)
+    input_grad = jnp.concatenate(
+        [
+            jnp.moveaxis(main_all[:, :, :di], 0, 1).reshape(dr, DI),
+            jnp.moveaxis(main_all[:, :, di:], 0, 1).reshape(dr, DI),
+            misc_all,
+        ],
+        axis=1,
+    )
+    output_grad = out_grad_all.reshape(output_weight.shape)
+    shared_up_grad = (
+        jnp.moveaxis(shared_all[:, :, : 2 * fs].reshape(ne, dr, 2, nd, fsl), 0, 3)
+        .reshape(dr, 2 * FS)
+        .astype(F32)
+    )
+    shared_down_grad = shared_all[:, :, 2 * fs :].reshape(fsr, D).astype(F32)
+    small_all = small_all.reshape(-1)
+    small, start = [], 0
+    for part, size in zip(small_parts, sizes):
+        small.append(small_all[start : start + size].reshape(part.shape))
+        start += size
     router_grad = lax.dynamic_slice_in_dim(small[8], me_d * dr, dr, 0)
+    block_output = (after_mixer + out_sum.astype(F32)).astype(BF)
     shape = (MB, 1, loc, D)
     return (
         block_output.reshape(shape),
         tokens_grad.reshape(shape),
-        input_grad.astype(F32),
+        input_grad,
         small[0],
         small[1],
         small[2],

time: 1340 us -> 974 us (0.73)
  waiting for transfers between devices: 678 us -> 56.3 us
  Pallas kernels: 0 us -> 405 us
  blocking collectives: 119 us -> 0 us
  local copies, waits for them, and re-layouts: 233 us -> 187 us
    pallas_call x0 -> x9, Pallas kernels: none -> 405 us  [the longest x3 170 us: gather(): pl.pallas_call(functools.partial(gather_kernel, axis), out_shape=jax.Shap...]
    psum x3 -> x0, waiting for transfers between devices: 277 us -> none  [the longest x2 177 us: body(): lax.psum((fw, fb, spread_heads(pulls[3], H, heads), spread_heads(pulls[4]...]
    unnamed x15 -> x4, waiting for transfers between devices: 236 us -> 0.73 us
    all_gather x5 -> x0, blocking collectives: 119 us -> none  [the longest x1 28.5 us: body(): sg_all = lax.all_gather(sg_part, 'expert')]
    reduce_scatter x0 -> x1, waiting for transfers between devices: none -> 55.6 us  [body(): lax.psum_scatter(out_part.astype(BF), 'expert', scatter_dimension=0, tile...]
    all_gather x3 -> x0, waiting for transfers between devices: 51.8 us -> none  [the longest x1 26 us: body(): grad_all = lax.all_gather(grad_payload, 'dp', axis=0, tiled=True)]
    concatenate x2 -> x1, local copies, waits for them, and re-layouts: 51.6 us -> 0.12 us  [body(): small_flat = jnp.concatenate([part.reshape(-1) for part in small_parts])]
    all_gather x1, waiting for transfers between devices: 49.8 us -> 0.01 us  [body(): inc_all = lax.all_gather(incoming, 'expert', axis=0, tiled=True)]
  transfers between devices with their start and end apart: 14 -> 5, of which waited for: 12 -> 1; matrix products, arithmetic and copies ran while one was open for 19% -> 41% of each run, Pallas kernels for 0% -> 38%
where the time goes in v2:
time: 974 us; the launch traced here: 964 us
  Pallas kernels  405 us (42%)
  local copies, waits for them, and re-layouts  187 us (19%)
  matrix products  171 us (18%)
  other arithmetic  121 us (12%)
  waiting for transfers between devices  56.3 us (6%)
  between operations  16.3 us (2%)
    pallas_call x3, Pallas kernels, gather(): pl.pallas_call(functools.partial(gather_kernel, axis), out_shape=jax.Shap...  170 us
    pallas_call x3, Pallas kernels, reduce_scatter(): pl.pallas_call(functools.partial(reduce_kernel, axis), out_shape=jax.Shap...  123 us
    pallas_call x3, Pallas kernels, exchange(): pl.pallas_call(functools.partial(exchange_kernel, plan), out_shape=shapes...  111 us
    reduce_scatter x1, waiting for transfers between devices, body(): lax.psum_scatter(out_part.astype(BF), 'expert', scatter_dimension=0, tile...  55.6 us
    dot_general x5, matrix products, mm_nt(): lax.dot_general(a, b, (((1,), (1,)), ((), ())), preferred_element_type=F32)  52.3 us
    dot_general x5, matrix products, mm(): return jnp.dot(a, b, preferred_element_type=F32)  42.6 us
    dot_general x5, matrix products, mm_tn(): lax.dot_general(a, b, (((0,), (0,)), ((), ())), preferred_element_type=F32)  41.2 us
    unnamed x294, local copies, waits for them, and re-layouts  33 us
  transfers between devices with their start and end apart: 5, of which 1 were waited for; matrix products, arithmetic and copies ran while one was open for 41% of the time, Pallas kernels for 38%

profile of v2, /device:TPU:1, one launch (start us, length us, event | category | flops | bytes accessed | tf_op | source)
XLA Modules:
  0.0 964.1 jit_solution(13527277749687732384)
XLA Ops:
  30.2 70.6 %gather_dp.2 = bf16[16,160,1792]{2,1,0:T(8,128)(2,1)} custom-call(bf16[160,1792]{1,0:T(8,128)(2,1)} %fusion.108.x), custom_call_target="tpu_custom_call" | custom-call | tf_op jit(solution)/shard_map/gather_dp/pallas_call | solution.py:207
  128.7 10.8 %fusion.48 = f32[16,2,80,768]{3,2,1,0:T(8,128)S(1)} fusion(bf16[16,2,80,1792]{3,2,1,0:T(8,128)(2,1)} %bitcast.267, bf16[1536,768]{1,0:T(8,128)(2,1)} %bitcast.8), kind=kOutput, calls=%fused_computation.105 | convolution fusion | flops 7046430720 | bytes 19398656 | tf_op jit(solution)/shard_map/dot_general | solution.py:30
  144.5 19.8 %fusion.176 = f32[16,2,80,3]{3,0,1,2:T(8,128)S(1)} fusion(f32[16,2,80,3]{3,0,1,2:T(8,128)S(1)} %copy.666), kind=kOutput, calls=%fused_computation.346 | output fusion | flops 606720 | bytes 61440 | tf_op jit(solution)/shard_map/jvp(jit(cumsum))/reduce_window_sum | solution.py:74
  243.7 42.5 %reduce_dp.2 = f32[160,1664]{1,0:T(8,128)} custom-call(bf16[16,160,1664]{2,1,0:T(8,128)(2,1)} %bitcast.275), custom_call_target="tpu_custom_call" | custom-call | tf_op jit(solution)/shard_map/reduce_dp/pallas_call | solution.py:326
  290.9 40.3 %gather_expert.1 = bf16[8,160,1664]{2,1,0:T(8,128)(2,1)} custom-call(bf16[160,1664]{1,0:T(8,128)(2,1)} %concatenate.67.x), custom_call_target="tpu_custom_call" | custom-call | tf_op jit(solution)/shard_map/gather_expert/pallas_call | solution.py:207
  333.3 15.4 %fusion.5 = f32[1280,2304]{1,0:T(8,128)} fusion(bf16[1280,1664]{1,0:T(8,128)(2,1)} %bitcast.284, bf16[1536,2304]{1,0:T(8,128)(2,1)} %slice_dynamic-update-slice_fusion.4), kind=kOutput, calls=%fused_computation.22 | convolution fusion | flops 9814671360 | bytes 23134208 | tf_op jit(solution)/shard_map/dot_general | solution.py:30
  352.1 15.1 %multiply_convert_fusion.1 = (bf16[1280,1152]{1,0:T(8,128)(2,1)}, bf16[1280,1152]{1,0:T(8,128)(2,1)}, f32[1280,1152]{1,0:T(8,128)}, bf16[1280,1152]{1,0:T(8,128)(2,1)}) fusion(f32[1280,2304]{1,0:T(8,128)} %fusion.5, f32[1280,512]{1,0:T(8,128)} %broadcast_in_dim.218, f32[1280,512]{1,0:T(8,128)} %broadcast_in_dim.216, f32[1152]{0:T(1024)S(1)} %pad.133.clone, ...), kind=kOutput, calls=%fused_computation.30 | convolution fusion | flops 4568481792 | bytes 39260672 | tf_op jit(solution)/shard_map/dot_general | solution.py:34
  377.9 9.2 convolution_convert_fusion.1
  387.2 15.2 %fusion.23 = bf16[1664,2304]{1,0:T(8,128)(2,1)S(1)} fusion(bf16[1280,1664]{1,0:T(8,128)(2,1)} %bitcast.285, bf16[1280,1152]{1,0:T(8,128)(2,1)} %get-tuple-element.213, bf16[1280,1152]{1,0:T(8,128)(2,1)} %get-tuple-element.212), kind=kOutput, calls=%fused_computation.65 | convolution fusion | flops 9826467840 | bytes 17825792 | tf_op jit(solution)/shard_map/dot_general | solution.py:38
  409.2 15.7 %fusion.3 = bf16[1280,1664]{1,0:T(8,128)(2,1)} fusion(bf16[1536,2304]{1,0:T(8,128)(2,1)} %slice_dynamic-update-slice_fusion.4, bf16[1280]{0:T(1024)(128)(2,1)S(1)} %get-tuple-element.269, bf16[1280]{0:T(1024)(128)(2,1)S(1)} %get-tuple-element.268, bf16[1280]{0:T(1024)(128)(2,1)S(1)} %get-tuple-element.267, bf16[1280]{0:T(1024)(128)(2,1)S(1)} %get-tuple-element.266, ...), kind=kOutput, calls=%fused_computation.11 | convolution fusion | flops 9834987520 | bytes 17252864 | tf_op jit(solution)/shard_map/dot_general | solution.py:34
  424.9 41.1 %reduce_expert.1 = f32[160,1664]{1,0:T(8,128)} custom-call(bf16[8,160,1664]{2,1,0:T(8,128)(2,1)} %bitcast.287), custom_call_target="tpu_custom_call" | custom-call | tf_op jit(solution)/shard_map/reduce_expert/pallas_call | solution.py:326
  476.3 55.6 %reduce-scatter.4.cloned.1.call-done = bf16[160,1536]{1,0:T(8,128)(2,1)} async-done(((bf16[1280,1536]{1,0:T(8,128)(2,1)}), bf16[160,1536]{1,0:T(8,128)(2,1)}) %reduce-scatter.4.cloned.1.call-update) | async-done | bytes 491536 | tf_op jit(solution)/shard_map/reduce_scatter | solution.py:576
  536.5 59.4 %gather_dp.3 = bf16[16,160,1664]{2,1,0:T(8,128)(2,1)} custom-call(bf16[160,1664]{1,0:T(8,128)(2,1)} %concatenate.72.x), custom_call_target="tpu_custom_call" | custom-call | tf_op jit(solution)/shard_map/gather_dp/pallas_call | solution.py:207
  597.4 8.6 multiply_reduce_fusion.9
  613.3 10.7 %multiply_reduce_fusion.5 = (f32[192]{0:T(256)}, f32[16,2,80,192]{2,0,3,1:T(8,128)S(1)}, f32[16,2,80,192]{2,0,3,1:T(8,128)}) fusion(f32[16,2,80,448]{2,0,3,1:T(8,128)} %bitcast.255, f32[16,2,80,192]{2,0,3,1:T(8,128)} %copy.706, f32[16,2,80,192]{2,0,3,1:T(8,128)S(1)} %copy-done.6, f32[16,2,80,192]{2,3,1,0:T(8,128)} %bitcast.258), kind=kLoop, calls=%fused_computation.79 | loop fusion | flops 6881088 | bytes 11797248 | tf_op jit(solution)/shard_map/transpose(jvp())/reduce_sum | solution.py:102
  656.0 7.9 multiply_reduce_fusion.2
  718.0 7.9 add_convert_fusion
  725.8 8.3 copy.741
  734.2 11.0 %convolution_convert_fusion = bf16[2560,1536]{1,0:T(8,128)(2,1)} fusion(bf16[2560,768]{1,0:T(8,128)(2,1)} %bitcast.290, bf16[1536,768]{1,0:T(8,128)(2,1)} %bitcast.8), kind=kOutput, calls=%fused_computation.3 | convolution fusion | flops 6043729920 | bytes 14155776 | tf_op jit(solution)/shard_map/dot_general | solution.py:34
  745.2 39.7 %reduce_dp.3 = f32[160,1536]{1,0:T(8,128)} custom-call(bf16[16,160,1536]{2,1,0:T(8,128)(2,1)} %bitcast.276), custom_call_target="tpu_custom_call" | custom-call | tf_op jit(solution)/shard_map/reduce_dp/pallas_call | solution.py:326
  785.1 11.1 %fusion.182 = bf16[1792,768]{1,0:T(8,128)(2,1)S(1)} fusion(bf16[2560,1792]{1,0:T(8,128)(2,1)} %bitcast.268, bf16[2560,768]{1,0:T(8,128)(2,1)} %bitcast.291), kind=kOutput, calls=%fused_computation.352 | convolution fusion | flops 7046430720 | bytes 15859712 | tf_op jit(solution)/shard_map/dot_general | solution.py:38
  800.5 44.4 %exchange.3 = (bf16[16,96,768]{2,1,0:T(8,128)(2,1)}, f32[16,24,128]{2,1,0:T(8,128)}) custom-call(bf16[16,96,768]{2,1,0:T(8,128)(2,1)} %bitcast.273, f32[16,24,128]{2,1,0:T(8,128)} %bitcast.295), custom_call_target="tpu_custom_call" | custom-call | tf_op jit(solution)/shard_map/exchange/pallas_call | solution.py:400
  851.6 29.1 %exchange.4 = (bf16[8,192,384]{2,1,0:T(8,128)(2,1)}, f32[8,32,128]{2,1,0:T(8,128)}, bf16[8,48,768]{2,1,0:T(8,128)(2,1)}, f32[8,24,128]{2,1,0:T(8,128)}) custom-call(bf16[8,192,384]{2,1,0:T(8,128)(2,1)} %bitcast.286, f32[8,32,128]{2,1,0:T(8,128)} %bitcast.298, bf16[8,48,768]{2,1,0:T(8,128)(2,1)} %reshape.647.refs_2_, f32[24,128]{1,0:T(8,128)} %reduce_sum.487.refs_3_), custom_call_target="tpu_custom_call" | custom-call | tf_op jit(solution)/shard_map/exchange/pallas_call | solution.py:400
  892.0 37.7 %exchange.5 = (bf16[8,192,384]{2,1,0:T(8,128)(2,1)}, f32[8,32,128]{2,1,0:T(8,128)}, bf16[8,48,768]{2,1,0:T(8,128)(2,1)}, bf16[8,96,384]{2,1,0:T(8,128)(2,1)}, f32[16,24,128]{2,1,0:T(8,128)}) custom-call(bf16[192,384]{1,0:T(8,128)(2,1)} %reduce_sum.488.refs_0_, f32[32,128]{1,0:T(8,128)} %reduce_sum.489.refs_1_, bf16[48,768]{1,0:T(8,128)(2,1)} %reduce_sum.490.refs_2_, ...), custom_call_target="tpu_custom_call" | custom-call | tf_op jit(solution)/shard_map/exchange/pallas_call | solution.py:400
  (593 shorter events, 320.8 us)
Async XLA Ops:
  16.9 111.8 %all-to-all-start = ((bf16[16,96,768]{2,1,0:T(8,128)(2,1)}), bf16[16,96,768]{2,1,0:T(8,128)(2,1)}, u32[]{:S(2)}, u32[]{:S(2)}) async-start(bf16[16,96,768]{2,1,0:T(8,128)(2,1)} %concatenate.65), calls=%async_computation | async-start | bytes 4718592 | tf_op jit(solution)/shard_map/all_to_all | solution.py:462
  24.4 324.2 %all-gather.2.cloned.1.call-start = ((), (), s32[]{:S(2)}) async-start(), calls=%async_computation.5 | async-start | bytes 4423680 | tf_op jit(solution)/shard_map/all_gather | solution.py:475
  25.2 447.8 %reduce-scatter.8.cloned.1.call-start = ((), (), s32[]{:S(2)}) async-start(), calls=%async_computation.7 | async-start | bytes 3760128 | tf_op jit(solution)/shard_map/reduce_scatter | solution.py:618
  29.1 71.7 %copy-start.117 = (f32[160]{0:T(256)}, f32[160]{0:T(256)S(1)}, u32[]{:S(2)}) copy-start(f32[160]{0:T(256)S(1)} %add.241) | copy-start | bytes 1924
  29.1 71.7 %copy-start.112 = (f32[160]{0:T(256)}, f32[160]{0:T(256)S(1)}, u32[]{:S(2)}) copy-start(f32[160]{0:T(256)S(1)} %rsqrt.23) | copy-start | bytes 1924
  101.1 68.8 %copy-start.76 = (f32[2,1280]{1,0:T(2,128)}, f32[2,1280]{1,0:T(2,128)S(1)}, u32[]{:S(2)}) copy-start(f32[2,1280]{1,0:T(2,128)S(1)} %get-tuple-element.260) | copy-start | bytes 30724
  101.1 68.8 %copy-start.78 = (f32[2,1280]{1,0:T(2,128)}, f32[2,1280]{1,0:T(2,128)S(1)}, u32[]{:S(2)}) copy-start(f32[2,1280]{1,0:T(2,128)S(1)} %get-tuple-element.261) | copy-start | bytes 30724
  101.1 68.8 %copy-start.80 = (f32[2,1280]{1,0:T(2,128)}, f32[2,1280]{1,0:T(2,128)S(1)}, u32[]{:S(2)}) copy-start(f32[2,1280]{1,0:T(2,128)S(1)} %get-tuple-element.262) | copy-start | bytes 30724
  101.1 68.8 %copy-start.82 = (f32[2,1280]{1,0:T(2,128)}, f32[2,1280]{1,0:T(2,128)S(1)}, u32[]{:S(2)}) copy-start(f32[2,1280]{1,0:T(2,128)S(1)} %get-tuple-element.263) | copy-start | bytes 30724
  101.2 95.4 %copy-start.67 = (f32[16,2,80]{2,0,1:T(8,128)}, f32[16,2,80]{2,0,1:T(8,128)S(1)}, u32[]{:S(2)}) copy-start(f32[16,2,80]{2,0,1:T(8,128)S(1)} %get-tuple-element.265) | copy-start | bytes 30724
  101.2 95.4 %copy-start.84 = (f32[16,2,80]{2,0,1:T(8,128)}, f32[16,2,80]{2,0,1:T(8,128)S(1)}, u32[]{:S(2)}) copy-start(f32[16,2,80]{2,0,1:T(8,128)S(1)} %get-tuple-element.264) | copy-start | bytes 30724
  101.3 117.6 %copy-start.99 = (pred[16,16,2]{1,0,2:T(8,128)(4,1)}, pred[16,16,2]{1,0,2:T(8,128)(4,1)S(1)}, u32[]{:S(2)}) copy-start(pred[16,16,2]{1,0,2:T(8,128)(4,1)S(1)} %compare_and_fusion.1) | copy-start | bytes 1540
  113.4 56.5 %copy-start.104 = (f32[1,448]{1,0:T(1,128)}, f32[1,448]{1,0:T(1,128)S(1)}, u32[]{:S(2)}) copy-start(f32[1,448]{1,0:T(1,128)S(1)} %get-tuple-element.270) | copy-start | bytes 5380
  113.4 56.5 %copy-start.106 = (f32[1,448]{1,0:T(1,128)}, f32[1,448]{1,0:T(1,128)S(1)}, u32[]{:S(2)}) copy-start(f32[1,448]{1,0:T(1,128)S(1)} %get-tuple-element.271) | copy-start | bytes 5380
  113.4 56.5 %copy-start.108 = (f32[1,448]{1,0:T(1,128)}, f32[1,448]{1,0:T(1,128)S(1)}, u32[]{:S(2)}) copy-start(f32[1,448]{1,0:T(1,128)S(1)} %get-tuple-element.272) | copy-start | bytes 5380
  113.4 56.5 %copy-start.110 = (f32[1,448]{1,0:T(1,128)}, f32[1,448]{1,0:T(1,128)S(1)}, u32[]{:S(2)}) copy-start(f32[1,448]{1,0:T(1,128)S(1)} %get-tuple-element.273) | copy-start | bytes 5380
  117.8 78.8 %copy-start.115 = (f32[3]{0:T(128)}, f32[3]{0:T(128)S(1)}, u32[]{:S(2)}) copy-start(f32[3]{0:T(128)S(1)} %dynamic_slice.35) | copy-start | bytes 40
  117.9 107.3 %copy-start.125 = (f32[3]{0:T(128)}, f32[3]{0:T(128)S(1)}, u32[]{:S(2)}) copy-start(f32[3]{0:T(128)S(1)} %dynamic_slice.37) | copy-start | bytes 40
  143.2 53.5 %copy-start.51 = (f32[16,2,80,3]{2,0,3,1:T(8,128)}, f32[16,2,80,3]{2,0,3,1:T(8,128)S(1)}, u32[]{:S(2)}) copy-start(f32[16,2,80,3]{2,0,3,1:T(8,128)S(1)} %copy.783) | copy-start | bytes 92164
  377.9 154.0 %reduce-scatter.4.cloned.1.call-start = ((), (), s32[]{:S(2)}) async-start(), calls=%async_computation.4 | async-start | bytes 4423680 | tf_op jit(solution)/shard_map/reduce_scatter | solution.py:576
  387.1 501.8 %reduce-scatter.6.cloned.1.call-start = ((), (), s32[]{:S(2)}) async-start(), calls=%async_computation.6 | async-start | bytes 7520256 | tf_op jit(solution)/shard_map/reduce_scatter | solution.py:617
  472.9 58.9 %copy-start.42 = (f32[160,1536]{1,0:T(8,128)S(1)}, f32[160,1536]{1,0:T(8,128)}, u32[]{:S(2)}) copy-start(f32[160,1536]{1,0:T(8,128)} %get-tuple-element.278) | copy-start | bytes 2949124
  472.9 61.2 %copy-start.27 = (f32[160,1664]{1,0:T(8,128)S(1)}, f32[160,1664]{1,0:T(8,128)}, u32[]{:S(2)}) copy-start(f32[160,1664]{1,0:T(8,128)} %reduce_dp.2) | copy-start | bytes 3194884
  536.5 60.9 %copy-start.50 = (f32[2560,192]{0,1:T(8,128)S(1)}, f32[2560,192]{0,1:T(8,128)}, u32[]{:S(2)}) copy-start(f32[2560,192]{0,1:T(8,128)} %copy.690) | copy-start | bytes 5898244
  (127 other events, 868.4 us)
Sparse Core Ops, SparseCore 0:
  27.6 84.1 all-gather.1
  378.0 61.6 reduce-scatter.7
  443.7 88.1 reduce-scatter.3
  534.3 88.6 reduce-scatter.5

commit v3 on v2

--- a/solution.py
+++ b/solution.py
@@ -42,65 +42,9 @@
     return values * lax.rsqrt(jnp.mean(values * values, axis=-1, keepdims=True) + EPSILON) * gain
 
 
-def doc_number(positions, lengths_rows):
-    first = (positions >= lengths_rows[:, :1]).astype(jnp.int32)
-    return first + (positions >= lengths_rows[:, :1] + lengths_rows[:, 1:2]).astype(jnp.int32)
-
-
 def hi_lo(v):
     hi = v.astype(BF)
     return hi, (v - hi.astype(F32)).astype(BF)
-
-
-def mixer_local(proj, taps, tap_bias, bias_steps, decay_log, skip, docs, docs_ext, heads):
-    nb, mb, loc, _ = proj.shape
-    di = heads * PS
-    width = di + 2 * S
-    gate = proj[..., :di]
-    seq = jnp.moveaxis(proj[..., di : di + width], 0, 1).reshape(mb, nb * loc, width)
-    seq = seq.astype(BF).astype(F32)
-    raw = proj[..., di + width : di + width + heads]
-    ext = jnp.pad(seq, ((0, 0), (K - 1, 0), (0, 0)))
-    count = nb * loc
-    total = jnp.zeros((mb, count, width), F32) + tap_bias
-    for k in range(K):
-        same = (docs_ext[:, k : k + count] == docs).astype(F32)
-        total = total + same[:, :, None] * taps[k] * ext[:, k : k + count]
-    filtered = jnp.moveaxis(jax.nn.silu(total).reshape(mb, nb, loc, width), 1, 0)
-    x = filtered[..., :di].reshape(nb, mb, loc, heads, PS)
-    write = filtered[..., di : di + S]
-    read = filtered[..., di + S :]
-    steps = jax.nn.softplus(raw + bias_steps)
-    cum = jnp.cumsum(steps * (-jnp.exp(decay_log)), axis=2)
-    bdocs = jnp.moveaxis(docs.reshape(mb, nb, loc), 1, 0)
-    last_doc = bdocs[:, :, -1]
-    prev_doc = jnp.concatenate([jnp.zeros_like(last_doc[:1]), last_doc[:-1]], axis=0)
-    keep = (bdocs == prev_doc[:, :, None]).astype(F32)
-    last = cum[:, :, -1]
-    same_last = (bdocs == last_doc[:, :, None]).astype(F32)
-    weight = jnp.exp(last[:, :, None] - cum) * same_last[..., None] * steps
-    scaled = x * weight[..., None]
-    states = jnp.einsum("bmshp,bmsn->mhbpn", scaled, write)
-    running = jnp.cumsum(last, axis=0)
-    before = running - last
-    spans = before[:, None] - running[None]
-    rows = lax.broadcasted_iota(jnp.int32, (nb, nb), 0)
-    cols = lax.broadcasted_iota(jnp.int32, (nb, nb), 1)
-    passes = (cols < rows)[:, :, None] & (prev_doc[:, None] == last_doc[None])
-    chain = jnp.exp(jnp.where(passes[..., None], spans, -1e30))
-    state_in = jnp.einsum("bcmh,mhcpn->mhbpn", chain, states)
-    scores = jnp.einsum("bmtn,bmsn->bmts", read, write)
-    r2 = lax.broadcasted_iota(jnp.int32, (loc, loc), 0)
-    c2 = lax.broadcasted_iota(jnp.int32, (loc, loc), 1)
-    allowed = (c2 <= r2) & (bdocs[:, :, :, None] == bdocs[:, :, None, :])
-    cum_t = jnp.moveaxis(cum, 3, 2)
-    inner_spans = cum_t[..., :, None] - cum_t[..., None, :]
-    weights = jnp.exp(jnp.where(allowed[:, :, None], inner_spans, -1e30)) * scores[:, :, None]
-    inner = jnp.einsum("bmhts,bmshp->bmthp", weights, x * steps[..., None])
-    carried = jnp.einsum("bmtn,mhbpn->bmthp", read, state_in)
-    carried = carried * (jnp.exp(cum) * keep[..., None])[..., None]
-    out = inner + carried + skip[:, None] * x
-    return out.reshape(nb, mb, loc, di) * jax.nn.silu(gate)
 
 
 def places(axis):
@@ -414,6 +358,339 @@
     )(*arrays)
 
 
+EDGE = 8
+HIGHEST = lax.Precision.HIGHEST
+
+
+def exact(a, b, dims):
+    return lax.dot_general(a, b, (dims, ((), ())), precision=HIGHEST, preferred_element_type=F32)
+
+
+def iota(shape, axis):
+    return lax.broadcasted_iota(jnp.int32, shape, axis)
+
+
+class Block:
+    def __init__(self, m, start, proj, ext, lengths, taps, heads_vec, heads):
+        loc = proj.shape[0]
+        di = heads * PS
+        width = di + 2 * S
+        self.heads, self.di = heads, di
+        first = lengths[m, 0]
+        second = first + lengths[m, 1]
+
+        def doc(p):
+            return (p >= first).astype(jnp.int32) + (p >= second).astype(jnp.int32)
+
+        self.doc = doc
+        self.at = start + iota((loc, 1), 0)
+        docs = doc(self.at)
+        docs_row = doc(start + iota((1, loc), 1))
+        last_doc, before_doc = doc(start + loc - 1), doc(start - 1)
+        self.keep = (docs == before_doc).astype(F32)
+        self.keep_last = (last_doc == before_doc).astype(F32)
+        self.same_last = (docs == last_doc).astype(F32)
+        self.gate = proj[:, :di]
+        ext[m, EDGE : EDGE + loc, :] = proj[:, di : di + width].astype(BF).astype(F32)
+        total = jnp.broadcast_to(taps[K : K + 1, :], (loc, width))
+        self.shifted = []
+        for k in range(K):
+            back = K - 1 - k
+            value = ext[m, EDGE - back : EDGE - back + loc, :]
+            if back:
+                value = value * (docs == doc(self.at - back)).astype(F32)
+            self.shifted.append(value)
+            total = total + taps[k : k + 1, :] * value
+        self.sig = jax.nn.sigmoid(total)
+        self.total = total
+        filtered = total * self.sig
+        self.x = filtered[:, :di]
+        self.write = filtered[:, di : di + S].astype(BF)
+        self.read = filtered[:, di + S :].astype(BF)
+        self.raw = proj[:, di + width :] + heads_vec[0:1, :]
+        self.steps = jnp.maximum(self.raw, 0.0) + jnp.log1p(jnp.exp(-jnp.abs(self.raw)))
+        self.rate = heads_vec[1:2, :]
+        rise = self.steps * self.rate
+        rows, cols = iota((loc, loc), 0), iota((loc, loc), 1)
+        self.lower = (cols <= rows).astype(F32)
+        self.cum = exact(self.lower, rise, ((1,), (0,)))
+        cum_rows = exact(rise, (rows <= cols).astype(F32), ((0,), (0,)))
+        self.last = self.cum[loc - 1 : loc, :]
+        self.grow = jnp.exp(self.cum) * self.keep
+        self.fall = jnp.exp(self.last - self.cum) * self.same_last
+        self.decay = jnp.exp(self.last) * self.keep_last
+        allowed = (cols <= rows) & (docs == docs_row)
+        scores = mm_nt(self.read, self.write)
+        self.spread, self.mixing = [], []
+        for h in range(heads):
+            span = self.cum[:, h : h + 1] - cum_rows[h : h + 1, :]
+            shape = jnp.exp(jnp.where(allowed, span, -1e30))
+            self.spread.append(shape)
+            self.mixing.append(shape * scores)
+        self.lane = iota((1, di), 1)
+        self.steps_wide = self.widen(self.steps)
+        self.grow_wide = self.widen(self.grow)
+        self.weight_wide = self.widen(self.fall * self.steps)
+        self.scaled = self.x * self.steps_wide
+        self.pushed = self.x * self.weight_wide
+
+    def widen(self, v):
+        out = jnp.broadcast_to(v[:, 0:1], (v.shape[0], self.di))
+        for h in range(1, self.heads):
+            out = jnp.where(self.lane >= h * PS, v[:, h : h + 1], out)
+        return out
+
+    def per_head(self, parts):
+        out = parts[0]
+        for h in range(1, self.heads):
+            out = jnp.where(self.lane >= h * PS, parts[h], out)
+        return out
+
+    def decay_rows(self):
+        rows = iota((self.di, 1), 0)
+        out = jnp.broadcast_to(self.decay[:, 0:1], (self.di, 1))
+        for h in range(1, self.heads):
+            out = jnp.where(rows >= h * PS, self.decay[:, h : h + 1], out)
+        return out
+
+
+def forward_kernel(
+    heads, lengths, g, w, w_out, taps, heads_vec, lanes_vec, payload, proj, scan, states, ext, state
+):
+    b = pl.program_id(0)
+    loc = g.shape[1] // MB
+    di = heads * PS
+
+    @pl.when(b == 0)
+    def _():
+        ext[...] = jnp.zeros_like(ext)
+        state[...] = jnp.zeros_like(state)
+
+    proj[0] = mm(g[0], w[...])
+    column = iota((1, payload.shape[2]), 1)
+    for m in range(MB):
+        rows = slice(m * loc, (m + 1) * loc)
+        ext[m, 0:EDGE, :] = ext[m, loc : loc + EDGE, :]
+        part = Block(m, b * loc, proj[0, rows, :], ext, lengths, taps, heads_vec, heads)
+        before = state[m]
+        states[0, m] = before
+        scaled = part.scaled.astype(BF)
+        inner = part.per_head([mm(part.mixing[h].astype(BF), scaled) for h in range(heads)])
+        carried = mm_nt(part.read, before.astype(BF)) * part.grow_wide
+        out = inner + carried + lanes_vec[1:2, :] * part.x
+        scan[0, rows, :] = out
+        state[m] = part.decay_rows() * before + mm_tn(part.pushed.astype(BF), part.write)
+        y = out * (part.gate * jax.nn.sigmoid(part.gate))
+        square = jnp.sum(y * y, axis=1, keepdims=True)
+        high = square.astype(BF).astype(F32)
+        sent = mm((y * lanes_vec[0:1, :]).astype(BF), w_out[...])
+        sent = jnp.where(column == D, high, jnp.where(column == D + 1, square - high, sent))
+        payload[0, rows, :] = sent.astype(BF)
+
+
+def backward_kernel(
+    heads,
+    lengths,
+    grad,
+    w,
+    w_out,
+    taps,
+    heads_vec,
+    lanes_vec,
+    proj,
+    proj_before,
+    scan,
+    states,
+    d_proj,
+    normed_part,
+    d_out,
+    d_taps,
+    d_heads,
+    d_lanes,
+    ext,
+    d_ext,
+    d_state,
+):
+    step = pl.program_id(0)
+    b = pl.num_programs(0) - 1 - step
+    loc = grad.shape[1] // MB
+    di = heads * PS
+    width = di + 2 * S
+
+    @pl.when(step == 0)
+    def _():
+        for ref in (d_ext, d_state, d_out, d_taps, d_heads, d_lanes):
+            ref[...] = jnp.zeros_like(ref)
+
+    gated_grad = mm_nt(grad[0], w_out[...])
+    extra = grad[0, :, D:].astype(F32)
+    has_before = (b > 0).astype(F32)
+    pick = (iota((di, S), 0) // PS == iota((di, S), 1)).astype(F32)
+    for m in range(MB):
+        rows = slice(m * loc, (m + 1) * loc)
+        edge = proj_before[0, (m + 1) * loc - EDGE : (m + 1) * loc, di : di + width]
+        ext[m, 0:EDGE, :] = edge.astype(BF).astype(F32) * has_before
+        part = Block(m, b * loc, proj[0, rows, :], ext, lengths, taps, heads_vec, heads)
+        gain, skip = lanes_vec[0:1, :], lanes_vec[1:2, :]
+        r = extra[rows, 0:1] + extra[rows, 1:2]
+        s = extra[rows, 2:3] + extra[rows, 3:4]
+        out = scan[0, rows, :]
+        sig = jax.nn.sigmoid(part.gate)
+        act = part.gate * sig
+        yr = out * act * r
+        gg = gated_grad[rows]
+        d_lanes[0:1, :] += jnp.sum(gg * yr, axis=0, keepdims=True)
+        d_out[...] += mm_tn((yr * gain).astype(BF), grad[0, rows, :])
+        dy = r * (gg * gain) - yr * (r * s / DI)
+        d_gate = dy * out * (sig + act * (1.0 - sig))
+        do = dy * act
+        do_low = do.astype(BF)
+        x = part.x
+        d_lanes[1:2, :] += jnp.sum(do * x, axis=0, keepdims=True)
+        dx = skip * do
+        before = states[0, m]
+        before_low = before.astype(BF)
+        ds = d_state[m]
+        ds_low = ds.astype(BF)
+
+        d_scores = jnp.zeros((loc, loc), F32)
+        d_scaled, d_cum = [], jnp.zeros((loc, S), F32)
+        head_lane = iota((loc, S), 1)
+        for h in range(heads):
+            inside = (part.lane >= h * PS) & (part.lane < (h + 1) * PS)
+            own = jnp.where(inside, part.scaled, 0.0).astype(BF)
+            d_mix = mm_nt(do_low, own)
+            d_scaled.append(mm_tn(part.mixing[h].astype(BF), do_low))
+            d_scores = d_scores + d_mix * part.spread[h]
+            d_span = d_mix * part.mixing[h]
+            ones = (head_lane == h).astype(F32)
+            d_cum = d_cum + exact(d_span, ones, ((1,), (0,))) - exact(d_span, ones, ((0,), (0,)))
+        d_scaled = part.per_head(d_scaled)
+        dx = dx + d_scaled * part.steps_wide
+        d_scores_low = d_scores.astype(BF)
+        d_read = mm(d_scores_low, part.write)
+        d_write = mm_tn(d_scores_low, part.read)
+
+        d_carry = do * part.grow_wide
+        d_carry_low = d_carry.astype(BF)
+        carried = mm_nt(part.read, before_low)
+        d_read = d_read + mm(d_carry_low, before_low)
+
+        d_pushed = mm_nt(part.write, ds_low)
+        d_write = d_write + mm(part.pushed.astype(BF), ds_low)
+        dx = dx + d_pushed * part.weight_wide
+        sums = exact(
+            jnp.concatenate([d_carry * carried, d_pushed * x, d_scaled * x], axis=0),
+            pick,
+            ((1,), (0,)),
+        )
+        d_weight = sums[loc : 2 * loc]
+        d_fall = d_weight * part.fall * part.steps
+        d_cum = d_cum + sums[:loc] - d_fall
+        d_steps = sums[2 * loc :] + d_weight * part.fall
+        state_dot = jnp.sum(ds * before, axis=1, keepdims=True)
+        d_decay = exact(jnp.broadcast_to(state_dot, (di, S)), pick, ((0,), (0,)))[0:1, :]
+        d_last = jnp.sum(d_fall, axis=0, keepdims=True) + d_decay * part.decay
+        d_cum = d_cum + jnp.where(iota((loc, 1), 0) == loc - 1, d_last, 0.0)
+        d_state[m] = part.decay_rows() * ds + mm_tn(d_carry_low, part.read)
+
+        d_rise = exact(part.lower, d_cum, ((0,), (0,)))
+        d_steps = d_steps + d_rise * part.rate
+        d_raw = d_steps * jax.nn.sigmoid(part.raw)
+        d_heads[0:1, :] += jnp.sum(d_raw, axis=0, keepdims=True)
+        d_heads[1:2, :] += jnp.sum(d_rise * part.steps * part.rate, axis=0, keepdims=True)
+
+        d_total = jnp.concatenate([dx, d_write, d_read], axis=1)
+        d_total = d_total * (part.sig + part.total * part.sig * (1.0 - part.sig))
+        for k in range(K):
+            d_taps[k : k + 1, :] += jnp.sum(d_total * part.shifted[k], axis=0, keepdims=True)
+        d_taps[K : K + 1, :] += jnp.sum(d_total, axis=0, keepdims=True)
+        d_ext[m, loc : loc + EDGE, :] = d_ext[m, 0:EDGE, :]
+        d_ext[m, 0:loc, :] = d_total
+        d_seq = taps[K - 1 : K, :] * d_total
+        docs = part.doc(part.at)
+        for ahead in range(1, K):
+            same = (docs == part.doc(part.at + ahead)).astype(F32)
+            d_seq = d_seq + taps[K - 1 - ahead : K - ahead, :] * (
+                same * d_ext[m, ahead : ahead + loc, :]
+            )
+        d_proj[0, rows, :di] = d_gate.astype(BF)
+        d_proj[0, rows, di : di + width] = d_seq.astype(BF)
+        d_proj[0, rows, di + width :] = jnp.where(head_lane < heads, d_raw, 0.0).astype(BF)
+    normed_part[0] = mm_nt(d_proj[0], w[0:D, :]).astype(BF)
+
+
+def block_spec(shape, index):
+    return pl.BlockSpec((1,) + shape[1:], lambda i: (index(i),) + (0,) * (len(shape) - 1))
+
+
+def whole_spec(shape):
+    return pl.BlockSpec(shape, lambda i: (0,) * len(shape))
+
+
+def mixer_forward(lengths, g, w, w_out, taps, heads_vec, lanes_vec, heads):
+    nb, rows, _ = g.shape
+    di = heads * PS
+    width = di + 2 * S
+    shapes = [
+        jax.ShapeDtypeStruct((nb, rows, w_out.shape[1]), BF),
+        jax.ShapeDtypeStruct((nb, rows, w.shape[1]), F32),
+        jax.ShapeDtypeStruct((nb, rows, di), F32),
+        jax.ShapeDtypeStruct((nb, MB, di, S), F32),
+    ]
+    same = lambda i: i
+    return pl.pallas_call(
+        functools.partial(forward_kernel, heads),
+        grid=(nb,),
+        out_shape=shapes,
+        in_specs=[pl.BlockSpec(memory_space=pltpu.SMEM), block_spec(g.shape, same)]
+        + [whole_spec(v.shape) for v in (w, w_out, taps, heads_vec, lanes_vec)],
+        out_specs=[block_spec(v.shape, same) for v in shapes],
+        scratch_shapes=[
+            pltpu.VMEM((MB, rows // MB + EDGE, width), F32),
+            pltpu.VMEM((MB, di, S), F32),
+        ],
+        compiler_params=pltpu.CompilerParams(vmem_limit_bytes=VMEM_LIMIT),
+        name="mixer_forward",
+    )(lengths, g, w, w_out, taps, heads_vec, lanes_vec)
+
+
+def mixer_backward(lengths, grad, w, w_out, taps, heads_vec, lanes_vec, proj, scan, states, heads):
+    nb, rows, _ = grad.shape
+    di = heads * PS
+    width = di + 2 * S
+    back = lambda i: nb - 1 - i
+    before = lambda i: jnp.maximum(nb - 2 - i, 0)
+    per_block = [
+        jax.ShapeDtypeStruct((nb, rows, w.shape[1]), BF),
+        jax.ShapeDtypeStruct((nb, rows, D), BF),
+    ]
+    sums = [
+        jax.ShapeDtypeStruct((di, w_out.shape[1]), F32),
+        jax.ShapeDtypeStruct((8, width), F32),
+        jax.ShapeDtypeStruct((8, S), F32),
+        jax.ShapeDtypeStruct((8, di), F32),
+    ]
+    return pl.pallas_call(
+        functools.partial(backward_kernel, heads),
+        grid=(nb,),
+        out_shape=per_block + sums,
+        in_specs=[pl.BlockSpec(memory_space=pltpu.SMEM), block_spec(grad.shape, back)]
+        + [whole_spec(v.shape) for v in (w, w_out, taps, heads_vec, lanes_vec)]
+        + [block_spec(proj.shape, back), block_spec(proj.shape, before)]
+        + [block_spec(scan.shape, back), block_spec(states.shape, back)],
+        out_specs=[block_spec(v.shape, back) for v in per_block]
+        + [whole_spec(v.shape) for v in sums],
+        scratch_shapes=[
+            pltpu.VMEM((MB, rows // MB + EDGE, width), F32),
+            pltpu.VMEM((MB, rows // MB + EDGE, width), F32),
+            pltpu.VMEM((MB, di, S), F32),
+        ],
+        compiler_params=pltpu.CompilerParams(vmem_limit_bytes=VMEM_LIMIT),
+        name="mixer_backward",
+    )(lengths, grad, w, w_out, taps, heads_vec, lanes_vec, proj, proj, scan, states)
+
+
 def body(
     tokens,
     lengths,
@@ -472,23 +749,17 @@
     stream = tokens.reshape(rows_t, D).astype(F32)
     incoming = cotangent.reshape(rows_t, D)
     route_rows = routes.reshape(rows_t, TOP)
-    inc_all = lax.all_gather(incoming, "expert", axis=0, tiled=True)
-
     normed_wide, norm_pull = jax.vjp(rms_scale, stream, norm_gain)
     normed = normed_wide.astype(BF)
     normed_all = gather(jnp.concatenate([normed, packed], axis=1), "dp", 1)
+    early, _ = lax.optimization_barrier((incoming, normed_all))
+    inc_all = lax.all_gather(early, "expert", axis=0, tiled=True)
     packed_all = normed_all[:, :, D:].reshape(nd, rows_t, 256)[:, :, : packed_cols]
     packed_all = packed_all.reshape(nd, -1)
     sg_full = packed_all[:, : sg.size].reshape(D, 2 * fs)
     sd_full = packed_all[:, sg.size : sg.size + sd.size].reshape(fs, D)
     router_full = packed_all[:, sg.size + sd.size :].reshape(D, experts)
-    normed_all = normed_all.reshape(nd * rows_t, D + 256)
     w_wide = jnp.pad(w_in, ((0, 256), (0, 0)))
-    proj = mm(normed_all, w_wide).reshape(nd, MB, loc, wcols)
-
-    count = nd * loc
-    docs = doc_number(jnp.arange(count, dtype=jnp.int32)[None], lengths[:, 0])
-    docs_ext = doc_number(jnp.arange(count + K - 1, dtype=jnp.int32)[None] - (K - 1), lengths[:, 0])
     taps = jnp.concatenate(
         [lax.dynamic_slice_in_dim(filter_weight, me_d * di, di, 1), filter_weight[:, DI:]], axis=1
     )
@@ -498,21 +769,19 @@
     my_heads = lambda v: lax.dynamic_slice_in_dim(v, me_d * heads, heads, 0)
     my_gain = lax.dynamic_slice_in_dim(gated_gain, me_d * di, di, 0)
 
-    def mixer(p, a, b, c, d, e):
-        return mixer_local(p, a, b, c, d, e, docs, docs_ext, heads)
-
-    y, mixer_pull = jax.vjp(
-        mixer, proj, taps, tap_bias, my_heads(step_bias), my_heads(decay_log), my_heads(skip_gain)
-    )
-    y = y.reshape(nd * rows_t, di)
-    square = jnp.sum(y * y, axis=1, keepdims=True)
+    taps_vec = jnp.concatenate([taps, tap_bias[None], jnp.zeros((3, di + 2 * S), F32)], axis=0)
+    heads_vec = jnp.stack([my_heads(step_bias), -jnp.exp(my_heads(decay_log))])
+    heads_vec = jnp.pad(heads_vec, ((0, 6), (0, S - heads)))
+    lanes_vec = jnp.pad(
+        jnp.stack([my_gain, jnp.repeat(my_heads(skip_gain), PS)]), ((0, 6), (0, 0))
+    )
     out_wide = jnp.pad(output_weight, ((0, 0), (0, 128)))
+    vectors = (taps_vec, heads_vec, lanes_vec)
+    payload, proj, scan, states = mixer_forward(
+        lengths[:, 0], normed_all, w_wide, out_wide, *vectors, heads
+    )
     column = lax.broadcasted_iota(jnp.int32, (1, D + 128), 1)
-    partial = mm((y * my_gain).astype(BF), out_wide)
-    sq_hi, sq_lo = hi_lo(square)
-    payload = jnp.where(column == D, sq_hi.astype(F32), partial)
-    payload = jnp.where(column == D + 1, sq_lo.astype(F32), payload).astype(BF)
-    summed = reduce_scatter(payload.reshape(nd, rows_t, D + 128), "dp", 2)
+    summed = reduce_scatter(payload, "dp", 2)
     r = lax.rsqrt((summed[:, D : D + 1] + summed[:, D + 1 : D + 2]) / DI + EPSILON)
     mixed = summed[:, :D] * r
     after_mixer = stream + mixed
@@ -573,7 +842,6 @@
         place = D + me_e * el + i
         dx_part = jnp.where(column == place, g_hi.astype(F32), dx_part)
         dx_part = jnp.where(column == place + experts, g_lo.astype(F32), dx_part)
-    out_sum = lax.psum_scatter(out_part.astype(BF), "expert", scatter_dimension=0, tiled=True)
     back_sum = reduce_scatter(dx_part.astype(BF).reshape(ne, rows_t, D + 128), "expert", 4)
     inc = incoming.astype(F32)
     spread_sum = back_sum[:, D : D + experts] + back_sum[:, D + experts : D + 2 * experts]
@@ -590,20 +858,16 @@
     grad_payload = jnp.concatenate(
         [after_low, r_hi, r_lo, d_hi, d_lo, jnp.zeros((rows_t, 124), BF)], axis=1
     )
-    grad_all = gather(grad_payload, "dp", 5).reshape(nd * rows_t, D + 128)
-    extra = grad_all[:, D : D + 4].astype(F32)
-    r_all = extra[:, 0:1] + extra[:, 1:2]
-    s_all = extra[:, 2:3] + extra[:, 3:4]
-    gated_grad = mm_nt(grad_all, out_wide)
-    yr = y * r_all
-    output_part = mm_tn((yr * my_gain).astype(BF), grad_all)[:, :D]
-    gated_gain_part = jnp.sum(gated_grad * yr, axis=0)
-    dy = r_all * (gated_grad * my_gain) - yr * (r_all * s_all / DI)
-    pulls = mixer_pull(dy.reshape(nd, MB, loc, di))
-    d_proj = pulls[0].astype(BF).reshape(nd * rows_t, wcols)
-    normed_part = mm_nt(d_proj, w_in)
-    normed_grad = reduce_scatter(normed_part.astype(BF).reshape(nd, rows_t, D), "dp", 6)
-    d_win = mm_tn(normed_all, d_proj)[:D].astype(BF)
+    grad_all = gather(grad_payload, "dp", 5)
+    d_proj, normed_part, output_part, d_taps, d_heads, d_lanes = mixer_backward(
+        lengths[:, 0], grad_all, w_wide, out_wide, *vectors, proj, scan, states, heads
+    )
+    output_part = output_part[:, :D]
+    out_part, _ = lax.optimization_barrier((out_part.astype(BF), d_proj))
+    out_sum = lax.psum_scatter(out_part, "expert", scatter_dimension=0, tiled=True)
+    normed_grad = reduce_scatter(normed_part, "dp", 6)
+    d_win = mm_tn(normed_all.reshape(nd * rows_t, -1), d_proj.reshape(nd * rows_t, wcols))
+    d_win = d_win[:D].astype(BF)
     stream_from_norm, norm_gain_grad = norm_pull(normed_grad)
     tokens_grad = after_grad + stream_from_norm
 
@@ -614,8 +878,10 @@
         [d_down[i * FE : (i + 1) * FE].reshape(nd, FE // nd, D) for i in range(el)], axis=1
     ).reshape(nd, el * FE // nd, D)
     down_blocks = jnp.concatenate([down_blocks, d_down[el * FE :].reshape(nd, fsl, D)], axis=1)
-    up_sum = lax.psum_scatter(up_blocks, "dp", scatter_dimension=0, tiled=True)[0]
-    down_sum = lax.psum_scatter(down_blocks, "dp", scatter_dimension=0, tiled=True)[0]
+    down_blocks = down_blocks.reshape(nd, -1, 2 * width)
+    all_blocks = jnp.concatenate([up_blocks, down_blocks], axis=1)
+    all_sum = lax.psum_scatter(all_blocks, "dp", scatter_dimension=0, tiled=True)[0]
+    up_sum, down_sum = all_sum[:dr], all_sum[dr:].reshape(-1, D)
     expert_up_grad = jnp.stack(
         [
             jnp.concatenate(
@@ -645,13 +911,13 @@
         )
 
     small_parts = (
-        jnp.concatenate([spread_heads(pulls[1][:, :di], DI, di), pulls[1][:, di:]], axis=1),
-        jnp.concatenate([spread_heads(pulls[2][:di], DI, di), pulls[2][di:]], axis=0),
-        spread_heads(pulls[3], H, heads),
-        spread_heads(pulls[4], H, heads),
-        spread_heads(pulls[5], H, heads),
+        jnp.concatenate([spread_heads(d_taps[:K, :di], DI, di), d_taps[:K, di:]], axis=1),
+        jnp.concatenate([spread_heads(d_taps[K, :di], DI, di), d_taps[K, di:]], axis=0),
+        spread_heads(d_heads[0, :heads], H, heads),
+        spread_heads(d_heads[1, :heads], H, heads),
+        spread_heads(jnp.sum(d_lanes[1].reshape(heads, PS), axis=1), H, heads),
         norm_gain_grad,
-        spread_heads(gated_gain_part, DI, di),
+        spread_heads(d_lanes[0], DI, di),
         moe_gain_grad,
         router_part,
     )

time: 974 us -> 809 us (0.83)
  Pallas kernels: 405 us -> 533 us
  local copies, waits for them, and re-layouts: 187 us -> 98.8 us
  matrix products: 171 us -> 92.3 us
  other arithmetic: 121 us -> 53 us
  waiting for transfers between devices: 56.3 us -> 0.08 us
    pallas_call x0 -> x2, Pallas kernels: none -> 125 us  [the longest x1 85.6 us: mixer_backward(): pl.pallas_call(functools.partial(backward_kernel, heads), grid=(nb,), out...]
    reduce_scatter x3 -> x2, waiting for transfers between devices: 55.6 us -> 0.01 us  [the longest x1 0.01 us: body(): lax.psum_scatter(out_part, 'expert', scatter_dimension=0, tiled=True)]
    dot_general x13 -> x0, matrix products: 30 us -> none  [the longest x3 11 us: mixer_local(): inner = jnp.einsum('bmhts,bmshp->bmthp', weights, x * steps[..., None])]
    another operation x5 -> x3, other arithmetic: 28.5 us -> 1.29 us  [the longest x2 0.69 us: body(): heads_vec = jnp.stack([my_heads(step_bias), -jnp.exp(my_heads(decay_log))])]
    reduce_sum x7 -> x1, other arithmetic: 26.1 us -> 0.12 us  [body(): jnp.sum(d_lanes[1].reshape(heads, PS), axis=1)]
    pallas_call x3, Pallas kernels: 111 us -> 134 us  [exchange(): pl.pallas_call(functools.partial(exchange_kernel, plan), out_shape=shapes...]
    unnamed x294 -> x90, local copies, waits for them, and re-layouts: 33 us -> 13.4 us
    dot_general x5 -> x3, matrix products: 52.3 us -> 33 us  [mm_nt(): lax.dot_general(a, b, (((1,), (1,)), ((), ())), preferred_element_type=F32)]
  transfers between devices with their start and end apart: 5 -> 4, of which waited for: 1 -> 0; matrix products, arithmetic and copies ran while one was open for 41% -> 18% of each run, Pallas kernels for 38% -> 41%
where the time goes in v3:
time: 809 us; the launch traced here: 800 us
  Pallas kernels  533 us (66%)
  local copies, waits for them, and re-layouts  98.8 us (12%)
  matrix products  92.3 us (11%)
  other arithmetic  53 us (7%)
  between operations  15.2 us (2%)
    pallas_call x3, Pallas kernels, gather(): pl.pallas_call(functools.partial(gather_kernel, axis), out_shape=jax.Shap...  153 us
    pallas_call x3, Pallas kernels, exchange(): pl.pallas_call(functools.partial(exchange_kernel, plan), out_shape=shapes...  134 us
    pallas_call x3, Pallas kernels, reduce_scatter(): pl.pallas_call(functools.partial(reduce_kernel, axis), out_shape=jax.Shap...  121 us
    pallas_call x1, Pallas kernels, mixer_backward(): pl.pallas_call(functools.partial(backward_kernel, heads), grid=(nb,), out...  85.6 us
    pallas_call x1, Pallas kernels, mixer_forward(): pl.pallas_call(functools.partial(forward_kernel, heads), grid=(nb,), out_...  39.1 us
    dot_general x4, matrix products, mm_tn(): lax.dot_general(a, b, (((0,), (0,)), ((), ())), preferred_element_type=F32)  33.9 us
    dot_general x3, matrix products, mm_nt(): lax.dot_general(a, b, (((1,), (1,)), ((), ())), preferred_element_type=F32)  33 us
    dot_general x3, matrix products, mm(): return jnp.dot(a, b, preferred_element_type=F32)  25.4 us
  transfers between devices with their start and end apart: 4, of which 0 were waited for; matrix products, arithmetic and copies ran while one was open for 18% of the time, Pallas kernels for 41%

profile of v3, /device:TPU:1, one launch (start us, length us, event | category | flops | bytes accessed | tf_op | source)
XLA Modules:
  0.0 800.0 jit_solution(9437359803931251850)
XLA Ops:
  12.1 4.8 concatenate.66
  16.9 7.5 all-to-all-start
  28.5 67.0 %gather_dp.2.g = bf16[16,160,1792]{2,1,0:T(8,128)(2,1)} custom-call(bf16[160,1792]{1,0:T(8,128)(2,1)} %fusion.17.x), custom_call_target="tpu_custom_call" | custom-call | tf_op jit(solution)/shard_map/gather_dp/pallas_call | solution.py:151
  101.3 5.2 slice_bitcast_fusion
  128.6 39.1 %mixer_forward.1 = (bf16[16,160,1664]{2,1,0:T(8,128)(2,1)}, f32[16,160,768]{2,1,0:T(8,128)}, f32[16,160,192]{2,1,0:T(8,128)}, f32[16,2,192,128]{3,2,1,0:T(8,128)}) custom-call(s32[2,3]{1,0:T(2,128)} %bitcast.140, bf16[16,160,1792]{2,1,0:T(8,128)(2,1)} %gather_dp.2.g, bf16[1792,768]{1,0:T(8,128)(2,1)} %pad.33.w, bf16[192,1664]{1,0:T(8,128)(2,1)} %pad.34.w_out, ...), custom_call_target="tpu_custom_call" | custom-call | tf_op jit(solution)/shard_map/mixer_forward/pallas_call | solution.py:642
  167.7 43.2 %reduce_dp.2 = f32[160,1664]{1,0:T(8,128)} custom-call(bf16[16,160,1664]{2,1,0:T(8,128)(2,1)} %get-tuple-element.40.x), custom_call_target="tpu_custom_call" | custom-call | tf_op jit(solution)/shard_map/reduce_dp/pallas_call | solution.py:270
  216.0 39.7 %gather_expert.1 = bf16[8,160,1664]{2,1,0:T(8,128)(2,1)} custom-call(bf16[160,1664]{1,0:T(8,128)(2,1)} %concatenate.70.x), custom_call_target="tpu_custom_call" | custom-call | tf_op jit(solution)/shard_map/gather_expert/pallas_call | solution.py:151
  257.7 15.9 %fusion.5 = f32[1280,2304]{1,0:T(8,128)} fusion(bf16[1280,1664]{1,0:T(8,128)(2,1)} %bitcast.111, bf16[1536,2304]{1,0:T(8,128)(2,1)} %slice_dynamic-update-slice_fusion.4), kind=kOutput, calls=%fused_computation.10 | convolution fusion | flops 9814671360 | bytes 23134208 | tf_op jit(solution)/shard_map/dot_general | solution.py:30
  277.1 15.4 %multiply_convert_fusion.1 = (bf16[1280,1152]{1,0:T(8,128)(2,1)}, bf16[1280,1152]{1,0:T(8,128)(2,1)}, f32[1280,1152]{1,0:T(8,128)}, bf16[1280,1152]{1,0:T(8,128)(2,1)}) fusion(f32[1280,2304]{1,0:T(8,128)} %fusion.5, f32[1280,512]{1,0:T(8,128)} %broadcast_in_dim.118, f32[1280,512]{1,0:T(8,128)} %broadcast_in_dim.116, f32[1152]{0:T(1024)S(1)} %pad.69.clone, ...), kind=kOutput, calls=%fused_computation.18 | convolution fusion | flops 4568481792 | bytes 39260672 | tf_op jit(solution)/shard_map/dot_general | solution.py:34
  295.9 15.9 %fusion.3 = bf16[1280,1664]{1,0:T(8,128)(2,1)} fusion(bf16[1536,2304]{1,0:T(8,128)(2,1)} %slice_dynamic-update-slice_fusion.4, bf16[1280]{0:T(1024)(128)(2,1)S(1)} %get-tuple-element.176, bf16[1280]{0:T(1024)(128)(2,1)S(1)} %get-tuple-element.175, bf16[1280]{0:T(1024)(128)(2,1)S(1)} %get-tuple-element.174, bf16[1280]{0:T(1024)(128)(2,1)S(1)} %get-tuple-element.173, ...), kind=kOutput, calls=%fused_computation.7 | convolution fusion | flops 9834987520 | bytes 17252864 | tf_op jit(solution)/shard_map/dot_general | solution.py:34
  311.8 37.6 %reduce_expert.1 = f32[160,1664]{1,0:T(8,128)} custom-call(bf16[8,160,1664]{2,1,0:T(8,128)(2,1)} %bitcast.114), custom_call_target="tpu_custom_call" | custom-call | tf_op jit(solution)/shard_map/reduce_expert/pallas_call | solution.py:270
  358.3 46.7 %gather_dp.3.grad = bf16[16,160,1664]{2,1,0:T(8,128)(2,1)} custom-call(bf16[160,1664]{1,0:T(8,128)(2,1)} %concatenate.75.x), custom_call_target="tpu_custom_call" | custom-call | tf_op jit(solution)/shard_map/gather_dp/pallas_call | solution.py:151
  405.0 9.3 %convolution_convert_fusion = bf16[1280,1536]{1,0:T(8,128)(2,1)} fusion(bf16[1280,1152]{1,0:T(8,128)(2,1)} %get-tuple-element.146, bf16[128,1536]{1,0:T(8,128)(2,1)S(1)} %reshape.351, bf16[512,1536]{1,0:T(8,128)(2,1)} %get-tuple-element.154, bf16[512,1536]{1,0:T(8,128)(2,1)} %get-tuple-element.153), kind=kOutput, calls=%fused_computation.6 | convolution fusion | flops 4542431232 | bytes 10420224 | tf_op jit(solution)/shard_map/dot_general | solution.py:30
  414.2 85.6 %mixer_backward.1 = (bf16[16,160,768]{2,1,0:T(8,128)(2,1)}, bf16[16,160,1536]{2,1,0:T(8,128)(2,1)}, f32[192,1664]{1,0:T(8,128)}, f32[8,448]{1,0:T(8,128)}, f32[8,128]{1,0:T(8,128)}, /*index=5*/f32[8,192]{1,0:T(8,128)}) custom-call(s32[2,3]{1,0:T(2,128)} %bitcast.141, bf16[16,160,1664]{2,1,0:T(8,128)(2,1)} %gather_dp.3.grad, bf16[1792,768]{1,0:T(8,128)(2,1)} %pad.33.w, ...), custom_call_target="tpu_custom_call" | custom-call | tf_op jit(solution)/shard_map/mixer_backward/pallas_call | solution.py:674
  499.9 14.8 %fusion.10 = bf16[1664,2304]{1,0:T(8,128)(2,1)S(1)} fusion(bf16[1280,1664]{1,0:T(8,128)(2,1)} %bitcast.112, bf16[1280,1152]{1,0:T(8,128)(2,1)} %get-tuple-element.144, bf16[1280,1152]{1,0:T(8,128)(2,1)} %get-tuple-element.143), kind=kOutput, calls=%fused_computation.23 | convolution fusion | flops 9826467840 | bytes 17825792 | tf_op jit(solution)/shard_map/dot_general | solution.py:38
  514.7 3.4 slice.439
  518.1 7.4 convolution_convert_fusion.1
  528.2 6.3 reshape.367
  534.5 9.4 %pad_maximum_fusion = bf16[16,144,2304]{2,1,0:T(8,128)(2,1)} fusion(bf16[16,48,2304]{2,1,0:T(8,128)(2,1)} %reshape.367, bf16[16,96,2304]{2,1,0:T(8,128)(2,1)} %bitcast.104), kind=kLoop, calls=%fused_computation.1 | loop fusion | flops 21233664 | bytes 21233664 | tf_op jit(solution)/shard_map/concatenate | solution.py:882
  545.9 39.8 %reduce_dp.3 = f32[160,1536]{1,0:T(8,128)} custom-call(bf16[16,160,1536]{2,1,0:T(8,128)(2,1)} %get-tuple-element.47.x), custom_call_target="tpu_custom_call" | custom-call | tf_op jit(solution)/shard_map/reduce_dp/pallas_call | solution.py:270
  586.5 11.3 %convolution_bitcast_fusion = bf16[1792,768]{1,0:T(8,128)(2,1)S(1)} fusion(bf16[16,160,1792]{2,1,0:T(8,128)(2,1)} %gather_dp.2.g, bf16[16,160,768]{2,1,0:T(8,128)(2,1)} %get-tuple-element.45), kind=kOutput, calls=%fused_computation.24 | convolution fusion | flops 7046430720 | bytes 15859712 | tf_op jit(solution)/shard_map/dot_general | solution.py:38
  604.8 53.0 %exchange.3 = (bf16[16,96,768]{2,1,0:T(8,128)(2,1)}, f32[16,24,128]{2,1,0:T(8,128)}) custom-call(bf16[16,96,768]{2,1,0:T(8,128)(2,1)} %bitcast.107, f32[16,24,128]{2,1,0:T(8,128)} %bitcast.121), custom_call_target="tpu_custom_call" | custom-call | tf_op jit(solution)/shard_map/exchange/pallas_call | solution.py:344
  667.8 45.0 %exchange.4 = (bf16[8,192,384]{2,1,0:T(8,128)(2,1)}, f32[8,32,128]{2,1,0:T(8,128)}, bf16[8,48,768]{2,1,0:T(8,128)(2,1)}, f32[8,24,128]{2,1,0:T(8,128)}) custom-call(bf16[8,192,384]{2,1,0:T(8,128)(2,1)} %bitcast.113, f32[8,32,128]{2,1,0:T(8,128)} %bitcast.123, bf16[8,48,768]{2,1,0:T(8,128)(2,1)} %reshape.363.refs_2_, f32[24,128]{1,0:T(8,128)} %reduce_sum.220.refs_3_), custom_call_target="tpu_custom_call" | custom-call | tf_op jit(solution)/shard_map/exchange/pallas_call | solution.py:344
  727.7 36.1 %exchange.5 = (bf16[8,192,384]{2,1,0:T(8,128)(2,1)}, f32[8,32,128]{2,1,0:T(8,128)}, bf16[8,48,768]{2,1,0:T(8,128)(2,1)}, bf16[8,96,384]{2,1,0:T(8,128)(2,1)}, f32[16,24,128]{2,1,0:T(8,128)}) custom-call(bf16[192,384]{1,0:T(8,128)(2,1)} %reduce_sum.221.refs_0_, f32[32,128]{1,0:T(8,128)} %reduce_sum.222.refs_1_, bf16[48,768]{1,0:T(8,128)(2,1)} %reduce_sum.223.refs_2_, ...), custom_call_target="tpu_custom_call" | custom-call | tf_op jit(solution)/shard_map/exchange/pallas_call | solution.py:344
  (292 shorter events, 125.6 us)
Async XLA Ops:
  7.2 17.3 %copy-start = (bf16[64,1536]{1,0:T(8,128)(2,1)S(1)}, bf16[64,1536]{1,0:T(8,128)(2,1)}, u32[]{:S(2)}) copy-start(bf16[64,1536]{1,0:T(8,128)(2,1)} %param.35) | copy-start | bytes 589828
  16.9 9.8 %copy-start.30 = (bf16[96,16]{0,1:T(8,128)(2,1)S(1)}, bf16[96,16]{0,1:T(8,128)(2,1)}, u32[]{:S(2)}) copy-start(bf16[96,16]{0,1:T(8,128)(2,1)} %param.33) | copy-start | bytes 9220
  16.9 10.2 %copy-start.2 = (bf16[2,1,80,1536]{3,2,1,0:T(8,128)(2,1)S(1)}, bf16[2,1,80,1536]{3,2,1,0:T(8,128)(2,1)}, u32[]{:S(2)}) copy-start(bf16[2,1,80,1536]{3,2,1,0:T(8,128)(2,1)} %param.19) | copy-start | bytes 1474564
  16.9 10.5 %copy-start.19 = (f32[1536]{0:T(1024)S(1)}, f32[1536]{0:T(1024)}, u32[]{:S(2)}) copy-start(f32[1536]{0:T(1024)} %param.29) | copy-start | bytes 18436
  16.9 108.3 %all-to-all-start = ((bf16[16,96,768]{2,1,0:T(8,128)(2,1)}), bf16[16,96,768]{2,1,0:T(8,128)(2,1)}, u32[]{:S(2)}, u32[]{:S(2)}) async-start(bf16[16,96,768]{2,1,0:T(8,128)(2,1)} %concatenate.66), calls=%async_computation | async-start | bytes 4718592 | tf_op jit(solution)/shard_map/all_to_all | solution.py:739
  24.4 249.1 %all-gather.2.cloned.1.call-start = ((), (), s32[]{:S(2)}) async-start(), calls=%async_computation.3 | async-start | bytes 4423680 | tf_op jit(solution)/shard_map/all_gather | solution.py:756
  27.4 68.1 %copy-start.25 = (f32[160]{0:T(256)}, f32[160]{0:T(256)S(1)}, u32[]{:S(2)}) copy-start(f32[160]{0:T(256)S(1)} %add.127) | copy-start | bytes 1924
  27.5 68.1 %copy-start.21 = (f32[160]{0:T(256)}, f32[160]{0:T(256)S(1)}, u32[]{:S(2)}) copy-start(f32[160]{0:T(256)S(1)} %rsqrt.23) | copy-start | bytes 1924
  28.5 67.3 %copy-start.31 = (f32[3328]{0:T(1024)S(1)}, f32[3328]{0:T(1024)}, u32[]{:S(2)}) copy-start(f32[3328]{0:T(1024)} %param.25) | copy-start | bytes 39940
  28.5 67.4 %copy-start.24 = (f32[4,3328]{1,0:T(4,128)S(1)}, f32[4,3328]{1,0:T(4,128)}, u32[]{:S(2)}) copy-start(f32[4,3328]{1,0:T(4,128)} %param.24) | copy-start | bytes 159748
  28.5 67.5 %copy-start.36 = (f32[48]{0:T(128)S(1)}, f32[48]{0:T(128)}, u32[]{:S(2)}) copy-start(f32[48]{0:T(128)} %param.28) | copy-start | bytes 580
  95.6 626.6 %reduce-scatter.3.cloned.1.call-start = ((), (), s32[]{:S(2)}) async-start(), calls=%async_computation.4 | async-start | bytes 4423680 | tf_op jit(solution)/shard_map/reduce_scatter | solution.py:867
  101.3 8.4 %slice-start.5 = ((f32[3328]{0:T(1024)}), f32[256]{0:T(256)S(1)}, s32[]{:S(2)}) async-start(f32[3328]{0:T(1024)} %param.25), calls=%async_computation.11 | async-start | bytes 2048 | tf_op jit(solution)/shard_map/slice | solution.py:767
  101.3 10.0 %copy-start.34 = (f32[48]{0:T(128)S(1)}, f32[48]{0:T(128)}, u32[]{:S(2)}) copy-start(f32[48]{0:T(128)} %param.27) | copy-start | bytes 580
  101.3 10.0 %copy-start.35 = (f32[48]{0:T(128)S(1)}, f32[48]{0:T(128)}, u32[]{:S(2)}) copy-start(f32[48]{0:T(128)} %param.26) | copy-start | bytes 580
  311.8 41.6 %copy-start.11 = (bf16[2,1,80,1536]{3,2,1,0:T(8,128)(2,1)S(1)}, bf16[2,1,80,1536]{3,2,1,0:T(8,128)(2,1)}, u32[]{:S(2)}) copy-start(bf16[2,1,80,1536]{3,2,1,0:T(8,128)(2,1)} %param.22) | copy-start | bytes 1474564
  499.9 224.2 %reduce-scatter.5.cloned.1.call-start = ((), (), s32[]{:S(2)}) async-start(), calls=%async_computation.5 | async-start | bytes 11280384 | tf_op jit(solution)/shard_map/reduce_scatter | solution.py:883
  663.2 56.6 %copy-start.26 = (f32[160]{0:T(256)S(1)}, f32[160]{0:T(256)}, u32[]{:S(2)}) copy-start(f32[160]{0:T(256)} %copy-done.25) | copy-start | bytes 1924
  663.2 56.5 %copy-start.29 = (f32[160]{0:T(256)S(1)}, f32[160]{0:T(256)}, u32[]{:S(2)}) copy-start(f32[160]{0:T(256)} %get-tuple-element.136) | copy-start | bytes 1924
  663.2 56.5 %copy-start.23 = (f32[160]{0:T(256)S(1)}, f32[160]{0:T(256)}, u32[]{:S(2)}) copy-start(f32[160]{0:T(256)} %copy-done.21) | copy-start | bytes 1924
  726.9 46.3 %copy-start.14 = (bf16[72,1536]{1,0:T(8,128)(2,1)}, bf16[72,1536]{1,0:T(8,128)(2,1)S(1)}, u32[]{:S(2)}) copy-start(bf16[72,1536]{1,0:T(8,128)(2,1)S(1)} %reshape.368) | copy-start | bytes 663556
  763.8 9.5 %copy-start.13 = (bf16[8,192,384]{2,1,0:T(8,128)(2,1)S(1)}, bf16[8,192,384]{2,1,0:T(8,128)(2,1)}, u32[]{:S(2)}) copy-start(bf16[8,192,384]{2,1,0:T(8,128)(2,1)} %get-tuple-element.58) | copy-start | bytes 3538948
  783.1 8.4 %copy-start.8 = (f32[96,3072]{1,0:T(8,128)S(1)}, f32[96,3072]{1,0:T(8,128)}, u32[]{:S(2)}) copy-start(f32[96,3072]{1,0:T(8,128)} %reshape.370) | copy-start | bytes 3538948
  783.1 8.4 %copy-start.9 = (f32[96,3072]{1,0:T(8,128)S(1)}, f32[96,3072]{1,0:T(8,128)}, u32[]{:S(2)}) copy-start(f32[96,3072]{1,0:T(8,128)} %reshape.371) | copy-start | bytes 3538948
  (25 other events, 103.6 us)
Sparse Core Ops, SparseCore 0:
  95.7 69.5 all-gather.1
  500.0 80.6 reduce-scatter.2
  583.2 118.8 reduce-scatter.4

commit v4 on v3

--- a/solution.py
+++ b/solution.py
@@ -47,6 +47,10 @@
     return hi, (v - hi.astype(F32)).astype(BF)
 
 
+ANY = pl.BlockSpec(memory_space=pl.ANY)
+IN_VMEM = pl.BlockSpec(memory_space=pltpu.VMEM)
+
+
 def places(axis):
     me = lax.axis_index(axis)
     if axis == "dp":
@@ -64,37 +68,74 @@
     return me, at
 
 
-def greet(axis, peers):
-    barrier = pltpu.get_barrier_semaphore()
-    for peer in peers:
-        pl.semaphore_signal(barrier, inc=1, device_id={axis: peer}, device_id_type=MESH)
-    pl.semaphore_wait(barrier, len(peers))
-
-
-def gather_kernel(axis, x, out, send, recv, own_sem):
+class Task:
+    ins, outs, scratch, reaches = (), (), (), ()
+
+
+def peers_of(axis, everyone):
     me, at = places(axis)
-    cores = axis == "dp"
-    half = x.shape[0] // 2
-    up, down, pair, sib = at(1, 0), at(-1, 0), at(0, 1), at(0, 0, 1)
-    greet(axis, [up, down, pair] + ([sib] if cores else []))
-    whole = pl.ds(0, 2 * half)
-    first, second = pl.ds(0, half), pl.ds(half, half)
-    started = []
-
-    def push(number, slot, rows, peer, src=None):
+    if everyone:
+        n = lax.axis_size(axis)
+        return [lax.rem(me + k, n) for k in range(1, n)]
+    near = [at(1, 0), at(-1, 0), at(0, 1)]
+    return near + [at(0, 0, 1)] if axis == "dp" else near
+
+
+class Links:
+    def __init__(self, axis, send, recv):
+        self.axis, self.send, self.recv, self.started = axis, send, recv, []
+
+    def push(self, number, src, dst, peer):
         copy = pltpu.make_async_remote_copy(
-            src_ref=(out.at[slot] if src is None else src).at[rows],
-            dst_ref=out.at[slot].at[rows],
-            send_sem=send.at[number],
-            recv_sem=recv.at[number],
-            device_id={axis: peer},
+            src_ref=src,
+            dst_ref=dst,
+            send_sem=self.send.at[number],
+            recv_sem=self.recv.at[number],
+            device_id={self.axis: peer},
             device_id_type=MESH,
         )
         copy.start()
-        started.append(copy)
+        self.started.append(copy)
+
+    def arrived(self, number, dst):
+        pltpu.make_async_copy(dst, dst, self.recv.at[number]).wait()
+
+    def finish(self):
+        for copy in self.started:
+            copy.wait_send()
+
+
+def halves(rows):
+    cut = rows // 32 * 16
+    return pl.ds(0, rows), pl.ds(0, cut), pl.ds(cut, rows - cut), cut
+
+
+class Gather(Task):
+    def __init__(self, axis, x):
+        self.axis, self.reaches = axis, ((axis, False),)
+        self.ins = ((x, ANY),)
+        n = lax.axis_size(axis)
+        self.outs = ((jax.ShapeDtypeStruct((n,) + x.shape, x.dtype), ANY),)
+        dma = pltpu.SemaphoreType.DMA
+        self.scratch = (dma((17,)), dma((17,)), dma)
+
+    def steps(self, ins, outs, scratch):
+        return gather_steps(self.axis, ins[0], outs[0], *scratch)
+
+
+def gather_steps(axis, x, out, send, recv, own_sem):
+    me, at = places(axis)
+    cores = axis == "dp"
+    up, down, pair, sib = at(1, 0), at(-1, 0), at(0, 1), at(0, 0, 1)
+    whole, first, second, _ = halves(x.shape[0])
+    links = Links(axis, send, recv)
+
+    def push(number, slot, rows, peer, src=None):
+        src = out.at[slot] if src is None else src
+        links.push(number, src.at[rows], out.at[slot].at[rows], peer)
 
     def arrived(number, slot, rows):
-        pltpu.make_async_copy(out.at[slot].at[rows], out.at[slot].at[rows], recv.at[number]).wait()
+        links.arrived(number, out.at[slot].at[rows])
 
     push(0, me, whole, up, x)
     push(1, me, whole, down, x)
@@ -103,11 +144,13 @@
         push(3, me, whole, sib, x)
     own = pltpu.make_async_copy(x, out.at[me], own_sem)
     own.start()
+    yield
     arrived(2, pair, whole)
     push(4, pair, whole, up)
     push(5, pair, whole, down)
     if cores:
         push(6, pair, whole, sib)
+    yield
     arrived(0, down, whole)
     push(7, down, first, up)
     arrived(1, up, whole)
@@ -115,6 +158,7 @@
     if cores:
         push(9, down, whole, sib)
         push(10, up, whole, sib)
+    yield
     arrived(4, at(-1, 1), whole)
     push(11, at(-1, 1), first, up)
     arrived(5, at(1, 1), whole)
@@ -122,14 +166,17 @@
     if cores:
         push(13, at(-1, 1), whole, sib)
         push(14, at(1, 1), whole, sib)
+    yield
     arrived(7, at(2, 0), first)
     arrived(8, at(2, 0), second)
     if cores:
         push(15, at(2, 0), whole, sib)
+    yield
     arrived(11, at(2, 1), first)
     arrived(12, at(2, 1), second)
     if cores:
         push(16, at(2, 1), whole, sib)
+        yield
         for number, hop, other in (
             (3, 0, 0),
             (6, 0, 1),
@@ -142,72 +189,64 @@
         ):
             arrived(number, at(hop, other, 1), whole)
     own.wait()
-    for copy in started:
-        copy.wait_send()
-
-
-def gather(x, axis, number):
-    n = lax.axis_size(axis)
-    return pl.pallas_call(
-        functools.partial(gather_kernel, axis),
-        out_shape=jax.ShapeDtypeStruct((n,) + x.shape, x.dtype),
-        in_specs=[pl.BlockSpec(memory_space=pl.ANY)],
-        out_specs=pl.BlockSpec(memory_space=pl.ANY),
-        scratch_shapes=[
-            pltpu.SemaphoreType.DMA((17,)),
-            pltpu.SemaphoreType.DMA((17,)),
-            pltpu.SemaphoreType.DMA,
-        ],
-        compiler_params=pltpu.CompilerParams(
-            collective_id=number, has_side_effects=True, vmem_limit_bytes=VMEM_LIMIT
-        ),
-        name="gather_" + axis,
-    )(x)
+    links.finish()
 
 
 ORDER = ((2, 1), (2, 0), (1, 1), (-1, 1), (1, 0), (-1, 0), (0, 1), (0, 0))
 
 
-def reduce_kernel(axis, x, out, acc, sib_buf, a_buf, b_buf, c_buf, d_buf, e_buf, send, recv, load):
+class Reduce(Task):
+    def __init__(self, axis, x, dtype=F32):
+        self.axis, self.reaches = axis, ((axis, False),)
+        n, rows, columns = x.shape
+        self.ins = ((x, ANY),)
+        self.outs = ((jax.ShapeDtypeStruct((rows, columns), dtype), IN_VMEM),)
+        _, _, _, cut = halves(rows)
+        buf = lambda *dims: pltpu.VMEM(dims + (columns,), BF)
+        dma = pltpu.SemaphoreType.DMA
+        dp = axis == "dp"
+        self.scratch = (
+            buf(8, rows),
+            buf(8 if dp else 1, rows if dp else 16),
+            buf(2, cut),
+            buf(2, rows - cut),
+            buf(2, rows),
+            buf(2, rows),
+            buf(rows),
+            dma((17,)),
+            dma((17,)),
+            dma((8,)),
+        )
+
+    def steps(self, ins, outs, scratch):
+        return reduce_steps(self.axis, ins[0], outs[0], *scratch)
+
+
+def reduce_steps(axis, x, out, acc, sib_buf, a_buf, b_buf, c_buf, d_buf, e_buf, send, recv, load):
     me, at = places(axis)
     cores = axis == "dp"
-    rows = x.shape[1]
-    half = rows // 2
-    step = 32 if half % 32 == 0 else 16
+    rows = acc.shape[1]
+    step = 16
+    block = lambda k: x.at[k] if len(x.shape) == 3 else x.at[pl.ds(pl.multiple_of(k * rows, 16), rows)]
     up, down, pair, sib = at(1, 0), at(-1, 0), at(0, 1), at(0, 0, 1)
-    greet(axis, [up, down, pair] + ([sib] if cores else []))
-    whole, first, second = pl.ds(0, rows), pl.ds(0, half), pl.ds(half, half)
-    started = []
-
-    def push(number, src, dst, peer):
-        copy = pltpu.make_async_remote_copy(
-            src_ref=src,
-            dst_ref=dst,
-            send_sem=send.at[number],
-            recv_sem=recv.at[number],
-            device_id={axis: peer},
-            device_id_type=MESH,
-        )
-        copy.start()
-        started.append(copy)
-
-    def arrived(number, dst):
-        pltpu.make_async_copy(dst, dst, recv.at[number]).wait()
+    whole, first, second, cut = halves(rows)
+    links = Links(axis, send, recv)
+    push, arrived = links.push, links.arrived
 
     def add(dst, offset, count, *srcs):
         @pl.loop(0, count // step)
         def _(i):
             at_rows = pl.ds(pl.multiple_of(offset + i * step, step), step)
             total = dst[at_rows, :].astype(F32)
-            for src, src_offset in srcs:
-                total += src[pl.ds(pl.multiple_of(src_offset + i * step, step), step), :].astype(F32)
+            for src in srcs:
+                total += src[pl.ds(pl.multiple_of(i * step, step), step), :].astype(F32)
             dst[at_rows, :] = total.astype(dst.dtype)
 
     loads = []
     for k, (hop, other) in enumerate(ORDER):
         if cores:
-            push(k, x.at[at(hop, other, 1)], sib_buf.at[k], sib)
-        copy = pltpu.make_async_copy(x.at[at(hop, other)], acc.at[k], load.at[k])
+            push(k, block(at(hop, other, 1)), sib_buf.at[k], sib)
+        copy = pltpu.make_async_copy(block(at(hop, other)), acc.at[k], load.at[k])
         copy.start()
         loads.append(copy)
 
@@ -215,147 +254,334 @@
         loads[k].wait()
         if cores:
             arrived(k, sib_buf.at[k])
-            add(acc.at[k], 0, rows, (sib_buf.at[k], 0))
-
-    ready(0)
-    push(8, acc.at[0].at[first], a_buf.at[0], up)
-    push(9, acc.at[0].at[second], b_buf.at[0], down)
-    ready(1)
-    push(10, acc.at[1].at[first], a_buf.at[1], up)
-    push(11, acc.at[1].at[second], b_buf.at[1], down)
-    ready(2)
-    ready(3)
-    arrived(8, a_buf.at[0])
-    add(acc.at[2], 0, half, (a_buf.at[0], 0))
-    push(12, acc.at[2], c_buf.at[0], up)
-    arrived(9, b_buf.at[0])
-    add(acc.at[3], half, half, (b_buf.at[0], 0))
-    push(13, acc.at[3], d_buf.at[0], down)
-    ready(4)
-    ready(5)
-    arrived(10, a_buf.at[1])
-    add(acc.at[4], 0, half, (a_buf.at[1], 0))
-    push(14, acc.at[4], c_buf.at[1], up)
-    arrived(11, b_buf.at[1])
-    add(acc.at[5], half, half, (b_buf.at[1], 0))
-    push(15, acc.at[5], d_buf.at[1], down)
+            add(acc.at[k], 0, rows, sib_buf.at[k])
+
+    yield
+    for k in range(2):
+        ready(k)
+        push(8 + 2 * k, acc.at[k].at[first], a_buf.at[k], up)
+        push(9 + 2 * k, acc.at[k].at[second], b_buf.at[k], down)
+    for k in range(2):
+        above, below = 2 + 2 * k, 3 + 2 * k
+        ready(above)
+        ready(below)
+        if k:
+            yield
+        arrived(8 + 2 * k, a_buf.at[k])
+        add(acc.at[above], 0, cut, a_buf.at[k])
+        push(12 + 2 * k, acc.at[above], c_buf.at[k], up)
+        arrived(9 + 2 * k, b_buf.at[k])
+        add(acc.at[below], cut, rows - cut, b_buf.at[k])
+        push(13 + 2 * k, acc.at[below], d_buf.at[k], down)
     ready(6)
     ready(7)
+    yield
     arrived(12, c_buf.at[0])
     arrived(13, d_buf.at[0])
-    add(acc.at[6], 0, rows, (c_buf.at[0], 0), (d_buf.at[0], 0))
+    add(acc.at[6], 0, rows, c_buf.at[0], d_buf.at[0])
     push(16, acc.at[6], e_buf, pair)
+    yield
     arrived(14, c_buf.at[1])
     arrived(15, d_buf.at[1])
+    yield
     arrived(16, e_buf)
 
     @pl.loop(0, rows // step)
     def _(i):
         at_rows = pl.ds(pl.multiple_of(i * step, step), step)
-        out[at_rows, :] = (
-            acc[7, at_rows, :].astype(F32)
-            + c_buf[1, at_rows, :].astype(F32)
-            + d_buf[1, at_rows, :].astype(F32)
-            + e_buf[at_rows, :].astype(F32)
-        )
-
-    for copy in started:
-        copy.wait_send()
-
-
-def reduce_scatter(x, axis, number):
-    n, rows, columns = x.shape
-    half = rows // 2
-    buf = lambda *shape: pltpu.VMEM(shape + (columns,), BF)
-    return pl.pallas_call(
-        functools.partial(reduce_kernel, axis),
-        out_shape=jax.ShapeDtypeStruct((rows, columns), F32),
-        in_specs=[pl.BlockSpec(memory_space=pl.ANY)],
-        out_specs=pl.BlockSpec(memory_space=pltpu.VMEM),
-        scratch_shapes=[
-            buf(8, rows),
-            buf(8 if axis == "dp" else 1, rows if axis == "dp" else 16),
-            buf(2, half),
-            buf(2, half),
-            buf(2, rows),
-            buf(2, rows),
-            buf(rows),
-            pltpu.SemaphoreType.DMA((17,)),
-            pltpu.SemaphoreType.DMA((17,)),
-            pltpu.SemaphoreType.DMA((8,)),
-        ],
+        total = acc[7, at_rows, :].astype(F32) + c_buf[1, at_rows, :].astype(F32)
+        total += d_buf[1, at_rows, :].astype(F32) + e_buf[at_rows, :].astype(F32)
+        out[at_rows, :] = total.astype(out.dtype)
+
+    links.finish()
+
+
+class Direct(Task):
+    def __init__(self, kind, axis, x):
+        self.kind, self.axis, self.reaches = kind, axis, ((axis, True),)
+        n = lax.axis_size(axis)
+        shape = (n,) + x.shape if kind == "gather" else x.shape
+        self.ins = ((x, ANY),)
+        self.outs = ((jax.ShapeDtypeStruct(shape, x.dtype), ANY),)
+        dma = pltpu.SemaphoreType.DMA
+        self.scratch = (dma((n,)), dma((n,)), dma)
+
+    def steps(self, ins, outs, scratch):
+        return direct_steps(self.kind, self.axis, ins[0], outs[0], *scratch)
+
+
+def direct_steps(kind, axis, x, out, send, recv, own_sem):
+    n, me = lax.axis_size(axis), lax.axis_index(axis)
+    links = Links(axis, send, recv)
+    piece = lambda k: x if kind == "gather" else x.at[k]
+    for k in range(1, n):
+        peer = lax.rem(me + k, n)
+        links.push(k, piece(peer), out.at[me], peer)
+    own = pltpu.make_async_copy(piece(me), out.at[me], own_sem)
+    own.start()
+    yield
+    for k in range(1, n):
+        links.arrived(k, out.at[lax.rem(me - k + n, n)])
+    own.wait()
+    links.finish()
+
+
+class Swap(Task):
+    reaches = (("dp", True),)
+
+    def __init__(self, x):
+        self.ins = ((x, ANY),)
+        relay = jax.ShapeDtypeStruct((2,) + x.shape[1:], x.dtype)
+        self.outs = ((jax.ShapeDtypeStruct(x.shape, x.dtype), ANY), (relay, ANY))
+        dma = pltpu.SemaphoreType.DMA
+        self.scratch = (dma((18,)), dma((18,)), dma)
+
+    def steps(self, ins, outs, scratch):
+        return swap_steps(ins[0], *outs, *scratch)
+
+
+def swap_steps(x, out, relay, send, recv, own_sem):
+    me, at = places("dp")
+    links = Links("dp", send, recv)
+    number = 2
+    plain = []
+    for sibling in range(2):
+        links.push(sibling, x.at[at(2, 1, sibling)], relay.at[sibling], at(-1, 0))
+    for hop in (1, -1, 2, 0):
+        for other in range(2):
+            for sibling in range(2):
+                if (hop, other) == (2, 1) or (hop, other, sibling) == (0, 0, 0):
+                    continue
+                peer = at(hop, other, sibling)
+                links.push(number, x.at[peer], out.at[me], peer)
+                plain.append((number, at(-hop, other, sibling)))
+                number += 1
+    own = pltpu.make_async_copy(x.at[me], out.at[me], own_sem)
+    own.start()
+    yield
+    for sibling in range(2):
+        links.arrived(sibling, relay.at[sibling])
+        links.push(number + sibling, relay.at[sibling], out.at[at(1, 0)], at(-1, 1, sibling))
+    yield
+    for k, source in plain:
+        links.arrived(k, out.at[source])
+    for sibling in range(2):
+        links.arrived(number + sibling, out.at[at(2, 1, sibling)])
+    own.wait()
+    links.finish()
+
+
+def run_tasks(tasks, number, name):
+    operands, in_specs, out_shapes, out_specs, scratch, spans = [], [], [], [], [], []
+    for task in tasks:
+        spans.append((len(operands), len(out_shapes), len(scratch)))
+        operands += [x for x, _ in task.ins]
+        in_specs += [spec for _, spec in task.ins]
+        out_shapes += [shape for shape, _ in task.outs]
+        out_specs += [spec for _, spec in task.outs]
+        scratch += list(task.scratch)
+
+    def kernel(*refs):
+        ins = refs[: len(operands)]
+        outs = refs[len(operands) : len(operands) + len(out_shapes)]
+        temps = refs[len(operands) + len(out_shapes) :]
+        barrier = pltpu.get_barrier_semaphore()
+        count = 0
+        for axis in ("dp", "expert"):
+            here = [everyone for task in tasks for name, everyone in task.reaches if name == axis]
+            if here:
+                peers = peers_of(axis, any(here))
+                for peer in peers:
+                    pl.semaphore_signal(
+                        barrier, inc=1, device_id={axis: peer}, device_id_type=MESH
+                    )
+                count += len(peers)
+        pl.semaphore_wait(barrier, count)
+        running = []
+        for task, (i, o, s) in zip(tasks, spans):
+            running.append(
+                task.steps(
+                    ins[i : i + len(task.ins)],
+                    outs[o : o + len(task.outs)],
+                    temps[s : s + len(task.scratch)],
+                )
+            )
+        while running:
+            running = [steps for steps in running if next(steps, "end") != "end"]
+
+    results = pl.pallas_call(
+        kernel,
+        out_shape=out_shapes,
+        in_specs=in_specs,
+        out_specs=out_specs,
+        scratch_shapes=scratch,
         compiler_params=pltpu.CompilerParams(
             collective_id=number, has_side_effects=True, vmem_limit_bytes=VMEM_LIMIT
         ),
-        name="reduce_" + axis,
-    )(x)
-
-
-def exchange_kernel(plan, *refs):
-    count = len(plan)
-    ins, outs = refs[:count], refs[count : 2 * count]
-    send, recv, own_sem = refs[2 * count :]
-    axes = sorted({axis for _, axis in plan})
-    barrier = pltpu.get_barrier_semaphore()
-    total = 0
-    for axis in axes:
-        n, me = lax.axis_size(axis), lax.axis_index(axis)
-        for k in range(1, n):
-            pl.semaphore_signal(
-                barrier, inc=1, device_id={axis: lax.rem(me + k, n)}, device_id_type=MESH
-            )
-        total += n - 1
-    pl.semaphore_wait(barrier, total)
-    copies = []
-    number = 0
-    for index, (kind, axis) in enumerate(plan):
-        n, me = lax.axis_size(axis), lax.axis_index(axis)
-        x, out = ins[index], outs[index]
-        for k in range(1, n):
-            peer = lax.rem(me + k, n)
-            copy = pltpu.make_async_remote_copy(
-                src_ref=x if kind == "gather" else x.at[peer],
-                dst_ref=out.at[me],
-                send_sem=send.at[number],
-                recv_sem=recv.at[number],
-                device_id={axis: peer},
-                device_id_type=MESH,
-            )
+        name=name,
+    )(*operands)
+    return [results[o : o + len(task.outs)] for task, (_, o, _) in zip(tasks, spans)]
+
+
+class Weights(Task):
+    def __init__(self, x):
+        self.reaches = (("dp", True), ("expert", False))
+        self.swap, self.spread = Direct("all", "dp", x), Gather("expert", x)
+        n = lax.axis_size("expert")
+        full = jax.ShapeDtypeStruct((n,) + x.shape, x.dtype)
+        self.ins = ((x, ANY),)
+        self.outs = self.swap.outs + ((full, ANY),)
+        self.scratch = self.swap.scratch + self.spread.scratch
+
+    def steps(self, ins, outs, scratch):
+        yield from direct_steps("all", "dp", ins[0], outs[0], *scratch[:3])
+        yield
+        yield from gather_steps("expert", outs[0], outs[1], *scratch[3:])
+
+
+class ExpertTail(Task):
+    def __init__(self, x, pre_grad, gh, inc, w_down, experts, blocks):
+        self.reaches = (("expert", False),)
+        self.experts = experts
+        tokens, width = gh.shape
+        depth = inc.shape[1]
+        n = lax.axis_size("expert")
+        part = jax.ShapeDtypeStruct((n, tokens // n, depth), BF)
+        self.reduce = Reduce("expert", part)
+        rows = depth // blocks + 2 * (FE // blocks)
+        grads = jax.ShapeDtypeStruct((blocks, rows, 2 * width), BF)
+        self.ins = tuple((v, ANY) for v in (x, pre_grad, gh, inc, w_down))
+        self.outs = self.reduce.outs + ((grads, ANY),)
+        dma = pltpu.SemaphoreType.DMA
+        vmem = lambda v: pltpu.VMEM(v.shape, BF)
+        self.scratch = (
+            tuple(vmem(v) for v in (x, pre_grad, gh, inc, w_down))
+            + (dma((6,)), vmem(part), pltpu.VMEM((depth, tokens), BF))
+            + (pltpu.VMEM((width, tokens), BF), vmem(grads))
+            + self.reduce.scratch
+        )
+
+    def steps(self, ins, outs, scratch):
+        x, pre_grad, gh, inc, w_down, sems, part, x_t, gh_t, grads = scratch[:10]
+        loads = []
+        for k, (src, dst) in enumerate(zip(ins, scratch[:5])):
+            copy = pltpu.make_async_copy(src, dst, sems.at[k])
             copy.start()
-            copies.append(copy)
-            number += 1
-        own = pltpu.make_async_copy(
-            x if kind == "gather" else x.at[me], out.at[me], own_sem.at[index]
+            loads.append(copy)
+        tokens, width = gh.shape
+        depth = inc.shape[1]
+        tile = 256
+        loads[2].wait()
+        loads[4].wait()
+        n, rows = part.shape[0], part.shape[1]
+        col = lambda i: pl.ds(pl.multiple_of(i * tile, tile), tile)
+        for half in range(2):
+
+            @pl.loop(half * depth // tile // 2, (half + 1) * depth // tile // 2)
+            def _(i):
+                part[:, :, col(i)] = mm(gh[...], w_down[:, col(i)]).astype(BF).reshape(
+                    n, rows, tile
+                )
+
+            yield
+        summing = reduce_steps("expert", part, outs[0], *scratch[10:])
+        next(summing)
+        yield
+        for load in (loads[0], loads[1], loads[3]):
+            load.wait()
+
+        @pl.loop(0, depth // tile)
+        def _(i):
+            x_t[col(i), :] = x[:, col(i)].T
+
+        @pl.loop(0, width // 128)
+        def _(i):
+            at_cols = pl.ds(pl.multiple_of(i * 128, 128), 128)
+            gh_t[at_cols, :] = gh[:, at_cols].T
+
+        next(summing)
+        yield
+        blocks = grads.shape[0]
+        up_rows = depth // blocks
+        for third in range(3):
+            steps = 2 * width // tile // 3
+
+            @pl.loop(third * steps, (third + 1) * steps)
+            def _(i):
+                value = mm(x_t[...], pre_grad[:, col(i)]).astype(BF)
+                grads[:, :up_rows, col(i)] = value.reshape(blocks, up_rows, tile)
+
+            next(summing, None)
+            yield
+        each = FE // blocks
+        shared = width - self.experts * FE
+        own = shared // blocks
+        span = depth // 2
+        spots = (((0, 0), (0, 2)), ((0, 1), (each, 0)))
+        for half in range(2):
+
+            @pl.loop(0, span // tile)
+            def _(i):
+                value = mm(gh_t[...], inc[:, col(half * span // tile + i)])
+                for e in range(self.experts):
+                    row, place = spots[half][e]
+                    piece = value[e * FE : (e + 1) * FE].astype(BF)
+                    grads[
+                        :, up_rows + row : up_rows + row + each, col(place * span // tile + i)
+                    ] = piece.reshape(blocks, each, tile)
+                piece = value[self.experts * FE :].reshape(blocks, own, tile)
+                empty = jnp.zeros((blocks, each - own, tile), F32)
+                piece = jnp.concatenate([piece, empty], axis=1).astype(BF)
+                grads[:, up_rows + each :, col((1 + half) * span // tile + i)] = piece
+
+            next(summing, None)
+            yield
+        store = pltpu.make_async_copy(grads, outs[1], sems.at[5])
+        store.start()
+        for _ in summing:
+            yield
+        store.wait()
+
+
+class InputGrad(Task):
+    def __init__(self, g, d_proj, out_grad):
+        self.reaches = (("expert", False),)
+        rows, wide = D + out_grad.shape[0], d_proj.shape[1]
+        n = lax.axis_size("expert")
+        self.reduce = Reduce("expert", jax.ShapeDtypeStruct((n, rows // n, wide), BF), BF)
+        self.ins = tuple((v, ANY) for v in (g, d_proj, out_grad))
+        self.outs = self.reduce.outs
+        dma = pltpu.SemaphoreType.DMA
+        self.scratch = (
+            pltpu.VMEM(g.shape[:2] + (D,), BF),
+            pltpu.VMEM(d_proj.shape, BF),
+            pltpu.VMEM((rows, wide), BF),
+            dma((3,)),
+        ) + self.reduce.scratch
+
+    def steps(self, ins, outs, scratch):
+        g, d_proj, total, sems = scratch[:4]
+        loads = (
+            pltpu.make_async_copy(ins[0].at[:, :, pl.ds(0, D)], g, sems.at[0]),
+            pltpu.make_async_copy(ins[1], d_proj, sems.at[1]),
+            pltpu.make_async_copy(ins[2], total.at[pl.ds(D, ins[2].shape[0])], sems.at[2]),
         )
-        own.start()
-        copies.append(own)
-    for copy in copies:
-        copy.wait()
-
-
-def exchange(plan, arrays, number):
-    shapes, transfers = [], 0
-    for (kind, axis), x in zip(plan, arrays):
-        n = lax.axis_size(axis)
-        transfers += n - 1
-        shapes.append(
-            jax.ShapeDtypeStruct((n,) + x.shape if kind == "gather" else x.shape, x.dtype)
-        )
-    return pl.pallas_call(
-        functools.partial(exchange_kernel, plan),
-        out_shape=shapes,
-        in_specs=[pl.BlockSpec(memory_space=pl.ANY)] * len(arrays),
-        out_specs=[pl.BlockSpec(memory_space=pl.ANY)] * len(arrays),
-        scratch_shapes=[
-            pltpu.SemaphoreType.DMA((transfers,)),
-            pltpu.SemaphoreType.DMA((transfers,)),
-            pltpu.SemaphoreType.DMA((len(arrays),)),
-        ],
-        compiler_params=pltpu.CompilerParams(
-            collective_id=number, has_side_effects=True, vmem_limit_bytes=VMEM_LIMIT
-        ),
-        name="exchange",
-    )(*arrays)
+        for load in loads:
+            load.start()
+        yield
+        for load in loads:
+            load.wait()
+        tile = 256
+        flat = g.shape[0] * g.shape[1]
+        for part in range(3):
+
+            @pl.loop(part * D // tile // 3, (part + 1) * D // tile // 3)
+            def _(i):
+                at_rows = pl.ds(pl.multiple_of(i * tile, tile), tile)
+                total[at_rows, :] = mm_tn(g[:, :, at_rows].reshape(flat, tile), d_proj[...]).astype(BF)
+
+            yield
+        yield from reduce_steps("expert", total, outs[0], *scratch[4:])
 
 
 EDGE = 8
@@ -466,8 +692,8 @@
         ext[...] = jnp.zeros_like(ext)
         state[...] = jnp.zeros_like(state)
 
-    proj[0] = mm(g[0], w[...])
-    column = iota((1, payload.shape[2]), 1)
+    proj[0] = mm(g[0, :, :D], w[...])
+    column = iota((loc, payload.shape[2] - D), 1)
     for m in range(MB):
         rows = slice(m * loc, (m + 1) * loc)
         ext[m, 0:EDGE, :] = ext[m, loc : loc + EDGE, :]
@@ -483,9 +709,9 @@
         y = out * (part.gate * jax.nn.sigmoid(part.gate))
         square = jnp.sum(y * y, axis=1, keepdims=True)
         high = square.astype(BF).astype(F32)
-        sent = mm((y * lanes_vec[0:1, :]).astype(BF), w_out[...])
-        sent = jnp.where(column == D, high, jnp.where(column == D + 1, square - high, sent))
-        payload[0, rows, :] = sent.astype(BF)
+        payload[0, rows, :D] = mm((y * lanes_vec[0:1, :]).astype(BF), w_out[...]).astype(BF)
+        sums = jnp.where(column == 0, high, jnp.where(column == 1, square - high, 0.0))
+        payload[0, rows, D:] = sums.astype(BF)
 
 
 def backward_kernel(
@@ -522,7 +748,7 @@
         for ref in (d_ext, d_state, d_out, d_taps, d_heads, d_lanes):
             ref[...] = jnp.zeros_like(ref)
 
-    gated_grad = mm_nt(grad[0], w_out[...])
+    gated_grad = mm_nt(grad[0, :, :D], w_out[...])
     extra = grad[0, :, D:].astype(F32)
     has_before = (b > 0).astype(F32)
     pick = (iota((di, S), 0) // PS == iota((di, S), 1)).astype(F32)
@@ -540,7 +766,7 @@
         yr = out * act * r
         gg = gated_grad[rows]
         d_lanes[0:1, :] += jnp.sum(gg * yr, axis=0, keepdims=True)
-        d_out[...] += mm_tn((yr * gain).astype(BF), grad[0, rows, :])
+        d_out[...] += mm_tn((yr * gain).astype(BF), grad[0, rows, :D])
         dy = r * (gg * gain) - yr * (r * s / DI)
         d_gate = dy * out * (sig + act * (1.0 - sig))
         do = dy * act
@@ -617,7 +843,7 @@
         d_proj[0, rows, :di] = d_gate.astype(BF)
         d_proj[0, rows, di : di + width] = d_seq.astype(BF)
         d_proj[0, rows, di + width :] = jnp.where(head_lane < heads, d_raw, 0.0).astype(BF)
-    normed_part[0] = mm_nt(d_proj[0], w[0:D, :]).astype(BF)
+    normed_part[0] = mm_nt(d_proj[0], w[...]).astype(BF)
 
 
 def block_spec(shape, index):
@@ -633,7 +859,7 @@
     di = heads * PS
     width = di + 2 * S
     shapes = [
-        jax.ShapeDtypeStruct((nb, rows, w_out.shape[1]), BF),
+        jax.ShapeDtypeStruct((nb, rows, D + 128), BF),
         jax.ShapeDtypeStruct((nb, rows, w.shape[1]), F32),
         jax.ShapeDtypeStruct((nb, rows, di), F32),
         jax.ShapeDtypeStruct((nb, MB, di, S), F32),
@@ -691,6 +917,36 @@
     )(lengths, grad, w, w_out, taps, heads_vec, lanes_vec, proj, proj, scan, states)
 
 
+def assemble_kernel(heads, got, out):
+    n, rows, _ = got.shape
+    di = heads * PS
+    piece = lambda j, start, size: got[j, :, start : start + size].astype(F32)
+    for j in range(0, n, 2):
+        for half in range(2):
+            pair = [piece(j + k, half * di, di) for k in range(2)]
+            start = half * n * di + j * di
+            out[:, start : start + 2 * di] = jnp.concatenate(pair, axis=1)
+    total = piece(0, 2 * di, 2 * S)
+    for j in range(1, n):
+        total = total + piece(j, 2 * di, 2 * S)
+    start = 2 * n * di
+    out[:, start : start + 2 * S] = total
+    steps = [piece(j, 2 * di + 2 * S, 128)[:, :heads] for j in range(n)]
+    out[:, start + 2 * S :] = jnp.concatenate(steps, axis=1)
+
+
+def assemble(got, heads):
+    n, rows, _ = got.shape
+    return pl.pallas_call(
+        functools.partial(assemble_kernel, heads),
+        out_shape=jax.ShapeDtypeStruct((rows, IN_W), F32),
+        in_specs=[IN_VMEM],
+        out_specs=IN_VMEM,
+        compiler_params=pltpu.CompilerParams(vmem_limit_bytes=VMEM_LIMIT),
+        name="assemble",
+    )(got)
+
+
 def body(
     tokens,
     lengths,
@@ -726,18 +982,20 @@
     fsl = fsr // ne
 
     pad = 128 - heads
+    piece = dr // ne
+    mine = lax.dynamic_slice_in_dim(input_weight, me_e * piece, piece, 0)
     blocks = jnp.concatenate(
         [
-            jnp.moveaxis(input_weight[:, :DI].reshape(dr, nd, di), 1, 0),
-            jnp.moveaxis(input_weight[:, DI : 2 * DI].reshape(dr, nd, di), 1, 0),
-            jnp.broadcast_to(input_weight[None, :, 2 * DI : 2 * DI + 2 * S], (nd, dr, 2 * S)),
-            jnp.moveaxis(input_weight[:, DI + CONV :].reshape(dr, nd, heads), 1, 0),
-            jnp.zeros((nd, dr, pad), BF),
+            jnp.moveaxis(mine[:, :DI].reshape(piece, nd, di), 1, 0),
+            jnp.moveaxis(mine[:, DI : 2 * DI].reshape(piece, nd, di), 1, 0),
+            jnp.broadcast_to(mine[None, :, 2 * DI : 2 * DI + 2 * S], (nd, piece, 2 * S)),
+            jnp.moveaxis(mine[:, DI + CONV :].reshape(piece, nd, heads), 1, 0),
+            jnp.zeros((nd, piece, pad), BF),
         ],
         axis=2,
     )
-    w_in = lax.all_to_all(blocks, "dp", 0, 0, tiled=True).reshape(D, -1)
-    wcols = w_in.shape[1]
+    blocks = jnp.pad(blocks, ((0, 0), (0, -piece % 16), (0, 0)))
+    wcols = blocks.shape[2]
 
     sg = shared_gate_up.reshape(dr, 2, nd, ne, fsl)
     sg = lax.dynamic_index_in_dim(sg, me_e, 3, False).reshape(dr, 2 * fs)
@@ -751,7 +1009,10 @@
     route_rows = routes.reshape(rows_t, TOP)
     normed_wide, norm_pull = jax.vjp(rms_scale, stream, norm_gain)
     normed = normed_wide.astype(BF)
-    normed_all = gather(jnp.concatenate([normed, packed], axis=1), "dp", 1)
+    (_, w_in), (normed_all,) = run_tasks(
+        [Weights(blocks), Gather("dp", jnp.concatenate([normed, packed], axis=1))], 1, "begin"
+    )
+    w_in = jnp.swapaxes(w_in[:, :, :piece], 0, 1).reshape(D, wcols)
     early, _ = lax.optimization_barrier((incoming, normed_all))
     inc_all = lax.all_gather(early, "expert", axis=0, tiled=True)
     packed_all = normed_all[:, :, D:].reshape(nd, rows_t, 256)[:, :, : packed_cols]
@@ -759,7 +1020,6 @@
     sg_full = packed_all[:, : sg.size].reshape(D, 2 * fs)
     sd_full = packed_all[:, sg.size : sg.size + sd.size].reshape(fs, D)
     router_full = packed_all[:, sg.size + sd.size :].reshape(D, experts)
-    w_wide = jnp.pad(w_in, ((0, 256), (0, 0)))
     taps = jnp.concatenate(
         [lax.dynamic_slice_in_dim(filter_weight, me_d * di, di, 1), filter_weight[:, DI:]], axis=1
     )
@@ -775,13 +1035,12 @@
     lanes_vec = jnp.pad(
         jnp.stack([my_gain, jnp.repeat(my_heads(skip_gain), PS)]), ((0, 6), (0, 0))
     )
-    out_wide = jnp.pad(output_weight, ((0, 0), (0, 128)))
     vectors = (taps_vec, heads_vec, lanes_vec)
     payload, proj, scan, states = mixer_forward(
-        lengths[:, 0], normed_all, w_wide, out_wide, *vectors, heads
+        lengths[:, 0], normed_all, w_in, output_weight, *vectors, heads
     )
     column = lax.broadcasted_iota(jnp.int32, (1, D + 128), 1)
-    summed = reduce_scatter(payload, "dp", 2)
+    summed = run_tasks([Reduce("dp", payload)], 2, "reduce_mixer")[0][0]
     r = lax.rsqrt((summed[:, D : D + 1] + summed[:, D + 1 : D + 2]) / DI + EPSILON)
     mixed = summed[:, :D] * r
     after_mixer = stream + mixed
@@ -796,7 +1055,8 @@
     moe_payload = jnp.concatenate(
         [moe_in, t_hi, t_lo, jnp.zeros((rows_t, 128 - 2 * experts), BF)], axis=1
     )
-    moe_all = gather(moe_payload, "expert", 3).reshape(ne * rows_t, D + 128)
+    moe_all = run_tasks([Gather("expert", moe_payload)], 3, "gather_moe")[0][0]
+    moe_all = moe_all.reshape(ne * rows_t, D + 128)
     table_all = moe_all[:, D : D + experts].astype(F32) + moe_all[
         :, D + experts : D + 2 * experts
     ].astype(F32)
@@ -833,16 +1093,15 @@
     pre_grad = jnp.concatenate(
         [gu * b * (sig + act * (1.0 - sig)), gu * act], axis=1
     ).astype(BF)
-    out_part = mm(gh, w_down)
     dx_part = mm_nt(pre_grad, w_up)
-    d_up = mm_tn(moe_all, pre_grad)[:D]
-    d_down = mm_tn(gh, inc_all)
     for i in range(el):
         g_hi, g_lo = hi_lo(gate_grad[:, i : i + 1])
         place = D + me_e * el + i
         dx_part = jnp.where(column == place, g_hi.astype(F32), dx_part)
         dx_part = jnp.where(column == place + experts, g_lo.astype(F32), dx_part)
-    back_sum = reduce_scatter(dx_part.astype(BF).reshape(ne, rows_t, D + 128), "expert", 4)
+    back_sum = run_tasks(
+        [Reduce("expert", dx_part.astype(BF).reshape(ne, rows_t, D + 128))], 4, "reduce_moe"
+    )[0][0]
     inc = incoming.astype(F32)
     spread_sum = back_sum[:, D : D + experts] + back_sum[:, D + experts : D + 2 * experts]
     logit_grad = table * (spread_sum - jnp.sum(table * spread_sum, axis=1, keepdims=True))
@@ -858,30 +1117,113 @@
     grad_payload = jnp.concatenate(
         [after_low, r_hi, r_lo, d_hi, d_lo, jnp.zeros((rows_t, 124), BF)], axis=1
     )
-    grad_all = gather(grad_payload, "dp", 5)
+    (grad_all,), (out_sum, grad_blocks) = run_tasks(
+        [
+            Gather("dp", grad_payload),
+            ExpertTail(moe_all[:, :D], pre_grad, gh, inc_all, w_down, el, nd),
+        ],
+        5,
+        "gather_grad",
+    )
+    all_sum = lax.psum_scatter(grad_blocks, "dp", scatter_dimension=0, tiled=True)[0]
+    up_sum = all_sum[:dr]
+    each, span = FE // nd, D // 2
+    down_sum = all_sum[dr : dr + each]
+    last_sum = all_sum[dr + each :]
     d_proj, normed_part, output_part, d_taps, d_heads, d_lanes = mixer_backward(
-        lengths[:, 0], grad_all, w_wide, out_wide, *vectors, proj, scan, states, heads
-    )
-    output_part = output_part[:, :D]
-    out_part, _ = lax.optimization_barrier((out_part.astype(BF), d_proj))
-    out_sum = lax.psum_scatter(out_part, "expert", scatter_dimension=0, tiled=True)
-    normed_grad = reduce_scatter(normed_part, "dp", 6)
-    d_win = mm_tn(normed_all.reshape(nd * rows_t, -1), d_proj.reshape(nd * rows_t, wcols))
-    d_win = d_win[:D].astype(BF)
+        lengths[:, 0], grad_all, w_in, output_weight, *vectors, proj, scan, states, heads
+    )
+    def rows_of(parts, count):
+        flat = jnp.concatenate([part.reshape(-1) for part in parts])
+        return jnp.pad(flat, (0, count * 128 - flat.size)).reshape(count, 128)
+
+    added = (d_taps[:K, di:], d_taps[K, di:], moe_gain_grad, router_part)
+    own = (
+        d_taps[:K, :di],
+        d_taps[K, :di],
+        d_heads[0, :heads],
+        d_heads[1, :heads],
+        jnp.sum(d_lanes[1].reshape(heads, PS), axis=1),
+        d_lanes[0],
+    )
+    added_size = sum(part.size for part in added)
+    added_rows = -(-added_size // (nd * 1024)) * 8
+    own_rows = -(-sum(part.size for part in own) // 128)
+    norm_rows = D // 128
+    (normed_grad,), (d_sum,), (added_in,) = run_tasks(
+        [
+            Reduce("dp", normed_part),
+            InputGrad(
+                normed_all,
+                d_proj.reshape(nd * rows_t, wcols),
+                output_part.astype(BF).reshape(-1, wcols),
+            ),
+            Direct("all", "dp", rows_of(added, nd * added_rows).reshape(nd, added_rows, 128)),
+        ],
+        6,
+        "reduce_grads",
+    )
     stream_from_norm, norm_gain_grad = norm_pull(normed_grad)
     tokens_grad = after_grad + stream_from_norm
-
-    d_up = d_up.astype(BF)
-    d_down = d_down.astype(BF)
-    up_blocks = d_up.reshape(nd, dr, 2 * width)
-    down_blocks = jnp.stack(
-        [d_down[i * FE : (i + 1) * FE].reshape(nd, FE // nd, D) for i in range(el)], axis=1
-    ).reshape(nd, el * FE // nd, D)
-    down_blocks = jnp.concatenate([down_blocks, d_down[el * FE :].reshape(nd, fsl, D)], axis=1)
-    down_blocks = down_blocks.reshape(nd, -1, 2 * width)
-    all_blocks = jnp.concatenate([up_blocks, down_blocks], axis=1)
-    all_sum = lax.psum_scatter(all_blocks, "dp", scatter_dimension=0, tiled=True)[0]
-    up_sum, down_sum = all_sum[:dr], all_sum[dr:].reshape(-1, D)
+    small = jnp.concatenate(
+        [jnp.sum(added_in, axis=0), rows_of(own, own_rows), rows_of((norm_gain_grad,), norm_rows)],
+        axis=0,
+    )
+    small = jnp.pad(small, ((0, -small.shape[0] % 8), (0, 0)))
+    shared_part = jnp.concatenate(
+        [
+            up_sum[:, el * FE : width],
+            up_sum[:, width + el * FE :],
+            last_sum[:fsl, span:].reshape(dr, -1),
+        ],
+        axis=1,
+    ).reshape(-1, wcols)
+    (d_full,), (small_in,) = run_tasks(
+        [
+            Gather("expert", jnp.concatenate([d_sum, shared_part], axis=0)),
+            Direct("gather", "expert", small),
+        ],
+        7,
+        "gather_grads",
+    )
+    shared_all = d_full[:, d_sum.shape[0] :].reshape(ne, dr, -1)
+    d_full = d_full[:, : d_sum.shape[0]].reshape(-1, wcols)
+    (got, _), (small_all,) = run_tasks(
+        [
+            Swap(d_full[:D].reshape(nd, dr, wcols)),
+            Direct("gather", "dp", jnp.sum(small_in, axis=0)),
+        ],
+        8,
+        "swap_grads",
+    )
+    input_grad = assemble(got, heads)
+    output_grad = d_full[D:].reshape(output_weight.shape)
+    added_all = small_all[:, :added_rows].reshape(-1)
+    own_all = small_all[:, added_rows : added_rows + own_rows].reshape(nd, -1)
+    norm_gain_grad = jnp.sum(
+        small_all[:, added_rows + own_rows : added_rows + own_rows + norm_rows], axis=0
+    ).reshape(D)
+
+    def split(flat, parts):
+        out, start = [], 0
+        for part in parts:
+            out.append(flat[..., start : start + part.size].reshape(flat.shape[:-1] + part.shape))
+            start += part.size
+        return out
+
+    added_taps, added_bias, moe_gain_grad, router_all = split(added_all, added)
+    own_taps, own_bias, own_steps, own_decay, own_skip, own_gain = split(own_all, own)
+    small = (
+        jnp.concatenate([jnp.moveaxis(own_taps, 0, 1).reshape(K, DI), added_taps], axis=1),
+        jnp.concatenate([own_bias.reshape(-1), added_bias]),
+        own_steps.reshape(-1),
+        own_decay.reshape(-1),
+        own_skip.reshape(-1),
+        norm_gain_grad,
+        own_gain.reshape(-1),
+        moe_gain_grad,
+    )
+    router_grad = lax.dynamic_slice_in_dim(router_all, me_d * dr, dr, 0)
     expert_up_grad = jnp.stack(
         [
             jnp.concatenate(
@@ -895,99 +1237,20 @@
         ],
         axis=0,
     ).astype(F32)
-    expert_down_grad = down_sum[: el * FE // nd].reshape(el, FE // nd, D).astype(F32)
-    shared_part = jnp.concatenate(
+    expert_down_grad = jnp.stack(
         [
-            up_sum[:, el * FE : width],
-            up_sum[:, width + el * FE :],
-            down_sum[el * FE // nd :].reshape(dr, -1),
+            down_sum[:, : 2 * span],
+            jnp.concatenate([down_sum[:, 2 * span :], last_sum[:, :span]], axis=1),
         ],
-        axis=1,
-    )
-
-    def spread_heads(v, size, chunk):
-        return lax.dynamic_update_slice(
-            jnp.zeros(v.shape[:-1] + (size,), F32), v, (0,) * (v.ndim - 1) + (me_d * chunk,)
-        )
-
-    small_parts = (
-        jnp.concatenate([spread_heads(d_taps[:K, :di], DI, di), d_taps[:K, di:]], axis=1),
-        jnp.concatenate([spread_heads(d_taps[K, :di], DI, di), d_taps[K, di:]], axis=0),
-        spread_heads(d_heads[0, :heads], H, heads),
-        spread_heads(d_heads[1, :heads], H, heads),
-        spread_heads(jnp.sum(d_lanes[1].reshape(heads, PS), axis=1), H, heads),
-        norm_gain_grad,
-        spread_heads(d_lanes[0], DI, di),
-        moe_gain_grad,
-        router_part,
-    )
-    sizes = [part.size for part in small_parts]
-    lanes = -(-sum(sizes) // (nd * 1024)) * 8
-    small_flat = jnp.concatenate([part.reshape(-1) for part in small_parts])
-    small_flat = jnp.pad(small_flat, (0, nd * lanes * 128 - sum(sizes))).reshape(nd, lanes, 128)
-
-    main = 2 * di
-    back_in, small_in = exchange(
-        (("all", "dp"), ("all", "dp")), (d_win.reshape(nd, dr, wcols), small_flat), 7
-    )
-    misc = jnp.concatenate(
-        [
-            jnp.sum(back_in[:, :, main : main + 2 * S].astype(F32), axis=0),
-            jnp.moveaxis(back_in[:, :, main + 2 * S : main + 2 * S + heads], 0, 1)
-            .reshape(dr, H)
-            .astype(F32),
-        ],
-        axis=1,
-    )
-    misc_size = misc.size
-    misc_rows = -(-misc_size // (ne * 1024)) * 8
-    misc = jnp.pad(misc.reshape(-1), (0, ne * misc_rows * 128 - misc_size))
-    got = exchange(
-        (("all", "expert"), ("all", "expert"), ("all", "expert"), ("gather", "expert")),
-        (
-            back_in[:, :, :main].reshape(ne, nd // ne * dr, main),
-            misc.reshape(ne, misc_rows, 128),
-            output_part.astype(BF).reshape(ne, 48, -1),
-            jnp.sum(small_in, axis=0),
-        ),
-        8,
-    )
-    main_sum, misc_sum, out_grad_sum, small_sum = [jnp.sum(v.astype(F32), axis=0) for v in got]
-    main_all, misc_all, out_grad_all, shared_all, small_all = exchange(
-        (
-            ("gather", "expert"),
-            ("gather", "expert"),
-            ("gather", "expert"),
-            ("gather", "expert"),
-            ("gather", "dp"),
-        ),
-        (main_sum.astype(BF), misc_sum, out_grad_sum.astype(BF), shared_part, small_sum),
-        9,
-    )
-    main_all = main_all.reshape(nd, dr, main).astype(F32)
-    misc_all = misc_all.reshape(-1)[:misc_size].reshape(dr, 2 * S + H)
-    input_grad = jnp.concatenate(
-        [
-            jnp.moveaxis(main_all[:, :, :di], 0, 1).reshape(dr, DI),
-            jnp.moveaxis(main_all[:, :, di:], 0, 1).reshape(dr, DI),
-            misc_all,
-        ],
-        axis=1,
-    )
-    output_grad = out_grad_all.reshape(output_weight.shape)
+        axis=0,
+    ).astype(F32)
     shared_up_grad = (
         jnp.moveaxis(shared_all[:, :, : 2 * fs].reshape(ne, dr, 2, nd, fsl), 0, 3)
         .reshape(dr, 2 * FS)
         .astype(F32)
     )
     shared_down_grad = shared_all[:, :, 2 * fs :].reshape(fsr, D).astype(F32)
-    small_all = small_all.reshape(-1)
-    small, start = [], 0
-    for part, size in zip(small_parts, sizes):
-        small.append(small_all[start : start + size].reshape(part.shape))
-        start += size
-    router_grad = lax.dynamic_slice_in_dim(small[8], me_d * dr, dr, 0)
-    block_output = (after_mixer + out_sum.astype(F32)).astype(BF)
+    block_output = (after_mixer + out_sum).astype(BF)
     shape = (MB, 1, loc, D)
     return (
         block_output.reshape(shape),

time: 809 us -> 728 us (0.90)
  matrix products: 92.3 us -> 47.7 us
  other arithmetic: 53 us -> 37.6 us
  local copies, waits for them, and re-layouts: 98.8 us -> 85.5 us
    dot_general x4 -> x1, matrix products: 33.9 us -> 1.3 us  [mm_tn(): lax.dot_general(a, b, (((0,), (0,)), ((), ())), preferred_element_type=F32)]
    dot_general x3 -> x2, matrix products: 25.4 us -> 13.6 us  [mm(): return jnp.dot(a, b, preferred_element_type=F32)]
    slice x26 -> x28, local copies, waits for them, and re-layouts: 20.5 us -> 21.7 us  [the longest x1 4.31 us: body(): moe_all[:, :D]]
  transfers between devices with their start and end apart: 4 -> 2, of which waited for: 0 -> 0; matrix products, arithmetic and copies ran while one was open for 18% -> 10% of each run, Pallas kernels for 41% -> 39%
where the time goes in v4:
time: 728 us; the launch traced here: 723 us
  Pallas kernels  536 us (74%)
  local copies, waits for them, and re-layouts  85.5 us (12%)
  matrix products  47.7 us (7%)
  other arithmetic  37.6 us (5%)
  between operations  15.3 us (2%)
    pallas_call x8, Pallas kernels, run_tasks(): pl.pallas_call(kernel, out_shape=out_shapes, in_specs=in_specs, out_specs...  411 us
    pallas_call x1, Pallas kernels, mixer_backward(): pl.pallas_call(functools.partial(backward_kernel, heads), grid=(nb,), out...  84.6 us
    pallas_call x1, Pallas kernels, mixer_forward(): pl.pallas_call(functools.partial(forward_kernel, heads), grid=(nb,), out_...  36.5 us
    dot_general x3, matrix products, mm_nt(): lax.dot_general(a, b, (((1,), (1,)), ((), ())), preferred_element_type=F32)  32.9 us
  transfers between devices with their start and end apart: 2, of which 0 were waited for; matrix products, arithmetic and copies ran while one was open for 10% of the time, Pallas kernels for 39%

profile of v4, /device:TPU:1, one launch (start us, length us, event | category | flops | bytes accessed | tf_op | source)
XLA Modules:
  0.0 722.6 jit_solution(13948078095135444914)
XLA Ops:
  16.8 63.2 %begin.1 = (bf16[16,16,768]{2,1,0:T(8,128)(2,1)}, bf16[8,16,16,768]{3,2,1,0:T(8,128)(2,1)}, bf16[16,160,1792]{2,1,0:T(8,128)(2,1)}) custom-call(bf16[16,16,768]{2,1,0:T(8,128)(2,1)} %pad.32.refs_0_, bf16[160,1792]{1,0:T(8,128)(2,1)} %fusion.15.refs_1_), custom_call_target="tpu_custom_call" | custom-call | tf_op jit(solution)/shard_map/begin/pallas_call | solution.py:412
  82.0 2.1 slice_bitcast_fusion.2
  86.2 5.0 reshape.345.w
  94.3 36.5 %mixer_forward.1 = (bf16[16,160,1664]{2,1,0:T(8,128)(2,1)}, f32[16,160,768]{2,1,0:T(8,128)}, f32[16,160,192]{2,1,0:T(8,128)}, f32[16,2,192,128]{3,2,1,0:T(8,128)}) custom-call(s32[2,3]{1,0:T(2,128)} %bitcast.132, bf16[16,160,1792]{2,1,0:T(8,128)(2,1)} %get-tuple-element.40.g.refs_1_, bf16[1536,768]{1,0:T(8,128)(2,1)} %reshape.345.w, ...), custom_call_target="tpu_custom_call" | custom-call | tf_op jit(solution)/shard_map/mixer_forward/pallas_call | solution.py:868
  130.9 46.1 %reduce_mixer.1 = f32[160,1664]{1,0:T(8,128)} custom-call(bf16[16,160,1664]{2,1,0:T(8,128)(2,1)} %get-tuple-element.42.refs_0_), custom_call_target="tpu_custom_call" | custom-call | tf_op jit(solution)/shard_map/reduce_mixer/pallas_call | solution.py:412
  180.2 2.9 reshape.347
  186.1 39.8 %gather_moe.1 = bf16[8,160,1664]{2,1,0:T(8,128)(2,1)} custom-call(bf16[160,1664]{1,0:T(8,128)(2,1)} %concatenate.74.refs_0_), custom_call_target="tpu_custom_call" | custom-call | tf_op jit(solution)/shard_map/gather_moe/pallas_call | solution.py:412
  225.9 2.1 fusion.27
  228.0 4.3 slice.345.refs_1_
  233.6 6.2 slice_bitcast_fusion
  251.7 13.3 %fusion.5 = f32[1280,2304]{1,0:T(8,128)} fusion(bf16[1280,1664]{1,0:T(8,128)(2,1)S(1)} %bitcast.103, bf16[1536,2304]{1,0:T(8,128)(2,1)S(1)} %slice_dynamic-update-slice_fusion.4), kind=kOutput, calls=%fused_computation.6 | convolution fusion | flops 9814671360 | bytes 23134208 | tf_op jit(solution)/shard_map/dot_general | solution.py:30
  268.5 15.5 %multiply_convert_fusion.1 = (bf16[1280,1152]{1,0:T(8,128)(2,1)}, bf16[1280,1152]{1,0:T(8,128)(2,1)}, f32[1280,1152]{1,0:T(8,128)}, bf16[1280,1152]{1,0:T(8,128)(2,1)}) fusion(f32[1280,2304]{1,0:T(8,128)} %fusion.5, f32[1280,512]{1,0:T(8,128)} %broadcast_in_dim.123, f32[1280,512]{1,0:T(8,128)} %broadcast_in_dim.121, f32[1152]{0:T(1024)S(1)} %pad.70.clone, ...), kind=kOutput, calls=%fused_computation.14 | convolution fusion | flops 4568481792 | bytes 39260672 | tf_op jit(solution)/shard_map/dot_general | solution.py:34
  284.0 3.1 slice_reduce_fusion.1
  287.4 4.9 pad_maximum_fusion.refs_2_
  292.3 15.7 %fusion.3 = bf16[1280,1664]{1,0:T(8,128)(2,1)} fusion(bf16[1536,2304]{1,0:T(8,128)(2,1)} %copy-done.23, bf16[1280]{0:T(1024)(128)(2,1)S(1)} %get-tuple-element.174, bf16[1280]{0:T(1024)(128)(2,1)S(1)} %get-tuple-element.173, bf16[1280]{0:T(1024)(128)(2,1)S(1)} %get-tuple-element.172, bf16[1280]{0:T(1024)(128)(2,1)S(1)} %get-tuple-element.171, ...), kind=kOutput, calls=%fused_computation.4 | convolution fusion | flops 9834987520 | bytes 17252864 | tf_op jit(solution)/shard_map/dot_general | solution.py:34
  308.0 38.5 %reduce_moe.1 = f32[160,1664]{1,0:T(8,128)} custom-call(bf16[8,160,1664]{2,1,0:T(8,128)(2,1)} %bitcast.108), custom_call_target="tpu_custom_call" | custom-call | tf_op jit(solution)/shard_map/reduce_moe/pallas_call | solution.py:412
  354.2 69.6 %gather_grad.1 = (bf16[16,160,1664]{2,1,0:T(8,128)(2,1)}, f32[160,1536]{1,0:T(8,128)}, bf16[16,160,2304]{2,1,0:T(8,128)(2,1)}) custom-call(bf16[160,1664]{1,0:T(8,128)(2,1)} %concatenate.78.refs_0_, bf16[1280,1536]{1,0:T(8,128)(2,1)} %slice.345.refs_1_, bf16[1280,2304]{1,0:T(8,128)(2,1)} %pad_maximum_fusion.refs_2_, ...), custom_call_target="tpu_custom_call" | custom-call | tf_op jit(solution)/shard_map/gather_grad/pallas_call | solution.py:412
  423.8 84.6 %mixer_backward.1 = (bf16[16,160,768]{2,1,0:T(8,128)(2,1)}, bf16[16,160,1536]{2,1,0:T(8,128)(2,1)}, f32[192,1536]{1,0:T(8,128)}, f32[8,448]{1,0:T(8,128)}, f32[8,128]{1,0:T(8,128)}, /*index=5*/f32[8,192]{1,0:T(8,128)}) custom-call(s32[2,3]{1,0:T(2,128)} %bitcast.133, bf16[16,160,1664]{2,1,0:T(8,128)(2,1)} %get-tuple-element.45.grad, ...), custom_call_target="tpu_custom_call" | custom-call | tf_op jit(solution)/shard_map/mixer_backward/pallas_call | solution.py:900
  518.2 75.4 %reduce_grads.1 = (f32[160,1536]{1,0:T(8,128)}, bf16[240,768]{1,0:T(8,128)(2,1)}, f32[16,16,128]{2,1,0:T(8,128)}) custom-call(bf16[16,160,1536]{2,1,0:T(8,128)(2,1)} %get-tuple-element.49.refs_0_, bf16[16,160,1792]{2,1,0:T(8,128)(2,1)} %get-tuple-element.40.g.refs_1_, bf16[2560,768]{1,0:T(8,128)(2,1)} %bitcast.110, bf16[384,768]{1,0:T(8,128)(2,1)} %reshape.355.refs_3_, ...), custom_call_target="tpu_custom_call" | custom-call | tf_op jit(solution)/shard_map/reduce_grads/pallas_call | solution.py:412
  597.6 2.1 add_convert_fusion
  606.6 33.5 %gather_grads.1 = (bf16[8,288,768]{2,1,0:T(8,128)(2,1)}, f32[8,40,128]{2,1,0:T(8,128)}) custom-call(bf16[288,768]{1,0:T(8,128)(2,1)} %pad_maximum_fusion.2.refs_0_, f32[40,128]{1,0:T(8,128)} %select_maximum_fusion.3.refs_1_), custom_call_target="tpu_custom_call" | custom-call | tf_op jit(solution)/shard_map/gather_grads/pallas_call | solution.py:412
  640.2 2.1 slice.298
  644.4 45.0 %swap_grads.1 = (bf16[16,96,768]{2,1,0:T(8,128)(2,1)}, bf16[2,96,768]{2,1,0:T(8,128)(2,1)}, f32[16,40,128]{2,1,0:T(8,128)}) custom-call(bf16[16,96,768]{2,1,0:T(8,128)(2,1)} %bitcast.107, f32[40,128]{1,0:T(8,128)} %reduce_sum.187.refs_1_), custom_call_target="tpu_custom_call" | custom-call | tf_op jit(solution)/shard_map/swap_grads/pallas_call | solution.py:412
  699.5 3.8 assemble.1
  (287 shorter events, 91.9 us)
Async XLA Ops:
  7.2 7.9 %copy-start.39 = (bf16[96,16]{0,1:T(8,128)(2,1)S(1)}, bf16[96,16]{0,1:T(8,128)(2,1)}, u32[]{:S(2)}) copy-start(bf16[96,16]{0,1:T(8,128)(2,1)} %param.33) | copy-start | bytes 9220
  7.2 8.3 %copy-start.2 = (bf16[2,1,80,1536]{3,2,1,0:T(8,128)(2,1)S(1)}, bf16[2,1,80,1536]{3,2,1,0:T(8,128)(2,1)}, u32[]{:S(2)}) copy-start(bf16[2,1,80,1536]{3,2,1,0:T(8,128)(2,1)} %param.19) | copy-start | bytes 1474564
  7.2 8.6 %copy-start.30 = (f32[1536]{0:T(1024)S(1)}, f32[1536]{0:T(1024)}, u32[]{:S(2)}) copy-start(f32[1536]{0:T(1024)} %param.29) | copy-start | bytes 18436
  7.2 257.8 %all-gather.2.cloned.1.call-start = ((), (), s32[]{:S(2)}) async-start(), calls=%async_computation.1 | async-start | bytes 4423680 | tf_op jit(solution)/shard_map/all_gather | solution.py:1017
  11.0 69.4 %copy-start.40 = (f32[3328]{0:T(1024)S(1)}, f32[3328]{0:T(1024)}, u32[]{:S(2)}) copy-start(f32[3328]{0:T(1024)} %param.25) | copy-start | bytes 39940
  11.0 69.5 %copy-start.31 = (f32[4,3328]{1,0:T(4,128)S(1)}, f32[4,3328]{1,0:T(4,128)}, u32[]{:S(2)}) copy-start(f32[4,3328]{1,0:T(4,128)} %param.24) | copy-start | bytes 159748
  15.8 68.4 %copy-start.36 = (f32[160]{0:T(256)}, f32[160]{0:T(256)S(1)}, u32[]{:S(2)}) copy-start(f32[160]{0:T(256)S(1)} %add.123) | copy-start | bytes 1924
  80.1 520.9 %reduce-scatter.2.cloned.1.call-start = ((), (), s32[]{:S(2)}) async-start(), calls=%async_computation.2 | async-start | bytes 12533760 | tf_op jit(solution)/shard_map/reduce_scatter | solution.py:1128
  86.1 5.3 slice-start.7
  86.1 6.8 copy-start.42
  86.1 6.8 copy-start.43
  86.1 7.5 %slice-start.6 = ((f32[4,3328]{1,0:T(4,128)}), f32[4,256]{1,0:T(4,128)S(1)}, s32[]{:S(2)}) async-start(f32[4,3328]{1,0:T(4,128)} %param.24), calls=%async_computation.9 | async-start | bytes 8192 | tf_op jit(solution)/shard_map/slice | solution.py:1024
  177.0 7.3 %copy-start.38 = (s32[2,1,80,6]{2,1,3,0:T(1,128)S(1)}, s32[2,1,80,6]{2,1,3,0:T(1,128)}, u32[]{:S(2)}) copy-start(s32[2,1,80,6]{2,1,3,0:T(1,128)} %param.21) | copy-start | bytes 11524
  177.0 7.4 %copy-start.29 = (f32[1536]{0:T(1024)S(1)}, f32[1536]{0:T(1024)}, u32[]{:S(2)}) copy-start(f32[1536]{0:T(1024)} %param.32) | copy-start | bytes 18436
  178.7 5.5 copy-start.32
  233.6 6.2 slice-start.3
  233.6 7.2 copy-start.16
  245.1 6.6 slice-start
  308.0 42.5 %copy-start.35 = (f32[160]{0:T(256)S(1)}, f32[160]{0:T(256)}, u32[]{:S(2)}) copy-start(f32[160]{0:T(256)} %copy-done.34) | copy-start | bytes 1924
  308.0 42.6 %copy-start.14 = (bf16[2,1,80,1536]{3,2,1,0:T(8,128)(2,1)S(1)}, bf16[2,1,80,1536]{3,2,1,0:T(8,128)(2,1)}, u32[]{:S(2)}) copy-start(bf16[2,1,80,1536]{3,2,1,0:T(8,128)(2,1)} %param.22) | copy-start | bytes 1474564
  518.2 79.4 %copy-start.37 = (f32[160]{0:T(256)S(1)}, f32[160]{0:T(256)}, u32[]{:S(2)}) copy-start(f32[160]{0:T(256)} %copy-done.36) | copy-start | bytes 1924
  597.6 8.2 %copy-start.22 = (bf16[240,768]{1,0:T(8,128)(2,1)S(1)}, bf16[240,768]{1,0:T(8,128)(2,1)}, u32[]{:S(2)}) copy-start(bf16[240,768]{1,0:T(8,128)(2,1)} %get-tuple-element.54) | copy-start | bytes 1105924
  699.1 9.4 %copy-start.8 = (f32[384,768]{1,0:T(8,128)S(1)}, f32[384,768]{1,0:T(8,128)}, u32[]{:S(2)}) copy-start(f32[384,768]{1,0:T(8,128)} %slice_convert_fusion) | copy-start | bytes 3538948
  710.1 5.3 copy-start.1
  (31 other events, 112.3 us)
Sparse Core Ops, SparseCore 0:
  80.2 67.8 all-gather.1
  424.0 82.1 reduce-scatter.1

commit v5 on v4

--- a/solution.py
+++ b/solution.py
@@ -145,6 +145,7 @@
     own = pltpu.make_async_copy(x, out.at[me], own_sem)
     own.start()
     yield
+    own.wait()
     arrived(2, pair, whole)
     push(4, pair, whole, up)
     push(5, pair, whole, down)
@@ -188,7 +189,6 @@
             (16, 2, 1),
         ):
             arrived(number, at(hop, other, 1), whole)
-    own.wait()
     links.finish()
 
 
@@ -243,7 +243,7 @@
             dst[at_rows, :] = total.astype(dst.dtype)
 
     loads = []
-    for k, (hop, other) in enumerate(ORDER):
+    for k, (hop, other) in enumerate(ORDER if x is not None else ()):
         if cores:
             push(k, block(at(hop, other, 1)), sib_buf.at[k], sib)
         copy = pltpu.make_async_copy(block(at(hop, other)), acc.at[k], load.at[k])
@@ -251,7 +251,8 @@
         loads.append(copy)
 
     def ready(k):
-        loads[k].wait()
+        if loads:
+            loads[k].wait()
         if cores:
             arrived(k, sib_buf.at[k])
             add(acc.at[k], 0, rows, sib_buf.at[k])
@@ -362,7 +363,8 @@
     for sibling in range(2):
         links.arrived(sibling, relay.at[sibling])
         links.push(number + sibling, relay.at[sibling], out.at[at(1, 0)], at(-1, 1, sibling))
-    yield
+    for _ in range(6):
+        yield
     for k, source in plain:
         links.arrived(k, out.at[source])
     for sibling in range(2):
@@ -439,67 +441,76 @@
         yield from gather_steps("expert", outs[0], outs[1], *scratch[3:])
 
 
-class ExpertTail(Task):
-    def __init__(self, x, pre_grad, gh, inc, w_down, experts, blocks):
-        self.reaches = (("expert", False),)
-        self.experts = experts
-        tokens, width = gh.shape
-        depth = inc.shape[1]
-        n = lax.axis_size("expert")
-        part = jax.ShapeDtypeStruct((n, tokens // n, depth), BF)
-        self.reduce = Reduce("expert", part)
-        rows = depth // blocks + 2 * (FE // blocks)
-        grads = jax.ShapeDtypeStruct((blocks, rows, 2 * width), BF)
-        self.ins = tuple((v, ANY) for v in (x, pre_grad, gh, inc, w_down))
-        self.outs = self.reduce.outs + ((grads, ANY),)
+class ExpertGrads(Task):
+    def __init__(self, x, pre_grad, gh, inc, w_down, s_down, blocks):
+        n, rows, _ = x.shape
+        width, depth = gh.shape[2], inc.shape[1]
+        experts, each, _ = w_down.shape
+        part = jax.ShapeDtypeStruct((n, rows, depth), BF)
+        grads = jax.ShapeDtypeStruct(
+            (blocks, depth // blocks + 2 * (each // blocks), 2 * width), BF
+        )
+        self.ins = tuple((v, ANY) for v in (x, pre_grad, gh, inc, w_down, s_down))
+        self.outs = ((part, ANY), (grads, ANY))
         dma = pltpu.SemaphoreType.DMA
-        vmem = lambda v: pltpu.VMEM(v.shape, BF)
+        vmem = lambda *dims: pltpu.VMEM(dims, BF)
         self.scratch = (
-            tuple(vmem(v) for v in (x, pre_grad, gh, inc, w_down))
-            + (dma((6,)), vmem(part), pltpu.VMEM((depth, tokens), BF))
-            + (pltpu.VMEM((width, tokens), BF), vmem(grads))
-            + self.reduce.scratch
+            vmem(n, rows, depth),
+            vmem(*pre_grad.shape),
+            vmem(*gh.shape),
+            vmem(*inc.shape),
+            vmem(width, depth),
+            dma((8 + experts,)),
+            vmem(*part.shape),
+            vmem(depth, n * rows),
+            vmem(width, n * rows),
+            vmem(*grads.shape),
         )
 
     def steps(self, ins, outs, scratch):
-        x, pre_grad, gh, inc, w_down, sems, part, x_t, gh_t, grads = scratch[:10]
-        loads = []
-        for k, (src, dst) in enumerate(zip(ins, scratch[:5])):
-            copy = pltpu.make_async_copy(src, dst, sems.at[k])
-            copy.start()
-            loads.append(copy)
-        tokens, width = gh.shape
-        depth = inc.shape[1]
+        x, pre_grad, gh, inc, w_down, sems, part, x_t, gh_t, grads = scratch
+        n, rows, depth = x.shape
+        width = gh.shape[2]
+        experts, each, _ = ins[4].shape
+        copy = lambda src, dst, k: pltpu.make_async_copy(src, dst, sems.at[k])
+        load_x = copy(ins[0].at[:, :, pl.ds(0, depth)], x, 0)
+        load_pre = copy(ins[1], pre_grad, 1)
+        load_inc = copy(ins[3], inc, 3)
+        load_first = [copy(ins[2], gh, 2)]
+        for e in range(experts):
+            load_first.append(copy(ins[4].at[e], w_down.at[pl.ds(e * each, each)], 8 + e))
+        rest = pl.ds(experts * each, width - experts * each)
+        load_first.append(copy(ins[5], w_down.at[rest], 4))
+        for load in load_first + [load_x, load_pre, load_inc]:
+            load.start()
+        yield
         tile = 256
-        loads[2].wait()
-        loads[4].wait()
-        n, rows = part.shape[0], part.shape[1]
         col = lambda i: pl.ds(pl.multiple_of(i * tile, tile), tile)
-        for half in range(2):
-
-            @pl.loop(half * depth // tile // 2, (half + 1) * depth // tile // 2)
-            def _(i):
-                part[:, :, col(i)] = mm(gh[...], w_down[:, col(i)]).astype(BF).reshape(
-                    n, rows, tile
-                )
-
-            yield
-        summing = reduce_steps("expert", part, outs[0], *scratch[10:])
-        next(summing)
-        yield
-        for load in (loads[0], loads[1], loads[3]):
+        for load in load_first:
             load.wait()
-
-        @pl.loop(0, depth // tile)
-        def _(i):
-            x_t[col(i), :] = x[:, col(i)].T
 
         @pl.loop(0, width // 128)
         def _(i):
             at_cols = pl.ds(pl.multiple_of(i * 128, 128), 128)
-            gh_t[at_cols, :] = gh[:, at_cols].T
-
-        next(summing)
+            gh_t[at_cols, :] = gh[:, :, at_cols].reshape(n * rows, 128).T
+
+        for half in range(2):
+
+            @pl.loop(half * depth // tile // 2, (half + 1) * depth // tile // 2)
+            def _(i):
+                value = mm(gh[...].reshape(n * rows, width), w_down[:, col(i)])
+                part[:, :, col(i)] = value.astype(BF).reshape(n, rows, tile)
+
+            yield
+        store_part = copy(part, outs[0], 5)
+        store_part.start()
+        load_x.wait()
+        load_pre.wait()
+
+        @pl.loop(0, depth // tile)
+        def _(i):
+            x_t[col(i), :] = x[:, :, col(i)].reshape(n * rows, tile).T
+
         yield
         blocks = grads.shape[0]
         up_rows = depth // blocks
@@ -508,38 +519,37 @@
 
             @pl.loop(third * steps, (third + 1) * steps)
             def _(i):
-                value = mm(x_t[...], pre_grad[:, col(i)]).astype(BF)
+                value = mm(x_t[...], pre_grad[:, :, col(i)].reshape(n * rows, tile)).astype(BF)
                 grads[:, :up_rows, col(i)] = value.reshape(blocks, up_rows, tile)
 
-            next(summing, None)
             yield
-        each = FE // blocks
-        shared = width - self.experts * FE
-        own = shared // blocks
+        load_inc.wait()
+        piece_rows = each // blocks
+        own = (width - experts * each) // blocks
         span = depth // 2
-        spots = (((0, 0), (0, 2)), ((0, 1), (each, 0)))
+        spots = (((0, 0), (0, 2)), ((0, 1), (piece_rows, 0)))
         for half in range(2):
 
             @pl.loop(0, span // tile)
             def _(i):
                 value = mm(gh_t[...], inc[:, col(half * span // tile + i)])
-                for e in range(self.experts):
+                for e in range(experts):
                     row, place = spots[half][e]
-                    piece = value[e * FE : (e + 1) * FE].astype(BF)
+                    piece = value[e * each : (e + 1) * each].astype(BF)
                     grads[
-                        :, up_rows + row : up_rows + row + each, col(place * span // tile + i)
-                    ] = piece.reshape(blocks, each, tile)
-                piece = value[self.experts * FE :].reshape(blocks, own, tile)
-                empty = jnp.zeros((blocks, each - own, tile), F32)
+                        :,
+                        up_rows + row : up_rows + row + piece_rows,
+                        col(place * span // tile + i),
+                    ] = piece.reshape(blocks, piece_rows, tile)
+                piece = value[experts * each :].reshape(blocks, own, tile)
+                empty = jnp.zeros((blocks, piece_rows - own, tile), F32)
                 piece = jnp.concatenate([piece, empty], axis=1).astype(BF)
-                grads[:, up_rows + each :, col((1 + half) * span // tile + i)] = piece
-
-            next(summing, None)
+                grads[:, up_rows + piece_rows :, col((1 + half) * span // tile + i)] = piece
+
             yield
-        store = pltpu.make_async_copy(grads, outs[1], sems.at[5])
+        store = copy(grads, outs[1], 6)
         store.start()
-        for _ in summing:
-            yield
+        store_part.wait()
         store.wait()
 
 
@@ -573,15 +583,154 @@
             load.wait()
         tile = 256
         flat = g.shape[0] * g.shape[1]
-        for part in range(3):
-
-            @pl.loop(part * D // tile // 3, (part + 1) * D // tile // 3)
+
+        @pl.loop(0, D // tile)
+        def _(i):
+            at_rows = pl.ds(pl.multiple_of(i * tile, tile), tile)
+            total[at_rows, :] = mm_tn(g[:, :, at_rows].reshape(flat, tile), d_proj[...]).astype(BF)
+
+        yield from reduce_steps("expert", total, outs[0], *scratch[4:])
+
+
+class Experts(Task):
+    def __init__(self, x, inc, w_up, w_down, s_up, s_down):
+        self.reaches = (("expert", False),)
+        self.gather = Gather("expert", x)
+        n = lax.axis_size("expert")
+        rows, wide = x.shape
+        depth = inc.shape[1]
+        experts, _, both = w_up.shape
+        self.experts = experts
+        all_rows = jax.ShapeDtypeStruct((n, rows, wide), BF)
+        self.reduce = Reduce("expert", all_rows)
+        hidden = experts * both // 2 + s_down.shape[0]
+        pre = jax.ShapeDtypeStruct((n, rows, 2 * hidden), BF)
+        gh = jax.ShapeDtypeStruct((n, rows, hidden), BF)
+        self.ins = tuple((v, ANY) for v in (x, inc, w_up, w_down, s_up, s_down))
+        self.outs = ((all_rows, IN_VMEM),) + self.reduce.outs + ((pre, ANY), (gh, ANY))
+        dma = pltpu.SemaphoreType.DMA
+        self.scratch = (
+            (pltpu.VMEM((n, rows, depth), BF),)
+            + tuple(pltpu.VMEM(v.shape, BF) for v in (w_up, w_down, s_up, s_down))
+            + (pltpu.VMEM((2 * rows, wide), BF), pltpu.VMEM((2 * rows, depth), BF))
+            + (pltpu.VMEM((2 * rows, 2 * hidden), BF), pltpu.VMEM((2 * rows, hidden), BF))
+            + (pltpu.VMEM(pre.shape, BF), pltpu.VMEM(gh.shape, BF))
+            + (pltpu.VMEM((2 * rows, 128), F32), dma((21,)))
+            + self.gather.scratch
+            + self.reduce.scratch
+        )
+
+    def steps(self, ins, outs, scratch):
+        x, inc_in = ins[:2]
+        x_all, dx_out, pre_out, gh_out = outs
+        inc, w_up, w_down, s_up, s_down, xs, incs, pg, ghs, pre, gh, extra, sems = scratch[:13]
+        gather_scratch, reduce_scratch = scratch[13:16], scratch[16:]
+        acc = reduce_scratch[0]
+        me, at = places("expert")
+        n, rows, depth = inc.shape
+        experts, _, both = w_up.shape
+        each = both // 2
+        shared = s_down.shape[0]
+        tile = min(256, each)
+        loads = [
+            pltpu.make_async_copy(src, dst, sems.at[k])
+            for k, (src, dst) in enumerate(zip(ins[2:], (w_up, w_down, s_up, s_down)))
+        ]
+        loads += [
+            pltpu.make_async_copy(inc_in.at[pl.ds(k * rows, rows)], inc.at[k], sems.at[13 + k])
+            for k in range(n)
+        ]
+        arriving = gather_steps("expert", x, x_all, *gather_scratch)
+        next(arriving)
+        for load in loads:
+            load.start()
+        next(arriving)
+        next(arriving)
+        for load in loads:
+            load.wait()
+        lane = lax.broadcasted_iota(jnp.int32, (1, 128), 1)
+        stores = []
+
+        def unit(a, b, u, scale):
+            sig = jax.nn.sigmoid(a)
+            act = a * sig
+            hidden = act * b
+            gu = u * scale
+            da = gu * b * (sig + act * (1.0 - sig))
+            return hidden * scale, da, gu * act, u * hidden
+
+        def compute(hop, places_in_acc):
+            slots = (at(hop, 0), at(hop, 1))
+            for k, slot in enumerate(slots):
+                part = pl.ds(k * rows, rows)
+                xs[part, :] = x_all[slot]
+                incs[part, :] = inc[slot]
+            extra[...] = jnp.zeros_like(extra)
+
+            @pl.loop(0, experts * (each // tile))
             def _(i):
-                at_rows = pl.ds(pl.multiple_of(i * tile, tile), tile)
-                total[at_rows, :] = mm_tn(g[:, :, at_rows].reshape(flat, tile), d_proj[...]).astype(BF)
-
-            yield
-        yield from reduce_steps("expert", total, outs[0], *scratch[4:])
+                e, f = i // (each // tile), lax.rem(i, each // tile)
+                place = me * experts + e
+                table = xs[:, depth:].astype(F32)
+                chosen = (lane == place) | (lane == place + n * experts)
+                scale = jnp.sum(jnp.where(chosen, table, 0.0), axis=1, keepdims=True)
+                left = pl.ds(pl.multiple_of(f * tile, tile), tile)
+                right = pl.ds(pl.multiple_of(each + f * tile, tile), tile)
+                a = mm(xs[:, :depth], w_up[e, :, left])
+                b = mm(xs[:, :depth], w_up[e, :, right])
+                u = mm_nt(incs[...], w_down[e, left, :])
+                h, da, db, dots = unit(a, b, u, scale)
+                ghs[:, pl.ds(pl.multiple_of(e * each + f * tile, tile), tile)] = h.astype(BF)
+                pg[:, pl.ds(pl.multiple_of(e * both + f * tile, tile), tile)] = da.astype(BF)
+                pg[:, pl.ds(pl.multiple_of(e * both + each + f * tile, tile), tile)] = db.astype(BF)
+                extra[...] += jnp.where(lane == place, jnp.sum(dots, axis=1, keepdims=True), 0.0)
+
+            a = mm(xs[:, :depth], s_up[:, :shared])
+            b = mm(xs[:, :depth], s_up[:, shared:])
+            u = mm_nt(incs[...], s_down[...])
+            h, da, db, _ = unit(a, b, u, 1.0)
+            ghs[:, experts * each :] = h.astype(BF)
+            pg[:, experts * both : experts * both + shared] = da.astype(BF)
+            pg[:, experts * both + shared :] = db.astype(BF)
+
+            @pl.loop(0, depth // tile)
+            def _(i):
+                columns = pl.ds(pl.multiple_of(i * tile, tile), tile)
+                total = mm_nt(pg[:, experts * both :], s_up[columns, :])
+                for e in range(experts):
+                    total += mm_nt(pg[:, e * both : (e + 1) * both], w_up[e, columns, :])
+                for k, place in enumerate(places_in_acc):
+                    acc[place, :, columns] = total[k * rows : (k + 1) * rows].astype(BF)
+
+            grads = extra[...]
+            high = grads.astype(BF).astype(F32)
+            turn = (
+                iota((128, 128), 0) + n * experts == iota((128, 128), 1)
+            ).astype(F32)
+            rest = exact(grads - high, turn, ((1,), (0,)))
+            both_parts = (high + rest).astype(BF)
+            for k, (slot, place) in enumerate(zip(slots, places_in_acc)):
+                part = pl.ds(k * rows, rows)
+                acc[place, :, depth:] = both_parts[k * rows : (k + 1) * rows]
+                pre[slot] = pg[part, :]
+                gh[slot] = ghs[part, :]
+                store = pltpu.make_async_copy(pre.at[slot], pre_out.at[slot], sems.at[4 + len(stores)])
+                store.start()
+                stores.append(store)
+
+        compute(0, (7, 6))
+        next(arriving)
+        compute(1, (4, 2))
+        compute(-1, (5, 3))
+        for _ in arriving:
+            pass
+        compute(2, (1, 0))
+        store = pltpu.make_async_copy(gh, gh_out, sems.at[12])
+        store.start()
+        stores.append(store)
+        yield from reduce_steps("expert", None, dx_out, *reduce_scratch)
+        for store in stores:
+            store.wait()
 
 
 EDGE = 8
@@ -1055,53 +1204,10 @@
     moe_payload = jnp.concatenate(
         [moe_in, t_hi, t_lo, jnp.zeros((rows_t, 128 - 2 * experts), BF)], axis=1
     )
-    moe_all = run_tasks([Gather("expert", moe_payload)], 3, "gather_moe")[0][0]
-    moe_all = moe_all.reshape(ne * rows_t, D + 128)
-    table_all = moe_all[:, D : D + experts].astype(F32) + moe_all[
-        :, D + experts : D + 2 * experts
-    ].astype(F32)
-    my_gates = lax.dynamic_slice_in_dim(table_all, me_e * el, el, 1)
-    n_tok = ne * rows_t
-
-    w_up = jnp.concatenate(
-        [expert_gate_up[i][:, :FE] for i in range(el)]
-        + [sg_full[:, :fs]]
-        + [expert_gate_up[i][:, FE:] for i in range(el)]
-        + [sg_full[:, fs:]],
-        axis=1,
-    )
-    w_up = jnp.pad(w_up, ((0, 128), (0, 0)))
-    w_down = jnp.concatenate([expert_down[i] for i in range(el)] + [sd_full], axis=0)
-    width = w_down.shape[0]
-    scale = jnp.concatenate(
-        [jnp.broadcast_to(my_gates[:, i : i + 1], (n_tok, FE)) for i in range(el)]
-        + [jnp.ones((n_tok, fs), F32)],
-        axis=1,
-    )
-    pre = mm(moe_all, w_up)
-    a, b = pre[:, :width], pre[:, width:]
-    sig = jax.nn.sigmoid(a)
-    act = a * sig
-    hidden = act * b
-    u = mm_nt(inc_all, w_down)
-    prod = u * hidden
-    gate_grad = jnp.concatenate(
-        [jnp.sum(prod[:, i * FE : (i + 1) * FE], axis=1, keepdims=True) for i in range(el)], axis=1
-    )
-    gh = (scale * hidden).astype(BF)
-    gu = scale * u
-    pre_grad = jnp.concatenate(
-        [gu * b * (sig + act * (1.0 - sig)), gu * act], axis=1
-    ).astype(BF)
-    dx_part = mm_nt(pre_grad, w_up)
-    for i in range(el):
-        g_hi, g_lo = hi_lo(gate_grad[:, i : i + 1])
-        place = D + me_e * el + i
-        dx_part = jnp.where(column == place, g_hi.astype(F32), dx_part)
-        dx_part = jnp.where(column == place + experts, g_lo.astype(F32), dx_part)
-    back_sum = run_tasks(
-        [Reduce("expert", dx_part.astype(BF).reshape(ne, rows_t, D + 128))], 4, "reduce_moe"
-    )[0][0]
+    (moe_all, back_sum, pre_grad, gh), = run_tasks(
+        [Experts(moe_payload, inc_all, expert_gate_up, expert_down, sg_full, sd_full)], 3, "experts"
+    )
+    width = gh.shape[2]
     inc = incoming.astype(F32)
     spread_sum = back_sum[:, D : D + experts] + back_sum[:, D + experts : D + 2 * experts]
     logit_grad = table * (spread_sum - jnp.sum(table * spread_sum, axis=1, keepdims=True))
@@ -1117,10 +1223,10 @@
     grad_payload = jnp.concatenate(
         [after_low, r_hi, r_lo, d_hi, d_lo, jnp.zeros((rows_t, 124), BF)], axis=1
     )
-    (grad_all,), (out_sum, grad_blocks) = run_tasks(
+    (grad_all,), (out_part, grad_blocks) = run_tasks(
         [
             Gather("dp", grad_payload),
-            ExpertTail(moe_all[:, :D], pre_grad, gh, inc_all, w_down, el, nd),
+            ExpertGrads(moe_all, pre_grad, gh, inc_all, expert_down, sd_full, nd),
         ],
         5,
         "gather_grad",
@@ -1172,8 +1278,7 @@
     small = jnp.pad(small, ((0, -small.shape[0] % 8), (0, 0)))
     shared_part = jnp.concatenate(
         [
-            up_sum[:, el * FE : width],
-            up_sum[:, width + el * FE :],
+            up_sum[:, 2 * el * FE :],
             last_sum[:fsl, span:].reshape(dr, -1),
         ],
         axis=1,
@@ -1188,9 +1293,10 @@
     )
     shared_all = d_full[:, d_sum.shape[0] :].reshape(ne, dr, -1)
     d_full = d_full[:, : d_sum.shape[0]].reshape(-1, wcols)
-    (got, _), (small_all,) = run_tasks(
+    (got, _), (out_sum,), (small_all,) = run_tasks(
         [
             Swap(d_full[:D].reshape(nd, dr, wcols)),
+            Reduce("expert", out_part),
             Direct("gather", "dp", jnp.sum(small_in, axis=0)),
         ],
         8,
@@ -1224,19 +1330,8 @@
         moe_gain_grad,
     )
     router_grad = lax.dynamic_slice_in_dim(router_all, me_d * dr, dr, 0)
-    expert_up_grad = jnp.stack(
-        [
-            jnp.concatenate(
-                [
-                    up_sum[:, i * FE : (i + 1) * FE],
-                    up_sum[:, width + i * FE : width + (i + 1) * FE],
-                ],
-                axis=1,
-            )
-            for i in range(el)
-        ],
-        axis=0,
-    ).astype(F32)
+    expert_up_grad = jnp.moveaxis(up_sum[:, : 2 * el * FE].reshape(dr, el, 2 * FE), 1, 0)
+    expert_up_grad = expert_up_grad.astype(F32)
     expert_down_grad = jnp.stack(
         [
             down_sum[:, : 2 * span],

time: 728 us -> 665 us (0.913)
  matrix products: 47.7 us -> 3.28 us
  local copies, waits for them, and re-layouts: 85.5 us -> 69.3 us
  other arithmetic: 37.6 us -> 28.4 us
    dot_general x3 -> x1, matrix products: 32.9 us -> 1.71 us  [mm_nt(): lax.dot_general(a, b, (((1,), (1,)), ((), ())), preferred_element_type=F32)]
    dot_general x2 -> x1, matrix products: 13.6 us -> 0.26 us  [mm(): return jnp.dot(a, b, preferred_element_type=F32)]
    slice x5 -> x1, local copies, waits for them, and re-layouts: 7.73 us -> 0.01 us  [body(): up_sum[:, 2 * el * FE:]]
    pallas_call x8 -> x7, Pallas kernels: 411 us -> 418 us  [run_tasks(): pl.pallas_call(kernel, out_shape=out_shapes, in_specs=in_specs, out_specs...]
  transfers between devices with their start and end apart: 2 -> 2, of which waited for: 0 -> 0; matrix products, arithmetic and copies ran while one was open for 10% -> 6% of each run, Pallas kernels for 39% -> 33%
where the time goes in v5:
time: 665 us; the launch traced here: 659 us
  Pallas kernels  543 us (82%)
  local copies, waits for them, and re-layouts  69.3 us (10%)
  other arithmetic  28.4 us (4%)
  between operations  14.9 us (2%)
    pallas_call x7, Pallas kernels, run_tasks(): pl.pallas_call(kernel, out_shape=out_shapes, in_specs=in_specs, out_specs...  418 us
    pallas_call x1, Pallas kernels, mixer_backward(): pl.pallas_call(functools.partial(backward_kernel, heads), grid=(nb,), out...  84.6 us
    pallas_call x1, Pallas kernels, mixer_forward(): pl.pallas_call(functools.partial(forward_kernel, heads), grid=(nb,), out_...  36.6 us
  transfers between devices with their start and end apart: 2, of which 0 were waited for; matrix products, arithmetic and copies ran while one was open for 6% of the time, Pallas kernels for 33%

profile of v5, /device:TPU:1, one launch (start us, length us, event | category | flops | bytes accessed | tf_op | source)
XLA Modules:
  0.0 659.1 jit_solution(16923103056625112398)
XLA Ops:
  17.5 66.0 %begin.1 = (bf16[16,16,768]{2,1,0:T(8,128)(2,1)}, bf16[8,16,16,768]{3,2,1,0:T(8,128)(2,1)}, bf16[16,160,1792]{2,1,0:T(8,128)(2,1)}) custom-call(bf16[16,16,768]{2,1,0:T(8,128)(2,1)} %pad.28.refs_0_, bf16[160,1792]{1,0:T(8,128)(2,1)} %fusion.4.refs_1_), custom_call_target="tpu_custom_call" | custom-call | tf_op jit(solution)/shard_map/begin/pallas_call | solution.py:414
  85.3 2.0 reshape.296
  88.7 2.1 slice_bitcast_fusion
  90.8 2.0 copy.97
  92.9 5.1 reshape.294.w
  101.2 36.6 %mixer_forward.1 = (bf16[16,160,1664]{2,1,0:T(8,128)(2,1)}, f32[16,160,768]{2,1,0:T(8,128)}, f32[16,160,192]{2,1,0:T(8,128)}, f32[16,2,192,128]{3,2,1,0:T(8,128)}) custom-call(s32[2,3]{1,0:T(2,128)} %bitcast.119, bf16[16,160,1792]{2,1,0:T(8,128)(2,1)} %get-tuple-element.45.g.refs_1_, bf16[1536,768]{1,0:T(8,128)(2,1)} %reshape.294.w, ...), custom_call_target="tpu_custom_call" | custom-call | tf_op jit(solution)/shard_map/mixer_forward/pallas_call | solution.py:1017
  137.8 45.0 %reduce_mixer.1 = f32[160,1664]{1,0:T(8,128)} custom-call(bf16[16,160,1664]{2,1,0:T(8,128)(2,1)} %get-tuple-element.47.refs_0_), custom_call_target="tpu_custom_call" | custom-call | tf_op jit(solution)/shard_map/reduce_mixer/pallas_call | solution.py:414
  182.8 1.7 subtract_convert_fusion.1
  187.7 2.4 reshape.298.refs_4_
  191.2 93.7 %experts.1 = (bf16[8,160,1664]{2,1,0:T(8,128)(2,1)}, f32[160,1664]{1,0:T(8,128)}, bf16[8,160,2304]{2,1,0:T(8,128)(2,1)}, bf16[8,160,1152]{2,1,0:T(8,128)(2,1)}) custom-call(bf16[160,1664]{1,0:T(8,128)(2,1)} %concatenate.54.refs_0_, bf16[1280,1536]{1,0:T(8,128)(2,1)} %all-gather.2.cloned.1.call-done.refs_1_.refs_4_, bf16[2,1536,1024]{2,1,0:T(8,128)(2,1)} %refs_2_.1, ...), custom_call_target="tpu_custom_call" | custom-call | tf_op jit(solution)/shard_map/experts/pallas_call | solution.py:414
  287.2 1.7 multiply_reduce_fusion.2
  294.3 1.7 concatenate.55.refs_0_
  296.0 64.8 %gather_grad.1 = (bf16[16,160,1664]{2,1,0:T(8,128)(2,1)}, bf16[8,160,1536]{2,1,0:T(8,128)(2,1)}, bf16[16,160,2304]{2,1,0:T(8,128)(2,1)}) custom-call(bf16[160,1664]{1,0:T(8,128)(2,1)} %concatenate.55.refs_0_, bf16[8,160,1664]{2,1,0:T(8,128)(2,1)} %get-tuple-element.50.refs_1_, bf16[8,160,2304]{2,1,0:T(8,128)(2,1)} %get-tuple-element.51.refs_2_, ...), custom_call_target="tpu_custom_call" | custom-call | tf_op jit(solution)/shard_map/gather_grad/pallas_call | solution.py:414
  360.9 84.6 %mixer_backward.1 = (bf16[16,160,768]{2,1,0:T(8,128)(2,1)}, bf16[16,160,1536]{2,1,0:T(8,128)(2,1)}, f32[192,1536]{1,0:T(8,128)}, f32[8,448]{1,0:T(8,128)}, f32[8,128]{1,0:T(8,128)}, /*index=5*/f32[8,192]{1,0:T(8,128)}) custom-call(s32[2,3]{1,0:T(2,128)} %bitcast.120, bf16[16,160,1664]{2,1,0:T(8,128)(2,1)} %get-tuple-element.53.grad, ...), custom_call_target="tpu_custom_call" | custom-call | tf_op jit(solution)/shard_map/mixer_backward/pallas_call | solution.py:1049
  455.2 50.4 %reduce_grads.1 = (f32[160,1536]{1,0:T(8,128)}, bf16[240,768]{1,0:T(8,128)(2,1)}, f32[16,16,128]{2,1,0:T(8,128)}) custom-call(bf16[16,160,1536]{2,1,0:T(8,128)(2,1)} %get-tuple-element.57.refs_0_, bf16[16,160,1792]{2,1,0:T(8,128)(2,1)} %get-tuple-element.45.g.refs_1_, bf16[2560,768]{1,0:T(8,128)(2,1)} %bitcast.95, bf16[384,768]{1,0:T(8,128)(2,1)} %reshape.301.refs_3_, ...), custom_call_target="tpu_custom_call" | custom-call | tf_op jit(solution)/shard_map/reduce_grads/pallas_call | solution.py:414
  515.3 36.2 %gather_grads.1 = (bf16[8,288,768]{2,1,0:T(8,128)(2,1)}, f32[8,40,128]{2,1,0:T(8,128)}) custom-call(bf16[288,768]{1,0:T(8,128)(2,1)} %pad_maximum_fusion.refs_0_, f32[40,128]{1,0:T(8,128)} %select_maximum_fusion.3.refs_1_), custom_call_target="tpu_custom_call" | custom-call | tf_op jit(solution)/shard_map/gather_grads/pallas_call | solution.py:414
  552.6 3.6 slice.207
  561.0 61.9 %swap_grads.1 = (bf16[16,96,768]{2,1,0:T(8,128)(2,1)}, bf16[2,96,768]{2,1,0:T(8,128)(2,1)}, f32[160,1536]{1,0:T(8,128)}, f32[16,40,128]{2,1,0:T(8,128)}) custom-call(bf16[16,96,768]{2,1,0:T(8,128)(2,1)} %bitcast.93, bf16[8,160,1536]{2,1,0:T(8,128)(2,1)} %get-tuple-element.68.refs_1_, f32[40,128]{1,0:T(8,128)} %reduce_sum.166.refs_2_), custom_call_target="tpu_custom_call" | custom-call | tf_op jit(solution)/shard_map/swap_grads/pallas_call | solution.py:414
  629.0 1.6 slice.212
  630.6 2.2 slice.223
  633.7 1.8 reshape.327
  637.0 2.4 copy.115
  639.4 2.1 add_convert_fusion
  646.4 3.6 assemble.1
  (220 shorter events, 68.8 us)
Async XLA Ops:
  7.2 6.9 %copy-start.10 = (bf16[96,2048]{1,0:T(8,128)(2,1)S(1)}, bf16[96,2048]{1,0:T(8,128)(2,1)}, u32[]{:S(2)}) copy-start(bf16[96,2048]{1,0:T(8,128)(2,1)} %param.34) | copy-start | bytes 1179652
  7.2 184.0 %all-gather.2.cloned.1.call-start = ((), (), s32[]{:S(2)}) async-start(), calls=%async_computation.1 | async-start | bytes 4423680 | tf_op jit(solution)/shard_map/all_gather | solution.py:1166
  83.6 427.3 %reduce-scatter.2.cloned.1.call-start = ((), (), s32[]{:S(2)}) async-start(), calls=%async_computation.2 | async-start | bytes 12533760 | tf_op jit(solution)/shard_map/reduce_scatter | solution.py:1234
  87.3 3.5 copy-start.5
  92.8 5.1 slice-start
  92.8 6.3 copy-start.25
  92.8 6.3 copy-start.26
  92.8 6.4 slice-start.6
  92.8 6.4 copy-start.21
  92.8 7.7 %slice-start.5 = ((f32[4,3328]{1,0:T(4,128)}), f32[4,256]{1,0:T(4,128)S(1)}, s32[]{:S(2)}) async-start(f32[4,3328]{1,0:T(4,128)} %param.24), calls=%async_computation.8 | async-start | bytes 8192 | tf_op jit(solution)/shard_map/slice | solution.py:1173
  285.0 4.0 copy-start.8
  505.6 4.0 copy-start.6
  510.9 3.6 copy-start.11
  622.9 12.6 %slice-start.3 = ((bf16[8,96,384]{2,1,0:T(8,128)(2,1)}), bf16[8,96,256]{2,1,0:T(8,128)(2,1)S(1)}, s32[]{:S(2)}) async-start(bf16[8,96,384]{2,1,0:T(8,128)(2,1)} %copy-done.7), calls=%async_computation.6 | async-start | bytes 786432 | tf_op jit(solution)/shard_map/slice | solution.py:1343
  639.4 3.5 copy-start.20
  639.4 4.1 copy-start.19
  639.4 4.7 copy-start.18
  639.4 6.0 copy-start.12
  641.6 4.1 slice-start.2
  645.7 4.3 copy-start.13
  645.7 4.3 copy-start.14
  646.4 5.6 copy-start.1
  646.4 4.4 copy-start.24
  646.4 5.0 slice-start.4
  (13 other events, 32.9 us)
Sparse Core Ops, SparseCore 0:
  83.7 69.2 all-gather.1
  361.0 76.0 reduce-scatter.1

commit v6 on v5

--- a/solution.py
+++ b/solution.py
@@ -69,7 +69,10 @@
 
 
 class Task:
-    ins, outs, scratch, reaches = (), (), (), ()
+    ins, outs, scratch, reaches, turns = (), (), (), (), 1
+
+    def greet(self, barrier):
+        return 0
 
 
 def peers_of(axis, everyone):
@@ -105,8 +108,9 @@
             copy.wait_send()
 
 
-def halves(rows):
-    cut = rows // 32 * 16
+def halves(shape):
+    rows = shape[0]
+    cut = rows // 2 if len(shape) == 3 else rows // 32 * 16
     return pl.ds(0, rows), pl.ds(0, cut), pl.ds(cut, rows - cut), cut
 
 
@@ -127,7 +131,7 @@
     me, at = places(axis)
     cores = axis == "dp"
     up, down, pair, sib = at(1, 0), at(-1, 0), at(0, 1), at(0, 0, 1)
-    whole, first, second, _ = halves(x.shape[0])
+    whole, first, second, _ = halves(x.shape)
     links = Links(axis, send, recv)
 
     def push(number, slot, rows, peer, src=None):
@@ -201,7 +205,7 @@
         n, rows, columns = x.shape
         self.ins = ((x, ANY),)
         self.outs = ((jax.ShapeDtypeStruct((rows, columns), dtype), IN_VMEM),)
-        _, _, _, cut = halves(rows)
+        _, _, _, cut = halves((rows, columns))
         buf = lambda *dims: pltpu.VMEM(dims + (columns,), BF)
         dma = pltpu.SemaphoreType.DMA
         dp = axis == "dp"
@@ -229,7 +233,7 @@
     step = 16
     block = lambda k: x.at[k] if len(x.shape) == 3 else x.at[pl.ds(pl.multiple_of(k * rows, 16), rows)]
     up, down, pair, sib = at(1, 0), at(-1, 0), at(0, 1), at(0, 0, 1)
-    whole, first, second, cut = halves(rows)
+    whole, first, second, cut = halves(acc.shape[1:])
     links = Links(axis, send, recv)
     push, arrived = links.push, links.arrived
 
@@ -262,6 +266,7 @@
         ready(k)
         push(8 + 2 * k, acc.at[k].at[first], a_buf.at[k], up)
         push(9 + 2 * k, acc.at[k].at[second], b_buf.at[k], down)
+    yield
     for k in range(2):
         above, below = 2 + 2 * k, 3 + 2 * k
         ready(above)
@@ -327,52 +332,6 @@
     links.finish()
 
 
-class Swap(Task):
-    reaches = (("dp", True),)
-
-    def __init__(self, x):
-        self.ins = ((x, ANY),)
-        relay = jax.ShapeDtypeStruct((2,) + x.shape[1:], x.dtype)
-        self.outs = ((jax.ShapeDtypeStruct(x.shape, x.dtype), ANY), (relay, ANY))
-        dma = pltpu.SemaphoreType.DMA
-        self.scratch = (dma((18,)), dma((18,)), dma)
-
-    def steps(self, ins, outs, scratch):
-        return swap_steps(ins[0], *outs, *scratch)
-
-
-def swap_steps(x, out, relay, send, recv, own_sem):
-    me, at = places("dp")
-    links = Links("dp", send, recv)
-    number = 2
-    plain = []
-    for sibling in range(2):
-        links.push(sibling, x.at[at(2, 1, sibling)], relay.at[sibling], at(-1, 0))
-    for hop in (1, -1, 2, 0):
-        for other in range(2):
-            for sibling in range(2):
-                if (hop, other) == (2, 1) or (hop, other, sibling) == (0, 0, 0):
-                    continue
-                peer = at(hop, other, sibling)
-                links.push(number, x.at[peer], out.at[me], peer)
-                plain.append((number, at(-hop, other, sibling)))
-                number += 1
-    own = pltpu.make_async_copy(x.at[me], out.at[me], own_sem)
-    own.start()
-    yield
-    for sibling in range(2):
-        links.arrived(sibling, relay.at[sibling])
-        links.push(number + sibling, relay.at[sibling], out.at[at(1, 0)], at(-1, 1, sibling))
-    for _ in range(6):
-        yield
-    for k, source in plain:
-        links.arrived(k, out.at[source])
-    for sibling in range(2):
-        links.arrived(number + sibling, out.at[at(2, 1, sibling)])
-    own.wait()
-    links.finish()
-
-
 def run_tasks(tasks, number, name):
     operands, in_specs, out_shapes, out_specs, scratch, spans = [], [], [], [], [], []
     for task in tasks:
@@ -398,18 +357,23 @@
                         barrier, inc=1, device_id={axis: peer}, device_id_type=MESH
                     )
                 count += len(peers)
+        for task in tasks:
+            count += task.greet(barrier)
         pl.semaphore_wait(barrier, count)
         running = []
         for task, (i, o, s) in zip(tasks, spans):
-            running.append(
-                task.steps(
-                    ins[i : i + len(task.ins)],
-                    outs[o : o + len(task.outs)],
-                    temps[s : s + len(task.scratch)],
-                )
+            steps = task.steps(
+                ins[i : i + len(task.ins)],
+                outs[o : o + len(task.outs)],
+                temps[s : s + len(task.scratch)],
             )
+            running.append((task.turns, steps))
         while running:
-            running = [steps for steps in running if next(steps, "end") != "end"]
+            left = []
+            for turns, steps in running:
+                if all(next(steps, "end") != "end" for _ in range(turns)):
+                    left.append((turns, steps))
+            running = left
 
     results = pl.pallas_call(
         kernel,
@@ -427,7 +391,7 @@
 
 class Weights(Task):
     def __init__(self, x):
-        self.reaches = (("dp", True), ("expert", False))
+        self.reaches, self.turns = (("dp", True), ("expert", False)), 2
         self.swap, self.spread = Direct("all", "dp", x), Gather("expert", x)
         n = lax.axis_size("expert")
         full = jax.ShapeDtypeStruct((n,) + x.shape, x.dtype)
@@ -442,16 +406,15 @@
 
 
 class ExpertGrads(Task):
-    def __init__(self, x, pre_grad, gh, inc, w_down, s_down, blocks):
+    def __init__(self, x, pre_grad, gh, inc, experts, each, blocks):
         n, rows, _ = x.shape
         width, depth = gh.shape[2], inc.shape[1]
-        experts, each, _ = w_down.shape
-        part = jax.ShapeDtypeStruct((n, rows, depth), BF)
+        self.experts, self.each = experts, each
         grads = jax.ShapeDtypeStruct(
             (blocks, depth // blocks + 2 * (each // blocks), 2 * width), BF
         )
-        self.ins = tuple((v, ANY) for v in (x, pre_grad, gh, inc, w_down, s_down))
-        self.outs = ((part, ANY), (grads, ANY))
+        self.ins = tuple((v, ANY) for v in (x, pre_grad, gh, inc))
+        self.outs = ((grads, ANY),)
         dma = pltpu.SemaphoreType.DMA
         vmem = lambda *dims: pltpu.VMEM(dims, BF)
         self.scratch = (
@@ -459,59 +422,41 @@
             vmem(*pre_grad.shape),
             vmem(*gh.shape),
             vmem(*inc.shape),
-            vmem(width, depth),
-            dma((8 + experts,)),
-            vmem(*part.shape),
+            dma((5,)),
             vmem(depth, n * rows),
             vmem(width, n * rows),
             vmem(*grads.shape),
         )
 
     def steps(self, ins, outs, scratch):
-        x, pre_grad, gh, inc, w_down, sems, part, x_t, gh_t, grads = scratch
+        x, pre_grad, gh, inc, sems, x_t, gh_t, grads = scratch
         n, rows, depth = x.shape
         width = gh.shape[2]
-        experts, each, _ = ins[4].shape
+        experts, each = self.experts, self.each
         copy = lambda src, dst, k: pltpu.make_async_copy(src, dst, sems.at[k])
         load_x = copy(ins[0].at[:, :, pl.ds(0, depth)], x, 0)
         load_pre = copy(ins[1], pre_grad, 1)
         load_inc = copy(ins[3], inc, 3)
-        load_first = [copy(ins[2], gh, 2)]
-        for e in range(experts):
-            load_first.append(copy(ins[4].at[e], w_down.at[pl.ds(e * each, each)], 8 + e))
-        rest = pl.ds(experts * each, width - experts * each)
-        load_first.append(copy(ins[5], w_down.at[rest], 4))
-        for load in load_first + [load_x, load_pre, load_inc]:
+        load_gh = copy(ins[2], gh, 2)
+        for load in (load_x, load_pre, load_gh, load_inc):
             load.start()
         yield
         tile = 256
         col = lambda i: pl.ds(pl.multiple_of(i * tile, tile), tile)
-        for load in load_first:
-            load.wait()
+        load_x.wait()
+
+        @pl.loop(0, depth // tile)
+        def _(i):
+            x_t[col(i), :] = x[:, :, col(i)].reshape(n * rows, tile).T
+
+        load_gh.wait()
 
         @pl.loop(0, width // 128)
         def _(i):
             at_cols = pl.ds(pl.multiple_of(i * 128, 128), 128)
             gh_t[at_cols, :] = gh[:, :, at_cols].reshape(n * rows, 128).T
 
-        for half in range(2):
-
-            @pl.loop(half * depth // tile // 2, (half + 1) * depth // tile // 2)
-            def _(i):
-                value = mm(gh[...].reshape(n * rows, width), w_down[:, col(i)])
-                part[:, :, col(i)] = value.astype(BF).reshape(n, rows, tile)
-
-            yield
-        store_part = copy(part, outs[0], 5)
-        store_part.start()
-        load_x.wait()
         load_pre.wait()
-
-        @pl.loop(0, depth // tile)
-        def _(i):
-            x_t[col(i), :] = x[:, :, col(i)].reshape(n * rows, tile).T
-
-        yield
         blocks = grads.shape[0]
         up_rows = depth // blocks
         for third in range(3):
@@ -547,49 +492,154 @@
                 grads[:, up_rows + piece_rows :, col((1 + half) * span // tile + i)] = piece
 
             yield
-        store = copy(grads, outs[1], 6)
+        store = copy(grads, outs[0], 4)
         store.start()
-        store_part.wait()
         store.wait()
 
 
 class InputGrad(Task):
     def __init__(self, g, d_proj, out_grad):
         self.reaches = (("expert", False),)
-        rows, wide = D + out_grad.shape[0], d_proj.shape[1]
         n = lax.axis_size("expert")
-        self.reduce = Reduce("expert", jax.ShapeDtypeStruct((n, rows // n, wide), BF), BF)
-        self.ins = tuple((v, ANY) for v in (g, d_proj, out_grad))
+        wide = d_proj.shape[1]
+        rows = (D + out_grad.size // wide) // n
+        self.reduce = Reduce("expert", jax.ShapeDtypeStruct((n, rows, wide), BF), BF)
+        self.ins = tuple((v, ANY) for v in (g, d_proj, out_grad.reshape(n, -1, wide)))
         self.outs = self.reduce.outs
         dma = pltpu.SemaphoreType.DMA
         self.scratch = (
             pltpu.VMEM(g.shape[:2] + (D,), BF),
             pltpu.VMEM(d_proj.shape, BF),
-            pltpu.VMEM((rows, wide), BF),
+            pltpu.VMEM((n, rows, wide), BF),
             dma((3,)),
         ) + self.reduce.scratch
 
     def steps(self, ins, outs, scratch):
         g, d_proj, total, sems = scratch[:4]
+        n, _, wide = total.shape
+        each = D // n
+        below = pl.ds(each, total.shape[1] - each)
         loads = (
             pltpu.make_async_copy(ins[0].at[:, :, pl.ds(0, D)], g, sems.at[0]),
             pltpu.make_async_copy(ins[1], d_proj, sems.at[1]),
-            pltpu.make_async_copy(ins[2], total.at[pl.ds(D, ins[2].shape[0])], sems.at[2]),
+            pltpu.make_async_copy(ins[2], total.at[:, below], sems.at[2]),
         )
         for load in loads:
             load.start()
         yield
         for load in loads:
             load.wait()
-        tile = 256
         flat = g.shape[0] * g.shape[1]
 
-        @pl.loop(0, D // tile)
+        @pl.loop(0, n // 2)
         def _(i):
-            at_rows = pl.ds(pl.multiple_of(i * tile, tile), tile)
-            total[at_rows, :] = mm_tn(g[:, :, at_rows].reshape(flat, tile), d_proj[...]).astype(BF)
+            columns = pl.ds(pl.multiple_of(i * 2 * each, 2 * each), 2 * each)
+            value = mm_tn(g[:, :, columns].reshape(flat, 2 * each), d_proj[...]).astype(BF)
+            total[pl.ds(2 * i, 2), :each, :] = value.reshape(2, each, wide)
 
         yield from reduce_steps("expert", total, outs[0], *scratch[4:])
+
+
+class InputRows(Task):
+    turns = 2
+
+    def __init__(self, x, heads):
+        nd, ne = lax.axis_size("dp"), lax.axis_size("expert")
+        self.heads = heads
+        self.slices = D // nd // 16
+        self.reaches = (("expert", False),)
+        wide = 2 * DI + 2 * S + 128
+        row = jax.ShapeDtypeStruct((16, wide), BF)
+        self.gather = Gather("expert", row)
+        self.ins = ((x, ANY),)
+        self.outs = ((jax.ShapeDtypeStruct((D // nd, IN_W), F32), IN_VMEM),)
+        dma = pltpu.SemaphoreType.DMA
+        self.scratch = (
+            pltpu.VMEM((nd, 16, x.shape[1]), BF),
+            pltpu.VMEM((16, wide), BF),
+            pltpu.VMEM((ne, 16, wide), BF),
+            dma((2 * ne,)),
+            dma((nd,)),
+        ) + self.gather.scratch
+
+    def greet(self, barrier):
+        nd = lax.axis_size("dp")
+        j = lax.axis_index("dp")
+        for source in range(nd):
+            pl.semaphore_signal(
+                barrier, inc=1, device_id={"dp": source, "expert": j // 2}, device_id_type=MESH
+            )
+        return 2 * lax.axis_size("expert")
+
+    def steps(self, ins, outs, scratch):
+        x = ins[0]
+        got, row, full, send, recv = scratch[:5]
+        nd, ne = lax.axis_size("dp"), lax.axis_size("expert")
+        j, e = lax.axis_index("dp"), lax.axis_index("expert")
+        heads, di = self.heads, self.heads * PS
+        sent = []
+        for k in range(2):
+            for c in range(ne):
+                src = x.at[pl.ds((k * self.slices + min(c, self.slices - 1)) * 16, 16)]
+                mine = (j == 2 * e + k) & (e == c)
+                away = pltpu.make_async_remote_copy(
+                    src_ref=src,
+                    dst_ref=got.at[j],
+                    send_sem=send.at[k * ne + c],
+                    recv_sem=recv.at[j],
+                    device_id={"dp": 2 * e + k, "expert": c},
+                    device_id_type=MESH,
+                )
+                here = pltpu.make_async_copy(src, got.at[j], recv.at[j])
+                pl.when(mine)(here.start)
+                pl.when(jnp.logical_not(mine))(away.start)
+                sent.append((mine, away))
+        yield
+        for source in range(nd):
+            pltpu.make_async_copy(got.at[source], got.at[source], recv.at[source]).wait()
+        piece = lambda source, start, size: got[source, :, start : start + size].astype(F32)
+        for source in range(0, nd, 2):
+            for half in range(2):
+                pair = [piece(source + k, half * di, di) for k in range(2)]
+                start = half * DI + source * di
+                row[:, start : start + 2 * di] = jnp.concatenate(pair, axis=1).astype(BF)
+        total = piece(0, 2 * di, 2 * S)
+        for source in range(1, nd):
+            total = total + piece(source, 2 * di, 2 * S)
+        row[:, 2 * DI : 2 * DI + 2 * S] = total.astype(BF)
+        steps = [piece(source, 2 * di + 2 * S, 128)[:, :heads] for source in range(nd)]
+        steps.append(jnp.zeros((16, 128 - nd * heads), F32))
+        row[:, 2 * DI + 2 * S :] = jnp.concatenate(steps, axis=1).astype(BF)
+        yield from gather_steps("expert", row, full, *scratch[5:])
+        for c in range(self.slices):
+            outs[0][c * 16 : (c + 1) * 16, :] = full[c, :, :IN_W].astype(F32)
+        for mine, away in sent:
+            pl.when(jnp.logical_not(mine))(away.wait_send)
+
+
+class Small(Task):
+    def __init__(self, x):
+        self.reaches = (("expert", True), ("dp", True))
+        nd, ne = lax.axis_size("dp"), lax.axis_size("expert")
+        self.ins = ((x, ANY),)
+        self.outs = ((jax.ShapeDtypeStruct((nd,) + x.shape, x.dtype), ANY),)
+        dma = pltpu.SemaphoreType.DMA
+        self.scratch = (
+            pltpu.VMEM((ne,) + x.shape, x.dtype),
+            pltpu.VMEM(x.shape, x.dtype),
+            dma((ne,)),
+            dma((ne,)),
+            dma,
+            dma((nd,)),
+            dma((nd,)),
+            dma,
+        )
+
+    def steps(self, ins, outs, scratch):
+        parts, total = scratch[:2]
+        yield from direct_steps("gather", "expert", ins[0], parts, *scratch[2:5])
+        total[...] = jnp.sum(parts[...], axis=0)
+        yield from direct_steps("gather", "dp", total, outs[0], *scratch[5:8])
 
 
 class Experts(Task):
@@ -607,7 +657,10 @@
         pre = jax.ShapeDtypeStruct((n, rows, 2 * hidden), BF)
         gh = jax.ShapeDtypeStruct((n, rows, hidden), BF)
         self.ins = tuple((v, ANY) for v in (x, inc, w_up, w_down, s_up, s_down))
-        self.outs = ((all_rows, IN_VMEM),) + self.reduce.outs + ((pre, ANY), (gh, ANY))
+        part = jax.ShapeDtypeStruct((n, rows, depth), BF)
+        self.outs = ((all_rows, IN_VMEM),) + self.reduce.outs + tuple(
+            (v, ANY) for v in (pre, gh, part)
+        )
         dma = pltpu.SemaphoreType.DMA
         self.scratch = (
             (pltpu.VMEM((n, rows, depth), BF),)
@@ -615,16 +668,16 @@
             + (pltpu.VMEM((2 * rows, wide), BF), pltpu.VMEM((2 * rows, depth), BF))
             + (pltpu.VMEM((2 * rows, 2 * hidden), BF), pltpu.VMEM((2 * rows, hidden), BF))
             + (pltpu.VMEM(pre.shape, BF), pltpu.VMEM(gh.shape, BF))
-            + (pltpu.VMEM((2 * rows, 128), F32), dma((21,)))
+            + (pltpu.VMEM((2 * rows, 128), F32), dma((22,)), pltpu.VMEM(part.shape, BF))
             + self.gather.scratch
             + self.reduce.scratch
         )
 
     def steps(self, ins, outs, scratch):
         x, inc_in = ins[:2]
-        x_all, dx_out, pre_out, gh_out = outs
+        x_all, dx_out, pre_out, gh_out, part_out = outs
         inc, w_up, w_down, s_up, s_down, xs, incs, pg, ghs, pre, gh, extra, sems = scratch[:13]
-        gather_scratch, reduce_scratch = scratch[13:16], scratch[16:]
+        part, gather_scratch, reduce_scratch = scratch[13], scratch[14:17], scratch[17:]
         acc = reduce_scratch[0]
         me, at = places("expert")
         n, rows, depth = inc.shape
@@ -728,17 +781,55 @@
         store = pltpu.make_async_copy(gh, gh_out, sems.at[12])
         store.start()
         stores.append(store)
-        yield from reduce_steps("expert", None, dx_out, *reduce_scratch)
+        summing = reduce_steps("expert", None, dx_out, *reduce_scratch)
+        next(summing)
+        for half in range(2):
+            next(summing)
+
+            @pl.loop(half * depth // tile // 2, (half + 1) * depth // tile // 2)
+            def _(i):
+                columns = pl.ds(pl.multiple_of(i * tile, tile), tile)
+                hid = lambda start, size: gh[:, :, start : start + size].reshape(n * rows, size)
+                total = mm(hid(experts * each, shared), s_down[:, columns])
+                for e in range(experts):
+                    total += mm(hid(e * each, each), w_down[e, :, columns])
+                part[:, :, columns] = total.astype(BF).reshape(n, rows, tile)
+
+        store = pltpu.make_async_copy(part, part_out, sems.at[21])
+        store.start()
+        stores.append(store)
+        yield from summing
         for store in stores:
             store.wait()
 
 
 EDGE = 8
-HIGHEST = lax.Precision.HIGHEST
-
-
-def exact(a, b, dims):
-    return lax.dot_general(a, b, (dims, ((), ())), precision=HIGHEST, preferred_element_type=F32)
+
+
+def pieces(v, count):
+    out = []
+    for _ in range(count):
+        out.append(v.astype(BF))
+        v = v - out[-1].astype(F32)
+    return out
+
+
+def exact(v, ones, dims, count=2):
+    ones = ones.astype(BF)
+    parts = [
+        lax.dot_general(p, ones, (dims, ((), ())), preferred_element_type=F32)
+        for p in pieces(v, count)
+    ]
+    return sum(parts[1:], parts[0])
+
+
+def exact_right(ones, v, dims, count=2):
+    ones = ones.astype(BF)
+    parts = [
+        lax.dot_general(ones, p, (dims, ((), ())), preferred_element_type=F32)
+        for p in pieces(v, count)
+    ]
+    return sum(parts[1:], parts[0])
 
 
 def iota(shape, axis):
@@ -788,8 +879,8 @@
         rise = self.steps * self.rate
         rows, cols = iota((loc, loc), 0), iota((loc, loc), 1)
         self.lower = (cols <= rows).astype(F32)
-        self.cum = exact(self.lower, rise, ((1,), (0,)))
-        cum_rows = exact(rise, (rows <= cols).astype(F32), ((0,), (0,)))
+        self.cum = exact_right(self.lower, rise, ((1,), (0,)), 3)
+        cum_rows = exact(rise, (rows <= cols).astype(F32), ((0,), (0,)), 3)
         self.last = self.cum[loc - 1 : loc, :]
         self.grow = jnp.exp(self.cum) * self.keep
         self.fall = jnp.exp(self.last - self.cum) * self.same_last
@@ -829,8 +920,33 @@
         return out
 
 
+def load_weights(pieces_ref, w, sem):
+    copies = [
+        pltpu.make_async_copy(pieces_ref.at[k], w.at[:, k], sem.at[k]) for k in range(w.shape[1])
+    ]
+    for copy in copies:
+        copy.start()
+    for copy in copies:
+        copy.wait()
+
+
 def forward_kernel(
-    heads, lengths, g, w, w_out, taps, heads_vec, lanes_vec, payload, proj, scan, states, ext, state
+    heads,
+    lengths,
+    g,
+    w_pieces,
+    w_out,
+    taps,
+    heads_vec,
+    lanes_vec,
+    payload,
+    proj,
+    scan,
+    states,
+    ext,
+    state,
+    w,
+    w_sem,
 ):
     b = pl.program_id(0)
     loc = g.shape[1] // MB
@@ -840,8 +956,9 @@
     def _():
         ext[...] = jnp.zeros_like(ext)
         state[...] = jnp.zeros_like(state)
-
-    proj[0] = mm(g[0, :, :D], w[...])
+        load_weights(w_pieces, w, w_sem)
+
+    proj[0] = mm(g[0, :, :D], w[...].reshape(D, -1))
     column = iota((loc, payload.shape[2] - D), 1)
     for m in range(MB):
         rows = slice(m * loc, (m + 1) * loc)
@@ -867,7 +984,7 @@
     heads,
     lengths,
     grad,
-    w,
+    w_pieces,
     w_out,
     taps,
     heads_vec,
@@ -885,6 +1002,8 @@
     ext,
     d_ext,
     d_state,
+    w,
+    w_sem,
 ):
     step = pl.program_id(0)
     b = pl.num_programs(0) - 1 - step
@@ -896,6 +1015,7 @@
     def _():
         for ref in (d_ext, d_state, d_out, d_taps, d_heads, d_lanes):
             ref[...] = jnp.zeros_like(ref)
+        load_weights(w_pieces, w, w_sem)
 
     gated_grad = mm_nt(grad[0, :, :D], w_out[...])
     extra = grad[0, :, D:].astype(F32)
@@ -969,7 +1089,7 @@
         d_cum = d_cum + jnp.where(iota((loc, 1), 0) == loc - 1, d_last, 0.0)
         d_state[m] = part.decay_rows() * ds + mm_tn(d_carry_low, part.read)
 
-        d_rise = exact(part.lower, d_cum, ((0,), (0,)))
+        d_rise = exact_right(part.lower, d_cum, ((0,), (0,)))
         d_steps = d_steps + d_rise * part.rate
         d_raw = d_steps * jax.nn.sigmoid(part.raw)
         d_heads[0:1, :] += jnp.sum(d_raw, axis=0, keepdims=True)
@@ -992,7 +1112,15 @@
         d_proj[0, rows, :di] = d_gate.astype(BF)
         d_proj[0, rows, di : di + width] = d_seq.astype(BF)
         d_proj[0, rows, di + width :] = jnp.where(head_lane < heads, d_raw, 0.0).astype(BF)
-    normed_part[0] = mm_nt(d_proj[0], w[...]).astype(BF)
+    normed_part[0] = mm_nt(d_proj[0], w[...].reshape(D, -1)).astype(BF)
+
+
+def weight_scratch(w):
+    slices = D // w.shape[1] // w.shape[2]
+    return [
+        pltpu.VMEM((w.shape[1], slices) + w.shape[2:], BF),
+        pltpu.SemaphoreType.DMA((slices,)),
+    ]
 
 
 def block_spec(shape, index):
@@ -1009,7 +1137,7 @@
     width = di + 2 * S
     shapes = [
         jax.ShapeDtypeStruct((nb, rows, D + 128), BF),
-        jax.ShapeDtypeStruct((nb, rows, w.shape[1]), F32),
+        jax.ShapeDtypeStruct((nb, rows, w.shape[-1]), F32),
         jax.ShapeDtypeStruct((nb, rows, di), F32),
         jax.ShapeDtypeStruct((nb, MB, di, S), F32),
     ]
@@ -1019,12 +1147,14 @@
         grid=(nb,),
         out_shape=shapes,
         in_specs=[pl.BlockSpec(memory_space=pltpu.SMEM), block_spec(g.shape, same)]
-        + [whole_spec(v.shape) for v in (w, w_out, taps, heads_vec, lanes_vec)],
+        + [pl.BlockSpec(memory_space=pl.ANY)]
+        + [whole_spec(v.shape) for v in (w_out, taps, heads_vec, lanes_vec)],
         out_specs=[block_spec(v.shape, same) for v in shapes],
         scratch_shapes=[
             pltpu.VMEM((MB, rows // MB + EDGE, width), F32),
             pltpu.VMEM((MB, di, S), F32),
-        ],
+        ]
+        + weight_scratch(w),
         compiler_params=pltpu.CompilerParams(vmem_limit_bytes=VMEM_LIMIT),
         name="mixer_forward",
     )(lengths, g, w, w_out, taps, heads_vec, lanes_vec)
@@ -1037,7 +1167,7 @@
     back = lambda i: nb - 1 - i
     before = lambda i: jnp.maximum(nb - 2 - i, 0)
     per_block = [
-        jax.ShapeDtypeStruct((nb, rows, w.shape[1]), BF),
+        jax.ShapeDtypeStruct((nb, rows, w.shape[-1]), BF),
         jax.ShapeDtypeStruct((nb, rows, D), BF),
     ]
     sums = [
@@ -1051,7 +1181,8 @@
         grid=(nb,),
         out_shape=per_block + sums,
         in_specs=[pl.BlockSpec(memory_space=pltpu.SMEM), block_spec(grad.shape, back)]
-        + [whole_spec(v.shape) for v in (w, w_out, taps, heads_vec, lanes_vec)]
+        + [pl.BlockSpec(memory_space=pl.ANY)]
+        + [whole_spec(v.shape) for v in (w_out, taps, heads_vec, lanes_vec)]
         + [block_spec(proj.shape, back), block_spec(proj.shape, before)]
         + [block_spec(scan.shape, back), block_spec(states.shape, back)],
         out_specs=[block_spec(v.shape, back) for v in per_block]
@@ -1060,40 +1191,11 @@
             pltpu.VMEM((MB, rows // MB + EDGE, width), F32),
             pltpu.VMEM((MB, rows // MB + EDGE, width), F32),
             pltpu.VMEM((MB, di, S), F32),
-        ],
+        ]
+        + weight_scratch(w),
         compiler_params=pltpu.CompilerParams(vmem_limit_bytes=VMEM_LIMIT),
         name="mixer_backward",
     )(lengths, grad, w, w_out, taps, heads_vec, lanes_vec, proj, proj, scan, states)
-
-
-def assemble_kernel(heads, got, out):
-    n, rows, _ = got.shape
-    di = heads * PS
-    piece = lambda j, start, size: got[j, :, start : start + size].astype(F32)
-    for j in range(0, n, 2):
-        for half in range(2):
-            pair = [piece(j + k, half * di, di) for k in range(2)]
-            start = half * n * di + j * di
-            out[:, start : start + 2 * di] = jnp.concatenate(pair, axis=1)
-    total = piece(0, 2 * di, 2 * S)
-    for j in range(1, n):
-        total = total + piece(j, 2 * di, 2 * S)
-    start = 2 * n * di
-    out[:, start : start + 2 * S] = total
-    steps = [piece(j, 2 * di + 2 * S, 128)[:, :heads] for j in range(n)]
-    out[:, start + 2 * S :] = jnp.concatenate(steps, axis=1)
-
-
-def assemble(got, heads):
-    n, rows, _ = got.shape
-    return pl.pallas_call(
-        functools.partial(assemble_kernel, heads),
-        out_shape=jax.ShapeDtypeStruct((rows, IN_W), F32),
-        in_specs=[IN_VMEM],
-        out_specs=IN_VMEM,
-        compiler_params=pltpu.CompilerParams(vmem_limit_bytes=VMEM_LIMIT),
-        name="assemble",
-    )(got)
 
 
 def body(
@@ -1131,8 +1233,9 @@
     fsl = fsr // ne
 
     pad = 128 - heads
-    piece = dr // ne
-    mine = lax.dynamic_slice_in_dim(input_weight, me_e * piece, piece, 0)
+    piece = 16
+    place = jnp.minimum(me_e, dr // piece - 1) * piece
+    mine = lax.dynamic_slice_in_dim(input_weight, place, piece, 0)
     blocks = jnp.concatenate(
         [
             jnp.moveaxis(mine[:, :DI].reshape(piece, nd, di), 1, 0),
@@ -1143,7 +1246,6 @@
         ],
         axis=2,
     )
-    blocks = jnp.pad(blocks, ((0, 0), (0, -piece % 16), (0, 0)))
     wcols = blocks.shape[2]
 
     sg = shared_gate_up.reshape(dr, 2, nd, ne, fsl)
@@ -1161,7 +1263,6 @@
     (_, w_in), (normed_all,) = run_tasks(
         [Weights(blocks), Gather("dp", jnp.concatenate([normed, packed], axis=1))], 1, "begin"
     )
-    w_in = jnp.swapaxes(w_in[:, :, :piece], 0, 1).reshape(D, wcols)
     early, _ = lax.optimization_barrier((incoming, normed_all))
     inc_all = lax.all_gather(early, "expert", axis=0, tiled=True)
     packed_all = normed_all[:, :, D:].reshape(nd, rows_t, 256)[:, :, : packed_cols]
@@ -1204,7 +1305,7 @@
     moe_payload = jnp.concatenate(
         [moe_in, t_hi, t_lo, jnp.zeros((rows_t, 128 - 2 * experts), BF)], axis=1
     )
-    (moe_all, back_sum, pre_grad, gh), = run_tasks(
+    (moe_all, back_sum, pre_grad, gh, out_part), = run_tasks(
         [Experts(moe_payload, inc_all, expert_gate_up, expert_down, sg_full, sd_full)], 3, "experts"
     )
     width = gh.shape[2]
@@ -1223,10 +1324,11 @@
     grad_payload = jnp.concatenate(
         [after_low, r_hi, r_lo, d_hi, d_lo, jnp.zeros((rows_t, 124), BF)], axis=1
     )
-    (grad_all,), (out_part, grad_blocks) = run_tasks(
+    (grad_all,), (out_sum,), (grad_blocks,) = run_tasks(
         [
             Gather("dp", grad_payload),
-            ExpertGrads(moe_all, pre_grad, gh, inc_all, expert_down, sd_full, nd),
+            Reduce("expert", out_part),
+            ExpertGrads(moe_all, pre_grad, gh, inc_all, el, FE, nd),
         ],
         5,
         "gather_grad",
@@ -1262,7 +1364,7 @@
             InputGrad(
                 normed_all,
                 d_proj.reshape(nd * rows_t, wcols),
-                output_part.astype(BF).reshape(-1, wcols),
+                output_part.astype(BF),
             ),
             Direct("all", "dp", rows_of(added, nd * added_rows).reshape(nd, added_rows, 128)),
         ],
@@ -1277,33 +1379,21 @@
     )
     small = jnp.pad(small, ((0, -small.shape[0] % 8), (0, 0)))
     shared_part = jnp.concatenate(
+        [up_sum[:, 2 * el * FE :], last_sum[:fsl, span:].reshape(dr, -1)], axis=1
+    ).reshape(-1, wcols)
+    main_rows = D // ne
+    (input_grad,), (rest_all,), (small_all,) = run_tasks(
         [
-            up_sum[:, 2 * el * FE :],
-            last_sum[:fsl, span:].reshape(dr, -1),
-        ],
-        axis=1,
-    ).reshape(-1, wcols)
-    (d_full,), (small_in,) = run_tasks(
-        [
-            Gather("expert", jnp.concatenate([d_sum, shared_part], axis=0)),
-            Direct("gather", "expert", small),
+            InputRows(d_sum[:main_rows], heads),
+            Gather("expert", jnp.concatenate([d_sum[main_rows:], shared_part], axis=0)),
+            Small(small),
         ],
         7,
-        "gather_grads",
-    )
-    shared_all = d_full[:, d_sum.shape[0] :].reshape(ne, dr, -1)
-    d_full = d_full[:, : d_sum.shape[0]].reshape(-1, wcols)
-    (got, _), (out_sum,), (small_all,) = run_tasks(
-        [
-            Swap(d_full[:D].reshape(nd, dr, wcols)),
-            Reduce("expert", out_part),
-            Direct("gather", "dp", jnp.sum(small_in, axis=0)),
-        ],
-        8,
-        "swap_grads",
-    )
-    input_grad = assemble(got, heads)
-    output_grad = d_full[D:].reshape(output_weight.shape)
+        "finish",
+    )
+    cut_rows = d_sum.shape[0] - main_rows
+    output_grad = rest_all[:, :cut_rows].reshape(output_weight.shape)
+    shared_all = rest_all[:, cut_rows:].reshape(ne, dr, -1)
     added_all = small_all[:, :added_rows].reshape(-1)
     own_all = small_all[:, added_rows : added_rows + own_rows].reshape(nd, -1)
     norm_gain_grad = jnp.sum(

time: 665 us -> 592 us (0.89)
  Pallas kernels: 543 us -> 487 us
  local copies, waits for them, and re-layouts: 69.3 us -> 52.9 us
    pallas_call x7 -> x6, Pallas kernels: 418 us -> 382 us  [run_tasks(): pl.pallas_call(kernel, out_shape=out_shapes, in_specs=in_specs, out_specs...]
    pallas_call x1, Pallas kernels: 84.6 us -> 67.3 us  [mixer_backward(): pl.pallas_call(functools.partial(backward_kernel, heads), grid=(nb,), out...]
  transfers between devices with their start and end apart: 2 -> 2, of which waited for: 0 -> 0; matrix products, arithmetic and copies ran while one was open for 6% -> 6% of each run, Pallas kernels for 33% -> 35%
where the time goes in v6:
time: 592 us; the launch traced here: 586 us
  Pallas kernels  487 us (82%)
  local copies, waits for them, and re-layouts  52.9 us (9%)
  other arithmetic  27.9 us (5%)
  between operations  15 us (3%)
    pallas_call x6, Pallas kernels, run_tasks(): pl.pallas_call(kernel, out_shape=out_shapes, in_specs=in_specs, out_specs...  382 us
    pallas_call x1, Pallas kernels, mixer_backward(): pl.pallas_call(functools.partial(backward_kernel, heads), grid=(nb,), out...  67.3 us
    pallas_call x1, Pallas kernels, mixer_forward(): pl.pallas_call(functools.partial(forward_kernel, heads), grid=(nb,), out_...  37.9 us
  transfers between devices with their start and end apart: 2, of which 0 were waited for; matrix products, arithmetic and copies ran while one was open for 6% of the time, Pallas kernels for 35%

profile of v6, /device:TPU:1, one launch (start us, length us, event | category | flops | bytes accessed | tf_op | source)
XLA Modules:
  0.0 586.2 jit_solution(16567054462896707886)
XLA Ops:
  16.6 76.0 %begin.1 = (bf16[16,16,768]{2,1,0:T(8,128)(2,1)}, bf16[8,16,16,768]{3,2,1,0:T(8,128)(2,1)}, bf16[16,160,1792]{2,1,0:T(8,128)(2,1)}) custom-call(bf16[16,16,768]{2,1,0:T(8,128)(2,1)} %concatenate.48.refs_0_, bf16[160,1792]{1,0:T(8,128)(2,1)} %fusion.4.refs_1_), custom_call_target="tpu_custom_call" | custom-call | tf_op jit(solution)/shard_map/begin/pallas_call | solution.py:378
  92.8 1.4 slice.182
  94.3 2.0 reshape.286
  101.5 37.9 %mixer_forward.1 = (bf16[16,160,1664]{2,1,0:T(8,128)(2,1)}, f32[16,160,768]{2,1,0:T(8,128)}, f32[16,160,192]{2,1,0:T(8,128)}, f32[16,2,192,128]{3,2,1,0:T(8,128)}) custom-call(s32[2,3]{1,0:T(2,128)} %bitcast.112, bf16[16,160,1792]{2,1,0:T(8,128)(2,1)} %get-tuple-element.44.g.refs_1_, bf16[8,16,16,768]{3,2,1,0:T(8,128)(2,1)} %get-tuple-element.45.w_pieces, ...), custom_call_target="tpu_custom_call" | custom-call | tf_op jit(solution)/shard_map/mixer_forward/pallas_call | solution.py:1145
  139.4 43.4 %reduce_mixer.1 = f32[160,1664]{1,0:T(8,128)} custom-call(bf16[16,160,1664]{2,1,0:T(8,128)(2,1)} %get-tuple-element.46.refs_0_), custom_call_target="tpu_custom_call" | custom-call | tf_op jit(solution)/shard_map/reduce_mixer/pallas_call | solution.py:378
  182.8 1.7 subtract_convert_fusion.1
  184.5 1.4 fusion.3
  190.6 88.6 %experts.1 = (bf16[8,160,1664]{2,1,0:T(8,128)(2,1)}, f32[160,1664]{1,0:T(8,128)}, bf16[8,160,2304]{2,1,0:T(8,128)(2,1)}, bf16[8,160,1152]{2,1,0:T(8,128)(2,1)}, bf16[8,160,1536]{2,1,0:T(8,128)(2,1)}) custom-call(bf16[160,1664]{1,0:T(8,128)(2,1)} %concatenate.54.refs_0_, bf16[1280,1536]{1,0:T(8,128)(2,1)} %all-gather.2.cloned.1.call-done.refs_1_.refs_5_, ...), custom_call_target="tpu_custom_call" | custom-call | tf_op jit(solution)/shard_map/experts/pallas_call | solution.py:378
  281.5 1.8 multiply_reduce_fusion.2
  286.5 1.6 subtract_convert_fusion
  288.6 1.7 concatenate.55.refs_0_
  290.3 67.3 %gather_grad.1 = (bf16[16,160,1664]{2,1,0:T(8,128)(2,1)}, f32[160,1536]{1,0:T(8,128)}, bf16[16,160,2304]{2,1,0:T(8,128)(2,1)}) custom-call(bf16[160,1664]{1,0:T(8,128)(2,1)} %concatenate.55.refs_0_, bf16[8,160,1536]{2,1,0:T(8,128)(2,1)} %get-tuple-element.49.refs_1_, bf16[8,160,1664]{2,1,0:T(8,128)(2,1)} %get-tuple-element.50.refs_2_, ...), custom_call_target="tpu_custom_call" | custom-call | tf_op jit(solution)/shard_map/gather_grad/pallas_call | solution.py:378
  357.7 67.3 %mixer_backward.1 = (bf16[16,160,768]{2,1,0:T(8,128)(2,1)}, bf16[16,160,1536]{2,1,0:T(8,128)(2,1)}, f32[192,1536]{1,0:T(8,128)}, f32[8,448]{1,0:T(8,128)}, f32[8,128]{1,0:T(8,128)}, /*index=5*/f32[8,192]{1,0:T(8,128)}) custom-call(s32[2,3]{1,0:T(2,128)} %bitcast.113, bf16[16,160,1664]{2,1,0:T(8,128)(2,1)} %get-tuple-element.54.grad, ...), custom_call_target="tpu_custom_call" | custom-call | tf_op jit(solution)/shard_map/mixer_backward/pallas_call | solution.py:1179
  429.3 1.4 reshape.294
  433.7 55.2 %reduce_grads.1 = (f32[160,1536]{1,0:T(8,128)}, bf16[240,768]{1,0:T(8,128)(2,1)}, f32[16,16,128]{2,1,0:T(8,128)}) custom-call(bf16[16,160,1536]{2,1,0:T(8,128)(2,1)} %get-tuple-element.58.refs_0_, bf16[16,160,1792]{2,1,0:T(8,128)(2,1)} %get-tuple-element.44.g.refs_1_, bf16[2560,768]{1,0:T(8,128)(2,1)} %bitcast.88, bf16[8,48,768]{2,1,0:T(8,128)(2,1)} %reshape.292.refs_3_, ...), custom_call_target="tpu_custom_call" | custom-call | tf_op jit(solution)/shard_map/reduce_grads/pallas_call | solution.py:378
  488.8 1.5 slice.192
  490.4 1.7 slice.191.refs_0_
  494.9 1.6 multiply_reduce_fusion
  503.2 51.2 %finish.1 = (f32[96,6448]{1,0:T(8,128)}, bf16[8,96,768]{2,1,0:T(8,128)(2,1)}, f32[16,40,128]{2,1,0:T(8,128)}) custom-call(bf16[192,768]{1,0:T(8,128)(2,1)} %slice.191.refs_0_, bf16[96,768]{1,0:T(8,128)(2,1)} %pad_maximum_fusion.refs_1_, f32[40,128]{1,0:T(8,128)} %select_maximum_fusion.3.refs_2_), custom_call_target="tpu_custom_call" | custom-call | tf_op jit(solution)/shard_map/finish/pallas_call | solution.py:378
  554.4 1.5 slice_reduce_fusion
  559.5 2.2 fusion.12
  561.7 2.0 reshape.311
  563.7 1.7 slice_convert_fusion.2
  575.8 3.4 copy.124
  (209 shorter events, 55.9 us)
Async XLA Ops:
  7.2 2.3 copy-start
  7.2 4.8 copy-start.12
  7.2 183.4 %all-gather.2.cloned.1.call-start = ((), (), s32[]{:S(2)}) async-start(), calls=%async_computation.1 | async-start | bytes 4423680 | tf_op jit(solution)/shard_map/all_gather | solution.py:1267
  12.3 2.2 copy-start.2
  12.4 2.2 copy-start.18
  92.6 406.6 %reduce-scatter.2.cloned.1.call-start = ((), (), s32[]{:S(2)}) async-start(), calls=%async_computation.2 | async-start | bytes 12533760 | tf_op jit(solution)/shard_map/reduce_scatter | solution.py:1336
  96.3 3.0 copy-start.23
  96.4 3.0 copy-start.24
  96.4 3.0 slice-start.5
  96.4 3.1 copy-start.19
  96.4 4.4 slice-start.4
  184.5 1.6 copy-start.17
  186.8 1.8 slice-start
  190.6 90.8 %copy-start.7 = (bf16[1536,16]{1,0:T(8,128)(2,1)S(1)}, bf16[1536,16]{1,0:T(8,128)(2,1)}, u32[]{:S(2)}) copy-start(bf16[1536,16]{1,0:T(8,128)(2,1)} %reshape.287) | copy-start | bytes 147460
  281.5 1.8 copy-start.8
  492.1 5.1 copy-start.10
  496.5 1.5 copy-start.5
  499.2 2.4 copy-start.11
  559.1 9.9 %copy-start.16 = (f32[128,256]{1,0:T(8,128)}, f32[128,256]{1,0:T(8,128)S(1)}, u32[]{:S(2)}) copy-start(f32[128,256]{1,0:T(8,128)S(1)} %slice.208) | copy-start | bytes 393220
  566.3 3.5 copy-start.9
  569.1 1.6 slice-start.2
  572.4 2.2 copy-start.22
  572.4 2.8 slice-start.3
  575.8 3.4 copy-start.1
  (11 other events, 12.0 us)
Sparse Core Ops, SparseCore 0:
  92.7 66.6 all-gather.1
  357.8 77.6 reduce-scatter.1

commit v7 on v6

--- a/solution.py
+++ b/solution.py
@@ -42,11 +42,6 @@
     return values * lax.rsqrt(jnp.mean(values * values, axis=-1, keepdims=True) + EPSILON) * gain
 
 
-def hi_lo(v):
-    hi = v.astype(BF)
-    return hi, (v - hi.astype(F32)).astype(BF)
-
-
 ANY = pl.BlockSpec(memory_space=pl.ANY)
 IN_VMEM = pl.BlockSpec(memory_space=pltpu.VMEM)
 
@@ -153,14 +148,12 @@
     arrived(2, pair, whole)
     push(4, pair, whole, up)
     push(5, pair, whole, down)
-    if cores:
-        push(6, pair, whole, sib)
-    yield
     arrived(0, down, whole)
     push(7, down, first, up)
     arrived(1, up, whole)
     push(8, up, second, down)
     if cores:
+        push(6, pair, whole, sib)
         push(9, down, whole, sib)
         push(10, up, whole, sib)
     yield
@@ -168,13 +161,11 @@
     push(11, at(-1, 1), first, up)
     arrived(5, at(1, 1), whole)
     push(12, at(1, 1), second, down)
+    arrived(7, at(2, 0), first)
+    arrived(8, at(2, 0), second)
     if cores:
         push(13, at(-1, 1), whole, sib)
         push(14, at(1, 1), whole, sib)
-    yield
-    arrived(7, at(2, 0), first)
-    arrived(8, at(2, 0), second)
-    if cores:
         push(15, at(2, 0), whole, sib)
     yield
     arrived(11, at(2, 1), first)
@@ -271,17 +262,15 @@
         above, below = 2 + 2 * k, 3 + 2 * k
         ready(above)
         ready(below)
-        if k:
-            yield
         arrived(8 + 2 * k, a_buf.at[k])
         add(acc.at[above], 0, cut, a_buf.at[k])
         push(12 + 2 * k, acc.at[above], c_buf.at[k], up)
         arrived(9 + 2 * k, b_buf.at[k])
         add(acc.at[below], cut, rows - cut, b_buf.at[k])
         push(13 + 2 * k, acc.at[below], d_buf.at[k], down)
+    yield
     ready(6)
     ready(7)
-    yield
     arrived(12, c_buf.at[0])
     arrived(13, d_buf.at[0])
     add(acc.at[6], 0, rows, c_buf.at[0], d_buf.at[0])
@@ -391,7 +380,7 @@
 
 class Weights(Task):
     def __init__(self, x):
-        self.reaches, self.turns = (("dp", True), ("expert", False)), 2
+        self.reaches = (("dp", True), ("expert", False))
         self.swap, self.spread = Direct("all", "dp", x), Gather("expert", x)
         n = lax.axis_size("expert")
         full = jax.ShapeDtypeStruct((n,) + x.shape, x.dtype)
@@ -449,6 +438,18 @@
         def _(i):
             x_t[col(i), :] = x[:, :, col(i)].reshape(n * rows, tile).T
 
+        load_pre.wait()
+        blocks = grads.shape[0]
+        up_rows = depth // blocks
+        steps = 2 * width // tile
+        for start, end in ((0, steps // 3), (steps // 3, steps)):
+
+            @pl.loop(start, end)
+            def _(i):
+                value = mm(x_t[...], pre_grad[:, :, col(i)].reshape(n * rows, tile)).astype(BF)
+                grads[:, :up_rows, col(i)] = value.reshape(blocks, up_rows, tile)
+
+            yield
         load_gh.wait()
 
         @pl.loop(0, width // 128)
@@ -456,18 +457,6 @@
             at_cols = pl.ds(pl.multiple_of(i * 128, 128), 128)
             gh_t[at_cols, :] = gh[:, :, at_cols].reshape(n * rows, 128).T
 
-        load_pre.wait()
-        blocks = grads.shape[0]
-        up_rows = depth // blocks
-        for third in range(3):
-            steps = 2 * width // tile // 3
-
-            @pl.loop(third * steps, (third + 1) * steps)
-            def _(i):
-                value = mm(x_t[...], pre_grad[:, :, col(i)].reshape(n * rows, tile)).astype(BF)
-                grads[:, :up_rows, col(i)] = value.reshape(blocks, up_rows, tile)
-
-            yield
         load_inc.wait()
         piece_rows = each // blocks
         own = (width - experts * each) // blocks
@@ -491,10 +480,101 @@
                 piece = jnp.concatenate([piece, empty], axis=1).astype(BF)
                 grads[:, up_rows + piece_rows :, col((1 + half) * span // tile + i)] = piece
 
-            yield
         store = copy(grads, outs[0], 4)
         store.start()
+        yield
         store.wait()
+
+
+def chunks(rows, step=16):
+    def over(work):
+        @pl.loop(0, rows // step)
+        def _(i):
+            work(pl.ds(pl.multiple_of(i * step, step), step))
+
+    return over
+
+
+def sides(v):
+    high = v.astype(BF).astype(F32)
+    turn = (iota((128, 128), 0) + 16 == iota((128, 128), 1)).astype(F32)
+    return (high + exact(v - high, turn, ((1,), (0,)))).astype(BF)
+
+
+def joined(v):
+    turn = (iota((128, 128), 0) - 16 == iota((128, 128), 1)).astype(F32)
+    back = exact(v, turn, ((1,), (0,)))
+    return jnp.where(iota((1, 128), 1) < 16, v + back, 0.0)
+
+
+class MixerOut(Task):
+    def __init__(self, payload, stream, gain, router, mask):
+        self.reaches = (("dp", False),)
+        self.reduce = Reduce("dp", payload)
+        rows, wide = payload.shape[1:]
+        self.ins = self.reduce.ins + tuple((v, IN_VMEM) for v in (stream, gain, router, mask))
+        shape = jax.ShapeDtypeStruct
+        self.outs = (
+            (shape((rows, wide), BF), IN_VMEM),
+            (shape((rows, D), F32), IN_VMEM),
+            (shape((rows, D), F32), IN_VMEM),
+            (shape((rows, 128), F32), IN_VMEM),
+        )
+        self.scratch = (pltpu.VMEM((rows, wide), F32),) + self.reduce.scratch
+
+    def steps(self, ins, outs, scratch):
+        x, stream, gain, router, mask = ins
+        payload, after, mixed, factors = outs
+        total = scratch[0]
+        yield from reduce_steps("dp", x, total, *scratch[1:])
+
+        @chunks(total.shape[0])
+        def _(rows):
+            squares = total[rows, D:]
+            lane = iota((1, 128), 1)
+            square = jnp.sum(jnp.where(lane < 2, squares, 0.0), axis=1, keepdims=True)
+            r = lax.rsqrt(square / DI + EPSILON)
+            mix = total[rows, :D] * r
+            v = stream[rows, :].astype(F32) + mix
+            inv = lax.rsqrt(jnp.mean(v * v, axis=1, keepdims=True) + EPSILON)
+            low = (v * inv * gain[...]).astype(BF)
+            logits = mm(low, router[...])
+            chosen = mask[rows, :]
+            top = jnp.max(jnp.where(chosen > 0.0, logits, -1e30), axis=1, keepdims=True)
+            e = jnp.where(chosen > 0.0, jnp.exp(jnp.minimum(logits - top, 0.0)), 0.0)
+            table = e / jnp.sum(e, axis=1, keepdims=True)
+            payload[rows, :D] = low
+            payload[rows, D:] = sides(table)
+            after[rows, :] = v
+            mixed[rows, :] = mix
+            factors[rows, :] = jnp.where(lane == 0, r, jnp.where(lane == 1, inv, 0.0))
+
+
+class StreamGrad(Task):
+    def __init__(self, parts, stream, gain, after_grad):
+        self.reaches = (("dp", False),)
+        self.reduce = Reduce("dp", parts)
+        self.ins = self.reduce.ins + tuple((v, IN_VMEM) for v in (stream, gain, after_grad))
+        shape = jax.ShapeDtypeStruct
+        self.outs = ((shape(stream.shape, F32), IN_VMEM), (shape((1, D), F32), IN_VMEM))
+        self.scratch = (pltpu.VMEM(stream.shape, F32),) + self.reduce.scratch
+
+    def steps(self, ins, outs, scratch):
+        x, stream, gain, after_grad = ins
+        out, gain_grad = outs
+        total = scratch[0]
+        yield from reduce_steps("dp", x, total, *scratch[1:])
+        gain_grad[...] = jnp.zeros_like(gain_grad)
+
+        @chunks(total.shape[0])
+        def _(rows):
+            v = stream[rows, :].astype(F32)
+            inv = lax.rsqrt(jnp.mean(v * v, axis=1, keepdims=True) + EPSILON)
+            g = total[rows, :]
+            gg = g * gain[...]
+            gain_grad[...] += jnp.sum(g * v * inv, axis=0, keepdims=True)
+            mean = jnp.mean(gg * v, axis=1, keepdims=True)
+            out[rows, :] = after_grad[rows, :] + inv * gg - v * (inv * inv * inv * mean)
 
 
 class InputGrad(Task):
@@ -541,8 +621,6 @@
 
 
 class InputRows(Task):
-    turns = 2
-
     def __init__(self, x, heads):
         nd, ne = lax.axis_size("dp"), lax.axis_size("expert")
         self.heads = heads
@@ -643,7 +721,7 @@
 
 
 class Experts(Task):
-    def __init__(self, x, inc, w_up, w_down, s_up, s_down):
+    def __init__(self, x, inc, w_up, w_down, s_up, s_down, after, mixed, factors, gain, router, own):
         self.reaches = (("expert", False),)
         self.gather = Gather("expert", x)
         n = lax.axis_size("expert")
@@ -656,10 +734,20 @@
         hidden = experts * both // 2 + s_down.shape[0]
         pre = jax.ShapeDtypeStruct((n, rows, 2 * hidden), BF)
         gh = jax.ShapeDtypeStruct((n, rows, hidden), BF)
-        self.ins = tuple((v, ANY) for v in (x, inc, w_up, w_down, s_up, s_down))
+        self.ins = tuple((v, ANY) for v in (x, inc, w_up, w_down, s_up, s_down)) + tuple(
+            (v, IN_VMEM) for v in (after, mixed, factors, gain, router, own)
+        )
         part = jax.ShapeDtypeStruct((n, rows, depth), BF)
-        self.outs = ((all_rows, IN_VMEM),) + self.reduce.outs + tuple(
-            (v, ANY) for v in (pre, gh, part)
+        shape = jax.ShapeDtypeStruct
+        self.outs = (
+            ((all_rows, IN_VMEM),)
+            + tuple((v, ANY) for v in (pre, gh, part))
+            + (
+                (shape((rows, depth), F32), IN_VMEM),
+                (shape((rows, wide), BF), IN_VMEM),
+                (shape((1, depth), F32), IN_VMEM),
+                (shape((16, depth), F32), IN_VMEM),
+            )
         )
         dma = pltpu.SemaphoreType.DMA
         self.scratch = (
@@ -669,15 +757,17 @@
             + (pltpu.VMEM((2 * rows, 2 * hidden), BF), pltpu.VMEM((2 * rows, hidden), BF))
             + (pltpu.VMEM(pre.shape, BF), pltpu.VMEM(gh.shape, BF))
             + (pltpu.VMEM((2 * rows, 128), F32), dma((22,)), pltpu.VMEM(part.shape, BF))
+            + (pltpu.VMEM((rows, wide), F32),)
             + self.gather.scratch
             + self.reduce.scratch
         )
 
     def steps(self, ins, outs, scratch):
         x, inc_in = ins[:2]
-        x_all, dx_out, pre_out, gh_out, part_out = outs
+        after, mixed, factors, gain, router, own = ins[6:]
+        x_all, pre_out, gh_out, part_out, after_grad, payload, gain_grad, router_grad = outs
         inc, w_up, w_down, s_up, s_down, xs, incs, pg, ghs, pre, gh, extra, sems = scratch[:13]
-        part, gather_scratch, reduce_scratch = scratch[13], scratch[14:17], scratch[17:]
+        part, dx, gather_scratch, reduce_scratch = scratch[13], scratch[14], scratch[15:18], scratch[18:]
         acc = reduce_scratch[0]
         me, at = places("expert")
         n, rows, depth = inc.shape
@@ -687,7 +777,7 @@
         tile = min(256, each)
         loads = [
             pltpu.make_async_copy(src, dst, sems.at[k])
-            for k, (src, dst) in enumerate(zip(ins[2:], (w_up, w_down, s_up, s_down)))
+            for k, (src, dst) in enumerate(zip(ins[2:6], (w_up, w_down, s_up, s_down)))
         ]
         loads += [
             pltpu.make_async_copy(inc_in.at[pl.ds(k * rows, rows)], inc.at[k], sems.at[13 + k])
@@ -697,7 +787,6 @@
         next(arriving)
         for load in loads:
             load.start()
-        next(arriving)
         next(arriving)
         for load in loads:
             load.wait()
@@ -756,12 +845,7 @@
                     acc[place, :, columns] = total[k * rows : (k + 1) * rows].astype(BF)
 
             grads = extra[...]
-            high = grads.astype(BF).astype(F32)
-            turn = (
-                iota((128, 128), 0) + n * experts == iota((128, 128), 1)
-            ).astype(F32)
-            rest = exact(grads - high, turn, ((1,), (0,)))
-            both_parts = (high + rest).astype(BF)
+            both_parts = sides(grads)
             for k, (slot, place) in enumerate(zip(slots, places_in_acc)):
                 part = pl.ds(k * rows, rows)
                 acc[place, :, depth:] = both_parts[k * rows : (k + 1) * rows]
@@ -781,7 +865,7 @@
         store = pltpu.make_async_copy(gh, gh_out, sems.at[12])
         store.start()
         stores.append(store)
-        summing = reduce_steps("expert", None, dx_out, *reduce_scratch)
+        summing = reduce_steps("expert", None, dx, *reduce_scratch)
         next(summing)
         for half in range(2):
             next(summing)
@@ -799,6 +883,33 @@
         store.start()
         stores.append(store)
         yield from summing
+        gain_grad[...] = jnp.zeros_like(gain_grad)
+        router_grad[...] = jnp.zeros_like(router_grad)
+
+        @chunks(rows)
+        def _(at_rows):
+            v, inv = after[at_rows, :], factors[at_rows, 1:2]
+            low = x_all[me, at_rows, :depth]
+            table = joined(x_all[me, at_rows, depth:].astype(F32))
+            spread = joined(dx[at_rows, depth:])
+            logit = table * (spread - jnp.sum(table * spread, axis=1, keepdims=True))
+            logit_low = logit.astype(BF)
+            router_grad[...] += mm_tn(logit_low, low)[:16]
+            g = dx[at_rows, :depth] + mm_nt(logit_low, router[...])
+            gg = g * gain[...]
+            gain_grad[...] += jnp.sum(g * v * inv, axis=0, keepdims=True)
+            mean = jnp.mean(gg * v, axis=1, keepdims=True)
+            total = own[at_rows, :].astype(F32) + inv * gg - v * (inv * inv * inv * mean)
+            after_grad[at_rows, :] = total
+            total_low = total.astype(BF)
+            payload[at_rows, :depth] = total_low
+            s = jnp.sum(total_low.astype(F32) * mixed[at_rows, :], axis=1, keepdims=True)
+            r = factors[at_rows, 0:1]
+            r_high, s_high = r.astype(BF).astype(F32), s.astype(BF).astype(F32)
+            extras = jnp.where(lane == 0, r_high, jnp.where(lane == 1, r - r_high, 0.0))
+            extras = jnp.where(lane == 2, s_high, jnp.where(lane == 3, s - s_high, extras))
+            payload[at_rows, depth:] = extras.astype(BF)
+
         for store in stores:
             store.wait()
 
@@ -1002,6 +1113,7 @@
     ext,
     d_ext,
     d_state,
+    out_sum,
     w,
     w_sem,
 ):
@@ -1013,7 +1125,7 @@
 
     @pl.when(step == 0)
     def _():
-        for ref in (d_ext, d_state, d_out, d_taps, d_heads, d_lanes):
+        for ref in (d_ext, d_state, out_sum, d_taps, d_heads, d_lanes):
             ref[...] = jnp.zeros_like(ref)
         load_weights(w_pieces, w, w_sem)
 
@@ -1035,7 +1147,7 @@
         yr = out * act * r
         gg = gated_grad[rows]
         d_lanes[0:1, :] += jnp.sum(gg * yr, axis=0, keepdims=True)
-        d_out[...] += mm_tn((yr * gain).astype(BF), grad[0, rows, :D])
+        out_sum[...] += mm_tn((yr * gain).astype(BF), grad[0, rows, :D])
         dy = r * (gg * gain) - yr * (r * s / DI)
         d_gate = dy * out * (sig + act * (1.0 - sig))
         do = dy * act
@@ -1112,6 +1224,8 @@
         d_proj[0, rows, :di] = d_gate.astype(BF)
         d_proj[0, rows, di : di + width] = d_seq.astype(BF)
         d_proj[0, rows, di + width :] = jnp.where(head_lane < heads, d_raw, 0.0).astype(BF)
+    for half in range(2):
+        d_out[half] = out_sum[:, half * D // 2 : (half + 1) * D // 2].astype(BF)
     normed_part[0] = mm_nt(d_proj[0], w[...].reshape(D, -1)).astype(BF)
 
 
@@ -1171,7 +1285,7 @@
         jax.ShapeDtypeStruct((nb, rows, D), BF),
     ]
     sums = [
-        jax.ShapeDtypeStruct((di, w_out.shape[1]), F32),
+        jax.ShapeDtypeStruct((2, di, D // 2), BF),
         jax.ShapeDtypeStruct((8, width), F32),
         jax.ShapeDtypeStruct((8, S), F32),
         jax.ShapeDtypeStruct((8, di), F32),
@@ -1191,6 +1305,7 @@
             pltpu.VMEM((MB, rows // MB + EDGE, width), F32),
             pltpu.VMEM((MB, rows // MB + EDGE, width), F32),
             pltpu.VMEM((MB, di, S), F32),
+            pltpu.VMEM((di, D), F32),
         ]
         + weight_scratch(w),
         compiler_params=pltpu.CompilerParams(vmem_limit_bytes=VMEM_LIMIT),
@@ -1258,8 +1373,7 @@
     stream = tokens.reshape(rows_t, D).astype(F32)
     incoming = cotangent.reshape(rows_t, D)
     route_rows = routes.reshape(rows_t, TOP)
-    normed_wide, norm_pull = jax.vjp(rms_scale, stream, norm_gain)
-    normed = normed_wide.astype(BF)
+    normed = rms_scale(stream, norm_gain).astype(BF)
     (_, w_in), (normed_all,) = run_tasks(
         [Weights(blocks), Gather("dp", jnp.concatenate([normed, packed], axis=1))], 1, "begin"
     )
@@ -1289,46 +1403,44 @@
     payload, proj, scan, states = mixer_forward(
         lengths[:, 0], normed_all, w_in, output_weight, *vectors, heads
     )
-    column = lax.broadcasted_iota(jnp.int32, (1, D + 128), 1)
-    summed = run_tasks([Reduce("dp", payload)], 2, "reduce_mixer")[0][0]
-    r = lax.rsqrt((summed[:, D : D + 1] + summed[:, D + 1 : D + 2]) / DI + EPSILON)
-    mixed = summed[:, :D] * r
-    after_mixer = stream + mixed
-    moe_wide, moe_pull = jax.vjp(rms_scale, after_mixer, moe_gain)
-    moe_in = moe_wide.astype(BF)
-    logits = mm(moe_in, router_full)
-    chosen = (route_rows[:, :, None] == jnp.arange(experts, dtype=jnp.int32)).astype(F32)
-    picked = jnp.sum(chosen * logits[:, None, :], axis=2)
-    gates = jax.nn.softmax(picked, axis=1)
-    table = jnp.sum(chosen * gates[:, :, None], axis=1)
-    t_hi, t_lo = hi_lo(table)
-    moe_payload = jnp.concatenate(
-        [moe_in, t_hi, t_lo, jnp.zeros((rows_t, 128 - 2 * experts), BF)], axis=1
-    )
-    (moe_all, back_sum, pre_grad, gh, out_part), = run_tasks(
-        [Experts(moe_payload, inc_all, expert_gate_up, expert_down, sg_full, sd_full)], 3, "experts"
+    mask = jnp.sum(
+        (route_rows[:, :, None] == jnp.arange(128, dtype=jnp.int32)).astype(F32), axis=1
+    )
+    router_wide = jnp.pad(router_full, ((0, 0), (0, 128 - experts)))
+    gain_row = moe_gain.reshape(1, D)
+    ((moe_payload, after_mixer, mixed, factors),) = run_tasks(
+        [MixerOut(payload, tokens.reshape(rows_t, D), gain_row, router_wide, mask)],
+        2,
+        "reduce_mixer",
+    )
+    ((moe_all, pre_grad, gh, out_part, after_grad, grad_payload, moe_gain_grad, router_part),) = (
+        run_tasks(
+            [
+                Experts(
+                    moe_payload,
+                    inc_all,
+                    expert_gate_up,
+                    expert_down,
+                    sg_full,
+                    sd_full,
+                    after_mixer,
+                    mixed,
+                    factors,
+                    gain_row,
+                    router_wide,
+                    incoming,
+                )
+            ],
+            3,
+            "experts",
+        )
     )
     width = gh.shape[2]
-    inc = incoming.astype(F32)
-    spread_sum = back_sum[:, D : D + experts] + back_sum[:, D + experts : D + 2 * experts]
-    logit_grad = table * (spread_sum - jnp.sum(table * spread_sum, axis=1, keepdims=True))
-    logit_low = logit_grad.astype(BF)
-    router_part = mm_tn(moe_in, logit_low)
-    moe_in_grad = back_sum[:, :D] + mm_nt(logit_low, router_full)
-    after_from_norm, moe_gain_grad = moe_pull(moe_in_grad)
-    after_grad = inc + after_from_norm
-    after_low = after_grad.astype(BF)
-    s = jnp.sum(after_low.astype(F32) * mixed, axis=1, keepdims=True)
-    r_hi, r_lo = hi_lo(r)
-    d_hi, d_lo = hi_lo(s)
-    grad_payload = jnp.concatenate(
-        [after_low, r_hi, r_lo, d_hi, d_lo, jnp.zeros((rows_t, 124), BF)], axis=1
-    )
-    (grad_all,), (out_sum,), (grad_blocks,) = run_tasks(
+    (out_sum,), (grad_blocks,), (grad_all,) = run_tasks(
         [
-            Gather("dp", grad_payload),
             Reduce("expert", out_part),
             ExpertGrads(moe_all, pre_grad, gh, inc_all, el, FE, nd),
+            Gather("dp", grad_payload),
         ],
         5,
         "gather_grad",
@@ -1358,21 +1470,19 @@
     added_rows = -(-added_size // (nd * 1024)) * 8
     own_rows = -(-sum(part.size for part in own) // 128)
     norm_rows = D // 128
-    (normed_grad,), (d_sum,), (added_in,) = run_tasks(
+    (tokens_grad, norm_gain_grad), (d_sum,), (added_in,) = run_tasks(
         [
-            Reduce("dp", normed_part),
+            StreamGrad(normed_part, tokens.reshape(rows_t, D), norm_gain.reshape(1, D), after_grad),
             InputGrad(
                 normed_all,
                 d_proj.reshape(nd * rows_t, wcols),
-                output_part.astype(BF),
+                output_part,
             ),
             Direct("all", "dp", rows_of(added, nd * added_rows).reshape(nd, added_rows, 128)),
         ],
         6,
         "reduce_grads",
     )
-    stream_from_norm, norm_gain_grad = norm_pull(normed_grad)
-    tokens_grad = after_grad + stream_from_norm
     small = jnp.concatenate(
         [jnp.sum(added_in, axis=0), rows_of(own, own_rows), rows_of((norm_gain_grad,), norm_rows)],
         axis=0,
@@ -1382,17 +1492,18 @@
         [up_sum[:, 2 * el * FE :], last_sum[:fsl, span:].reshape(dr, -1)], axis=1
     ).reshape(-1, wcols)
     main_rows = D // ne
-    (input_grad,), (rest_all,), (small_all,) = run_tasks(
+    (small_all,), (rest_all,), (input_grad,) = run_tasks(
         [
+            Small(small),
+            Gather("expert", jnp.concatenate([d_sum[main_rows:], shared_part], axis=0)),
             InputRows(d_sum[:main_rows], heads),
-            Gather("expert", jnp.concatenate([d_sum[main_rows:], shared_part], axis=0)),
-            Small(small),
         ],
         7,
         "finish",
     )
     cut_rows = d_sum.shape[0] - main_rows
-    output_grad = rest_all[:, :cut_rows].reshape(output_weight.shape)
+    output_grad = rest_all[:, :cut_rows].reshape(2, di, D // 2)
+    output_grad = jnp.moveaxis(output_grad, 0, 1).reshape(output_weight.shape)
     shared_all = rest_all[:, cut_rows:].reshape(ne, dr, -1)
     added_all = small_all[:, :added_rows].reshape(-1)
     own_all = small_all[:, added_rows : added_rows + own_rows].reshape(nd, -1)
@@ -1417,9 +1528,9 @@
         own_skip.reshape(-1),
         norm_gain_grad,
         own_gain.reshape(-1),
-        moe_gain_grad,
-    )
-    router_grad = lax.dynamic_slice_in_dim(router_all, me_d * dr, dr, 0)
+        moe_gain_grad.reshape(D),
+    )
+    router_grad = lax.dynamic_slice_in_dim(router_all, me_d * dr, dr, 1).T
     expert_up_grad = jnp.moveaxis(up_sum[:, : 2 * el * FE].reshape(dr, el, 2 * FE), 1, 0)
     expert_up_grad = expert_up_grad.astype(F32)
     expert_down_grad = jnp.stack(

time: 592 us -> 583 us (0.985)
  other arithmetic: 27.9 us -> 14.8 us
  Pallas kernels: 487 us -> 494 us
    pallas_call x6, Pallas kernels: 382 us -> 389 us  [run_tasks(): pl.pallas_call(kernel, out_shape=out_shapes, in_specs=in_specs, out_specs...]
  transfers between devices with their start and end apart: 2 -> 2, of which waited for: 0 -> 0; matrix products, arithmetic and copies ran while one was open for 6% -> 4% of each run, Pallas kernels for 35% -> 38%
where the time goes in v7:
time: 583 us; the launch traced here: 574 us
  Pallas kernels  494 us (85%)
  local copies, waits for them, and re-layouts  50.3 us (9%)
  between operations  15.1 us (3%)
  other arithmetic  14.8 us (3%)
    pallas_call x6, Pallas kernels, run_tasks(): pl.pallas_call(kernel, out_shape=out_shapes, in_specs=in_specs, out_specs...  389 us
    pallas_call x1, Pallas kernels, mixer_backward(): pl.pallas_call(functools.partial(backward_kernel, heads), grid=(nb,), out...  67.4 us
    pallas_call x1, Pallas kernels, mixer_forward(): pl.pallas_call(functools.partial(forward_kernel, heads), grid=(nb,), out_...  38 us
  transfers between devices with their start and end apart: 2, of which 0 were waited for; matrix products, arithmetic and copies ran while one was open for 4% of the time, Pallas kernels for 38%

profile of v7, /device:TPU:1, one launch (start us, length us, event | category | flops | bytes accessed | tf_op | source)
XLA Modules:
  0.0 574.4 jit_solution(12318702608701548850)
XLA Ops:
  9.8 1.3 copy.63
  15.9 64.2 %begin.1 = (bf16[16,16,768]{2,1,0:T(8,128)(2,1)}, bf16[8,16,16,768]{3,2,1,0:T(8,128)(2,1)}, bf16[16,160,1792]{2,1,0:T(8,128)(2,1)}) custom-call(bf16[16,16,768]{2,1,0:T(8,128)(2,1)} %concatenate.42.refs_0_, bf16[160,1792]{1,0:T(8,128)(2,1)} %fusion.1.refs_1_), custom_call_target="tpu_custom_call" | custom-call | tf_op jit(solution)/shard_map/begin/pallas_call | solution.py:367
  80.3 1.4 slice.158
  81.7 2.0 reshape.209
  86.1 1.2 reshape.212.refs_4_
  91.2 38.0 %mixer_forward.1 = (bf16[16,160,1664]{2,1,0:T(8,128)(2,1)}, f32[16,160,768]{2,1,0:T(8,128)}, f32[16,160,192]{2,1,0:T(8,128)}, f32[16,2,192,128]{3,2,1,0:T(8,128)}) custom-call(s32[2,3]{1,0:T(2,128)} %bitcast.114, bf16[16,160,1792]{2,1,0:T(8,128)(2,1)} %get-tuple-element.52.g.refs_4_, bf16[8,16,16,768]{3,2,1,0:T(8,128)(2,1)} %get-tuple-element.53.w_pieces, ...), custom_call_target="tpu_custom_call" | custom-call | tf_op jit(solution)/shard_map/mixer_forward/pallas_call | solution.py:1259
  130.1 54.6 %reduce_mixer.1 = (bf16[160,1664]{1,0:T(8,128)(2,1)}, f32[160,1536]{1,0:T(8,128)}, f32[160,1536]{1,0:T(8,128)}, f32[160,128]{1,0:T(8,128)}) custom-call(bf16[16,160,1664]{2,1,0:T(8,128)(2,1)} %get-tuple-element.54.refs_0_, bf16[160,1536]{1,0:T(8,128)(2,1)} %bitcast.85, f32[1,1536]{1,0:T(1,128)} %reshape.208.refs_2_.refs_9_, ...), custom_call_target="tpu_custom_call" | custom-call | tf_op jit(solution)/shard_map/reduce_mixer/pallas_call | solution.py:367
  184.7 108.9 %experts.1 = (bf16[8,160,1664]{2,1,0:T(8,128)(2,1)}, bf16[8,160,2304]{2,1,0:T(8,128)(2,1)}, bf16[8,160,1152]{2,1,0:T(8,128)(2,1)}, bf16[8,160,1536]{2,1,0:T(8,12...) custom-call(bf16[160,1664]{1,0:T(8,128)(2,1)} %get-tuple-element.56.refs_0_, ...), custom_call_target="tpu_custom_call" | custom-call | tf_op jit(solution)/shard_map/experts/pallas_call | solution.py:367
  293.6 56.8 %gather_grad.1 = (f32[160,1536]{1,0:T(8,128)}, bf16[16,160,2304]{2,1,0:T(8,128)(2,1)}, bf16[16,160,1664]{2,1,0:T(8,128)(2,1)}) custom-call(bf16[8,160,1536]{2,1,0:T(8,128)(2,1)} %get-tuple-element.60.refs_0_, bf16[8,160,1664]{2,1,0:T(8,128)(2,1)} %get-tuple-element.61.refs_1_, bf16[8,160,2304]{2,1,0:T(8,128)(2,1)} %get-tuple-element.62.refs_2_, ...), custom_call_target="tpu_custom_call" | custom-call | tf_op jit(solution)/shard_map/gather_grad/pallas_call | solution.py:367
  351.0 67.4 %mixer_backward.1 = (bf16[16,160,768]{2,1,0:T(8,128)(2,1)}, bf16[16,160,1536]{2,1,0:T(8,128)(2,1)}, bf16[2,192,768]{2,1,0:T(8,128)(2,1)}, f32[8,448]{1,0:T(8,128)}, f32[8,128]{1,0:T(8,128)}, /*index=5*/f32[8,192]{1,0:T(8,128)}) custom-call(s32[2,3]{1,0:T(2,128)} %bitcast.115, bf16[16,160,1664]{2,1,0:T(8,128)(2,1)} %get-tuple-element.66.grad, ...), custom_call_target="tpu_custom_call" | custom-call | tf_op jit(solution)/shard_map/mixer_backward/pallas_call | solution.py:1293
  422.1 56.2 %reduce_grads.1 = (f32[160,1536]{1,0:T(8,128)}, f32[1,1536]{1,0:T(1,128)}, bf16[240,768]{1,0:T(8,128)(2,1)}, f32[16,16,128]{2,1,0:T(8,128)}) custom-call(bf16[16,160,1536]{2,1,0:T(8,128)(2,1)} %get-tuple-element.70.refs_0_, bf16[160,1536]{1,0:T(8,128)(2,1)} %bitcast.86, f32[1,1536]{1,0:T(1,128)} %broadcast_in_dim.28.refs_2_, ...), custom_call_target="tpu_custom_call" | custom-call | tf_op jit(solution)/shard_map/reduce_grads/pallas_call | solution.py:367
  479.2 1.7 slice.177.refs_2_
  490.7 47.9 %finish.1 = (f32[16,40,128]{2,1,0:T(8,128)}, bf16[8,96,768]{2,1,0:T(8,128)(2,1)}, f32[96,6448]{1,0:T(8,128)}) custom-call(f32[40,128]{1,0:T(8,128)} %select_maximum_fusion.3.refs_0_, bf16[96,768]{1,0:T(8,128)(2,1)} %pad_maximum_fusion.refs_1_, bf16[192,768]{1,0:T(8,128)(2,1)} %slice.177.refs_2_), custom_call_target="tpu_custom_call" | custom-call | tf_op jit(solution)/shard_map/finish/pallas_call | solution.py:367
  541.2 1.3 fusion.3
  546.1 1.5 slice_reduce_fusion
  548.2 1.2 copy.74
  551.0 2.0 reshape.240
  553.6 1.4 reshape.235
  555.0 1.3 reshape.231
  556.3 1.3 reshape.232
  557.6 1.3 reshape.233
  561.4 1.2 pad_maximum_fusion.4
  563.3 1.4 dynamic-slice_bitcast_fusion
  565.7 1.5 copy.89
  (165 shorter events, 42.4 us)
Async XLA Ops:
  7.2 2.6 copy-start
  7.2 5.8 %copy-start.16 = (bf16[96,16]{0,1:T(8,128)(2,1)S(1)}, bf16[96,16]{0,1:T(8,128)(2,1)}, u32[]{:S(2)}) copy-start(bf16[96,16]{0,1:T(8,128)(2,1)} %param.33) | copy-start | bytes 9220
  7.2 6.2 %copy-start.2 = (bf16[2,1,80,1536]{3,2,1,0:T(8,128)(2,1)S(1)}, bf16[2,1,80,1536]{3,2,1,0:T(8,128)(2,1)}, u32[]{:S(2)}) copy-start(bf16[2,1,80,1536]{3,2,1,0:T(8,128)(2,1)} %param.19) | copy-start | bytes 1474564
  7.2 177.5 %all-gather.2.cloned.1.call-start = ((), (), s32[]{:S(2)}) async-start(), calls=%async_computation.1 | async-start | bytes 4423680 | tf_op jit(solution)/shard_map/all_gather | solution.py:1381
  7.3 6.6 %copy-start.11 = (f32[1536]{0:T(1024)S(1)}, f32[1536]{0:T(1024)}, u32[]{:S(2)}) copy-start(f32[1536]{0:T(1024)} %param.29) | copy-start | bytes 18436
  11.2 3.7 dynamic-slice-start
  80.0 405.9 %reduce-scatter.2.cloned.1.call-start = ((), (), s32[]{:S(2)}) async-start(), calls=%async_computation.2 | async-start | bytes 12533760 | tf_op jit(solution)/shard_map/reduce_scatter | solution.py:1448
  81.7 3.7 copy-start.13
  81.7 4.3 copy-start.14
  83.8 5.3 copy-start.18
  83.8 5.2 copy-start.19
  83.9 5.3 slice-start.2
  83.9 5.4 copy-start.12
  83.9 6.7 %slice-start.1 = ((f32[4,3328]{1,0:T(4,128)}), f32[4,256]{1,0:T(4,128)S(1)}, s32[]{:S(2)}) async-start(f32[4,3328]{1,0:T(4,128)} %param.24), calls=%async_computation.5 | async-start | bytes 8192 | tf_op jit(solution)/shard_map/slice | solution.py:1388
  351.0 70.4 %copy-start.10 = (f32[16,1536]{1,0:T(8,128)S(1)}, f32[16,1536]{1,0:T(8,128)}, u32[]{:S(2)}) copy-start(f32[16,1536]{1,0:T(8,128)} %get-tuple-element.76) | copy-start | bytes 294916
  351.0 70.4 %copy-start.15 = (f32[1,1536]{1,0:T(1,128)S(1)}, f32[1,1536]{1,0:T(1,128)}, u32[]{:S(2)}) copy-start(f32[1,1536]{1,0:T(1,128)} %get-tuple-element.75) | copy-start | bytes 18436
  422.1 63.0 %copy-start.3 = (f32[160,1536]{1,0:T(8,128)S(1)}, f32[160,1536]{1,0:T(8,128)}, u32[]{:S(2)}) copy-start(f32[160,1536]{1,0:T(8,128)} %get-tuple-element.55.refs_6_) | copy-start | bytes 2949124
  422.1 63.0 %copy-start.6 = (f32[160,1536]{1,0:T(8,128)S(1)}, f32[160,1536]{1,0:T(8,128)}, u32[]{:S(2)}) copy-start(f32[160,1536]{1,0:T(8,128)} %get-tuple-element.65) | copy-start | bytes 2949124
  543.6 7.4 %copy-start.9 = (f32[128,256]{1,0:T(8,128)}, f32[128,256]{1,0:T(8,128)S(1)}, u32[]{:S(2)}) copy-start(f32[128,256]{1,0:T(8,128)S(1)} %slice.181) | copy-start | bytes 393220
  549.4 3.5 copy-start.8
  549.5 11.2 %copy-start.7 = (bf16[1,32,1536]{2,1,0:T(8,128)(2,1)S(1)}, bf16[1,32,1536]{2,1,0:T(8,128)(2,1)}, u32[]{:S(2)}) copy-start(bf16[1,32,1536]{2,1,0:T(8,128)(2,1)} %slice_bitcast_fusion.3) | copy-start | bytes 294916
  551.0 11.7 %slice-start = ((f32[128,256]{1,0:T(8,128)}), f32[4,256]{1,0:T(4,128)S(1)}, s32[]{:S(2)}) async-start(f32[128,256]{1,0:T(8,128)} %copy-done.9), calls=%async_computation.3 | async-start | bytes 8192 | tf_op jit(solution)/shard_map/slice | solution.py:1517
  551.0 14.7 %copy-start.4 = (f32[96,6448]{1,0:T(8,128)S(1)}, f32[96,6448]{1,0:T(8,128)}, u32[]{:S(2)}) copy-start(f32[96,6448]{1,0:T(8,128)} %get-tuple-element.176) | copy-start | bytes 7428100
  558.9 5.8 %copy-start.5 = (f32[160,1536]{1,0:T(8,128)S(1)}, f32[160,1536]{1,0:T(8,128)}, u32[]{:S(2)}) copy-start(f32[160,1536]{1,0:T(8,128)} %get-tuple-element.77) | copy-start | bytes 2949124
  (3 other events, 7.0 us)
Sparse Core Ops, SparseCore 0:
  80.2 70.9 all-gather.1
  350.5 76.7 reduce-scatter.1

commit v8 on v7

--- a/solution.py
+++ b/solution.py
@@ -507,49 +507,6 @@
     return jnp.where(iota((1, 128), 1) < 16, v + back, 0.0)
 
 
-class MixerOut(Task):
-    def __init__(self, payload, stream, gain, router, mask):
-        self.reaches = (("dp", False),)
-        self.reduce = Reduce("dp", payload)
-        rows, wide = payload.shape[1:]
-        self.ins = self.reduce.ins + tuple((v, IN_VMEM) for v in (stream, gain, router, mask))
-        shape = jax.ShapeDtypeStruct
-        self.outs = (
-            (shape((rows, wide), BF), IN_VMEM),
-            (shape((rows, D), F32), IN_VMEM),
-            (shape((rows, D), F32), IN_VMEM),
-            (shape((rows, 128), F32), IN_VMEM),
-        )
-        self.scratch = (pltpu.VMEM((rows, wide), F32),) + self.reduce.scratch
-
-    def steps(self, ins, outs, scratch):
-        x, stream, gain, router, mask = ins
-        payload, after, mixed, factors = outs
-        total = scratch[0]
-        yield from reduce_steps("dp", x, total, *scratch[1:])
-
-        @chunks(total.shape[0])
-        def _(rows):
-            squares = total[rows, D:]
-            lane = iota((1, 128), 1)
-            square = jnp.sum(jnp.where(lane < 2, squares, 0.0), axis=1, keepdims=True)
-            r = lax.rsqrt(square / DI + EPSILON)
-            mix = total[rows, :D] * r
-            v = stream[rows, :].astype(F32) + mix
-            inv = lax.rsqrt(jnp.mean(v * v, axis=1, keepdims=True) + EPSILON)
-            low = (v * inv * gain[...]).astype(BF)
-            logits = mm(low, router[...])
-            chosen = mask[rows, :]
-            top = jnp.max(jnp.where(chosen > 0.0, logits, -1e30), axis=1, keepdims=True)
-            e = jnp.where(chosen > 0.0, jnp.exp(jnp.minimum(logits - top, 0.0)), 0.0)
-            table = e / jnp.sum(e, axis=1, keepdims=True)
-            payload[rows, :D] = low
-            payload[rows, D:] = sides(table)
-            after[rows, :] = v
-            mixed[rows, :] = mix
-            factors[rows, :] = jnp.where(lane == 0, r, jnp.where(lane == 1, inv, 0.0))
-
-
 class StreamGrad(Task):
     def __init__(self, parts, stream, gain, after_grad):
         self.reaches = (("dp", False),)
@@ -578,20 +535,20 @@
 
 
 class InputGrad(Task):
-    def __init__(self, g, d_proj, out_grad):
+    def __init__(self, gathered, d_proj, out_grad):
         self.reaches = (("expert", False),)
         n = lax.axis_size("expert")
         wide = d_proj.shape[1]
         rows = (D + out_grad.size // wide) // n
         self.reduce = Reduce("expert", jax.ShapeDtypeStruct((n, rows, wide), BF), BF)
-        self.ins = tuple((v, ANY) for v in (g, d_proj, out_grad.reshape(n, -1, wide)))
+        self.ins = tuple((v, ANY) for v in (*gathered, d_proj, out_grad.reshape(n, -1, wide)))
         self.outs = self.reduce.outs
         dma = pltpu.SemaphoreType.DMA
         self.scratch = (
-            pltpu.VMEM(g.shape[:2] + (D,), BF),
+            pltpu.VMEM((gathered[0].shape[0], MB * gathered[0].shape[1], D), BF),
             pltpu.VMEM(d_proj.shape, BF),
             pltpu.VMEM((n, rows, wide), BF),
-            dma((3,)),
+            dma((4,)),
         ) + self.reduce.scratch
 
     def steps(self, ins, outs, scratch):
@@ -600,9 +557,15 @@
         each = D // n
         below = pl.ds(each, total.shape[1] - each)
         loads = (
-            pltpu.make_async_copy(ins[0].at[:, :, pl.ds(0, D)], g, sems.at[0]),
-            pltpu.make_async_copy(ins[1], d_proj, sems.at[1]),
-            pltpu.make_async_copy(ins[2], total.at[:, below], sems.at[2]),
+            pltpu.make_async_copy(ins[2], d_proj, sems.at[0]),
+            pltpu.make_async_copy(ins[3], total.at[:, below], sems.at[1]),
+        ) + tuple(
+            pltpu.make_async_copy(
+                ins[m].at[:, :, pl.ds(0, D)],
+                g.at[:, pl.ds(m * ins[m].shape[1], ins[m].shape[1])],
+                sems.at[2 + m],
+            )
+            for m in range(MB)
         )
         for load in loads:
             load.start()
@@ -721,7 +684,10 @@
 
 
 class Experts(Task):
-    def __init__(self, x, inc, w_up, w_down, s_up, s_down, after, mixed, factors, gain, router, own):
+    def __init__(
+        self, low, mask, inc, w_up, w_down, s_up, s_down, after, mixed, factors, gain, router, own
+    ):
+        x = jax.ShapeDtypeStruct((low.shape[0], low.shape[1] + 128), BF)
         self.reaches = (("expert", False),)
         self.gather = Gather("expert", x)
         n = lax.axis_size("expert")
@@ -734,8 +700,8 @@
         hidden = experts * both // 2 + s_down.shape[0]
         pre = jax.ShapeDtypeStruct((n, rows, 2 * hidden), BF)
         gh = jax.ShapeDtypeStruct((n, rows, hidden), BF)
-        self.ins = tuple((v, ANY) for v in (x, inc, w_up, w_down, s_up, s_down)) + tuple(
-            (v, IN_VMEM) for v in (after, mixed, factors, gain, router, own)
+        self.ins = tuple((v, ANY) for v in (inc, w_up, w_down, s_up, s_down)) + tuple(
+            (v, IN_VMEM) for v in (low, mask, after, mixed, factors, gain, router, own)
         )
         part = jax.ShapeDtypeStruct((n, rows, depth), BF)
         shape = jax.ShapeDtypeStruct
@@ -757,17 +723,18 @@
             + (pltpu.VMEM((2 * rows, 2 * hidden), BF), pltpu.VMEM((2 * rows, hidden), BF))
             + (pltpu.VMEM(pre.shape, BF), pltpu.VMEM(gh.shape, BF))
             + (pltpu.VMEM((2 * rows, 128), F32), dma((22,)), pltpu.VMEM(part.shape, BF))
-            + (pltpu.VMEM((rows, wide), F32),)
+            + (pltpu.VMEM((rows, wide), F32), pltpu.VMEM((rows, wide), BF))
             + self.gather.scratch
             + self.reduce.scratch
         )
 
     def steps(self, ins, outs, scratch):
-        x, inc_in = ins[:2]
-        after, mixed, factors, gain, router, own = ins[6:]
+        inc_in = ins[0]
+        low_in, mask, after, mixed, factors, gain, router, own = ins[5:]
         x_all, pre_out, gh_out, part_out, after_grad, payload, gain_grad, router_grad = outs
         inc, w_up, w_down, s_up, s_down, xs, incs, pg, ghs, pre, gh, extra, sems = scratch[:13]
-        part, dx, gather_scratch, reduce_scratch = scratch[13], scratch[14], scratch[15:18], scratch[18:]
+        part, dx, gather_scratch, reduce_scratch = scratch[13], scratch[14], scratch[16:19], scratch[19:]
+        x = scratch[15]
         acc = reduce_scratch[0]
         me, at = places("expert")
         n, rows, depth = inc.shape
@@ -777,16 +744,24 @@
         tile = min(256, each)
         loads = [
             pltpu.make_async_copy(src, dst, sems.at[k])
-            for k, (src, dst) in enumerate(zip(ins[2:6], (w_up, w_down, s_up, s_down)))
+            for k, (src, dst) in enumerate(zip(ins[1:5], (w_up, w_down, s_up, s_down)))
         ]
         loads += [
             pltpu.make_async_copy(inc_in.at[pl.ds(k * rows, rows)], inc.at[k], sems.at[13 + k])
             for k in range(n)
         ]
+        for load in loads:
+            load.start()
+
+        logits = mm(low_in[...], router[...])
+        chosen = mask[...]
+        top = jnp.max(jnp.where(chosen > 0.0, logits, -1e30), axis=1, keepdims=True)
+        e = jnp.where(chosen > 0.0, jnp.exp(jnp.minimum(logits - top, 0.0)), 0.0)
+        table = e / jnp.sum(e, axis=1, keepdims=True)
+        x[:, :depth] = low_in[...]
+        x[:, depth:] = sides(table)
         arriving = gather_steps("expert", x, x_all, *gather_scratch)
         next(arriving)
-        for load in loads:
-            load.start()
         next(arriving)
         for load in loads:
             load.wait()
@@ -884,18 +859,16 @@
         stores.append(store)
         yield from summing
         gain_grad[...] = jnp.zeros_like(gain_grad)
-        router_grad[...] = jnp.zeros_like(router_grad)
+        spread = joined(dx[:, depth:])
+        logit = table * (spread - jnp.sum(table * spread, axis=1, keepdims=True))
+        logit_low = logit.astype(BF)
+        router_grad[...] = mm_tn(logit_low, low_in[...])[:16]
+        dx[:, :depth] += mm_nt(logit_low, router[...])
 
         @chunks(rows)
         def _(at_rows):
             v, inv = after[at_rows, :], factors[at_rows, 1:2]
-            low = x_all[me, at_rows, :depth]
-            table = joined(x_all[me, at_rows, depth:].astype(F32))
-            spread = joined(dx[at_rows, depth:])
-            logit = table * (spread - jnp.sum(table * spread, axis=1, keepdims=True))
-            logit_low = logit.astype(BF)
-            router_grad[...] += mm_tn(logit_low, low)[:16]
-            g = dx[at_rows, :depth] + mm_nt(logit_low, router[...])
+            g = dx[at_rows, :depth]
             gg = g * gain[...]
             gain_grad[...] += jnp.sum(g * v * inv, axis=0, keepdims=True)
             mean = jnp.mean(gg * v, axis=1, keepdims=True)
@@ -948,7 +921,7 @@
 
 
 class Block:
-    def __init__(self, m, start, proj, ext, lengths, taps, heads_vec, heads):
+    def __init__(self, m, slot, start, proj, ext, lengths, taps, heads_vec, heads):
         loc = proj.shape[0]
         di = heads * PS
         width = di + 2 * S
@@ -968,12 +941,12 @@
         self.keep_last = (last_doc == before_doc).astype(F32)
         self.same_last = (docs == last_doc).astype(F32)
         self.gate = proj[:, :di]
-        ext[m, EDGE : EDGE + loc, :] = proj[:, di : di + width].astype(BF).astype(F32)
+        ext[slot, EDGE : EDGE + loc, :] = proj[:, di : di + width].astype(BF).astype(F32)
         total = jnp.broadcast_to(taps[K : K + 1, :], (loc, width))
         self.shifted = []
         for k in range(K):
             back = K - 1 - k
-            value = ext[m, EDGE - back : EDGE - back + loc, :]
+            value = ext[slot, EDGE - back : EDGE - back + loc, :]
             if back:
                 value = value * (docs == doc(self.at - back)).astype(F32)
             self.shifted.append(value)
@@ -1041,54 +1014,197 @@
         copy.wait()
 
 
-def forward_kernel(
-    heads,
-    lengths,
-    g,
-    w_pieces,
-    w_out,
-    taps,
-    heads_vec,
-    lanes_vec,
-    payload,
-    proj,
-    scan,
-    states,
-    ext,
-    state,
-    w,
-    w_sem,
-):
-    b = pl.program_id(0)
-    loc = g.shape[1] // MB
-    di = heads * PS
-
-    @pl.when(b == 0)
-    def _():
-        ext[...] = jnp.zeros_like(ext)
-        state[...] = jnp.zeros_like(state)
-        load_weights(w_pieces, w, w_sem)
-
-    proj[0] = mm(g[0, :, :D], w[...].reshape(D, -1))
-    column = iota((loc, payload.shape[2] - D), 1)
-    for m in range(MB):
-        rows = slice(m * loc, (m + 1) * loc)
-        ext[m, 0:EDGE, :] = ext[m, loc : loc + EDGE, :]
-        part = Block(m, b * loc, proj[0, rows, :], ext, lengths, taps, heads_vec, heads)
-        before = state[m]
-        states[0, m] = before
-        scaled = part.scaled.astype(BF)
-        inner = part.per_head([mm(part.mixing[h].astype(BF), scaled) for h in range(heads)])
-        carried = mm_nt(part.read, before.astype(BF)) * part.grow_wide
-        out = inner + carried + lanes_vec[1:2, :] * part.x
-        scan[0, rows, :] = out
-        state[m] = part.decay_rows() * before + mm_tn(part.pushed.astype(BF), part.write)
-        y = out * (part.gate * jax.nn.sigmoid(part.gate))
-        square = jnp.sum(y * y, axis=1, keepdims=True)
-        high = square.astype(BF).astype(F32)
-        payload[0, rows, :D] = mm((y * lanes_vec[0:1, :]).astype(BF), w_out[...]).astype(BF)
-        sums = jnp.where(column == 0, high, jnp.where(column == 1, square - high, 0.0))
-        payload[0, rows, D:] = sums.astype(BF)
+class Forward(Task):
+    def __init__(self, blocks, x, incoming, lengths, w_out, vectors, stream, gain, heads):
+        self.heads = heads
+        self.reaches = (("dp", True), ("expert", False))
+        nd = lax.axis_size("dp")
+        loc = stream.shape[0] // MB
+        di = heads * PS
+        wide = blocks.shape[2]
+        shape = jax.ShapeDtypeStruct
+        self.weights = Weights(blocks)
+        self.gathers = [Gather("dp", v) for v in x] + [Gather("expert", incoming)]
+        part = shape((nd, loc, D + 128), BF)
+        self.reduces = [Reduce("dp", part) for _ in range(MB)]
+        self.saved = (
+            shape((MB, nd, loc, wide), F32),
+            shape((MB, nd, loc, di), F32),
+            shape((MB, nd, di, S), F32),
+        )
+        self.ins = (
+            ((blocks, ANY),)
+            + tuple((v, ANY) for v in (*x, incoming))
+            + ((lengths, pl.BlockSpec(memory_space=pltpu.SMEM)),)
+            + tuple((v, IN_VMEM) for v in (w_out,) + tuple(vectors) + (stream, gain))
+        )
+        full = self.weights.outs[1][0]
+        rows = stream.shape[0]
+        self.outs = (
+            ((full, ANY),)
+            + tuple((gather.outs[0][0], ANY) for gather in self.gathers)
+            + tuple((v, ANY) for v in self.saved)
+            + (
+                (shape((rows, D), BF), IN_VMEM),
+                (shape((rows, D), F32), IN_VMEM),
+                (shape((rows, D), F32), IN_VMEM),
+                (shape((rows, 128), F32), IN_VMEM),
+            )
+        )
+        vmem = lambda v: pltpu.VMEM(v.shape, v.dtype)
+        dma = pltpu.SemaphoreType.DMA
+        slices = D // nd // full.shape[2]
+        self.scratch = (
+            (vmem(self.weights.outs[0][0]), vmem(full))
+            + tuple(vmem(gather.outs[0][0]) for gather in self.gathers[:MB])
+            + tuple(vmem(v) for v in self.saved)
+            + tuple(vmem(part) for _ in range(MB))
+            + tuple(pltpu.VMEM((loc, D + 128), F32) for _ in range(MB))
+            + (pltpu.VMEM((nd, slices, full.shape[2], wide), BF), dma((slices,)), dma((9,)))
+            + (pltpu.VMEM((2, loc + EDGE, di + 2 * S), F32), pltpu.VMEM((di, S), F32))
+            + (pltpu.VMEM((4, loc, di), BF),)
+            + self.weights.scratch
+            + self.gathers[0].scratch
+            + self.gathers[1].scratch
+            + self.gathers[2].scratch
+            + self.reduces[0].scratch
+            + self.reduces[1].scratch
+        )
+
+    def steps(self, ins, outs, scratch):
+        x, incoming, lengths = ins[1:3], ins[3], ins[4]
+        w_out, taps, heads_vec, lanes_vec, stream, gain = ins[5:]
+        w_full, g_out, inc_out, saved_out = outs[0], outs[1:3], outs[3], outs[4:7]
+        low_out, after, mixed, factors = outs[7:]
+        swapped, pieces_all = scratch[:2]
+        g, (proj, scan, states), parts, totals = scratch[2:4], scratch[4:7], scratch[7:9], scratch[9:11]
+        w, w_sem, sems, ext, state, gated = scratch[11:17]
+        rest = scratch[17:]
+        rest, weight_sems = rest[6:], rest[:6]
+        gather_sems, rest = (rest[:3], rest[3:6], rest[6:9]), rest[9:]
+        count = len(self.reduces[0].scratch)
+        reduce_scratch = (rest[:count], rest[count:])
+        heads = self.heads
+        nd, loc, _ = g[0].shape
+        di = heads * PS
+        stores = []
+
+        def store(src, dst):
+            copy = pltpu.make_async_copy(src, dst, sems.at[len(stores)])
+            copy.start()
+            stores.append(copy)
+
+        def work(m, start, end):
+            many = end - start
+            rows = g[m][start:end, :, :D].reshape(many * loc, D)
+            value = mm(rows, w[...].reshape(D, -1))
+            proj[m, start:end] = value.reshape(many, loc, value.shape[1])
+
+            @pl.loop(start // 2, end // 2)
+            def _(pair):
+                for k in range(2):
+                    b = pair * 2 + k
+                    ext[k, 0:EDGE, :] = ext[1 - k, loc : loc + EDGE, :]
+                    part = Block(
+                        m, k, b * loc, proj[m, b], ext, lengths, taps, heads_vec, heads
+                    )
+                    before = state[...]
+                    states[m, b] = before
+                    scaled = part.scaled.astype(BF)
+                    inner = part.per_head(
+                        [mm(part.mixing[h].astype(BF), scaled) for h in range(heads)]
+                    )
+                    carried = mm_nt(part.read, before.astype(BF)) * part.grow_wide
+                    out = inner + carried + lanes_vec[1:2, :] * part.x
+                    scan[m, b] = out
+                    state[...] = part.decay_rows() * before + mm_tn(
+                        part.pushed.astype(BF), part.write
+                    )
+                    y = out * (part.gate * jax.nn.sigmoid(part.gate))
+                    square = jnp.sum(y * y, axis=1, keepdims=True)
+                    high = square.astype(BF).astype(F32)
+                    gated[b - start] = (y * lanes_vec[0:1, :]).astype(BF)
+                    column = iota((loc, 128), 1)
+                    sums = jnp.where(column == 0, high, jnp.where(column == 1, square - high, 0.0))
+                    parts[m][b, :, D:] = sums.astype(BF)
+
+            value = mm(gated[...].reshape(many * loc, di), w_out[...])
+            parts[m][start:end, :, :D] = value.astype(BF).reshape(many, loc, D)
+
+        def reset():
+            ext[...] = jnp.zeros_like(ext)
+            state[...] = jnp.zeros_like(state)
+
+        def norm(m):
+            @chunks(loc, 16)
+            def _(rows):
+                at_rows = pl.ds(pl.multiple_of(m * loc + rows.start, 16), rows.size)
+                lane = iota((1, 128), 1)
+                total = totals[m]
+                squares = total[rows, D:]
+                square = jnp.sum(jnp.where(lane < 2, squares, 0.0), axis=1, keepdims=True)
+                r = lax.rsqrt(square / DI + EPSILON)
+                mix = total[rows, :D] * r
+                v = stream[at_rows, :].astype(F32) + mix
+                inv = lax.rsqrt(jnp.mean(v * v, axis=1, keepdims=True) + EPSILON)
+                low_out[at_rows, :] = (v * inv * gain[...]).astype(BF)
+                after[at_rows, :] = v
+                mixed[at_rows, :] = mix
+                factors[at_rows, :] = jnp.where(lane == 0, r, jnp.where(lane == 1, inv, 0.0))
+
+        weights = self.weights.steps(ins[:1], (swapped, pieces_all), weight_sems)
+        first = gather_steps("dp", x[0], g[0], *gather_sems[0])
+        second = gather_steps("dp", x[1], g[1], *gather_sems[1])
+        third = gather_steps("expert", incoming, inc_out, *gather_sems[2])
+        next(weights)
+        next(first)
+        next(weights)
+        next(weights, None)
+        next(first)
+        next(weights, None)
+        next(first)
+        next(second)
+        next(weights, None)
+        next(first)
+        for _ in weights:
+            pass
+        for _ in first:
+            pass
+        load_weights(pieces_all, w, w_sem)
+        store(pieces_all, w_full)
+        store(g[0], g_out[0])
+        reset()
+        for k in range(4):
+            next(third, None)
+            work(0, 4 * k, 4 * k + 4)
+            next(second, None)
+        for steps in (second, third):
+            for _ in steps:
+                pass
+        store(g[1], g_out[1])
+        sums = [
+            reduce_steps("dp", parts[m], totals[m], *reduce_scratch[m]) for m in range(MB)
+        ]
+        next(sums[0])
+        for src, dst in zip((proj, scan, states), saved_out):
+            store(src.at[0], dst.at[0])
+        reset()
+        for k in range(4):
+            next(sums[0])
+            work(1, 4 * k, 4 * k + 4)
+        next(sums[1])
+        for src, dst in zip((proj, scan, states), saved_out):
+            store(src.at[1], dst.at[1])
+        for _ in sums[0]:
+            pass
+        next(sums[1])
+        norm(0)
+        for _ in sums[1]:
+            pass
+        norm(1)
+        for copy in stores:
+            copy.wait()
+        yield
 
 
 def backward_kernel(
@@ -1135,13 +1251,13 @@
     pick = (iota((di, S), 0) // PS == iota((di, S), 1)).astype(F32)
     for m in range(MB):
         rows = slice(m * loc, (m + 1) * loc)
-        edge = proj_before[0, (m + 1) * loc - EDGE : (m + 1) * loc, di : di + width]
+        edge = proj_before[m, 0, loc - EDGE : loc, di : di + width]
         ext[m, 0:EDGE, :] = edge.astype(BF).astype(F32) * has_before
-        part = Block(m, b * loc, proj[0, rows, :], ext, lengths, taps, heads_vec, heads)
+        part = Block(m, m, b * loc, proj[m, 0], ext, lengths, taps, heads_vec, heads)
         gain, skip = lanes_vec[0:1, :], lanes_vec[1:2, :]
         r = extra[rows, 0:1] + extra[rows, 1:2]
         s = extra[rows, 2:3] + extra[rows, 3:4]
-        out = scan[0, rows, :]
+        out = scan[m, 0]
         sig = jax.nn.sigmoid(part.gate)
         act = part.gate * sig
         yr = out * act * r
@@ -1155,7 +1271,7 @@
         x = part.x
         d_lanes[1:2, :] += jnp.sum(do * x, axis=0, keepdims=True)
         dx = skip * do
-        before = states[0, m]
+        before = states[m, 0]
         before_low = before.astype(BF)
         ds = d_state[m]
         ds_low = ds.astype(BF)
@@ -1241,37 +1357,12 @@
     return pl.BlockSpec((1,) + shape[1:], lambda i: (index(i),) + (0,) * (len(shape) - 1))
 
 
+def pair_spec(shape, index):
+    return pl.BlockSpec((MB, 1) + shape[2:], lambda i: (0, index(i)) + (0,) * (len(shape) - 2))
+
+
 def whole_spec(shape):
     return pl.BlockSpec(shape, lambda i: (0,) * len(shape))
-
-
-def mixer_forward(lengths, g, w, w_out, taps, heads_vec, lanes_vec, heads):
-    nb, rows, _ = g.shape
-    di = heads * PS
-    width = di + 2 * S
-    shapes = [
-        jax.ShapeDtypeStruct((nb, rows, D + 128), BF),
-        jax.ShapeDtypeStruct((nb, rows, w.shape[-1]), F32),
-        jax.ShapeDtypeStruct((nb, rows, di), F32),
-        jax.ShapeDtypeStruct((nb, MB, di, S), F32),
-    ]
-    same = lambda i: i
-    return pl.pallas_call(
-        functools.partial(forward_kernel, heads),
-        grid=(nb,),
-        out_shape=shapes,
-        in_specs=[pl.BlockSpec(memory_space=pltpu.SMEM), block_spec(g.shape, same)]
-        + [pl.BlockSpec(memory_space=pl.ANY)]
-        + [whole_spec(v.shape) for v in (w_out, taps, heads_vec, lanes_vec)],
-        out_specs=[block_spec(v.shape, same) for v in shapes],
-        scratch_shapes=[
-            pltpu.VMEM((MB, rows // MB + EDGE, width), F32),
-            pltpu.VMEM((MB, di, S), F32),
-        ]
-        + weight_scratch(w),
-        compiler_params=pltpu.CompilerParams(vmem_limit_bytes=VMEM_LIMIT),
-        name="mixer_forward",
-    )(lengths, g, w, w_out, taps, heads_vec, lanes_vec)
 
 
 def mixer_backward(lengths, grad, w, w_out, taps, heads_vec, lanes_vec, proj, scan, states, heads):
@@ -1297,8 +1388,8 @@
         in_specs=[pl.BlockSpec(memory_space=pltpu.SMEM), block_spec(grad.shape, back)]
         + [pl.BlockSpec(memory_space=pl.ANY)]
         + [whole_spec(v.shape) for v in (w_out, taps, heads_vec, lanes_vec)]
-        + [block_spec(proj.shape, back), block_spec(proj.shape, before)]
-        + [block_spec(scan.shape, back), block_spec(states.shape, back)],
+        + [pair_spec(proj.shape, back), pair_spec(proj.shape, before)]
+        + [pair_spec(scan.shape, back), pair_spec(states.shape, back)],
         out_specs=[block_spec(v.shape, back) for v in per_block]
         + [whole_spec(v.shape) for v in sums],
         scratch_shapes=[
@@ -1367,23 +1458,13 @@
     sg = lax.dynamic_index_in_dim(sg, me_e, 3, False).reshape(dr, 2 * fs)
     sd = lax.dynamic_slice_in_dim(shared_down, me_e * fsl, fsl, 0)
     packed = jnp.concatenate([sg.reshape(-1), sd.reshape(-1), router_weight.reshape(-1)])
-    packed_cols = packed.size // rows_t
-    packed = jnp.pad(packed.reshape(rows_t, -1), ((0, 0), (0, 256 - packed_cols)))
+    packed_cols = packed.size // loc
+    packed = jnp.pad(packed.reshape(loc, -1), ((0, 0), (0, -packed_cols % 128)))
 
     stream = tokens.reshape(rows_t, D).astype(F32)
     incoming = cotangent.reshape(rows_t, D)
     route_rows = routes.reshape(rows_t, TOP)
     normed = rms_scale(stream, norm_gain).astype(BF)
-    (_, w_in), (normed_all,) = run_tasks(
-        [Weights(blocks), Gather("dp", jnp.concatenate([normed, packed], axis=1))], 1, "begin"
-    )
-    early, _ = lax.optimization_barrier((incoming, normed_all))
-    inc_all = lax.all_gather(early, "expert", axis=0, tiled=True)
-    packed_all = normed_all[:, :, D:].reshape(nd, rows_t, 256)[:, :, : packed_cols]
-    packed_all = packed_all.reshape(nd, -1)
-    sg_full = packed_all[:, : sg.size].reshape(D, 2 * fs)
-    sd_full = packed_all[:, sg.size : sg.size + sd.size].reshape(fs, D)
-    router_full = packed_all[:, sg.size + sd.size :].reshape(D, experts)
     taps = jnp.concatenate(
         [lax.dynamic_slice_in_dim(filter_weight, me_d * di, di, 1), filter_weight[:, DI:]], axis=1
     )
@@ -1400,24 +1481,37 @@
         jnp.stack([my_gain, jnp.repeat(my_heads(skip_gain), PS)]), ((0, 6), (0, 0))
     )
     vectors = (taps_vec, heads_vec, lanes_vec)
-    payload, proj, scan, states = mixer_forward(
-        lengths[:, 0], normed_all, w_in, output_weight, *vectors, heads
+    gain_row = moe_gain.reshape(1, D)
+    own_tokens = tokens.reshape(rows_t, D)
+    forward = Forward(
+        blocks,
+        (normed[:loc], jnp.concatenate([normed[loc:], packed], axis=1)),
+        incoming,
+        lengths[:, 0],
+        output_weight,
+        vectors,
+        own_tokens,
+        gain_row,
+        heads,
     )
+    (results,) = run_tasks([forward], 1, "forward")
+    w_in, *gathered, inc_all, proj, scan, states, moe_in, after_mixer, mixed, factors = results
+    inc_all = inc_all.reshape(ne * rows_t, D)
+    packed_all = gathered[1][:, :, D : D + packed_cols]
+    packed_all = packed_all.reshape(nd, -1)
+    sg_full = packed_all[:, : sg.size].reshape(D, 2 * fs)
+    sd_full = packed_all[:, sg.size : sg.size + sd.size].reshape(fs, D)
+    router_full = packed_all[:, sg.size + sd.size :].reshape(D, experts)
     mask = jnp.sum(
         (route_rows[:, :, None] == jnp.arange(128, dtype=jnp.int32)).astype(F32), axis=1
     )
     router_wide = jnp.pad(router_full, ((0, 0), (0, 128 - experts)))
-    gain_row = moe_gain.reshape(1, D)
-    ((moe_payload, after_mixer, mixed, factors),) = run_tasks(
-        [MixerOut(payload, tokens.reshape(rows_t, D), gain_row, router_wide, mask)],
-        2,
-        "reduce_mixer",
-    )
     ((moe_all, pre_grad, gh, out_part, after_grad, grad_payload, moe_gain_grad, router_part),) = (
         run_tasks(
             [
                 Experts(
-                    moe_payload,
+                    moe_in,
+                    mask,
                     inc_all,
                     expert_gate_up,
                     expert_down,
@@ -1472,9 +1566,9 @@
     norm_rows = D // 128
     (tokens_grad, norm_gain_grad), (d_sum,), (added_in,) = run_tasks(
         [
-            StreamGrad(normed_part, tokens.reshape(rows_t, D), norm_gain.reshape(1, D), after_grad),
+            StreamGrad(normed_part, own_tokens, norm_gain.reshape(1, D), after_grad),
             InputGrad(
-                normed_all,
+                gathered,
                 d_proj.reshape(nd * rows_t, wcols),
                 output_part,
             ),

time: 583 us -> 571 us (0.979)
  Pallas kernels: 494 us -> 477 us
  local copies, waits for them, and re-layouts: 50.3 us -> 57.1 us
    pallas_call x1 -> x0, Pallas kernels: 38 us -> none  [mixer_forward(): pl.pallas_call(functools.partial(forward_kernel, heads), grid=(nb,), out_...]
    pallas_call x6 -> x5, Pallas kernels: 389 us -> 409 us  [run_tasks(): pl.pallas_call(kernel, out_shape=out_shapes, in_specs=in_specs, out_specs...]
  transfers between devices with their start and end apart: 2 -> 1, of which waited for: 0 -> 0; matrix products, arithmetic and copies ran while one was open for 4% -> 2% of each run, Pallas kernels for 38% -> 22%
where the time goes in v8:
time: 571 us; the launch traced here: 563 us
  Pallas kernels  477 us (84%)
  local copies, waits for them, and re-layouts  57.1 us (10%)
  other arithmetic  14.7 us (3%)
  between operations  14.7 us (3%)
    pallas_call x5, Pallas kernels, run_tasks(): pl.pallas_call(kernel, out_shape=out_shapes, in_specs=in_specs, out_specs...  409 us
    pallas_call x1, Pallas kernels, mixer_backward(): pl.pallas_call(functools.partial(backward_kernel, heads), grid=(nb,), out...  67.4 us
  transfers between devices with their start and end apart: 1, of which 0 were waited for; matrix products, arithmetic and copies ran while one was open for 2% of the time, Pallas kernels for 22%

profile of v8, /device:TPU:1, one launch (start us, length us, event | category | flops | bytes accessed | tf_op | source)
XLA Modules:
  0.0 563.2 jit_solution(15573302859056404733)
XLA Ops:
  12.3 1.3 copy.63
  13.6 1.1 copy.64
  22.4 143.8 %forward.1 = (bf16[8,16,16,768]{3,2,1,0:T(8,128)(2,1)}, bf16[16,80,1536]{2,1,0:T(8,128)(2,1)}, bf16[16,80,2048]{2,1,0:T(8,128)(2,1)}, bf16[8,160,1536]{2,1,0:T(8...) custom-call(bf16[16,16,768]{2,1,0:T(8,128)(2,1)} %concatenate.42.ref, ...), custom_call_target="tpu_custom_call" | custom-call | tf_op jit(solution)/shard_map/forward/pallas_call | solution.py:367
  166.2 1.4 slice.164
  167.6 2.0 reshape.213
  169.8 1.2 reshape.214.refs_3_
  174.0 98.3 %experts.1 = (bf16[8,160,1664]{2,1,0:T(8,128)(2,1)}, bf16[8,160,2304]{2,1,0:T(8,128)(2,1)}, bf16[8,160,1152]{2,1,0:T(8,128)(2,1)}, bf16[8,160,1536]{2,1,0:T(8,12...) custom-call(bf16[1280,1536]{1,0:T(8,128)(2,1)} %bitcast.86, ...), custom_call_target="tpu_custom_call" | custom-call | tf_op jit(solution)/shard_map/experts/pallas_call | solution.py:367
  272.2 62.3 %gather_grad.1 = (f32[160,1536]{1,0:T(8,128)}, bf16[16,160,2304]{2,1,0:T(8,128)(2,1)}, bf16[16,160,1664]{2,1,0:T(8,128)(2,1)}) custom-call(bf16[8,160,1536]{2,1,0:T(8,128)(2,1)} %get-tuple-element.58.refs_0_, bf16[8,160,1664]{2,1,0:T(8,128)(2,1)} %get-tuple-element.59.refs_1_, bf16[8,160,2304]{2,1,0:T(8,128)(2,1)} %get-tuple-element.60.refs_2_, ...), custom_call_target="tpu_custom_call" | custom-call | tf_op jit(solution)/shard_map/gather_grad/pallas_call | solution.py:367
  335.2 67.4 %mixer_backward.1 = (bf16[16,160,768]{2,1,0:T(8,128)(2,1)}, bf16[16,160,1536]{2,1,0:T(8,128)(2,1)}, bf16[2,192,768]{2,1,0:T(8,128)(2,1)}, f32[8,448]{1,0:T(8,128)}, f32[8,128]{1,0:T(8,128)}, /*index=5*/f32[8,192]{1,0:T(8,128)}) custom-call(s32[2,3]{1,0:T(2,128)} %bitcast.118, bf16[16,160,1664]{2,1,0:T(8,128)(2,1)} %get-tuple-element.64.grad, ...), custom_call_target="tpu_custom_call" | custom-call | tf_op jit(solution)/shard_map/mixer_backward/pallas_call | solution.py:1384
  406.3 56.0 %reduce_grads.1 = (f32[160,1536]{1,0:T(8,128)}, f32[1,1536]{1,0:T(1,128)}, bf16[240,768]{1,0:T(8,128)(2,1)}, f32[16,16,128]{2,1,0:T(8,128)}) custom-call(bf16[16,160,1536]{2,1,0:T(8,128)(2,1)} %get-tuple-element.69.refs_0_, bf16[160,1536]{1,0:T(8,128)(2,1)} %bitcast.89, f32[1,1536]{1,0:T(1,128)} %broadcast_in_dim.28.refs_2_, ...), custom_call_target="tpu_custom_call" | custom-call | tf_op jit(solution)/shard_map/reduce_grads/pallas_call | solution.py:367
  463.2 1.7 slice.183.refs_2_
  474.7 48.9 %finish.1 = (f32[16,40,128]{2,1,0:T(8,128)}, bf16[8,96,768]{2,1,0:T(8,128)(2,1)}, f32[96,6448]{1,0:T(8,128)}) custom-call(f32[40,128]{1,0:T(8,128)} %select_maximum_fusion.3.refs_0_, bf16[96,768]{1,0:T(8,128)(2,1)} %pad_maximum_fusion.refs_1_, bf16[192,768]{1,0:T(8,128)(2,1)} %slice.183.refs_2_), custom_call_target="tpu_custom_call" | custom-call | tf_op jit(solution)/shard_map/finish/pallas_call | solution.py:367
  526.8 1.3 fusion.3
  532.3 1.5 slice_reduce_fusion
  534.4 1.2 copy.74
  535.7 1.2 copy.77
  540.1 1.8 reshape.243
  542.6 1.4 reshape.238
  544.0 1.3 reshape.234
  545.3 1.3 reshape.235
  546.6 1.3 reshape.236
  550.5 1.3 pad_maximum_fusion.4
  552.4 1.4 dynamic-slice_bitcast_fusion
  554.7 1.5 copy.89
  (155 shorter events, 46.7 us)
Async XLA Ops:
  7.2 5.0 copy-start
  7.2 8.3 %copy-start.15 = (bf16[96,16]{0,1:T(8,128)(2,1)S(1)}, bf16[96,16]{0,1:T(8,128)(2,1)}, u32[]{:S(2)}) copy-start(bf16[96,16]{0,1:T(8,128)(2,1)} %param.33) | copy-start | bytes 9220
  7.2 8.7 %copy-start.2 = (bf16[2,1,80,1536]{3,2,1,0:T(8,128)(2,1)S(1)}, bf16[2,1,80,1536]{3,2,1,0:T(8,128)(2,1)}, u32[]{:S(2)}) copy-start(bf16[2,1,80,1536]{3,2,1,0:T(8,128)(2,1)} %param.19) | copy-start | bytes 1474564
  7.2 9.0 %copy-start.11 = (f32[1536]{0:T(1024)S(1)}, f32[1536]{0:T(1024)}, u32[]{:S(2)}) copy-start(f32[1536]{0:T(1024)} %param.29) | copy-start | bytes 18436
  7.2 462.7 %reduce-scatter.2.cloned.1.call-start = ((), (), s32[]{:S(2)}) async-start(), calls=%async_computation.1 | async-start | bytes 12533760 | tf_op jit(solution)/shard_map/reduce_scatter | solution.py:1542
  9.9 7.2 %copy-start.12 = (f32[1536]{0:T(1024)S(1)}, f32[1536]{0:T(1024)}, u32[]{:S(2)}) copy-start(f32[1536]{0:T(1024)} %param.32) | copy-start | bytes 18436
  11.1 6.7 %slice-start.2 = ((f32[3328]{0:T(1024)}), f32[256]{0:T(256)S(1)}, s32[]{:S(2)}) async-start(f32[3328]{0:T(1024)} %param.25), calls=%async_computation.5 | async-start | bytes 2048 | tf_op jit(solution)/shard_map/slice | solution.py:1472
  13.6 6.6 %copy-start.16 = (f32[48]{0:T(128)S(1)}, f32[48]{0:T(128)}, u32[]{:S(2)}) copy-start(f32[48]{0:T(128)} %param.27) | copy-start | bytes 580
  13.6 6.5 %copy-start.17 = (f32[48]{0:T(128)S(1)}, f32[48]{0:T(128)}, u32[]{:S(2)}) copy-start(f32[48]{0:T(128)} %param.26) | copy-start | bytes 580
  13.6 7.2 %slice-start.1 = ((f32[4,3328]{1,0:T(4,128)}), f32[4,256]{1,0:T(4,128)S(1)}, s32[]{:S(2)}) async-start(f32[4,3328]{1,0:T(4,128)} %param.24), calls=%async_computation.4 | async-start | bytes 8192 | tf_op jit(solution)/shard_map/slice | solution.py:1469
  13.6 7.9 %dynamic-slice-start = ((bf16[96,6448]{1,0:T(8,128)(2,1)}, s32[]{:T(128)}, s32[]{:T(128)}), bf16[16,256]{1,0:T(8,128)(2,1)S(1)}, s32[]{:S(2)}) async-start(bf16[96,6448]{1,0:T(8,128)(2,1)} %param.23, s32[]{:T(128)} %select_n.25, s32[]{:T(128)} %add.71), calls=%async_computation.3 | async-start | bytes 16896 | tf_op jit(solution)/shard_map/slice | solution.py:1449
  169.6 3.4 copy-start.13
  335.2 70.4 %copy-start.9 = (f32[16,1536]{1,0:T(8,128)S(1)}, f32[16,1536]{1,0:T(8,128)}, u32[]{:S(2)}) copy-start(f32[16,1536]{1,0:T(8,128)} %get-tuple-element.76) | copy-start | bytes 294916
  335.2 70.4 %copy-start.14 = (f32[1,1536]{1,0:T(1,128)S(1)}, f32[1,1536]{1,0:T(1,128)}, u32[]{:S(2)}) copy-start(f32[1,1536]{1,0:T(1,128)} %get-tuple-element.75) | copy-start | bytes 18436
  406.2 62.8 %copy-start.3 = (f32[160,1536]{1,0:T(8,128)S(1)}, f32[160,1536]{1,0:T(8,128)}, u32[]{:S(2)}) copy-start(f32[160,1536]{1,0:T(8,128)} %get-tuple-element.52.refs_7_) | copy-start | bytes 2949124
  406.3 62.8 %copy-start.6 = (f32[160,1536]{1,0:T(8,128)S(1)}, f32[160,1536]{1,0:T(8,128)}, u32[]{:S(2)}) copy-start(f32[160,1536]{1,0:T(8,128)} %get-tuple-element.63) | copy-start | bytes 2949124
  534.4 7.5 %copy-start.8 = (f32[24576]{0:T(1024)S(1)}, f32[24576]{0:T(1024)}, u32[]{:S(2)}) copy-start(f32[24576]{0:T(1024)} %slice.226) | copy-start | bytes 294916
  535.7 14.0 %copy-start.7 = (bf16[1,32,1536]{2,1,0:T(8,128)(2,1)S(1)}, bf16[1,32,1536]{2,1,0:T(8,128)(2,1)}, u32[]{:S(2)}) copy-start(bf16[1,32,1536]{2,1,0:T(8,128)(2,1)} %slice_bitcast_fusion.3) | copy-start | bytes 294916
  536.9 17.8 %copy-start.4 = (f32[96,6448]{1,0:T(8,128)S(1)}, f32[96,6448]{1,0:T(8,128)}, u32[]{:S(2)}) copy-start(f32[96,6448]{1,0:T(8,128)} %get-tuple-element.178) | copy-start | bytes 7428100
  539.2 11.3 %copy-start.10 = (f32[3072]{0:T(1024)S(1)}, f32[3072]{0:T(1024)}, u32[]{:S(2)}) copy-start(f32[3072]{0:T(1024)} %reshape.232) | copy-start | bytes 36868
  539.2 12.5 %slice-start = ((f32[128,256]{1,0:T(8,128)}), f32[4,256]{1,0:T(4,128)S(1)}, s32[]{:S(2)}) async-start(f32[128,256]{1,0:T(8,128)} %slice.187), calls=%async_computation.2 | async-start | bytes 8192 | tf_op jit(solution)/shard_map/slice | solution.py:1611
  547.9 5.9 %copy-start.5 = (f32[160,1536]{1,0:T(8,128)S(1)}, f32[160,1536]{1,0:T(8,128)}, u32[]{:S(2)}) copy-start(f32[160,1536]{1,0:T(8,128)} %get-tuple-element.77) | copy-start | bytes 2949124
  553.7 2.4 copy-start.1
Sparse Core Ops, SparseCore 0:
  334.7 77.0 reduce-scatter.1

commit v9 on v8

--- a/solution.py
+++ b/solution.py
@@ -221,7 +221,7 @@
     me, at = places(axis)
     cores = axis == "dp"
     rows = acc.shape[1]
-    step = 16
+    widest = lambda count: max(k for k in range(16, 129, 16) if count % k == 0)
     block = lambda k: x.at[k] if len(x.shape) == 3 else x.at[pl.ds(pl.multiple_of(k * rows, 16), rows)]
     up, down, pair, sib = at(1, 0), at(-1, 0), at(0, 1), at(0, 0, 1)
     whole, first, second, cut = halves(acc.shape[1:])
@@ -229,12 +229,14 @@
     push, arrived = links.push, links.arrived
 
     def add(dst, offset, count, *srcs):
+        step = widest(count)
+
         @pl.loop(0, count // step)
         def _(i):
-            at_rows = pl.ds(pl.multiple_of(offset + i * step, step), step)
+            at_rows = pl.ds(pl.multiple_of(offset + i * step, 16), step)
             total = dst[at_rows, :].astype(F32)
             for src in srcs:
-                total += src[pl.ds(pl.multiple_of(i * step, step), step), :].astype(F32)
+                total += src[pl.ds(pl.multiple_of(i * step, 16), step), :].astype(F32)
             dst[at_rows, :] = total.astype(dst.dtype)
 
     loads = []
@@ -280,10 +282,11 @@
     arrived(15, d_buf.at[1])
     yield
     arrived(16, e_buf)
+    step = widest(rows)
 
     @pl.loop(0, rows // step)
     def _(i):
-        at_rows = pl.ds(pl.multiple_of(i * step, step), step)
+        at_rows = pl.ds(pl.multiple_of(i * step, 16), step)
         total = acc[7, at_rows, :].astype(F32) + c_buf[1, at_rows, :].astype(F32)
         total += d_buf[1, at_rows, :].astype(F32) + e_buf[at_rows, :].astype(F32)
         out[at_rows, :] = total.astype(out.dtype)
@@ -486,11 +489,11 @@
         store.wait()
 
 
-def chunks(rows, step=16):
+def chunks(rows, step=80):
     def over(work):
         @pl.loop(0, rows // step)
         def _(i):
-            work(pl.ds(pl.multiple_of(i * step, step), step))
+            work(pl.ds(pl.multiple_of(i * step, 16), step))
 
     return over
 
@@ -1102,24 +1105,29 @@
 
             @pl.loop(start // 2, end // 2)
             def _(pair):
+                two = []
                 for k in range(2):
                     b = pair * 2 + k
                     ext[k, 0:EDGE, :] = ext[1 - k, loc : loc + EDGE, :]
-                    part = Block(
-                        m, k, b * loc, proj[m, b], ext, lengths, taps, heads_vec, heads
+                    two.append(
+                        Block(m, k, b * loc, proj[m, b], ext, lengths, taps, heads_vec, heads)
                     )
-                    before = state[...]
-                    states[m, b] = before
+                before = [state[...]]
+                for part in two:
+                    before.append(
+                        part.decay_rows() * before[-1] + mm_tn(part.pushed.astype(BF), part.write)
+                    )
+                state[...] = before[2]
+                for k, part in enumerate(two):
+                    b = pair * 2 + k
+                    states[m, b] = before[k]
                     scaled = part.scaled.astype(BF)
                     inner = part.per_head(
                         [mm(part.mixing[h].astype(BF), scaled) for h in range(heads)]
                     )
-                    carried = mm_nt(part.read, before.astype(BF)) * part.grow_wide
+                    carried = mm_nt(part.read, before[k].astype(BF)) * part.grow_wide
                     out = inner + carried + lanes_vec[1:2, :] * part.x
                     scan[m, b] = out
-                    state[...] = part.decay_rows() * before + mm_tn(
-                        part.pushed.astype(BF), part.write
-                    )
                     y = out * (part.gate * jax.nn.sigmoid(part.gate))
                     square = jnp.sum(y * y, axis=1, keepdims=True)
                     high = square.astype(BF).astype(F32)
@@ -1136,7 +1144,7 @@
             state[...] = jnp.zeros_like(state)
 
         def norm(m):
-            @chunks(loc, 16)
+            @chunks(loc)
             def _(rows):
                 at_rows = pl.ds(pl.multiple_of(m * loc + rows.start, 16), rows.size)
                 lane = iota((1, 128), 1)

time: 571 us -> 568 us (level)
  no operation moved by 1% of the time
where the time goes in v9:
time: 568 us; the launch traced here: 560 us
  Pallas kernels  473 us (83%)
  local copies, waits for them, and re-layouts  57.3 us (10%)
  other arithmetic  14.7 us (3%)
  between operations  14.7 us (3%)
    pallas_call x5, Pallas kernels, run_tasks(): pl.pallas_call(kernel, out_shape=out_shapes, in_specs=in_specs, out_specs...  406 us
    pallas_call x1, Pallas kernels, mixer_backward(): pl.pallas_call(functools.partial(backward_kernel, heads), grid=(nb,), out...  67.4 us
  transfers between devices with their start and end apart: 1, of which 0 were waited for; matrix products, arithmetic and copies ran while one was open for 2% of the time, Pallas kernels for 22%

profile of v9, /device:TPU:1, one launch (start us, length us, event | category | flops | bytes accessed | tf_op | source)
XLA Modules:
  0.0 559.8 jit_solution(2022764933201327908)
XLA Ops:
  12.3 1.3 copy.63
  13.6 1.1 copy.64
  22.4 142.5 %forward.1 = (bf16[8,16,16,768]{3,2,1,0:T(8,128)(2,1)}, bf16[16,80,1536]{2,1,0:T(8,128)(2,1)}, bf16[16,80,2048]{2,1,0:T(8,128)(2,1)}, bf16[8,160,1536]{2,1,0:T(8...) custom-call(bf16[16,16,768]{2,1,0:T(8,128)(2,1)} %concatenate.42.ref, ...), custom_call_target="tpu_custom_call" | custom-call | tf_op jit(solution)/shard_map/forward/pallas_call | solution.py:370
  165.0 1.4 slice.164
  166.4 2.2 reshape.213
  168.7 1.2 reshape.214.refs_3_
  173.0 96.4 %experts.1 = (bf16[8,160,1664]{2,1,0:T(8,128)(2,1)}, bf16[8,160,2304]{2,1,0:T(8,128)(2,1)}, bf16[8,160,1152]{2,1,0:T(8,128)(2,1)}, bf16[8,160,1536]{2,1,0:T(8,12...) custom-call(bf16[1280,1536]{1,0:T(8,128)(2,1)} %bitcast.86, ...), custom_call_target="tpu_custom_call" | custom-call | tf_op jit(solution)/shard_map/experts/pallas_call | solution.py:370
  269.4 62.2 %gather_grad.1 = (f32[160,1536]{1,0:T(8,128)}, bf16[16,160,2304]{2,1,0:T(8,128)(2,1)}, bf16[16,160,1664]{2,1,0:T(8,128)(2,1)}) custom-call(bf16[8,160,1536]{2,1,0:T(8,128)(2,1)} %get-tuple-element.58.refs_0_, bf16[8,160,1664]{2,1,0:T(8,128)(2,1)} %get-tuple-element.59.refs_1_, bf16[8,160,2304]{2,1,0:T(8,128)(2,1)} %get-tuple-element.60.refs_2_, ...), custom_call_target="tpu_custom_call" | custom-call | tf_op jit(solution)/shard_map/gather_grad/pallas_call | solution.py:370
  332.2 67.4 %mixer_backward.1 = (bf16[16,160,768]{2,1,0:T(8,128)(2,1)}, bf16[16,160,1536]{2,1,0:T(8,128)(2,1)}, bf16[2,192,768]{2,1,0:T(8,128)(2,1)}, f32[8,448]{1,0:T(8,128)}, f32[8,128]{1,0:T(8,128)}, /*index=5*/f32[8,192]{1,0:T(8,128)}) custom-call(s32[2,3]{1,0:T(2,128)} %bitcast.118, bf16[16,160,1664]{2,1,0:T(8,128)(2,1)} %get-tuple-element.64.grad, ...), custom_call_target="tpu_custom_call" | custom-call | tf_op jit(solution)/shard_map/mixer_backward/pallas_call | solution.py:1392
  403.3 55.8 %reduce_grads.1 = (f32[160,1536]{1,0:T(8,128)}, f32[1,1536]{1,0:T(1,128)}, bf16[240,768]{1,0:T(8,128)(2,1)}, f32[16,16,128]{2,1,0:T(8,128)}) custom-call(bf16[16,160,1536]{2,1,0:T(8,128)(2,1)} %get-tuple-element.69.refs_0_, bf16[160,1536]{1,0:T(8,128)(2,1)} %bitcast.89, f32[1,1536]{1,0:T(1,128)} %broadcast_in_dim.28.refs_2_, ...), custom_call_target="tpu_custom_call" | custom-call | tf_op jit(solution)/shard_map/reduce_grads/pallas_call | solution.py:370
  459.9 1.7 slice.183.refs_2_
  471.5 48.7 %finish.1 = (f32[16,40,128]{2,1,0:T(8,128)}, bf16[8,96,768]{2,1,0:T(8,128)(2,1)}, f32[96,6448]{1,0:T(8,128)}) custom-call(f32[40,128]{1,0:T(8,128)} %select_maximum_fusion.3.refs_0_, bf16[96,768]{1,0:T(8,128)(2,1)} %pad_maximum_fusion.refs_1_, bf16[192,768]{1,0:T(8,128)(2,1)} %slice.183.refs_2_), custom_call_target="tpu_custom_call" | custom-call | tf_op jit(solution)/shard_map/finish/pallas_call | solution.py:370
  523.4 1.3 fusion.3
  528.9 1.5 slice_reduce_fusion
  531.0 1.2 copy.74
  532.3 1.2 copy.77
  536.8 1.8 reshape.243
  539.2 1.4 reshape.238
  540.6 1.3 reshape.234
  541.9 1.3 reshape.235
  543.2 1.3 reshape.236
  547.1 1.3 pad_maximum_fusion.4
  549.0 1.4 dynamic-slice_bitcast_fusion
  551.3 1.5 copy.89
  (155 shorter events, 46.7 us)
Async XLA Ops:
  7.2 5.0 copy-start
  7.2 8.3 %copy-start.15 = (bf16[96,16]{0,1:T(8,128)(2,1)S(1)}, bf16[96,16]{0,1:T(8,128)(2,1)}, u32[]{:S(2)}) copy-start(bf16[96,16]{0,1:T(8,128)(2,1)} %param.33) | copy-start | bytes 9220
  7.2 8.7 %copy-start.2 = (bf16[2,1,80,1536]{3,2,1,0:T(8,128)(2,1)S(1)}, bf16[2,1,80,1536]{3,2,1,0:T(8,128)(2,1)}, u32[]{:S(2)}) copy-start(bf16[2,1,80,1536]{3,2,1,0:T(8,128)(2,1)} %param.19) | copy-start | bytes 1474564
  7.2 9.0 %copy-start.11 = (f32[1536]{0:T(1024)S(1)}, f32[1536]{0:T(1024)}, u32[]{:S(2)}) copy-start(f32[1536]{0:T(1024)} %param.29) | copy-start | bytes 18436
  7.2 459.5 %reduce-scatter.2.cloned.1.call-start = ((), (), s32[]{:S(2)}) async-start(), calls=%async_computation.1 | async-start | bytes 12533760 | tf_op jit(solution)/shard_map/reduce_scatter | solution.py:1550
  9.9 7.2 %copy-start.12 = (f32[1536]{0:T(1024)S(1)}, f32[1536]{0:T(1024)}, u32[]{:S(2)}) copy-start(f32[1536]{0:T(1024)} %param.32) | copy-start | bytes 18436
  11.1 6.7 %slice-start.2 = ((f32[3328]{0:T(1024)}), f32[256]{0:T(256)S(1)}, s32[]{:S(2)}) async-start(f32[3328]{0:T(1024)} %param.25), calls=%async_computation.5 | async-start | bytes 2048 | tf_op jit(solution)/shard_map/slice | solution.py:1480
  13.6 6.6 %copy-start.16 = (f32[48]{0:T(128)S(1)}, f32[48]{0:T(128)}, u32[]{:S(2)}) copy-start(f32[48]{0:T(128)} %param.27) | copy-start | bytes 580
  13.6 6.5 %copy-start.17 = (f32[48]{0:T(128)S(1)}, f32[48]{0:T(128)}, u32[]{:S(2)}) copy-start(f32[48]{0:T(128)} %param.26) | copy-start | bytes 580
  13.6 7.2 %slice-start.1 = ((f32[4,3328]{1,0:T(4,128)}), f32[4,256]{1,0:T(4,128)S(1)}, s32[]{:S(2)}) async-start(f32[4,3328]{1,0:T(4,128)} %param.24), calls=%async_computation.4 | async-start | bytes 8192 | tf_op jit(solution)/shard_map/slice | solution.py:1477
  13.6 7.9 %dynamic-slice-start = ((bf16[96,6448]{1,0:T(8,128)(2,1)}, s32[]{:T(128)}, s32[]{:T(128)}), bf16[16,256]{1,0:T(8,128)(2,1)S(1)}, s32[]{:S(2)}) async-start(bf16[96,6448]{1,0:T(8,128)(2,1)} %param.23, s32[]{:T(128)} %select_n.25, s32[]{:T(128)} %add.71), calls=%async_computation.3 | async-start | bytes 16896 | tf_op jit(solution)/shard_map/slice | solution.py:1457
  168.6 3.4 copy-start.13
  332.2 70.4 %copy-start.9 = (f32[16,1536]{1,0:T(8,128)S(1)}, f32[16,1536]{1,0:T(8,128)}, u32[]{:S(2)}) copy-start(f32[16,1536]{1,0:T(8,128)} %get-tuple-element.76) | copy-start | bytes 294916
  332.2 70.4 %copy-start.14 = (f32[1,1536]{1,0:T(1,128)S(1)}, f32[1,1536]{1,0:T(1,128)}, u32[]{:S(2)}) copy-start(f32[1,1536]{1,0:T(1,128)} %get-tuple-element.75) | copy-start | bytes 18436
  403.3 62.6 %copy-start.3 = (f32[160,1536]{1,0:T(8,128)S(1)}, f32[160,1536]{1,0:T(8,128)}, u32[]{:S(2)}) copy-start(f32[160,1536]{1,0:T(8,128)} %get-tuple-element.52.refs_7_) | copy-start | bytes 2949124
  403.3 62.6 %copy-start.6 = (f32[160,1536]{1,0:T(8,128)S(1)}, f32[160,1536]{1,0:T(8,128)}, u32[]{:S(2)}) copy-start(f32[160,1536]{1,0:T(8,128)} %get-tuple-element.63) | copy-start | bytes 2949124
  531.0 7.5 %copy-start.8 = (f32[24576]{0:T(1024)S(1)}, f32[24576]{0:T(1024)}, u32[]{:S(2)}) copy-start(f32[24576]{0:T(1024)} %slice.226) | copy-start | bytes 294916
  532.3 14.0 %copy-start.7 = (bf16[1,32,1536]{2,1,0:T(8,128)(2,1)S(1)}, bf16[1,32,1536]{2,1,0:T(8,128)(2,1)}, u32[]{:S(2)}) copy-start(bf16[1,32,1536]{2,1,0:T(8,128)(2,1)} %slice_bitcast_fusion.3) | copy-start | bytes 294916
  533.5 17.8 %copy-start.4 = (f32[96,6448]{1,0:T(8,128)S(1)}, f32[96,6448]{1,0:T(8,128)}, u32[]{:S(2)}) copy-start(f32[96,6448]{1,0:T(8,128)} %get-tuple-element.178) | copy-start | bytes 7428100
  535.8 11.3 %copy-start.10 = (f32[3072]{0:T(1024)S(1)}, f32[3072]{0:T(1024)}, u32[]{:S(2)}) copy-start(f32[3072]{0:T(1024)} %reshape.232) | copy-start | bytes 36868
  535.8 12.5 %slice-start = ((f32[128,256]{1,0:T(8,128)}), f32[4,256]{1,0:T(4,128)S(1)}, s32[]{:S(2)}) async-start(f32[128,256]{1,0:T(8,128)} %slice.187), calls=%async_computation.2 | async-start | bytes 8192 | tf_op jit(solution)/shard_map/slice | solution.py:1619
  544.5 5.9 %copy-start.5 = (f32[160,1536]{1,0:T(8,128)S(1)}, f32[160,1536]{1,0:T(8,128)}, u32[]{:S(2)}) copy-start(f32[160,1536]{1,0:T(8,128)} %get-tuple-element.77) | copy-start | bytes 2949124
  550.4 2.4 copy-start.1
Sparse Core Ops, SparseCore 0:
  331.7 77.0 reduce-scatter.1

commit v10 on v9

--- a/solution.py
+++ b/solution.py
@@ -116,7 +116,7 @@
         n = lax.axis_size(axis)
         self.outs = ((jax.ShapeDtypeStruct((n,) + x.shape, x.dtype), ANY),)
         dma = pltpu.SemaphoreType.DMA
-        self.scratch = (dma((17,)), dma((17,)), dma)
+        self.scratch = (dma((19,)), dma((19,)), dma)
 
     def steps(self, ins, outs, scratch):
         return gather_steps(self.axis, ins[0], outs[0], *scratch)
@@ -146,20 +146,26 @@
     yield
     own.wait()
     arrived(2, pair, whole)
-    push(4, pair, whole, up)
-    push(5, pair, whole, down)
+    share = first if cores else whole
+    push(4, pair, share, up)
+    push(5, pair, share, down)
     arrived(0, down, whole)
     push(7, down, first, up)
     arrived(1, up, whole)
     push(8, up, second, down)
     if cores:
+        push(17, down, second, pair)
+        push(18, up, second, pair)
         push(6, pair, whole, sib)
         push(9, down, whole, sib)
         push(10, up, whole, sib)
     yield
-    arrived(4, at(-1, 1), whole)
+    arrived(4, at(-1, 1), share)
     push(11, at(-1, 1), first, up)
-    arrived(5, at(1, 1), whole)
+    arrived(5, at(1, 1), share)
+    if cores:
+        arrived(17, at(-1, 1), second)
+        arrived(18, at(1, 1), second)
     push(12, at(1, 1), second, down)
     arrived(7, at(2, 0), first)
     arrived(8, at(2, 0), second)
@@ -208,8 +214,9 @@
             buf(2, rows),
             buf(2, rows),
             buf(rows),
-            dma((17,)),
-            dma((17,)),
+            buf(2 if dp else 1, rows - cut if dp else 16),
+            dma((19,)),
+            dma((19,)),
             dma((8,)),
         )
 
@@ -217,7 +224,9 @@
         return reduce_steps(self.axis, ins[0], outs[0], *scratch)
 
 
-def reduce_steps(axis, x, out, acc, sib_buf, a_buf, b_buf, c_buf, d_buf, e_buf, send, recv, load):
+def reduce_steps(
+    axis, x, out, acc, sib_buf, a_buf, b_buf, c_buf, d_buf, e_buf, p_buf, send, recv, load
+):
     me, at = places(axis)
     cores = axis == "dp"
     rows = acc.shape[1]
@@ -260,22 +269,54 @@
         push(8 + 2 * k, acc.at[k].at[first], a_buf.at[k], up)
         push(9 + 2 * k, acc.at[k].at[second], b_buf.at[k], down)
     yield
-    for k in range(2):
-        above, below = 2 + 2 * k, 3 + 2 * k
-        ready(above)
-        ready(below)
-        arrived(8 + 2 * k, a_buf.at[k])
-        add(acc.at[above], 0, cut, a_buf.at[k])
-        push(12 + 2 * k, acc.at[above], c_buf.at[k], up)
-        arrived(9 + 2 * k, b_buf.at[k])
-        add(acc.at[below], cut, rows - cut, b_buf.at[k])
-        push(13 + 2 * k, acc.at[below], d_buf.at[k], down)
-    yield
-    ready(6)
-    ready(7)
-    arrived(12, c_buf.at[0])
-    arrived(13, d_buf.at[0])
-    add(acc.at[6], 0, rows, c_buf.at[0], d_buf.at[0])
+    upper, lower = pl.ds(0, cut), pl.ds(0, rows - cut)
+    if cores:
+        ready(2)
+        push(17, acc.at[2].at[second], p_buf.at[0].at[lower], pair)
+        ready(3)
+        push(18, acc.at[3].at[first], p_buf.at[1].at[upper], pair)
+        arrived(8, a_buf.at[0])
+        add(acc.at[2], 0, cut, a_buf.at[0])
+        push(12, acc.at[2].at[first], c_buf.at[0].at[upper], up)
+        arrived(9, b_buf.at[0])
+        add(acc.at[3], cut, rows - cut, b_buf.at[0])
+        push(13, acc.at[3].at[second], d_buf.at[0].at[lower], down)
+        ready(4)
+        ready(5)
+        arrived(10, a_buf.at[1])
+        add(acc.at[4], 0, cut, a_buf.at[1])
+        arrived(17, p_buf.at[0].at[lower])
+        add(acc.at[4], cut, rows - cut, p_buf.at[0])
+        push(14, acc.at[4], c_buf.at[1], up)
+        arrived(11, b_buf.at[1])
+        add(acc.at[5], cut, rows - cut, b_buf.at[1])
+        arrived(18, p_buf.at[1].at[upper])
+        add(acc.at[5], 0, cut, p_buf.at[1])
+        push(15, acc.at[5], d_buf.at[1], down)
+        yield
+        ready(6)
+        ready(7)
+        arrived(12, c_buf.at[0].at[upper])
+        add(acc.at[6], 0, cut, c_buf.at[0])
+        arrived(13, d_buf.at[0].at[lower])
+        add(acc.at[6], cut, rows - cut, d_buf.at[0])
+    else:
+        for k in range(2):
+            above, below = 2 + 2 * k, 3 + 2 * k
+            ready(above)
+            ready(below)
+            arrived(8 + 2 * k, a_buf.at[k])
+            add(acc.at[above], 0, cut, a_buf.at[k])
+            push(12 + 2 * k, acc.at[above], c_buf.at[k], up)
+            arrived(9 + 2 * k, b_buf.at[k])
+            add(acc.at[below], cut, rows - cut, b_buf.at[k])
+            push(13 + 2 * k, acc.at[below], d_buf.at[k], down)
+        yield
+        ready(6)
+        ready(7)
+        arrived(12, c_buf.at[0])
+        arrived(13, d_buf.at[0])
+        add(acc.at[6], 0, rows, c_buf.at[0], d_buf.at[0])
     push(16, acc.at[6], e_buf, pair)
     yield
     arrived(14, c_buf.at[1])
@@ -596,12 +637,11 @@
         row = jax.ShapeDtypeStruct((16, wide), BF)
         self.gather = Gather("expert", row)
         self.ins = ((x, ANY),)
-        self.outs = ((jax.ShapeDtypeStruct((D // nd, IN_W), F32), IN_VMEM),)
+        self.outs = self.gather.outs
         dma = pltpu.SemaphoreType.DMA
         self.scratch = (
             pltpu.VMEM((nd, 16, x.shape[1]), BF),
             pltpu.VMEM((16, wide), BF),
-            pltpu.VMEM((ne, 16, wide), BF),
             dma((2 * ne,)),
             dma((nd,)),
         ) + self.gather.scratch
@@ -617,7 +657,7 @@
 
     def steps(self, ins, outs, scratch):
         x = ins[0]
-        got, row, full, send, recv = scratch[:5]
+        got, row, send, recv = scratch[:4]
         nd, ne = lax.axis_size("dp"), lax.axis_size("expert")
         j, e = lax.axis_index("dp"), lax.axis_index("expert")
         heads, di = self.heads, self.heads * PS
@@ -654,23 +694,67 @@
         steps = [piece(source, 2 * di + 2 * S, 128)[:, :heads] for source in range(nd)]
         steps.append(jnp.zeros((16, 128 - nd * heads), F32))
         row[:, 2 * DI + 2 * S :] = jnp.concatenate(steps, axis=1).astype(BF)
-        yield from gather_steps("expert", row, full, *scratch[5:])
-        for c in range(self.slices):
-            outs[0][c * 16 : (c + 1) * 16, :] = full[c, :, :IN_W].astype(F32)
+        yield from gather_steps("expert", row, outs[0], *scratch[4:])
         for mine, away in sent:
             pl.when(jnp.logical_not(mine))(away.wait_send)
 
 
+class Rest(Task):
+    def __init__(self, d_sum, sums):
+        self.reaches = (("expert", False),)
+        self.top = d_sum.shape[0] - D // lax.axis_size("expert")
+        wide = d_sum.shape[1]
+        x = jax.ShapeDtypeStruct((self.top + 64, wide), BF)
+        self.gather = Gather("expert", x)
+        self.ins = ((d_sum, ANY), (sums, ANY))
+        self.outs = self.gather.outs
+        self.scratch = (
+            pltpu.VMEM(x.shape, BF),
+            pltpu.SemaphoreType.DMA((6,)),
+        ) + self.gather.scratch
+
+    def steps(self, ins, outs, scratch):
+        d_sum, sums = ins
+        x, sems = scratch[:2]
+        top, wide = self.top, x.shape[1]
+        third = wide // 3
+        last = sums.shape[1] - third
+        moves = [(d_sum.at[pl.ds(d_sum.shape[0] - top, top)], x.at[pl.ds(0, top)])]
+        for q in range(3):
+            moves.append(
+                (
+                    sums.at[pl.ds(32 * q, 32), pl.ds(last, third)],
+                    x.at[pl.ds(top, 32), pl.ds(third * q, third)],
+                )
+            )
+        for half in range(2):
+            moves.append(
+                (
+                    sums.at[pl.ds(128, 16), pl.ds(wide * (1 + half), wide)],
+                    x.at[pl.ds(top + 32 + 16 * half, 16)],
+                )
+            )
+        copies = [pltpu.make_async_copy(a, b, sems.at[k]) for k, (a, b) in enumerate(moves)]
+        for copy in copies:
+            copy.start()
+        for copy in copies:
+            copy.wait()
+        yield from gather_steps("expert", x, outs[0], *scratch[2:])
+
+
 class Small(Task):
-    def __init__(self, x):
+    def __init__(self, added, own, row):
         self.reaches = (("expert", True), ("dp", True))
         nd, ne = lax.axis_size("dp"), lax.axis_size("expert")
-        self.ins = ((x, ANY),)
-        self.outs = ((jax.ShapeDtypeStruct((nd,) + x.shape, x.dtype), ANY),)
+        self.ins = ((added, IN_VMEM), (own, IN_VMEM), (row, IN_VMEM))
+        rows = added.shape[1] + own.shape[0] + row.shape[1] // 128
+        shape = (rows + -rows % 8, 128)
+        self.outs = ((jax.ShapeDtypeStruct((nd,) + shape, F32), ANY),)
         dma = pltpu.SemaphoreType.DMA
         self.scratch = (
-            pltpu.VMEM((ne,) + x.shape, x.dtype),
-            pltpu.VMEM(x.shape, x.dtype),
+            pltpu.VMEM(shape, F32),
+            pltpu.VMEM((ne,) + shape, F32),
+            pltpu.VMEM(shape, F32),
             dma((ne,)),
             dma((ne,)),
             dma,
@@ -680,10 +764,67 @@
         )
 
     def steps(self, ins, outs, scratch):
-        parts, total = scratch[:2]
-        yield from direct_steps("gather", "expert", ins[0], parts, *scratch[2:5])
+        added, own, row = ins
+        x, parts, total = scratch[:3]
+        x[...] = jnp.zeros_like(x)
+        first = added.shape[1]
+        second = first + own.shape[0]
+        x[:first, :] = jnp.sum(added[...], axis=0)
+        x[first:second, :] = own[...]
+        for k in range(row.shape[1] // 128):
+            x[second + k : second + k + 1, :] = row[:, k * 128 : (k + 1) * 128]
+        yield from direct_steps("gather", "expert", x, parts, *scratch[3:6])
         total[...] = jnp.sum(parts[...], axis=0)
-        yield from direct_steps("gather", "dp", total, outs[0], *scratch[5:8])
+        yield from direct_steps("gather", "dp", total, outs[0], *scratch[6:9])
+
+
+def results_kernel(full, rest, sums, after, out_sum, *outs):
+    input_grad, output_grad, shared_up, shared_down, up, down, block_output = outs
+    for c in range(input_grad.shape[0] // 16):
+        input_grad[c * 16 : (c + 1) * 16, :] = full[c, :, :IN_W].astype(F32)
+    ne, rows, wide = rest.shape
+    top = rows - 64
+    for half in range(2):
+        value = rest[half * ne // 2 : (half + 1) * ne // 2, :top, :].reshape(-1, wide)
+        output_grad[:, half * wide : (half + 1) * wide] = value.astype(F32)
+
+    each = shared_up.shape[1] // 2
+    fs = each // ne
+    unit = shared_down.shape[0] // ne
+    column = iota((1, each), 1)
+    source = lax.rem(column // unit, ne) * fs + column // (unit * ne) * unit + lax.rem(column, unit)
+    order = (iota((each, each), 0) == source).astype(BF)
+    for half in range(2):
+        groups = []
+        for q in range(3):
+            start = q * 2 * fs + half * fs
+            pieces = [rest[e, top : top + 32, start : start + fs] for e in range(ne)]
+            groups.append(jnp.concatenate(pieces, axis=1))
+        value = mm(jnp.concatenate(groups, axis=0), order)
+        shared_up[:, half * each : (half + 1) * each] = value
+        for e in range(ne):
+            low = top + 32 + 16 * half
+            value = rest[e, low : low + 16, :].astype(F32)[:unit]
+            shared_down[e * unit : (e + 1) * unit, half * wide : (half + 1) * wide] = value
+    experts, dr, both = up.shape
+    for e in range(experts):
+        up[e] = sums[:dr, e * both : (e + 1) * both].astype(F32)
+    below = down.shape[1]
+    down[0] = sums[dr : dr + below, : 2 * wide].astype(F32)
+    down[1, :, :wide] = sums[dr : dr + below, 2 * wide :].astype(F32)
+    down[1, :, wide:] = sums[dr + below :, :wide].astype(F32)
+    block_output[...] = (after[...] + out_sum[...]).astype(BF)
+
+
+def write_results(full, rest, sums, after, out_sum, shapes):
+    return pl.pallas_call(
+        results_kernel,
+        out_shape=[jax.ShapeDtypeStruct(*shape) for shape in shapes],
+        in_specs=[IN_VMEM] * 5,
+        out_specs=[IN_VMEM] * len(shapes),
+        compiler_params=pltpu.CompilerParams(vmem_limit_bytes=VMEM_LIMIT),
+        name="results",
+    )(full, rest, sums, after, out_sum)
 
 
 class Experts(Task):
@@ -1548,10 +1689,6 @@
         "gather_grad",
     )
     all_sum = lax.psum_scatter(grad_blocks, "dp", scatter_dimension=0, tiled=True)[0]
-    up_sum = all_sum[:dr]
-    each, span = FE // nd, D // 2
-    down_sum = all_sum[dr : dr + each]
-    last_sum = all_sum[dr + each :]
     d_proj, normed_part, output_part, d_taps, d_heads, d_lanes = mixer_backward(
         lengths[:, 0], grad_all, w_in, output_weight, *vectors, proj, scan, states, heads
     )
@@ -1585,28 +1722,33 @@
         6,
         "reduce_grads",
     )
-    small = jnp.concatenate(
-        [jnp.sum(added_in, axis=0), rows_of(own, own_rows), rows_of((norm_gain_grad,), norm_rows)],
-        axis=0,
-    )
-    small = jnp.pad(small, ((0, -small.shape[0] % 8), (0, 0)))
-    shared_part = jnp.concatenate(
-        [up_sum[:, 2 * el * FE :], last_sum[:fsl, span:].reshape(dr, -1)], axis=1
-    ).reshape(-1, wcols)
-    main_rows = D // ne
-    (small_all,), (rest_all,), (input_grad,) = run_tasks(
+    (small_all,), (rest_all,), (slices_all,) = run_tasks(
         [
-            Small(small),
-            Gather("expert", jnp.concatenate([d_sum[main_rows:], shared_part], axis=0)),
-            InputRows(d_sum[:main_rows], heads),
+            Small(added_in, rows_of(own, own_rows), norm_gain_grad),
+            Rest(d_sum, all_sum),
+            InputRows(d_sum, heads),
         ],
         7,
         "finish",
     )
-    cut_rows = d_sum.shape[0] - main_rows
-    output_grad = rest_all[:, :cut_rows].reshape(2, di, D // 2)
-    output_grad = jnp.moveaxis(output_grad, 0, 1).reshape(output_weight.shape)
-    shared_all = rest_all[:, cut_rows:].reshape(ne, dr, -1)
+    input_grad, output_grad, shared_up_grad, shared_down_grad, expert_up_grad, expert_down_grad, (
+        block_output
+    ) = write_results(
+        slices_all,
+        rest_all,
+        all_sum,
+        after_mixer,
+        out_sum,
+        (
+            ((dr, IN_W), F32),
+            (output_weight.shape, F32),
+            ((dr, 2 * FS), F32),
+            ((fsr, D), F32),
+            ((el, dr, 2 * FE), F32),
+            ((el, FE // nd, D), F32),
+            ((rows_t, D), BF),
+        ),
+    )
     added_all = small_all[:, :added_rows].reshape(-1)
     own_all = small_all[:, added_rows : added_rows + own_rows].reshape(nd, -1)
     norm_gain_grad = jnp.sum(
@@ -1633,22 +1775,6 @@
         moe_gain_grad.reshape(D),
     )
     router_grad = lax.dynamic_slice_in_dim(router_all, me_d * dr, dr, 1).T
-    expert_up_grad = jnp.moveaxis(up_sum[:, : 2 * el * FE].reshape(dr, el, 2 * FE), 1, 0)
-    expert_up_grad = expert_up_grad.astype(F32)
-    expert_down_grad = jnp.stack(
-        [
-            down_sum[:, : 2 * span],
-            jnp.concatenate([down_sum[:, 2 * span :], last_sum[:, :span]], axis=1),
-        ],
-        axis=0,
-    ).astype(F32)
-    shared_up_grad = (
-        jnp.moveaxis(shared_all[:, :, : 2 * fs].reshape(ne, dr, 2, nd, fsl), 0, 3)
-        .reshape(dr, 2 * FS)
-        .astype(F32)
-    )
-    shared_down_grad = shared_all[:, :, 2 * fs :].reshape(fsr, D).astype(F32)
-    block_output = (after_mixer + out_sum).astype(BF)
     shape = (MB, 1, loc, D)
     return (
         block_output.reshape(shape),

time: 568 us -> 543 us (0.956)
  local copies, waits for them, and re-layouts: 57.3 us -> 31.7 us
  other arithmetic: 14.7 us -> 7.61 us
    slice x10 -> x0, local copies, waits for them, and re-layouts: 7.22 us -> none  [the longest x1 1.69 us: body(): d_sum[:main_rows]]
    pallas_call x0 -> x1, Pallas kernels: none -> 6.45 us  [write_results(): pl.pallas_call(results_kernel, out_shape=[jax.ShapeDtypeStruct(*shape) fo...]
  transfers between devices with their start and end apart: 1 -> 1, of which waited for: 0 -> 0; matrix products, arithmetic and copies ran while one was open for 2% -> 1% of each run, Pallas kernels for 22% -> 24%
where the time goes in v10:
time: 543 us; the launch traced here: 533 us
  Pallas kernels  478 us (88%)
  local copies, waits for them, and re-layouts  31.7 us (6%)
  between operations  14.9 us (3%)
  other arithmetic  7.61 us (1%)
    pallas_call x5, Pallas kernels, run_tasks(): pl.pallas_call(kernel, out_shape=out_shapes, in_specs=in_specs, out_specs...  404 us
    pallas_call x1, Pallas kernels, mixer_backward(): pl.pallas_call(functools.partial(backward_kernel, heads), grid=(nb,), out...  67.6 us
  transfers between devices with their start and end apart: 1, of which 0 were waited for; matrix products, arithmetic and copies ran while one was open for 1% of the time, Pallas kernels for 24%

profile of v10, /device:TPU:1, one launch (start us, length us, event | category | flops | bytes accessed | tf_op | source)
XLA Modules:
  0.0 532.5 jit_solution(588381268729028365)
XLA Ops:
  7.3 0.9 dynamic_slice.35
  8.9 1.0 fusion.2
  12.3 1.3 copy.55
  13.6 1.1 copy.56
  21.5 0.9 concatenate.30.refs_0_
  22.4 141.0 %forward.1 = (bf16[8,16,16,768]{3,2,1,0:T(8,128)(2,1)}, bf16[16,80,1536]{2,1,0:T(8,128)(2,1)}, bf16[16,80,2048]{2,1,0:T(8,128)(2,1)}, bf16[8,160,1536]{2,1,0:T(8...) custom-call(bf16[16,16,768]{2,1,0:T(8,128)(2,1)} %concatenate.30.ref, ...), custom_call_target="tpu_custom_call" | custom-call | tf_op jit(solution)/shard_map/forward/pallas_call | solution.py:411
  163.5 1.4 slice.110
  164.9 2.0 reshape.178
  167.0 1.2 reshape.179.refs_3_
  168.6 0.8 pad.27.refs_11_
  169.4 0.9 reshape.180.refs_4_
  170.4 0.8 convert_reduce_fusion.refs_6_
  171.2 96.7 %experts.1 = (bf16[8,160,1664]{2,1,0:T(8,128)(2,1)}, bf16[8,160,2304]{2,1,0:T(8,128)(2,1)}, bf16[8,160,1152]{2,1,0:T(8,128)(2,1)}, bf16[8,160,1536]{2,1,0:T(8,12...) custom-call(bf16[1280,1536]{1,0:T(8,128)(2,1)} %bitcast.56, ...), custom_call_target="tpu_custom_call" | custom-call | tf_op jit(solution)/shard_map/experts/pallas_call | solution.py:411
  267.9 54.9 %gather_grad.1 = (f32[160,1536]{1,0:T(8,128)}, bf16[16,160,2304]{2,1,0:T(8,128)(2,1)}, bf16[16,160,1664]{2,1,0:T(8,128)(2,1)}) custom-call(bf16[8,160,1536]{2,1,0:T(8,128)(2,1)} %get-tuple-element.65.refs_0_, bf16[8,160,1664]{2,1,0:T(8,128)(2,1)} %get-tuple-element.66.refs_1_, bf16[8,160,2304]{2,1,0:T(8,128)(2,1)} %get-tuple-element.67.refs_2_, ...), custom_call_target="tpu_custom_call" | custom-call | tf_op jit(solution)/shard_map/gather_grad/pallas_call | solution.py:411
  322.9 67.6 %mixer_backward.1 = (bf16[16,160,768]{2,1,0:T(8,128)(2,1)}, bf16[16,160,1536]{2,1,0:T(8,128)(2,1)}, bf16[2,192,768]{2,1,0:T(8,128)(2,1)}, f32[8,448]{1,0:T(8,128)}, f32[8,128]{1,0:T(8,128)}, /*index=5*/f32[8,192]{1,0:T(8,128)}) custom-call(s32[2,3]{1,0:T(2,128)} %bitcast.82, bf16[16,160,1664]{2,1,0:T(8,128)(2,1)} %get-tuple-element.70.grad, ...), custom_call_target="tpu_custom_call" | custom-call | tf_op jit(solution)/shard_map/mixer_backward/pallas_call | solution.py:1533
  393.4 0.8 fusion.6
  394.4 0.8 slice_bitcast_fusion
  395.9 59.6 %reduce_grads.1 = (f32[160,1536]{1,0:T(8,128)}, f32[1,1536]{1,0:T(1,128)}, bf16[240,768]{1,0:T(8,128)(2,1)}, f32[16,16,128]{2,1,0:T(8,128)}) custom-call(bf16[16,160,1536]{2,1,0:T(8,128)(2,1)} %get-tuple-element.75.refs_0_, bf16[160,1536]{1,0:T(8,128)(2,1)} %bitcast.59, f32[1,1536]{1,0:T(1,128)} %broadcast_in_dim.28.refs_2_, ...), custom_call_target="tpu_custom_call" | custom-call | tf_op jit(solution)/shard_map/reduce_grads/pallas_call | solution.py:411
  457.0 51.8 %finish.1 = (f32[16,40,128]{2,1,0:T(8,128)}, bf16[8,112,768]{2,1,0:T(8,128)(2,1)}, bf16[8,16,6528]{2,1,0:T(8,128)(2,1)}) custom-call(f32[16,16,128]{2,1,0:T(8,128)} %get-tuple-element.83.refs_0_, f32[10,128]{1,0:T(8,128)} %pad_bitcast_fusion.refs_1_, f32[1,1536]{1,0:T(1,128)} %get-tuple-element.86.refs_2_, ...), custom_call_target="tpu_custom_call" | custom-call | tf_op jit(solution)/shard_map/finish/pallas_call | solution.py:411
  508.9 0.9 slice.122
  509.8 0.9 slice.124
  511.6 1.5 slice_reduce_fusion
  517.8 6.4 %results.1 = (f32[96,6448]{1,0:T(8,128)}, f32[192,1536]{1,0:T(8,128)}, f32[96,2048]{1,0:T(8,128)}, f32[64,1536]{1,0:T(8,128)}, f32[2,96,1024]{2,1,0:T(8,128)}, /...) custom-call(bf16[8,16,6528]{2,1,0:T(8,128)(2,1)} %get-tuple-element.89.full, ...), custom_call_target="tpu_custom_call" | custom-call | tf_op jit(solution)/shard_map/results/pallas_call | solution.py:820
  524.3 0.9 copy.69
  (110 shorter events, 21.2 us)
Async XLA Ops:
  7.2 5.0 copy-start
  7.2 8.3 %copy-start.9 = (bf16[96,16]{0,1:T(8,128)(2,1)S(1)}, bf16[96,16]{0,1:T(8,128)(2,1)}, u32[]{:S(2)}) copy-start(bf16[96,16]{0,1:T(8,128)(2,1)} %param.33) | copy-start | bytes 9220
  7.2 8.7 %copy-start.2 = (bf16[2,1,80,1536]{3,2,1,0:T(8,128)(2,1)S(1)}, bf16[2,1,80,1536]{3,2,1,0:T(8,128)(2,1)}, u32[]{:S(2)}) copy-start(bf16[2,1,80,1536]{3,2,1,0:T(8,128)(2,1)} %param.19) | copy-start | bytes 1474564
  7.2 9.0 %copy-start.5 = (f32[1536]{0:T(1024)S(1)}, f32[1536]{0:T(1024)}, u32[]{:S(2)}) copy-start(f32[1536]{0:T(1024)} %param.29) | copy-start | bytes 18436
  7.2 449.8 %reduce-scatter.2.cloned.1.call-start = ((), (), s32[]{:S(2)}) async-start(), calls=%async_computation.1 | async-start | bytes 12533760 | tf_op jit(solution)/shard_map/reduce_scatter | solution.py:1691
  9.9 7.2 %copy-start.6 = (f32[1536]{0:T(1024)S(1)}, f32[1536]{0:T(1024)}, u32[]{:S(2)}) copy-start(f32[1536]{0:T(1024)} %param.32) | copy-start | bytes 18436
  11.1 6.7 %slice-start.1 = ((f32[3328]{0:T(1024)}), f32[256]{0:T(256)S(1)}, s32[]{:S(2)}) async-start(f32[3328]{0:T(1024)} %param.25), calls=%async_computation.4 | async-start | bytes 2048 | tf_op jit(solution)/shard_map/slice | solution.py:1621
  13.6 6.6 %copy-start.10 = (f32[48]{0:T(128)S(1)}, f32[48]{0:T(128)}, u32[]{:S(2)}) copy-start(f32[48]{0:T(128)} %param.27) | copy-start | bytes 580
  13.6 6.5 %copy-start.11 = (f32[48]{0:T(128)S(1)}, f32[48]{0:T(128)}, u32[]{:S(2)}) copy-start(f32[48]{0:T(128)} %param.26) | copy-start | bytes 580
  13.6 7.2 %slice-start = ((f32[4,3328]{1,0:T(4,128)}), f32[4,256]{1,0:T(4,128)S(1)}, s32[]{:S(2)}) async-start(f32[4,3328]{1,0:T(4,128)} %param.24), calls=%async_computation.3 | async-start | bytes 8192 | tf_op jit(solution)/shard_map/slice | solution.py:1618
  13.6 7.9 %dynamic-slice-start = ((bf16[96,6448]{1,0:T(8,128)(2,1)}, s32[]{:T(128)}, s32[]{:T(128)}), bf16[16,256]{1,0:T(8,128)(2,1)S(1)}, s32[]{:S(2)}) async-start(bf16[96,6448]{1,0:T(8,128)(2,1)} %param.23, s32[]{:T(128)} %select_n.25, s32[]{:T(128)} %add.64), calls=%async_computation.2 | async-start | bytes 16896 | tf_op jit(solution)/shard_map/slice | solution.py:1598
  166.9 3.4 copy-start.7
  322.9 72.3 %copy-start.4 = (f32[16,1536]{1,0:T(8,128)S(1)}, f32[16,1536]{1,0:T(8,128)}, u32[]{:S(2)}) copy-start(f32[16,1536]{1,0:T(8,128)} %get-tuple-element.82) | copy-start | bytes 294916
  322.9 72.3 %copy-start.8 = (f32[1,1536]{1,0:T(1,128)S(1)}, f32[1,1536]{1,0:T(1,128)}, u32[]{:S(2)}) copy-start(f32[1,1536]{1,0:T(1,128)} %get-tuple-element.81) | copy-start | bytes 18436
  513.3 11.0 %copy-start.3 = (f32[160,1536]{1,0:T(8,128)S(1)}, f32[160,1536]{1,0:T(8,128)}, u32[]{:S(2)}) copy-start(f32[160,1536]{1,0:T(8,128)} %get-tuple-element.93) | copy-start | bytes 2949124
  517.8 7.4 %copy-start.1 = (bf16[64,1536]{1,0:T(8,128)(2,1)S(1)}, bf16[64,1536]{1,0:T(8,128)(2,1)}, u32[]{:S(2)}) copy-start(bf16[64,1536]{1,0:T(8,128)(2,1)} %param.35) | copy-start | bytes 589828
Sparse Core Ops, SparseCore 0:
  323.0 78.8 reduce-scatter.1

commit v11 on v10

--- a/solution.py
+++ b/solution.py
@@ -591,40 +591,59 @@
         self.scratch = (
             pltpu.VMEM((gathered[0].shape[0], MB * gathered[0].shape[1], D), BF),
             pltpu.VMEM(d_proj.shape, BF),
-            pltpu.VMEM((n, rows, wide), BF),
-            dma((4,)),
+            dma((3 + n,)),
         ) + self.reduce.scratch
 
     def steps(self, ins, outs, scratch):
-        g, d_proj, total, sems = scratch[:4]
-        n, _, wide = total.shape
+        g, d_proj, sems = scratch[:3]
+        reduce_scratch = scratch[3:]
+        acc = reduce_scratch[0]
+        me, at = places("expert")
+        n, rows, wide = acc.shape
         each = D // n
-        below = pl.ds(each, total.shape[1] - each)
-        loads = (
-            pltpu.make_async_copy(ins[2], d_proj, sems.at[0]),
-            pltpu.make_async_copy(ins[3], total.at[:, below], sems.at[1]),
-        ) + tuple(
-            pltpu.make_async_copy(
-                ins[m].at[:, :, pl.ds(0, D)],
-                g.at[:, pl.ds(m * ins[m].shape[1], ins[m].shape[1])],
-                sems.at[2 + m],
+        below = pl.ds(each, rows - each)
+        loads = [pltpu.make_async_copy(ins[2], d_proj, sems.at[0])]
+        for m in range(MB):
+            part = pl.ds(m * ins[m].shape[1], ins[m].shape[1])
+            loads.append(
+                pltpu.make_async_copy(
+                    ins[m].at[:, :, pl.ds(0, D)], g.at[:, part], sems.at[1 + m]
+                )
             )
-            for m in range(MB)
-        )
+        for k, (hop, other) in enumerate(ORDER):
+            loads.append(
+                pltpu.make_async_copy(
+                    ins[3].at[at(hop, other)], acc.at[k].at[below], sems.at[3 + k]
+                )
+            )
         for load in loads:
             load.start()
         yield
         for load in loads:
             load.wait()
         flat = g.shape[0] * g.shape[1]
-
-        @pl.loop(0, n // 2)
-        def _(i):
-            columns = pl.ds(pl.multiple_of(i * 2 * each, 2 * each), 2 * each)
+        ring, pair = me // 2, lax.rem(me, 2)
+
+        def compute(hop):
+            place = lax.rem(ring + hop + 4, 4)
+            columns = pl.ds(pl.multiple_of(place * 2 * each, 2 * each), 2 * each)
             value = mm_tn(g[:, :, columns].reshape(flat, 2 * each), d_proj[...]).astype(BF)
-            total[pl.ds(2 * i, 2), :each, :] = value.reshape(2, each, wide)
-
-        yield from reduce_steps("expert", total, outs[0], *scratch[4:])
+            same, across = ORDER.index((hop, 0)), ORDER.index((hop, 1))
+            for side in range(2):
+                slot = same + (across - same) * lax.rem(pair + side, 2)
+                acc[slot, :each, :] = value[side * each : (side + 1) * each]
+
+        summing = reduce_steps("expert", None, outs[0], *reduce_scratch)
+        next(summing)
+        compute(2)
+        next(summing)
+        yield
+        compute(1)
+        compute(-1)
+        next(summing)
+        yield
+        compute(0)
+        yield from summing
 
 
 class InputRows(Task):
@@ -1305,10 +1324,9 @@
         first = gather_steps("dp", x[0], g[0], *gather_sems[0])
         second = gather_steps("dp", x[1], g[1], *gather_sems[1])
         third = gather_steps("expert", incoming, inc_out, *gather_sems[2])
-        next(weights)
+        for _ in range(3):
+            next(weights)
         next(first)
-        next(weights)
-        next(weights, None)
         next(first)
         next(weights, None)
         next(first)

time: 543 us -> 533 us (0.982)
  Pallas kernels: 478 us -> 470 us
    pallas_call x5, Pallas kernels: 404 us -> 396 us  [run_tasks(): pl.pallas_call(kernel, out_shape=out_shapes, in_specs=in_specs, out_specs...]
  transfers between devices with their start and end apart: 1 -> 1, of which waited for: 0 -> 0; matrix products, arithmetic and copies ran while one was open for 1% -> 1% of each run, Pallas kernels for 24% -> 23%
where the time goes in v11:
time: 533 us; the launch traced here: 524 us
  Pallas kernels  470 us (88%)
  local copies, waits for them, and re-layouts  31.7 us (6%)
  between operations  14.7 us (3%)
  other arithmetic  7.61 us (1%)
    pallas_call x5, Pallas kernels, run_tasks(): pl.pallas_call(kernel, out_shape=out_shapes, in_specs=in_specs, out_specs...  396 us
    pallas_call x1, Pallas kernels, mixer_backward(): pl.pallas_call(functools.partial(backward_kernel, heads), grid=(nb,), out...  67.8 us
  transfers between devices with their start and end apart: 1, of which 0 were waited for; matrix products, arithmetic and copies ran while one was open for 1% of the time, Pallas kernels for 23%

profile of v11, /device:TPU:1, one launch (start us, length us, event | category | flops | bytes accessed | tf_op | source)
XLA Modules:
  0.0 524.3 jit_solution(14064969630700801946)
XLA Ops:
  7.3 0.9 dynamic_slice.35
  8.9 1.0 fusion.2
  12.3 1.3 copy.55
  13.6 1.1 copy.56
  21.5 0.9 concatenate.30.refs_0_
  22.4 141.1 %forward.1 = (bf16[8,16,16,768]{3,2,1,0:T(8,128)(2,1)}, bf16[16,80,1536]{2,1,0:T(8,128)(2,1)}, bf16[16,80,2048]{2,1,0:T(8,128)(2,1)}, bf16[8,160,1536]{2,1,0:T(8...) custom-call(bf16[16,16,768]{2,1,0:T(8,128)(2,1)} %concatenate.30.ref, ...), custom_call_target="tpu_custom_call" | custom-call | tf_op jit(solution)/shard_map/forward/pallas_call | solution.py:411
  163.6 1.4 slice.110
  165.0 2.0 reshape.178
  167.1 1.2 reshape.179.refs_3_
  168.6 0.8 pad.27.refs_11_
  169.5 0.9 reshape.180.refs_4_
  170.5 0.8 convert_reduce_fusion.refs_6_
  171.3 97.1 %experts.1 = (bf16[8,160,1664]{2,1,0:T(8,128)(2,1)}, bf16[8,160,2304]{2,1,0:T(8,128)(2,1)}, bf16[8,160,1152]{2,1,0:T(8,128)(2,1)}, bf16[8,160,1536]{2,1,0:T(8,12...) custom-call(bf16[1280,1536]{1,0:T(8,128)(2,1)} %bitcast.56, ...), custom_call_target="tpu_custom_call" | custom-call | tf_op jit(solution)/shard_map/experts/pallas_call | solution.py:411
  268.5 56.7 %gather_grad.1 = (f32[160,1536]{1,0:T(8,128)}, bf16[16,160,2304]{2,1,0:T(8,128)(2,1)}, bf16[16,160,1664]{2,1,0:T(8,128)(2,1)}) custom-call(bf16[8,160,1536]{2,1,0:T(8,128)(2,1)} %get-tuple-element.65.refs_0_, bf16[8,160,1664]{2,1,0:T(8,128)(2,1)} %get-tuple-element.66.refs_1_, bf16[8,160,2304]{2,1,0:T(8,128)(2,1)} %get-tuple-element.67.refs_2_, ...), custom_call_target="tpu_custom_call" | custom-call | tf_op jit(solution)/shard_map/gather_grad/pallas_call | solution.py:411
  325.2 67.8 %mixer_backward.1 = (bf16[16,160,768]{2,1,0:T(8,128)(2,1)}, bf16[16,160,1536]{2,1,0:T(8,128)(2,1)}, bf16[2,192,768]{2,1,0:T(8,128)(2,1)}, f32[8,448]{1,0:T(8,128)}, f32[8,128]{1,0:T(8,128)}, /*index=5*/f32[8,192]{1,0:T(8,128)}) custom-call(s32[2,3]{1,0:T(2,128)} %bitcast.82, bf16[16,160,1664]{2,1,0:T(8,128)(2,1)} %get-tuple-element.70.grad, ...), custom_call_target="tpu_custom_call" | custom-call | tf_op jit(solution)/shard_map/mixer_backward/pallas_call | solution.py:1551
  394.4 0.8 slice.115
  395.8 0.8 fusion.6
  398.3 51.4 %reduce_grads.1 = (f32[160,1536]{1,0:T(8,128)}, f32[1,1536]{1,0:T(1,128)}, bf16[240,768]{1,0:T(8,128)(2,1)}, f32[16,16,128]{2,1,0:T(8,128)}) custom-call(bf16[16,160,1536]{2,1,0:T(8,128)(2,1)} %get-tuple-element.75.refs_0_, bf16[160,1536]{1,0:T(8,128)(2,1)} %bitcast.59, f32[1,1536]{1,0:T(1,128)} %broadcast_in_dim.28.refs_2_, ...), custom_call_target="tpu_custom_call" | custom-call | tf_op jit(solution)/shard_map/reduce_grads/pallas_call | solution.py:411
  451.2 49.7 %finish.1 = (f32[16,40,128]{2,1,0:T(8,128)}, bf16[8,112,768]{2,1,0:T(8,128)(2,1)}, bf16[8,16,6528]{2,1,0:T(8,128)(2,1)}) custom-call(f32[16,16,128]{2,1,0:T(8,128)} %get-tuple-element.83.refs_0_, f32[10,128]{1,0:T(8,128)} %pad_bitcast_fusion.refs_1_, f32[1,1536]{1,0:T(1,128)} %get-tuple-element.86.refs_2_, ...), custom_call_target="tpu_custom_call" | custom-call | tf_op jit(solution)/shard_map/finish/pallas_call | solution.py:411
  500.9 0.9 slice.122
  501.8 0.9 slice.124
  503.6 1.5 slice_reduce_fusion
  509.8 6.4 %results.1 = (f32[96,6448]{1,0:T(8,128)}, f32[192,1536]{1,0:T(8,128)}, f32[96,2048]{1,0:T(8,128)}, f32[64,1536]{1,0:T(8,128)}, f32[2,96,1024]{2,1,0:T(8,128)}, /...) custom-call(bf16[8,16,6528]{2,1,0:T(8,128)(2,1)} %get-tuple-element.89.full, ...), custom_call_target="tpu_custom_call" | custom-call | tf_op jit(solution)/shard_map/results/pallas_call | solution.py:839
  516.3 0.9 copy.69
  (110 shorter events, 21.1 us)
Async XLA Ops:
  7.2 5.0 copy-start
  7.2 8.3 %copy-start.9 = (bf16[96,16]{0,1:T(8,128)(2,1)S(1)}, bf16[96,16]{0,1:T(8,128)(2,1)}, u32[]{:S(2)}) copy-start(bf16[96,16]{0,1:T(8,128)(2,1)} %param.33) | copy-start | bytes 9220
  7.2 8.7 %copy-start.2 = (bf16[2,1,80,1536]{3,2,1,0:T(8,128)(2,1)S(1)}, bf16[2,1,80,1536]{3,2,1,0:T(8,128)(2,1)}, u32[]{:S(2)}) copy-start(bf16[2,1,80,1536]{3,2,1,0:T(8,128)(2,1)} %param.19) | copy-start | bytes 1474564
  7.2 9.0 %copy-start.5 = (f32[1536]{0:T(1024)S(1)}, f32[1536]{0:T(1024)}, u32[]{:S(2)}) copy-start(f32[1536]{0:T(1024)} %param.29) | copy-start | bytes 18436
  7.2 444.0 %reduce-scatter.2.cloned.1.call-start = ((), (), s32[]{:S(2)}) async-start(), calls=%async_computation.1 | async-start | bytes 12533760 | tf_op jit(solution)/shard_map/reduce_scatter | solution.py:1709
  9.9 7.2 %copy-start.6 = (f32[1536]{0:T(1024)S(1)}, f32[1536]{0:T(1024)}, u32[]{:S(2)}) copy-start(f32[1536]{0:T(1024)} %param.32) | copy-start | bytes 18436
  11.1 6.7 %slice-start.1 = ((f32[3328]{0:T(1024)}), f32[256]{0:T(256)S(1)}, s32[]{:S(2)}) async-start(f32[3328]{0:T(1024)} %param.25), calls=%async_computation.4 | async-start | bytes 2048 | tf_op jit(solution)/shard_map/slice | solution.py:1639
  13.6 6.6 %copy-start.10 = (f32[48]{0:T(128)S(1)}, f32[48]{0:T(128)}, u32[]{:S(2)}) copy-start(f32[48]{0:T(128)} %param.27) | copy-start | bytes 580
  13.6 6.5 %copy-start.11 = (f32[48]{0:T(128)S(1)}, f32[48]{0:T(128)}, u32[]{:S(2)}) copy-start(f32[48]{0:T(128)} %param.26) | copy-start | bytes 580
  13.6 7.2 %slice-start = ((f32[4,3328]{1,0:T(4,128)}), f32[4,256]{1,0:T(4,128)S(1)}, s32[]{:S(2)}) async-start(f32[4,3328]{1,0:T(4,128)} %param.24), calls=%async_computation.3 | async-start | bytes 8192 | tf_op jit(solution)/shard_map/slice | solution.py:1636
  13.6 7.9 %dynamic-slice-start = ((bf16[96,6448]{1,0:T(8,128)(2,1)}, s32[]{:T(128)}, s32[]{:T(128)}), bf16[16,256]{1,0:T(8,128)(2,1)S(1)}, s32[]{:S(2)}) async-start(bf16[96,6448]{1,0:T(8,128)(2,1)} %param.23, s32[]{:T(128)} %select_n.25, s32[]{:T(128)} %add.64), calls=%async_computation.2 | async-start | bytes 16896 | tf_op jit(solution)/shard_map/slice | solution.py:1616
  167.0 3.4 copy-start.7
  325.2 72.4 %copy-start.4 = (f32[16,1536]{1,0:T(8,128)S(1)}, f32[16,1536]{1,0:T(8,128)}, u32[]{:S(2)}) copy-start(f32[16,1536]{1,0:T(8,128)} %get-tuple-element.82) | copy-start | bytes 294916
  325.2 72.4 %copy-start.8 = (f32[1,1536]{1,0:T(1,128)S(1)}, f32[1,1536]{1,0:T(1,128)}, u32[]{:S(2)}) copy-start(f32[1,1536]{1,0:T(1,128)} %get-tuple-element.81) | copy-start | bytes 18436
  505.3 11.0 %copy-start.3 = (f32[160,1536]{1,0:T(8,128)S(1)}, f32[160,1536]{1,0:T(8,128)}, u32[]{:S(2)}) copy-start(f32[160,1536]{1,0:T(8,128)} %get-tuple-element.93) | copy-start | bytes 2949124
  509.8 7.4 %copy-start.1 = (bf16[64,1536]{1,0:T(8,128)(2,1)S(1)}, bf16[64,1536]{1,0:T(8,128)(2,1)}, u32[]{:S(2)}) copy-start(bf16[64,1536]{1,0:T(8,128)(2,1)} %param.35) | copy-start | bytes 589828
Sparse Core Ops, SparseCore 0:
  325.3 76.2 reduce-scatter.1
